TPU v7x, 32 devices: a whole 2x2x4 slice. The times are simulated.
32 devices in a mesh: groups: 2 (over y), patch: 4 (over z), sub: 4 (over x, core).
Axes of the slice: x: 2, y: 2, z: 4, core: 2. Of those that a mesh axis runs over, the one named last changes fastest.
Arguments:
- points: float32 [1024, 3, 128], P(('groups', 'patch', 'sub')), parts along dimension 0, may hold values from -3 to 3
- normals: float32 [1024, 3, 128], P(('groups', 'patch', 'sub')), parts along dimension 0, may hold values from -2 to 2
- density: float32 [1024, 128], P(('groups', 'patch', 'sub')), parts along dimension 0
- counts: int32 [32], P(('groups', 'patch', 'sub')), parts along dimension 0, may hold values from 16 to 32, as said below
- near_list: int32 [1024, 9], P(('groups', 'patch', 'sub')), parts along dimension 0, may hold values from 0 to 511, as said below
- leaf_far: int32 [1024, 8], P(('groups', 'patch', 'sub')), parts along dimension 0, may hold values from 0 to 511, as said below
- leaf_basis: float32 [1024, 64, 128], P(('groups', 'patch', 'sub')), parts along dimension 0, may hold values from -0.5 to 0.5
- leaf_to_box_transfer: float32 [1024, 64, 64], P(('groups', 'patch', 'sub')), parts along dimension 0, may hold values from -0.25 to 0.25
- leaf_coupling: float32 [8, 64, 64], replicated, may hold values from -0.25 to 0.25
- box_far: int32 [32, 8], P(('groups', 'patch', 'sub')), parts along dimension 0, may hold values from 0 to 15
- box_coupling: float32 [8, 64, 64], replicated, may hold values from -0.25 to 0.25
Outputs:
- next_basis: float32 [1024, 128], P(('groups', 'patch', 'sub')), parts along dimension 0
- hessenberg: float32 [6, 2], P('groups'), parts along dimension 0
There are 2 independent parts, one for each index of `groups`. A program takes and returns all parts, laid end to end along the dimension named above; an argument that names none is the same for every part. Nothing has to cross between parts.
Inputs may be any that keep to these rules, and one draw needn't show every extreme that they name: `counts`: between 16 and 32 slots of each device are in use; some device of each surface uses all 32. `near_list`: entry 0 of every slot is the slot itself; all entries of a slot not in use are the slot itself. The other entries of a slot in use name slots in use of the same patch. The leaves of one other device that a device's lists name are at most 4, and exactly 4 for some pair of devices in every draw. `leaf_far`: every entry names a slot in use of the same patch.
All inputs are finite; a program needn't handle non-finite values.
Results may differ from a plain program's by a relative error of at most 0.0003.
Values sent between devices are 32-bit elements; how exact they have to be, the bound alone decides.
No kernel may reach another device: no remote copies, remote signals or barrier semaphores. Data moves between devices by JAX's collectives and lax.ppermute only.
A program may use at most 64 MiB of HBM per device.

v0:
```python
import math

import jax
import jax.numpy as jnp
from jax import lax
from jax.sharding import PartitionSpec as P

SOFTEN = 0.05
EPSILON = 1e-06
HIGH_PRECISION = lax.Precision.HIGHEST


def kernel_tile(target, source, normal):
    delta_x = source[:, 0, None, :] - target[:, 0, :, None]
    delta_y = source[:, 1, None, :] - target[:, 1, :, None]
    delta_z = source[:, 2, None, :] - target[:, 2, :, None]
    radius_sq = delta_x * delta_x + delta_y * delta_y + delta_z * delta_z + SOFTEN
    inverse = lax.rsqrt(radius_sq)
    normal_part = (
        delta_x * normal[:, 0, None, :]
        + delta_y * normal[:, 1, None, :]
        + delta_z * normal[:, 2, None, :]
    )
    return normal_part * inverse * inverse * inverse * (0.25 / math.pi)


def shards(
    points,
    normals,
    density,
    counts,
    near_list,
    leaf_far,
    leaf_basis,
    leaf_to_box_transfer,
    leaf_coupling,
    box_far,
    box_coupling,
):
    leaf_slots = points.shape[0]
    leaf_width = points.shape[2]
    neighbours = near_list.shape[1]
    sub_count = lax.axis_size("sub")
    patch_span = leaf_slots * sub_count
    patch_start = lax.axis_index("patch") * patch_span
    in_use = jnp.arange(leaf_slots) < counts[0]
    geometry = jnp.concatenate([points, normals], axis=1).reshape(leaf_slots, 6 * leaf_width)
    near_flat = (near_list - patch_start).reshape(-1)
    gathered = lax.all_gather(geometry, "sub", axis=0, tiled=True)
    source_geometry = gathered[near_flat]

    def fetch_rows(vector):
        return lax.all_gather(vector, "sub", axis=0, tiled=True)[near_flat]

    sources = source_geometry.reshape(leaf_slots, neighbours, 6, leaf_width)

    def near_field(vector):
        values = fetch_rows(vector).reshape(leaf_slots, neighbours, leaf_width)
        summed = jnp.zeros((leaf_slots, leaf_width), jnp.float32)
        for column in range(neighbours):
            block_tile = kernel_tile(points, sources[:, column, :3], sources[:, column, 3:])
            summed = summed + jnp.sum(block_tile * values[:, column, None, :], axis=2)
        return summed

    far_rows = leaf_far - patch_start
    rows_per_box = box_far[0]
    rank_width = leaf_basis.shape[1]

    def operator(vector):
        vector = jnp.where(in_use[:, None], vector, 0.0)
        moments = jnp.einsum("lrp,lp->lr", leaf_basis, vector, precision=HIGH_PRECISION)
        patch_moments = lax.all_gather(moments.reshape(-1), "sub", axis=0, tiled=True).reshape(
            patch_span, rank_width
        )
        local_field = jnp.einsum(
            "krs,lks->lr", leaf_coupling, patch_moments[far_rows], precision=HIGH_PRECISION
        )
        box_moment = jnp.einsum(
            "lrs,ls->r", leaf_to_box_transfer, moments, precision=HIGH_PRECISION
        )
        all_boxes = lax.all_gather(box_moment, ("patch", "sub"), axis=0, tiled=True).reshape(
            -1, rank_width
        )
        box_local_part = jnp.einsum(
            "krs,ks->r", box_coupling, all_boxes[rows_per_box], precision=HIGH_PRECISION
        )
        local_field = local_field + jnp.einsum(
            "idc,d->ic", leaf_to_box_transfer, box_local_part, precision=HIGH_PRECISION
        )
        far_part = jnp.einsum("lrp,lr->lp", leaf_basis, local_field, precision=HIGH_PRECISION)
        return jnp.where(in_use[:, None], 0.5 * vector + near_field(vector) + far_part, 0.0)

    initial = jnp.where(in_use[:, None], density, 0.0)
    square_sum, box_total = lax.psum(
        (jnp.sum(initial * initial), counts[0].astype(jnp.float32)), ("patch", "sub")
    )
    unknowns = leaf_width * box_total
    start_scale = jnp.sqrt(square_sum / unknowns + EPSILON)
    basis_one = initial / start_scale
    one_one = square_sum / (start_scale * start_scale)
    mapped = operator(basis_one)
    along_first, image_sq = lax.psum(
        (jnp.sum(basis_one * mapped), jnp.sum(mapped * mapped)), ("patch", "sub")
    )
    upper_first = along_first / unknowns
    residual_squared = (
        image_sq - 2.0 * upper_first * along_first + upper_first * upper_first * one_one
    )
    lower_first = jnp.sqrt(residual_squared / unknowns + EPSILON)
    basis_two = (mapped - upper_first * basis_one) / lower_first
    one_two = (along_first - upper_first * one_one) / lower_first
    two_two = residual_squared / (lower_first * lower_first)
    mapped = operator(basis_two)
    along_one, along_two, second_sq = lax.psum(
        (jnp.sum(basis_one * mapped), jnp.sum(basis_two * mapped), jnp.sum(mapped * mapped)),
        ("patch", "sub"),
    )
    upper_second = along_one / unknowns
    partial_along = along_two - upper_second * one_two
    middle_second = partial_along / unknowns
    partial_sq = second_sq - 2.0 * upper_second * along_one + upper_second * upper_second * one_one
    final_sq = (
        partial_sq - 2.0 * middle_second * partial_along + middle_second * middle_second * two_two
    )
    mapped = mapped - upper_second * basis_one - middle_second * basis_two
    lower_second = jnp.sqrt(final_sq / unknowns + EPSILON)
    basis_three = mapped / lower_second
    zero_entry = jnp.zeros_like(upper_first)
    hessenberg = jnp.stack(
        [
            jnp.stack([upper_first, upper_second]),
            jnp.stack([lower_first, middle_second]),
            jnp.stack([zero_entry, lower_second]),
        ]
    )
    return (basis_three, hessenberg)


def solution(mesh):
    in_specs = (
        P(("groups", "patch", "sub"), None, None),
        P(("groups", "patch", "sub"), None, None),
        P(("groups", "patch", "sub"), None),
        P(("groups", "patch", "sub")),
        P(("groups", "patch", "sub"), None),
        P(("groups", "patch", "sub"), None),
        P(("groups", "patch", "sub"), None, None),
        P(("groups", "patch", "sub"), None, None),
        P(),
        P(("groups", "patch", "sub"), None),
        P(),
    )
    out_specs = (P(("groups", "patch", "sub"), None), P("groups", None))
    return jax.shard_map(shards, mesh=mesh, in_specs=in_specs, out_specs=out_specs, check_vma=False)
```

profile of v0, /device:TPU:0, one launch (start us, length us, event | category | flops | bytes accessed | tf_op | source)
XLA Modules:
  0.0 261.1 jit_solution(6140912628099046634)
XLA Ops:
  0.7 0.8 broadcast_subtract_fusion
  1.7 0.8 copy_bitcast_fusion
  2.5 7.9 %all_gather.21 = f32[128,768]{1,0:T(8,128)S(1)} all-gather(f32[32,768]{1,0:T(8,128)S(1)} %copy_bitcast_fusion), channel_id=1, replica_groups=mesh['groups'=2,'patch'=4,'sub'=4] {'sub'}, dimensions={0}, use_global_device_ids=true | all-gather | bytes 491520 | tf_op jit(solution)/shard_map/all_gather | solution.py:49
  10.4 1.9 gather_fusion
  14.2 34.3 %all-reduce.4 = (f32[]{:T(128)}, f32[]{:T(128)}) all-reduce(f32[]{:T(128)} %multiply_reduce_fusion.23, f32[]{:T(128)S(6)} %convert_element_type.3), channel_id=1, replica_groups=mesh['groups'=2,'patch'=4,'sub'=4] {'patch','sub'}, use_global_device_ids=true, to_apply=%region_1.2 | all-reduce | flops 2 | bytes 16 | tf_op jit(solution)/shard_map/psum | solution.py:94
  49.8 5.2 %all_gather.22 = f32[128,128]{1,0:T(8,128)S(1)} all-gather(f32[32,128]{1,0:T(8,128)S(1)} %broadcast_select_fusion.1), channel_id=1, replica_groups=mesh['groups'=2,'patch'=4,'sub'=4] {'sub'}, dimensions={0}, use_global_device_ids=true | all-gather | bytes 81920 | tf_op jit(solution)/shard_map/all_gather | solution.py:53
  55.0 1.1 gather_fusion.1
  56.3 4.9 %multiply_reduce_fusion.16 = (f32[32,128]{1,0:T(8,128)}, f32[32,128]{1,0:T(8,128)}) fusion(f32[32,128]{1,0:T(8,128)S(1)} %bitcast.359, f32[32,128]{1,0:T(8,128)S(1)} %bitcast.254, f32[32,128]{1,0:T(8,128)S(1)} %get-tuple-element.133, f32[32,128]{1,0:T(8,128)S(1)} %bitcast.248, f32[32,128]{1,0:T(8,128)S(1)} %bitcast.252, ...), kind=kLoop, calls=%fused_computation.140 | loop fusion | flops 19914752 | bytes 311296 | tf_op jit(solution)/shard_map/reduce_sum | solution.py:62
  61.4 4.9 %multiply_reduce_fusion.17 = (f32[32,128]{1,0:T(8,128)}, f32[32,128]{1,0:T(8,128)}) fusion(f32[32,128]{1,0:T(8,128)S(1)} %bitcast.354, f32[32,128]{1,0:T(8,128)S(1)} %bitcast.290, f32[32,128]{1,0:T(8,128)S(1)} %get-tuple-element.133, f32[32,128]{1,0:T(8,128)S(1)} %bitcast.284, f32[32,128]{1,0:T(8,128)S(1)} %bitcast.288, ...), kind=kLoop, calls=%fused_computation.141 | loop fusion | flops 19914752 | bytes 311296 | tf_op jit(solution)/shard_map/reduce_sum | solution.py:62
  66.6 4.9 %multiply_reduce_fusion.13 = (f32[32,128]{1,0:T(8,128)S(1)}, f32[32,128]{1,0:T(8,128)}) fusion(f32[32,128]{1,0:T(8,128)S(1)} %bitcast.348, f32[32,128]{1,0:T(8,128)S(1)} %bitcast.326, f32[32,128]{1,0:T(8,128)S(1)} %get-tuple-element.133, f32[32,128]{1,0:T(8,128)S(1)} %bitcast.320, f32[32,128]{1,0:T(8,128)S(1)} %bitcast.324, ...), kind=kLoop, calls=%fused_computation.137 | loop fusion | flops 19914752 | bytes 311296 | tf_op jit(solution)/shard_map/reduce_sum | solution.py:62
  71.7 4.3 %multiply_reduce_fusion.11 = (f32[32,128]{1,0:T(8,128)S(1)}, f32[32,128]{1,0:T(8,128)S(1)}) fusion(f32[32,128]{1,0:T(8,128)S(1)} %bitcast.344, f32[32,128]{1,0:T(8,128)S(1)} %bitcast.338, f32[32,128]{1,0:T(8,128)S(1)} %get-tuple-element.133, f32[32,128]{1,0:T(8,128)S(1)} %bitcast.332, f32[32,128]{1,0:T(8,128)S(1)} %bitcast.336, ...), kind=kLoop, calls=%fused_computation.135 | loop fusion | flops 19914752 | bytes 311296 | tf_op jit(solution)/shard_map/reduce_sum | solution.py:62
  76.2 2.7 %multiply_reduce_fusion.9 = f32[32,128]{1,0:T(8,128)S(1)} fusion(f32[32,128]{1,0:T(8,128)S(1)} %bitcast.342, f32[32,128]{1,0:T(8,128)S(1)} %bitcast.302, f32[32,128]{1,0:T(8,128)S(1)} %get-tuple-element.133, f32[32,128]{1,0:T(8,128)S(1)} %bitcast.296, f32[32,128]{1,0:T(8,128)S(1)} %bitcast.300, f32[32,128]{1,0:T(8,128)S(1)} %get-tuple-element.134, ...), kind=kLoop, calls=%fused_computation.133 | loop fusion | flops 9957376 | bytes 180224 | tf_op jit(solution)/shard_map/reduce_sum | solution.py:62
  79.0 1.7 fusion.80
  80.8 5.2 %all_gather.23 = f32[8192]{0:T(1024)S(1)} all-gather(f32[2048]{0:T(1024)S(1)} %reshape.140), channel_id=1, replica_groups=mesh['groups'=2,'patch'=4,'sub'=4] {'sub'}, dimensions={0}, use_global_device_ids=true | all-gather | bytes 40960 | tf_op jit(solution)/shard_map/all_gather | solution.py:72
  87.1 0.9 convolution_bitcast_fusion.3
  89.6 29.9 %all-reduce = f32[1024]{0:T(1024)S(1)} all-reduce(f32[1024]{0:T(1024)S(1)} %dynamic-update-slice), channel_id=1, replica_groups=mesh['groups'=2,'patch'=4,'sub'=4] {'patch','sub'}, use_global_device_ids=true, to_apply=%add | all-reduce | flops 1024 | bytes 8192
  121.5 1.0 fusion.82
  123.2 30.1 %all-reduce.3 = (f32[]{:T(128)}, f32[]{:T(128)}) all-reduce(f32[]{:T(128)} %get-tuple-element.30, f32[]{:T(128)} %get-tuple-element.29), channel_id=1, replica_groups=mesh['groups'=2,'patch'=4,'sub'=4] {'patch','sub'}, use_global_device_ids=true, to_apply=%region_15.16 | all-reduce | flops 2 | bytes 16 | tf_op jit(solution)/shard_map/psum | solution.py:102
  156.0 5.2 %all_gather.25 = f32[128,128]{1,0:T(8,128)S(1)} all-gather(f32[32,128]{1,0:T(8,128)S(1)} %get-tuple-element.39), channel_id=1, replica_groups=mesh['groups'=2,'patch'=4,'sub'=4] {'sub'}, dimensions={0}, use_global_device_ids=true | all-gather | bytes 81920 | tf_op jit(solution)/shard_map/all_gather | solution.py:53
  161.3 1.1 gather_fusion.4
  162.7 5.1 %multiply_reduce_fusion.7 = (f32[32,128]{1,0:T(8,128)S(1)}, f32[32,128]{1,0:T(8,128)S(1)}) fusion(f32[32,128]{1,0:T(8,128)S(1)} %bitcast.357, f32[32,128]{1,0:T(8,128)S(1)} %bitcast.255, f32[32,128]{1,0:T(8,128)} %copy-done.69, f32[32,128]{1,0:T(8,128)S(1)} %bitcast.249, f32[32,128]{1,0:T(8,128)S(1)} %bitcast.253, f32[32,128]{1,0:T(8,128)} %copy-done.71, ...), kind=kLoop, calls=%fused_computation.131 | loop fusion | flops 19914752 | bytes 311296 | tf_op jit(solution)/shard_map/reduce_sum | solution.py:62
  167.9 2.7 %multiply_reduce_fusion.3 = f32[32,128]{1,0:T(8,128)S(1)} fusion(f32[32,128]{1,0:T(8,128)S(1)} %bitcast.355, f32[32,128]{1,0:T(8,128)S(1)} %bitcast.315, f32[32,128]{1,0:T(8,128)S(1)} %copy-done.70, f32[32,128]{1,0:T(8,128)S(1)} %bitcast.309, f32[32,128]{1,0:T(8,128)S(1)} %bitcast.313, f32[32,128]{1,0:T(8,128)S(1)} %copy-done.72, ...), kind=kLoop, calls=%fused_computation.127 | loop fusion | flops 9957376 | bytes 180224 | tf_op jit(solution)/shard_map/reduce_sum | solution.py:62
  170.7 4.3 %multiply_reduce_fusion.4 = (f32[32,128]{1,0:T(8,128)S(1)}, f32[32,128]{1,0:T(8,128)S(1)}) fusion(f32[32,128]{1,0:T(8,128)S(1)} %bitcast.352, f32[32,128]{1,0:T(8,128)S(1)} %bitcast.327, f32[32,128]{1,0:T(8,128)S(1)} %copy-done.70, f32[32,128]{1,0:T(8,128)S(1)} %bitcast.321, f32[32,128]{1,0:T(8,128)S(1)} %bitcast.325, f32[32,128]{1,0:T(8,128)S(1)} %copy-done.72, ...), kind=kLoop, calls=%fused_computation.128 | loop fusion | flops 19914752 | bytes 311296 | tf_op jit(solution)/shard_map/reduce_sum | solution.py:62
  175.1 4.3 %multiply_reduce_fusion.5 = (f32[32,128]{1,0:T(8,128)S(1)}, f32[32,128]{1,0:T(8,128)S(1)}) fusion(f32[32,128]{1,0:T(8,128)S(1)} %bitcast.350, f32[32,128]{1,0:T(8,128)S(1)} %bitcast.267, f32[32,128]{1,0:T(8,128)S(1)} %copy-done.70, f32[32,128]{1,0:T(8,128)S(1)} %bitcast.261, f32[32,128]{1,0:T(8,128)S(1)} %bitcast.265, f32[32,128]{1,0:T(8,128)S(1)} %copy-done.72, ...), kind=kLoop, calls=%fused_computation.129 | loop fusion | flops 19914752 | bytes 311296 | tf_op jit(solution)/shard_map/reduce_sum | solution.py:62
  179.4 4.3 %multiply_reduce_fusion.6 = (f32[32,128]{1,0:T(8,128)S(1)}, f32[32,128]{1,0:T(8,128)S(1)}) fusion(f32[32,128]{1,0:T(8,128)S(1)} %bitcast.346, f32[32,128]{1,0:T(8,128)S(1)} %bitcast.243, f32[32,128]{1,0:T(8,128)S(1)} %copy-done.70, f32[32,128]{1,0:T(8,128)S(1)} %bitcast.237, f32[32,128]{1,0:T(8,128)S(1)} %bitcast.241, f32[32,128]{1,0:T(8,128)S(1)} %copy-done.72, ...), kind=kLoop, calls=%fused_computation.130 | loop fusion | flops 19914752 | bytes 311296 | tf_op jit(solution)/shard_map/reduce_sum | solution.py:62
  183.7 1.7 fusion.83
  185.5 5.2 %all_gather.26 = f32[8192]{0:T(1024)S(1)} all-gather(f32[2048]{0:T(1024)S(1)} %reshape.144), channel_id=1, replica_groups=mesh['groups'=2,'patch'=4,'sub'=4] {'sub'}, dimensions={0}, use_global_device_ids=true | all-gather | bytes 40960 | tf_op jit(solution)/shard_map/all_gather | solution.py:72
  191.5 0.9 convolution_bitcast_fusion.2
  192.6 29.8 %all-reduce.1 = f32[1024]{0:T(1024)S(1)} all-reduce(f32[1024]{0:T(1024)S(1)} %dynamic-update-slice.1), channel_id=1, replica_groups=mesh['groups'=2,'patch'=4,'sub'=4] {'patch','sub'}, use_global_device_ids=true, to_apply=%add.1 | all-reduce | flops 1024 | bytes 8192
  224.3 1.0 fusion.85
  225.2 0.8 multiply_reduce_fusion.19
  226.0 30.2 %all-reduce.2 = (f32[]{:T(128)}, f32[]{:T(128)}, f32[]{:T(128)}) all-reduce(f32[]{:T(128)} %get-tuple-element.27, f32[]{:T(128)} %get-tuple-element.28, f32[]{:T(128)} %get-tuple-element.26), channel_id=1, replica_groups=mesh['groups'=2,'patch'=4,'sub'=4] {'patch','sub'}, use_global_device_ids=true, to_apply=%region_30.31 | all-reduce | flops 3 | bytes 24 | tf_op jit(solution)/shard_map/psum | solution.py:114
  (210 shorter events, 11.9 us)
Async XLA Ops:
  0.6 78.4 %copy-start = (f32[32,64,128]{2,1,0:T(8,128)S(1)}, f32[32,64,128]{2,1,0:T(8,128)}, u32[]{:S(2)}) copy-start(f32[32,64,128]{2,1,0:T(8,128)} %param.17) | copy-start | bytes 3145732
  12.7 43.5 %copy-start.5 = (f32[32,3,128]{2,0,1:T(8,128)S(1)}, f32[32,3,128]{2,0,1:T(8,128)}, u32[]{:S(2)}) copy-start(f32[32,3,128]{2,0,1:T(8,128)} %param.11) | copy-start | bytes 147460
  56.3 19.9 %copy-start.67 = (f32[32,128]{1,0:T(8,128)}, f32[32,128]{1,0:T(8,128)S(1)}, u32[]{:S(2)}) copy-start(f32[32,128]{1,0:T(8,128)S(1)} %get-tuple-element.132) | copy-start | bytes 49156
  56.3 19.9 %copy-start.69 = (f32[32,128]{1,0:T(8,128)}, f32[32,128]{1,0:T(8,128)S(1)}, u32[]{:S(2)}) copy-start(f32[32,128]{1,0:T(8,128)S(1)} %get-tuple-element.133) | copy-start | bytes 49156
  56.3 19.9 %copy-start.71 = (f32[32,128]{1,0:T(8,128)}, f32[32,128]{1,0:T(8,128)S(1)}, u32[]{:S(2)}) copy-start(f32[32,128]{1,0:T(8,128)S(1)} %get-tuple-element.134) | copy-start | bytes 49156
  61.4 14.7 %copy-start.8 = (f32[32,1,128]{2,1,0:T(1,128)}, f32[32,1,128]{2,1,0:T(1,128)S(1)}, u32[]{:S(2)}) copy-start(f32[32,1,128]{2,1,0:T(1,128)S(1)} %get-tuple-element.96) | copy-start | bytes 49156
  61.4 14.7 %copy-start.9 = (f32[32,1,128]{2,1,0:T(1,128)}, f32[32,1,128]{2,1,0:T(1,128)S(1)}, u32[]{:S(2)}) copy-start(f32[32,1,128]{2,1,0:T(1,128)S(1)} %get-tuple-element.97) | copy-start | bytes 49156
  61.4 14.7 %copy-start.10 = (f32[32,1,128]{2,1,0:T(1,128)}, f32[32,1,128]{2,1,0:T(1,128)S(1)}, u32[]{:S(2)}) copy-start(f32[32,1,128]{2,1,0:T(1,128)S(1)} %get-tuple-element.98) | copy-start | bytes 49156
  61.4 14.7 %copy-start.11 = (f32[32,1,128]{2,1,0:T(1,128)}, f32[32,1,128]{2,1,0:T(1,128)S(1)}, u32[]{:S(2)}) copy-start(f32[32,1,128]{2,1,0:T(1,128)S(1)} %get-tuple-element.144) | copy-start | bytes 49156
  76.1 10.1 %copy-start.16 = (f32[32,1,128]{2,1,0:T(1,128)}, f32[32,1,128]{2,1,0:T(1,128)S(1)}, u32[]{:S(2)}) copy-start(f32[32,1,128]{2,1,0:T(1,128)S(1)} %get-tuple-element.127) | copy-start | bytes 49156
  76.2 10.1 %copy-start.18 = (f32[32,1,128]{2,1,0:T(1,128)}, f32[32,1,128]{2,1,0:T(1,128)S(1)}, u32[]{:S(2)}) copy-start(f32[32,1,128]{2,1,0:T(1,128)S(1)} %get-tuple-element.128) | copy-start | bytes 49156
  76.2 10.1 %copy-start.20 = (f32[32,1,128]{2,1,0:T(1,128)}, f32[32,1,128]{2,1,0:T(1,128)S(1)}, u32[]{:S(2)}) copy-start(f32[32,1,128]{2,1,0:T(1,128)S(1)} %get-tuple-element.159) | copy-start | bytes 49156
  76.2 10.1 %copy-start.22 = (f32[32,1,128]{2,1,0:T(1,128)}, f32[32,1,128]{2,1,0:T(1,128)S(1)}, u32[]{:S(2)}) copy-start(f32[32,1,128]{2,1,0:T(1,128)S(1)} %get-tuple-element.160) | copy-start | bytes 49156
  76.2 10.9 %copy-start.14 = (f32[32,1,128]{2,1,0:T(1,128)}, f32[32,1,128]{2,1,0:T(1,128)S(1)}, u32[]{:S(2)}) copy-start(f32[32,1,128]{2,1,0:T(1,128)S(1)} %get-tuple-element.126) | copy-start | bytes 49156
  76.2 10.9 %copy-start.24 = (f32[32,1,128]{2,1,0:T(1,128)}, f32[32,1,128]{2,1,0:T(1,128)S(1)}, u32[]{:S(2)}) copy-start(f32[32,1,128]{2,1,0:T(1,128)S(1)} %get-tuple-element.161) | copy-start | bytes 49156
  76.2 9.9 %copy-start.73 = (s32[32,8]{0,1:T(8,128)S(1)}, s32[32,8]{0,1:T(8,128)}, u32[]{:S(2)}) copy-start(s32[32,8]{0,1:T(8,128)} %param.16) | copy-start | bytes 3076
  79.0 8.1 %copy-start.1 = (f32[32,64,64]{2,1,0:T(8,128)S(1)}, f32[32,64,64]{2,1,0:T(8,128)}, u32[]{:S(2)}) copy-start(f32[32,64,64]{2,1,0:T(8,128)} %param.18) | copy-start | bytes 1572868
  86.1 33.5 %copy-start.74 = (s32[1,8]{1,0:T(1,128)S(1)}, s32[1,8]{1,0:T(1,128)}, u32[]{:S(2)}) copy-start(s32[1,8]{1,0:T(1,128)} %param.20) | copy-start | bytes 100
  86.3 33.8 %copy-start.2 = (f32[8,64,64]{2,1,0:T(8,128)S(1)}, f32[8,64,64]{2,1,0:T(8,128)}, u32[]{:S(2)}) copy-start(f32[8,64,64]{2,1,0:T(8,128)} %param.21) | copy-start | bytes 393220
  87.1 34.0 %copy-start.3 = (f32[8,64,64]{2,1,0:T(8,128)S(1)}, f32[8,64,64]{2,1,0:T(8,128)}, u32[]{:S(2)}) copy-start(f32[8,64,64]{2,1,0:T(8,128)} %param.19) | copy-start | bytes 393220
  162.6 8.0 %copy-start.39 = (f32[32,1,128]{2,1,0:T(1,128)S(1)}, f32[32,1,128]{2,1,0:T(1,128)}, u32[]{:S(2)}) copy-start(f32[32,1,128]{2,1,0:T(1,128)} %copy-done.38) | copy-start | bytes 49156
  162.6 8.0 %copy-start.41 = (f32[32,1,128]{2,1,0:T(1,128)S(1)}, f32[32,1,128]{2,1,0:T(1,128)}, u32[]{:S(2)}) copy-start(f32[32,1,128]{2,1,0:T(1,128)} %copy-done.40) | copy-start | bytes 49156
  162.6 8.0 %copy-start.43 = (f32[32,1,128]{2,1,0:T(1,128)S(1)}, f32[32,1,128]{2,1,0:T(1,128)}, u32[]{:S(2)}) copy-start(f32[32,1,128]{2,1,0:T(1,128)} %copy-done.42) | copy-start | bytes 49156
  162.6 8.0 %copy-start.45 = (f32[32,1,128]{2,1,0:T(1,128)S(1)}, f32[32,1,128]{2,1,0:T(1,128)}, u32[]{:S(2)}) copy-start(f32[32,1,128]{2,1,0:T(1,128)} %copy-done.44) | copy-start | bytes 49156
  162.7 8.0 %copy-start.47 = (f32[32,1,128]{2,1,0:T(1,128)S(1)}, f32[32,1,128]{2,1,0:T(1,128)}, u32[]{:S(2)}) copy-start(f32[32,1,128]{2,1,0:T(1,128)} %copy-done.46) | copy-start | bytes 49156
  162.7 8.0 %copy-start.49 = (f32[32,1,128]{2,1,0:T(1,128)S(1)}, f32[32,1,128]{2,1,0:T(1,128)}, u32[]{:S(2)}) copy-start(f32[32,1,128]{2,1,0:T(1,128)} %copy-done.48) | copy-start | bytes 49156
  162.7 8.0 %copy-start.51 = (f32[32,1,128]{2,1,0:T(1,128)S(1)}, f32[32,1,128]{2,1,0:T(1,128)}, u32[]{:S(2)}) copy-start(f32[32,1,128]{2,1,0:T(1,128)} %copy-done.50) | copy-start | bytes 49156
  162.7 8.0 %copy-start.53 = (f32[32,1,128]{2,1,0:T(1,128)S(1)}, f32[32,1,128]{2,1,0:T(1,128)}, u32[]{:S(2)}) copy-start(f32[32,1,128]{2,1,0:T(1,128)} %copy-done.52) | copy-start | bytes 49156
  162.7 8.0 %copy-start.55 = (f32[32,1,128]{2,1,0:T(1,128)S(1)}, f32[32,1,128]{2,1,0:T(1,128)}, u32[]{:S(2)}) copy-start(f32[32,1,128]{2,1,0:T(1,128)} %copy-done.54) | copy-start | bytes 49156
  162.7 8.0 %copy-start.57 = (f32[32,1,128]{2,1,0:T(1,128)S(1)}, f32[32,1,128]{2,1,0:T(1,128)}, u32[]{:S(2)}) copy-start(f32[32,1,128]{2,1,0:T(1,128)} %copy-done.56) | copy-start | bytes 49156
  162.7 8.0 %copy-start.59 = (f32[32,1,128]{2,1,0:T(1,128)S(1)}, f32[32,1,128]{2,1,0:T(1,128)}, u32[]{:S(2)}) copy-start(f32[32,1,128]{2,1,0:T(1,128)} %copy-done.58) | copy-start | bytes 49156
  162.7 8.0 %copy-start.61 = (f32[32,1,128]{2,1,0:T(1,128)S(1)}, f32[32,1,128]{2,1,0:T(1,128)}, u32[]{:S(2)}) copy-start(f32[32,1,128]{2,1,0:T(1,128)} %copy-done.60) | copy-start | bytes 49156
  (44 other events, 209.6 us)
where the time goes:
time: 262 us; the launch traced here: 261 us
  blocking collectives  183 us (70%)
  other arithmetic  47.3 us (18%)
  local copies, waits for them, and re-layouts  10.5 us (4%)
  between operations  10.5 us (4%)
  matrix products  9.72 us (4%)
    unnamed x2, blocking collectives  59.7 us
    reduce_sum x10, other arithmetic, near_field(): summed = summed + jnp.sum(block_tile * values[:, column, None, :], axis=2)  42.1 us
    psum x1, blocking collectives, shards(): lax.psum((jnp.sum(initial * initial), counts[0].astype(jnp.float32)), ('p...  34.3 us
    psum x1, blocking collectives, shards(): lax.psum((jnp.sum(basis_one * mapped), jnp.sum(basis_two * mapped), jnp.s...  30.2 us
    psum x1, blocking collectives, shards(): lax.psum((jnp.sum(basis_one * mapped), jnp.sum(mapped * mapped)), ('patch...  30.1 us
    all_gather x2, blocking collectives, fetch_rows(): return lax.all_gather(vector, 'sub', axis=0, tiled=True)[near_flat]  10.5 us
    all_gather x2, blocking collectives, operator(): lax.all_gather(moments.reshape(-1), 'sub', axis=0, tiled=True)  10.4 us
    all_gather x1, blocking collectives, shards(): gathered = lax.all_gather(geometry, 'sub', axis=0, tiled=True)  7.89 us

commit v1 on v0

v1 whole, which is shorter than its diff:
```python
import math

import jax
import jax.numpy as jnp
from jax import lax
from jax.sharding import PartitionSpec as P

SOFTEN = 0.05
EPSILON = 1e-06
HIGH_PRECISION = lax.Precision.HIGHEST


def from_peers(value, axis):
    size = lax.axis_size(axis)
    arrived = [
        lax.ppermute(value, axis, [(i, i ^ turn) for i in range(size)]) for turn in range(1, size)
    ]
    return [value] + arrived


def place_of(owner, axis):
    return lax.axis_index(axis) ^ owner


def tree_sum(parts):
    while len(parts) > 1:
        parts = [parts[i] + parts[i + 1] for i in range(0, len(parts), 2)]
    return parts[0]


def kernel_tile(target, source, normal):
    delta_x = source[:, 0, None, :] - target[:, 0, :, None]
    delta_y = source[:, 1, None, :] - target[:, 1, :, None]
    delta_z = source[:, 2, None, :] - target[:, 2, :, None]
    radius_sq = delta_x * delta_x + delta_y * delta_y + delta_z * delta_z + SOFTEN
    inverse = lax.rsqrt(radius_sq)
    normal_part = (
        delta_x * normal[:, 0, None, :]
        + delta_y * normal[:, 1, None, :]
        + delta_z * normal[:, 2, None, :]
    )
    return normal_part * inverse * inverse * inverse * (0.25 / math.pi)


def shards(
    points,
    normals,
    density,
    counts,
    near_list,
    leaf_far,
    leaf_basis,
    leaf_to_box_transfer,
    leaf_coupling,
    box_far,
    box_coupling,
):
    leaf_slots = points.shape[0]
    leaf_width = points.shape[2]
    rank_width = leaf_basis.shape[1]
    neighbours = near_list.shape[1]
    sub_count = lax.axis_size("sub")
    patch_start = lax.axis_index("patch") * (leaf_slots * sub_count)
    in_use = (jnp.arange(leaf_slots) < counts[0])[:, None]

    def row_of(leaf):
        leaf = leaf - patch_start
        return place_of(leaf // leaf_slots, "sub") * leaf_slots + leaf % leaf_slots

    near_rows = row_of(near_list)
    far_rows = row_of(leaf_far)
    box_rows = (
        place_of(box_far[0] // sub_count, "patch") * sub_count
        + box_far[0] % sub_count
    )

    initial = jnp.where(in_use, density, 0.0)
    geometry = jnp.concatenate([points, normals, initial[:, None]], axis=1)
    gathered = jnp.concatenate(from_peers(geometry, "sub"), axis=0)
    sources = gathered[near_rows]

    def near_field(values):
        summed = jnp.zeros((leaf_slots, leaf_width), jnp.float32)
        for column in range(neighbours):
            tile = kernel_tile(points, sources[:, column, :3], sources[:, column, 3:6])
            summed = summed + jnp.sum(tile * values[:, column, None, :], axis=2)
        return summed

    def coefficients(vector, sums):
        moments = jnp.einsum("lrp,lp->lr", leaf_basis, vector, precision=HIGH_PRECISION)
        box_moment = jnp.einsum(
            "lrs,ls->r", leaf_to_box_transfer, moments, precision=HIGH_PRECISION
        )
        row = jnp.zeros((rank_width,), jnp.float32).at[: len(sums)].set(jnp.stack(sums))
        message = jnp.concatenate([moments, box_moment[None], row[None]], axis=0)
        parts = from_peers(message, "sub")
        patch_moments = jnp.concatenate([part[:leaf_slots] for part in parts], axis=0)
        stacked = jnp.stack([part[leaf_slots] for part in parts])
        order = place_of(jnp.arange(sub_count), "sub")
        summed = tree_sum([part[leaf_slots + 1] for part in parts])
        parts = from_peers(jnp.concatenate([stacked[order], summed[None]], axis=0), "patch")
        all_boxes = jnp.concatenate([part[:sub_count] for part in parts], axis=0)
        return patch_moments, all_boxes, tree_sum([part[sub_count] for part in parts])

    def far_field(patch_moments, all_boxes):
        local_field = jnp.einsum(
            "krs,lks->lr", leaf_coupling, patch_moments[far_rows], precision=HIGH_PRECISION
        )
        box_local_part = jnp.einsum(
            "krs,ks->r", box_coupling, all_boxes[box_rows], precision=HIGH_PRECISION
        )
        local_field = local_field + jnp.einsum(
            "idc,d->ic", leaf_to_box_transfer, box_local_part, precision=HIGH_PRECISION
        )
        return jnp.einsum("lrp,lr->lp", leaf_basis, local_field, precision=HIGH_PRECISION)

    patch_moments, all_boxes, sums = coefficients(
        initial, [jnp.sum(initial * initial), counts[0].astype(jnp.float32)]
    )
    square_sum, unknowns = sums[0], leaf_width * sums[1]
    start_scale = jnp.sqrt(square_sum / unknowns + EPSILON)
    near = near_field(sources[:, :, 6])
    image = jnp.where(in_use, near + far_field(patch_moments, all_boxes), 0.0) / start_scale
    basis_one = initial / start_scale
    one_one = square_sum / (start_scale * start_scale)

    rows = jnp.concatenate(from_peers(image, "sub"), axis=0)
    patch_moments, all_boxes, sums = coefficients(
        image, [jnp.sum(basis_one * image), jnp.sum(image * image)]
    )
    along, image_sq = sums[0], sums[1]
    near = near_field(rows[near_rows])
    second = jnp.where(in_use, near + far_field(patch_moments, all_boxes), 0.0)

    upper_first = 0.5 * one_one / unknowns + along / unknowns
    shift = upper_first - 0.5
    residual_squared = image_sq - 2.0 * shift * along + shift * shift * one_one
    lower_first = jnp.sqrt(residual_squared / unknowns + EPSILON)
    basis_two = (image - shift * basis_one) / lower_first
    one_two = (along - shift * one_one) / lower_first
    two_two = residual_squared / (lower_first * lower_first)
    image_two = (second - shift * image) / lower_first

    partial = jnp.stack(
        [
            jnp.sum(basis_one * image_two),
            jnp.sum(basis_two * image_two),
            jnp.sum(image_two * image_two),
        ]
    )
    partial = jnp.zeros((8, 128), jnp.float32).at[0, :3].set(partial)
    partial = tree_sum(from_peers(partial, "sub"))
    partial = tree_sum(from_peers(partial, "patch"))
    k_one, k_two, k_sq = partial[0, 0], partial[0, 1], partial[0, 2]
    upper_second = (0.5 * one_two + k_one) / unknowns
    first_part = upper_second
    middle_second = (0.5 * two_two + k_two - upper_second * one_two) / unknowns
    second_part = middle_second - 0.5
    final_sq = (
        k_sq
        - 2.0 * first_part * k_one
        - 2.0 * second_part * k_two
        + first_part * first_part * one_one
        + 2.0 * first_part * second_part * one_two
        + second_part * second_part * two_two
    )
    lower_second = jnp.sqrt(final_sq / unknowns + EPSILON)
    basis_three = (
        image_two - first_part * basis_one - second_part * basis_two
    ) / lower_second
    zero_entry = jnp.zeros_like(upper_first)
    hessenberg = jnp.stack(
        [
            jnp.stack([upper_first, upper_second]),
            jnp.stack([lower_first, middle_second]),
            jnp.stack([zero_entry, lower_second]),
        ]
    )
    return (basis_three, hessenberg)


def solution(mesh):
    in_specs = (
        P(("groups", "patch", "sub"), None, None),
        P(("groups", "patch", "sub"), None, None),
        P(("groups", "patch", "sub"), None),
        P(("groups", "patch", "sub")),
        P(("groups", "patch", "sub"), None),
        P(("groups", "patch", "sub"), None),
        P(("groups", "patch", "sub"), None, None),
        P(("groups", "patch", "sub"), None, None),
        P(),
        P(("groups", "patch", "sub"), None),
        P(),
    )
    out_specs = (P(("groups", "patch", "sub"), None), P("groups", None))
    return jax.shard_map(shards, mesh=mesh, in_specs=in_specs, out_specs=out_specs, check_vma=False)
```

time: 262 us -> 127 us (0.48)
  blocking collectives: 183 us -> 0 us
  starting transfers between devices: 0 us -> 24.3 us
  waiting for transfers between devices: 0 us -> 11.5 us
  local copies, waits for them, and re-layouts: 10.5 us -> 17.4 us
  other arithmetic: 47.3 us -> 52.3 us
    psum x3 -> x0, blocking collectives: 94.6 us -> none  [the longest x1 34.3 us: shards(): lax.psum((jnp.sum(initial * initial), counts[0].astype(jnp.float32)), ('p...]
    unnamed x2 -> x0, blocking collectives: 59.7 us -> none
    all_gather x5 -> x0, blocking collectives: 28.7 us -> none  [the longest x2 10.5 us: fetch_rows(): return lax.all_gather(vector, 'sub', axis=0, tiled=True)[near_flat]]
    ppermute x0 -> x24, starting transfers between devices: none -> 24.3 us  [from_peers(): lax.ppermute(value, axis, [(i, i ^ turn) for i in range(size)])]
    ppermute x0 -> x24, waiting for transfers between devices: none -> 11.5 us  [from_peers(): lax.ppermute(value, axis, [(i, i ^ turn) for i in range(size)])]
    slice x0 -> x24, local copies, waits for them, and re-layouts: none -> 3.43 us  [the longest x2 1.44 us: shards(): near = near_field(sources[:, :, 6])]
    reduce_sum x12, other arithmetic: 43.6 us -> 40.9 us  [the longest x10 39.4 us: near_field(): summed = summed + jnp.sum(tile * values[:, column, None, :], axis=2)]
    gather x7 -> x9, local copies, waits for them, and re-layouts: 6.54 us -> 7.56 us  [the longest x1 2.57 us: shards(): sources = gathered[near_rows]]
  transfers between devices with their start and end apart: 0 -> 24, of which waited for: 0 -> 9; matrix products, arithmetic and copies ran while one was open for 0% -> 14% of each run, Pallas kernels for 0% -> 0%
where the time goes in v1:
time: 127 us
  other arithmetic  52.3 us (41%)
  starting transfers between devices  24.3 us (19%)
  local copies, waits for them, and re-layouts  17.4 us (14%)
  waiting for transfers between devices  11.5 us (9%)
  between operations  11.2 us (9%)
  matrix products  9.79 us (8%)
    reduce_sum x10, other arithmetic, near_field(): summed = summed + jnp.sum(tile * values[:, column, None, :], axis=2)  39.4 us
    ppermute x24, starting transfers between devices, from_peers(): lax.ppermute(value, axis, [(i, i ^ turn) for i in range(size)])  24.3 us
    ppermute x24, waiting for transfers between devices, from_peers(): lax.ppermute(value, axis, [(i, i ^ turn) for i in range(size)])  11.5 us
    dot_general x2, matrix products, coefficients(): jnp.einsum('lrp,lp->lr', leaf_basis, vector, precision=HIGH_PRECISION)  3.47 us
    unnamed x145, local copies, waits for them, and re-layouts  2.64 us
    gather x1, local copies, waits for them, and re-layouts, shards(): sources = gathered[near_rows]  2.57 us
  transfers between devices with their start and end apart: 24, of which 9 were waited for; matrix products, arithmetic and copies ran while one was open for 14% of the time, Pallas kernels for 0%

profile of v1, /device:TPU:0, one launch (start us, length us, event | category | flops | bytes accessed | tf_op | source)
XLA Modules:
  0.0 126.5 jit_solution(7249611757093958830)
XLA Ops:
  3.1 1.4 %multiply_reduce_fusion.23 = (f32[]{:T(128)}, f32[32,128]{1,0:T(8,128)S(1)}) fusion(f32[32,128]{1,0:T(8,128)} %param.19, pred[32]{0:T(512)(128)(4,1)S(1)} %iota_compare_fusion.1), kind=kLoop, calls=%fused_computation.219 | loop fusion | flops 12287 | bytes 32804 | tf_op jit(solution)/shard_map/reduce_sum | solution.py:118
  5.1 2.6 %collective-permute-start.1 = (f32[32,7,128]{2,1,0:T(8,128)S(1)}, f32[32,7,128]{2,1,0:T(8,128)}, u32[]{:S(2)}, u32[]{:S(2)}) collective-permute-start(f32[32,7,128]{2,1,0:T(8,128)S(1)} %pad_maximum_fusion.1), channel_id=1, source_target_pairs={{0,2},{1,3},{2,0},{3,1},{4,6},{5,7},{6,4},{7,5},{8,10},{9,11},{10,... | collective-permute-start | bytes 344072 | tf_op jit(solution)/shard_map/ppermute | solution.py:16
  7.7 1.7 %fusion.120 = f32[32,1,64]{2,1,0:T(1,128)S(1)} fusion(f32[32,128,1]{1,2,0:T(1,128)S(1)} %bitcast.328, f32[32,64,128]{2,1,0:T(8,128)S(1)} %copy-done), kind=kOutput, calls=%fused_computation.328 | convolution fusion | flops 3145728 | bytes 1073152 | tf_op jit(solution)/shard_map/lrp,lp->lr/dot_general | solution.py:90
  11.5 1.4 %collective-permute-start.5 = (f32[34,64]{1,0:T(8,128)S(1)}, f32[34,64]{1,0:T(8,128)S(1)}, u32[]{:S(2)}, u32[]{:S(2)}) collective-permute-start(f32[34,64]{1,0:T(8,128)S(1)} %select_maximum_fusion.1), channel_id=1, source_target_pairs={{0,3},{1,2},{2,1},{3,0},{4,7},{5,6},{6,5},{7,4},{8,11},{9,10},{10,... | collective-permute-start | bytes 26120 | tf_op jit(solution)/shard_map/ppermute | solution.py:16
  16.3 1.8 %collective-permute-start.6 = (f32[5,64]{1,0:T(8,128)S(1)}, f32[5,64]{1,0:T(8,128)S(1)}, u32[]{:S(2)}, u32[]{:S(2)}) collective-permute-start(f32[5,64]{1,0:T(8,128)S(1)} %pad_maximum_fusion.7), channel_id=1, source_target_pairs={{0,4},{4,0},{8,12},{12,8},{1,5},{5,1},{9,13},{13,9},{2,6},{6,2},{1... | collective-permute-start | bytes 3848 | tf_op jit(solution)/shard_map/ppermute | solution.py:16
  18.1 2.6 %collective-permute-start.7 = (f32[5,64]{1,0:T(8,128)S(1)}, f32[5,64]{1,0:T(8,128)S(1)}, u32[]{:S(2)}, u32[]{:S(2)}) collective-permute-start(f32[5,64]{1,0:T(8,128)S(1)} %pad_maximum_fusion.7), channel_id=1, source_target_pairs={{0,8},{4,12},{8,0},{12,4},{1,9},{5,13},{9,1},{13,5},{2,10},{6,14},... | collective-permute-start | bytes 3848 | tf_op jit(solution)/shard_map/ppermute | solution.py:16
  22.6 3.5 %collective-permute-done.8 = f32[5,64]{1,0:T(8,128)S(1)} collective-permute-done((f32[5,64]{1,0:T(8,128)S(1)}, f32[5,64]{1,0:T(8,128)S(1)}, u32[]{:S(2)}, u32[]{:S(2)}) %collective-permute-start.8) | collective-permute-done | bytes 1312 | tf_op jit(solution)/shard_map/ppermute | solution.py:16
  31.9 2.6 %gather_fusion = f32[288,7,128]{2,1,0:T(8,128)} fusion(f32[128,7,128]{2,1,0:T(8,128)S(1)} %pad_maximum_fusion, s32[1024]{0:T(1024)S(1)} %pad_clamp_fusion.3), kind=kCustom, calls=%fused_computation | custom fusion | bytes 2065536 | tf_op jit(solution)/shard_map/gather | solution.py:80
  34.5 2.0 %slice_bitcast_fusion.13 = (f32[32,3,128]{2,1,0:T(4,128)S(1)}, f32[32,3,128]{2,1,0:T(4,128)S(1)}, f32[32,3,128]{2,1,0:T(4,128)S(1)}, f32[32,3,128]{2,1,0:T(4,128...) fusion(f32[32,9,7,128]{3,2,1,0:T(8,128)} %bitcast.325), kind=kLoop, calls=%fused_computation.169 | loop fusion | bytes 1769472 | tf_op jit(solution)/shard_map/squeeze | solution.py:85
  36.5 1.4 %slice.714 = f32[32,9,1,128]{3,2,1,0:T(1,128)S(1)} slice(f32[32,9,7,128]{3,2,1,0:T(8,128)} %bitcast.326), slice={[0:32], [0:9], [6:7], [0:128]} | slice | bytes 294912 | tf_op jit(solution)/shard_map/slice | solution.py:122
  39.0 2.7 %multiply_reduce_fusion.9 = f32[32,128]{1,0:T(8,128)S(1)} fusion(f32[32,128]{1,0:T(8,128)S(1)} %get-tuple-element.99, f32[32,128]{1,0:T(8,128)S(1)} %bitcast.399, f32[32,128]{1,0:T(8,128)S(1)} %copy-done.61, f32[32,128]{1,0:T(8,128)S(1)} %bitcast.393, f32[32,128]{1,0:T(8,128)S(1)} %bitcast.397, f32[32,128]{1,0:T(8,128)S(1)} %copy-done.63, ...), kind=kLoop, calls=%fused_computation.134 | loop fusion | flops 9957376 | bytes 180224 | tf_op jit(solution)/shard_map/reduce_sum | solution.py:86
  41.7 4.3 %multiply_reduce_fusion.16 = (f32[32,128]{1,0:T(8,128)S(1)}, f32[32,128]{1,0:T(8,128)S(1)}) fusion(f32[32,128]{1,0:T(8,128)S(1)} %get-tuple-element.105, f32[32,128]{1,0:T(8,128)S(1)} %bitcast.387, f32[32,128]{1,0:T(8,128)S(1)} %copy-done.61, f32[32,128]{1,0:T(8,128)S(1)} %bitcast.381, f32[32,128]{1,0:T(8,128)S(1)} %bitcast.385, ...), kind=kLoop, calls=%fused_computation.141 | loop fusion | flops 19914752 | bytes 311296 | tf_op jit(solution)/shard_map/reduce_sum | solution.py:86
  46.1 4.3 %multiply_reduce_fusion.17 = (f32[32,128]{1,0:T(8,128)S(1)}, f32[32,128]{1,0:T(8,128)S(1)}) fusion(f32[32,128]{1,0:T(8,128)S(1)} %get-tuple-element.106, f32[32,128]{1,0:T(8,128)S(1)} %bitcast.423, f32[32,128]{1,0:T(8,128)S(1)} %copy-done.61, f32[32,128]{1,0:T(8,128)S(1)} %bitcast.417, f32[32,128]{1,0:T(8,128)S(1)} %bitcast.421, ...), kind=kLoop, calls=%fused_computation.142 | loop fusion | flops 19914752 | bytes 311296 | tf_op jit(solution)/shard_map/reduce_sum | solution.py:86
  50.5 4.3 %multiply_reduce_fusion.13 = (f32[32,128]{1,0:T(8,128)S(1)}, f32[32,128]{1,0:T(8,128)S(1)}) fusion(f32[32,128]{1,0:T(8,128)S(1)} %get-tuple-element.103, f32[32,128]{1,0:T(8,128)S(1)} %bitcast.435, f32[32,128]{1,0:T(8,128)S(1)} %copy-done.61, f32[32,128]{1,0:T(8,128)S(1)} %bitcast.429, f32[32,128]{1,0:T(8,128)S(1)} %bitcast.433, ...), kind=kLoop, calls=%fused_computation.138 | loop fusion | flops 19914752 | bytes 311296 | tf_op jit(solution)/shard_map/reduce_sum | solution.py:86
  54.8 4.3 %multiply_reduce_fusion.11 = (f32[32,128]{1,0:T(8,128)S(1)}, f32[32,128]{1,0:T(8,128)S(1)}) fusion(f32[32,128]{1,0:T(8,128)S(1)} %get-tuple-element.101, f32[32,128]{1,0:T(8,128)S(1)} %bitcast.447, f32[32,128]{1,0:T(8,128)S(1)} %copy-done.61, f32[32,128]{1,0:T(8,128)S(1)} %bitcast.441, f32[32,128]{1,0:T(8,128)S(1)} %bitcast.445, ...), kind=kLoop, calls=%fused_computation.136 | loop fusion | flops 19914752 | bytes 311296 | tf_op jit(solution)/shard_map/reduce_sum | solution.py:86
  59.8 1.7 %fusion.123 = f32[32,1,64]{2,1,0:T(1,128)S(1)} fusion(f32[32,128,1]{1,2,0:T(1,128)S(1)} %bitcast.333, f32[32,64,128]{2,1,0:T(8,128)S(1)} %copy-done), kind=kOutput, calls=%fused_computation.331 | convolution fusion | flops 3145728 | bytes 1073152 | tf_op jit(solution)/shard_map/lrp,lp->lr/dot_general | solution.py:90
  62.5 1.3 %fusion.94 = f32[1,2]{1,0:T(1,128)S(1)} fusion(f32[1]{0:T(128)} %bitcast.141, f32[1]{0:T(128)} %bitcast.140), kind=kLoop, calls=%fused_computation.302 | loop fusion | flops 2 | bytes 16 | tf_op jit(solution)/shard_map/broadcast_in_dim | solution.py:95
  64.6 1.3 %collective-permute-start.13 = (f32[34,64]{1,0:T(8,128)S(1)}, f32[34,64]{1,0:T(8,128)S(1)}, u32[]{:S(2)}, u32[]{:S(2)}) collective-permute-start(f32[34,64]{1,0:T(8,128)S(1)} %select_maximum_fusion), channel_id=1, source_target_pairs={{0,2},{1,3},{2,0},{3,1},{4,6},{5,7},{6,4},{7,5},{8,10},{9,11},{10,... | collective-permute-start | bytes 26120 | tf_op jit(solution)/shard_map/ppermute | solution.py:16
  66.5 1.3 collective-permute-start.10
  69.7 1.3 %fusion.89 = f32[64]{0:T(128)S(1)} fusion(f32[64]{0:T(128)S(1)} %get-tuple-element.165, f32[34,64]{1,0:T(8,128)S(1)} %collective-permute-done.12, f32[1]{0:T(128)} %bitcast.141, f32[1]{0:T(128)} %bitcast.140), kind=kLoop, calls=%fused_computation.280 | loop fusion | flops 4 | bytes 776 | tf_op jit(solution)/shard_map/add | solution.py:27
  71.9 3.6 %collective-permute-start.17 = (f32[5,64]{1,0:T(8,128)S(1)}, f32[5,64]{1,0:T(8,128)S(1)}, u32[]{:S(2)}, u32[]{:S(2)}) collective-permute-start(f32[5,64]{1,0:T(8,128)S(1)} %pad_maximum_fusion.8), channel_id=1, source_target_pairs={{0,12},{4,8},{8,4},{12,0},{1,13},{5,9},{9,5},{13,1},{2,14},{6,10},... | collective-permute-start | bytes 3848 | tf_op jit(solution)/shard_map/ppermute | solution.py:16
  83.0 1.3 %gather_fusion.4 = f32[288,128]{1,0:T(8,128)S(1)} fusion(f32[128,128]{1,0:T(8,128)S(1)} %pad_maximum_fusion.3, s32[1024]{0:T(1024)S(1)} %pad_clamp_fusion.3), kind=kCustom, calls=%fused_computation.4 | custom fusion | bytes 296064 | tf_op jit(solution)/shard_map/gather | solution.py:132
  84.6 2.7 %multiply_reduce_fusion.3 = f32[32,128]{1,0:T(8,128)S(1)} fusion(f32[32,128]{1,0:T(8,128)S(1)} %multiply_bitcast_fusion.3, f32[32,128]{1,0:T(8,128)S(1)} %bitcast.460, f32[32,128]{1,0:T(8,128)S(1)} %copy-done.62, f32[32,128]{1,0:T(8,128)S(1)} %bitcast.454, f32[32,128]{1,0:T(8,128)S(1)} %bitcast.458, f32[32,128]{1,0:T(8,128)S(1)} %copy-done.64, ...), kind=kLoop, calls=%fused_computation.128 | loop fusion | flops 9957376 | bytes 180224 | tf_op jit(solution)/shard_map/reduce_sum | solution.py:86
  87.5 4.3 %multiply_reduce_fusion.7 = (f32[32,128]{1,0:T(8,128)S(1)}, f32[32,128]{1,0:T(8,128)S(1)}) fusion(f32[32,128]{1,0:T(8,128)S(1)} %multiply_bitcast_fusion.7, f32[32,128]{1,0:T(8,128)S(1)} %bitcast.388, f32[32,128]{1,0:T(8,128)S(1)} %copy-done.62, f32[32,128]{1,0:T(8,128)S(1)} %bitcast.382, f32[32,128]{1,0:T(8,128)S(1)} %bitcast.386, ...), kind=kLoop, calls=%fused_computation.132 | loop fusion | flops 19914752 | bytes 311296 | tf_op jit(solution)/shard_map/reduce_sum | solution.py:86
  91.9 4.3 %multiply_reduce_fusion.4 = (f32[32,128]{1,0:T(8,128)S(1)}, f32[32,128]{1,0:T(8,128)S(1)}) fusion(f32[32,128]{1,0:T(8,128)S(1)} %multiply_bitcast_fusion.4, f32[32,128]{1,0:T(8,128)S(1)} %bitcast.436, f32[32,128]{1,0:T(8,128)S(1)} %copy-done.62, f32[32,128]{1,0:T(8,128)S(1)} %bitcast.430, f32[32,128]{1,0:T(8,128)S(1)} %bitcast.434, ...), kind=kLoop, calls=%fused_computation.129 | loop fusion | flops 19914752 | bytes 311296 | tf_op jit(solution)/shard_map/reduce_sum | solution.py:86
  96.2 4.3 %multiply_reduce_fusion.5 = (f32[32,128]{1,0:T(8,128)S(1)}, f32[32,128]{1,0:T(8,128)S(1)}) fusion(f32[32,128]{1,0:T(8,128)S(1)} %multiply_bitcast_fusion.5, f32[32,128]{1,0:T(8,128)S(1)} %bitcast.376, f32[32,128]{1,0:T(8,128)S(1)} %copy-done.62, f32[32,128]{1,0:T(8,128)S(1)} %bitcast.370, f32[32,128]{1,0:T(8,128)S(1)} %bitcast.374, ...), kind=kLoop, calls=%fused_computation.130 | loop fusion | flops 19914752 | bytes 311296 | tf_op jit(solution)/shard_map/reduce_sum | solution.py:86
  100.5 4.3 %multiply_reduce_fusion.6 = (f32[32,128]{1,0:T(8,128)S(1)}, f32[32,128]{1,0:T(8,128)S(1)}) fusion(f32[32,128]{1,0:T(8,128)S(1)} %multiply_bitcast_fusion.6, f32[32,128]{1,0:T(8,128)S(1)} %bitcast.364, f32[32,128]{1,0:T(8,128)S(1)} %copy-done.62, f32[32,128]{1,0:T(8,128)S(1)} %bitcast.358, f32[32,128]{1,0:T(8,128)S(1)} %bitcast.362, ...), kind=kLoop, calls=%fused_computation.131 | loop fusion | flops 19914752 | bytes 311296 | tf_op jit(solution)/shard_map/reduce_sum | solution.py:86
  105.5 1.9 %maximum_bitcast_fusion = f32[1,3]{1,0:T(1,128)S(1)} fusion(f32[1]{0:T(128)} %bitcast.166, f32[1]{0:T(128)} %bitcast.165, f32[1]{0:T(128)} %bitcast.164), kind=kLoop, calls=%fused_computation.291 | loop fusion | flops 6 | bytes 24 | tf_op jit(solution)/shard_map/reshape.67
  107.4 1.4 %collective-permute-start.19 = (f32[8,128]{1,0:T(8,128)S(1)}, f32[8,128]{1,0:T(8,128)S(1)}, u32[]{:S(2)}, u32[]{:S(2)}) collective-permute-start(f32[8,128]{1,0:T(8,128)S(1)} %scatter.25), channel_id=1, source_target_pairs={{0,2},{1,3},{2,0},{3,1},{4,6},{5,7},{6,4},{7,5},{8,10},{9,11},{10,... | collective-permute-start | bytes 12296 | tf_op jit(solution)/shard_map/ppermute | solution.py:16
  109.3 1.9 %slice_add_fusion.2 = f32[1,3]{1,0:T(1,128)S(1)} fusion(f32[8,128]{1,0:T(8,128)S(1)} %collective-permute-done.18, f32[1]{0:T(128)} %bitcast.166, f32[1]{0:T(128)} %bitcast.165, f32[1]{0:T(128)} %bitcast.164), kind=kLoop, calls=%fused_computation.300 | loop fusion | flops 9 | bytes 36 | tf_op jit(solution)/shard_map/scatter | solution.py:151
  111.9 3.7 %collective-permute-start.22 = (f32[8,128]{1,0:T(8,128)S(1)}, f32[8,128]{1,0:T(8,128)S(1)}, u32[]{:S(2)}, u32[]{:S(2)}) collective-permute-start(f32[8,128]{1,0:T(8,128)S(1)} %add_add_fusion.1), channel_id=1, source_target_pairs={{0,8},{4,12},{8,0},{12,4},{1,9},{5,13},{9,1},{13,5},{2,10},{6,14},... | collective-permute-start | bytes 12296 | tf_op jit(solution)/shard_map/ppermute | solution.py:16
  117.2 3.8 %collective-permute-done.23 = f32[8,128]{1,0:T(8,128)S(1)} collective-permute-done((f32[8,128]{1,0:T(8,128)S(1)}, f32[8,128]{1,0:T(8,128)S(1)}, u32[]{:S(2)}, u32[]{:S(2)}) %collective-permute-start.23) | collective-permute-done | bytes 4128 | tf_op jit(solution)/shard_map/ppermute | solution.py:16
  (285 shorter events, 30.3 us)
Async XLA Ops:
  4.6 26.3 %collective-permute-start = (f32[32,7,128]{2,1,0:T(8,128)S(1)}, f32[32,7,128]{2,1,0:T(8,128)S(1)}, u32[]{:S(2)}, u32[]{:S(2)}) collective-permute-start(f32[32,7,128]{2,1,0:T(8,128)S(1)} %pad_maximum_fusion.1), channel_id=1, source_target_pairs={{0,1},{1,0},{2,3},{3,2},{4,5},{5,4},{6,7},{7,6},{8,9},{9,8},{10,11... | collective-permute-start | bytes 344072 | tf_op jit(solution)/shard_map/ppermute | solution.py:16
  5.1 25.8 %collective-permute-start.1 = (f32[32,7,128]{2,1,0:T(8,128)S(1)}, f32[32,7,128]{2,1,0:T(8,128)}, u32[]{:S(2)}, u32[]{:S(2)}) collective-permute-start(f32[32,7,128]{2,1,0:T(8,128)S(1)} %pad_maximum_fusion.1), channel_id=1, source_target_pairs={{0,2},{1,3},{2,0},{3,1},{4,6},{5,7},{6,4},{7,5},{8,10},{9,11},{10,... | collective-permute-start | bytes 344072 | tf_op jit(solution)/shard_map/ppermute | solution.py:16
  10.3 16.3 %copy-start.2 = (f32[8,64,64]{2,1,0:T(8,128)S(1)}, f32[8,64,64]{2,1,0:T(8,128)}, u32[]{:S(2)}) copy-start(f32[8,64,64]{2,1,0:T(8,128)} %param.27) | copy-start | bytes 393220
  11.0 3.1 %collective-permute-start.3 = (f32[34,64]{1,0:T(8,128)S(1)}, f32[34,64]{1,0:T(8,128)S(1)}, u32[]{:S(2)}, u32[]{:S(2)}) collective-permute-start(f32[34,64]{1,0:T(8,128)S(1)} %select_maximum_fusion.1), channel_id=1, source_target_pairs={{0,1},{1,0},{2,3},{3,2},{4,5},{5,4},{6,7},{7,6},{8,9},{9,8},{10,11... | collective-permute-start | bytes 26120 | tf_op jit(solution)/shard_map/ppermute | solution.py:16
  11.3 3.8 %collective-permute-start.4 = (f32[34,64]{1,0:T(8,128)S(1)}, f32[34,64]{1,0:T(8,128)S(1)}, u32[]{:S(2)}, u32[]{:S(2)}) collective-permute-start(f32[34,64]{1,0:T(8,128)S(1)} %select_maximum_fusion.1), channel_id=1, source_target_pairs={{0,2},{1,3},{2,0},{3,1},{4,6},{5,7},{6,4},{7,5},{8,10},{9,11},{10,... | collective-permute-start | bytes 26120 | tf_op jit(solution)/shard_map/ppermute | solution.py:16
  11.5 3.5 %collective-permute-start.5 = (f32[34,64]{1,0:T(8,128)S(1)}, f32[34,64]{1,0:T(8,128)S(1)}, u32[]{:S(2)}, u32[]{:S(2)}) collective-permute-start(f32[34,64]{1,0:T(8,128)S(1)} %select_maximum_fusion.1), channel_id=1, source_target_pairs={{0,3},{1,2},{2,1},{3,0},{4,7},{5,6},{6,5},{7,4},{8,11},{9,10},{10,... | collective-permute-start | bytes 26120 | tf_op jit(solution)/shard_map/ppermute | solution.py:16
  16.3 5.2 %collective-permute-start.6 = (f32[5,64]{1,0:T(8,128)S(1)}, f32[5,64]{1,0:T(8,128)S(1)}, u32[]{:S(2)}, u32[]{:S(2)}) collective-permute-start(f32[5,64]{1,0:T(8,128)S(1)} %pad_maximum_fusion.7), channel_id=1, source_target_pairs={{0,4},{4,0},{8,12},{12,8},{1,5},{5,1},{9,13},{13,9},{2,6},{6,2},{1... | collective-permute-start | bytes 3848 | tf_op jit(solution)/shard_map/ppermute | solution.py:16
  18.1 4.5 %collective-permute-start.7 = (f32[5,64]{1,0:T(8,128)S(1)}, f32[5,64]{1,0:T(8,128)S(1)}, u32[]{:S(2)}, u32[]{:S(2)}) collective-permute-start(f32[5,64]{1,0:T(8,128)S(1)} %pad_maximum_fusion.7), channel_id=1, source_target_pairs={{0,8},{4,12},{8,0},{12,4},{1,9},{5,13},{9,1},{13,5},{2,10},{6,14},... | collective-permute-start | bytes 3848 | tf_op jit(solution)/shard_map/ppermute | solution.py:16
  20.7 5.4 %collective-permute-start.8 = (f32[5,64]{1,0:T(8,128)S(1)}, f32[5,64]{1,0:T(8,128)S(1)}, u32[]{:S(2)}, u32[]{:S(2)}) collective-permute-start(f32[5,64]{1,0:T(8,128)S(1)} %pad_maximum_fusion.7), channel_id=1, source_target_pairs={{0,12},{4,8},{8,4},{12,0},{1,13},{5,9},{9,5},{13,1},{2,14},{6,10},... | collective-permute-start | bytes 3848 | tf_op jit(solution)/shard_map/ppermute | solution.py:16
  21.5 9.4 %collective-permute-start.2 = (f32[32,7,128]{2,1,0:T(8,128)S(1)}, f32[32,7,128]{2,1,0:T(8,128)}, u32[]{:S(2)}, u32[]{:S(2)}) collective-permute-start(f32[32,7,128]{2,1,0:T(8,128)S(1)} %pad_maximum_fusion.1), channel_id=1, source_target_pairs={{0,3},{1,2},{2,1},{3,0},{4,7},{5,6},{6,5},{7,4},{8,11},{9,10},{10,... | collective-permute-start | bytes 344072 | tf_op jit(solution)/shard_map/ppermute | solution.py:16
  38.8 16.0 %copy-start.5 = (f32[32,1,128]{2,1,0:T(1,128)}, f32[32,1,128]{2,1,0:T(1,128)S(1)}, u32[]{:S(2)}) copy-start(f32[32,1,128]{2,1,0:T(1,128)S(1)} %get-tuple-element.193) | copy-start | bytes 49156
  38.8 16.0 %copy-start.7 = (f32[32,1,128]{2,1,0:T(1,128)}, f32[32,1,128]{2,1,0:T(1,128)S(1)}, u32[]{:S(2)}) copy-start(f32[32,1,128]{2,1,0:T(1,128)S(1)} %get-tuple-element.194) | copy-start | bytes 49156
  38.8 16.0 %copy-start.9 = (f32[32,1,128]{2,1,0:T(1,128)}, f32[32,1,128]{2,1,0:T(1,128)S(1)}, u32[]{:S(2)}) copy-start(f32[32,1,128]{2,1,0:T(1,128)S(1)} %get-tuple-element.195) | copy-start | bytes 49156
  38.9 15.9 %copy-start.35 = (f32[32,1,128]{2,1,0:T(1,128)}, f32[32,1,128]{2,1,0:T(1,128)S(1)}, u32[]{:S(2)}) copy-start(f32[32,1,128]{2,1,0:T(1,128)S(1)} %get-tuple-element.149) | copy-start | bytes 49156
  38.9 15.9 %copy-start.37 = (f32[32,1,128]{2,1,0:T(1,128)}, f32[32,1,128]{2,1,0:T(1,128)S(1)}, u32[]{:S(2)}) copy-start(f32[32,1,128]{2,1,0:T(1,128)S(1)} %get-tuple-element.150) | copy-start | bytes 49156
  38.9 15.9 %copy-start.39 = (f32[32,1,128]{2,1,0:T(1,128)}, f32[32,1,128]{2,1,0:T(1,128)S(1)}, u32[]{:S(2)}) copy-start(f32[32,1,128]{2,1,0:T(1,128)S(1)} %get-tuple-element.151) | copy-start | bytes 49156
  38.9 15.9 %copy-start.41 = (f32[32,1,128]{2,1,0:T(1,128)}, f32[32,1,128]{2,1,0:T(1,128)S(1)}, u32[]{:S(2)}) copy-start(f32[32,1,128]{2,1,0:T(1,128)S(1)} %get-tuple-element.196) | copy-start | bytes 49156
  63.8 4.3 %collective-permute-start.12 = (f32[34,64]{1,0:T(8,128)S(1)}, f32[34,64]{1,0:T(8,128)S(1)}, u32[]{:S(2)}, u32[]{:S(2)}) collective-permute-start(f32[34,64]{1,0:T(8,128)S(1)} %select_maximum_fusion), channel_id=1, source_target_pairs={{0,1},{1,0},{2,3},{3,2},{4,5},{5,4},{6,7},{7,6},{8,9},{9,8},{10,11... | collective-permute-start | bytes 26120 | tf_op jit(solution)/shard_map/ppermute | solution.py:16
  64.6 3.8 %collective-permute-start.13 = (f32[34,64]{1,0:T(8,128)S(1)}, f32[34,64]{1,0:T(8,128)S(1)}, u32[]{:S(2)}, u32[]{:S(2)}) collective-permute-start(f32[34,64]{1,0:T(8,128)S(1)} %select_maximum_fusion), channel_id=1, source_target_pairs={{0,2},{1,3},{2,0},{3,1},{4,6},{5,7},{6,4},{7,5},{8,10},{9,11},{10,... | collective-permute-start | bytes 26120 | tf_op jit(solution)/shard_map/ppermute | solution.py:16
  65.9 3.2 %collective-permute-start.14 = (f32[34,64]{1,0:T(8,128)S(1)}, f32[34,64]{1,0:T(8,128)S(1)}, u32[]{:S(2)}, u32[]{:S(2)}) collective-permute-start(f32[34,64]{1,0:T(8,128)S(1)} %select_maximum_fusion), channel_id=1, source_target_pairs={{0,3},{1,2},{2,1},{3,0},{4,7},{5,6},{6,5},{7,4},{8,11},{9,10},{10,... | collective-permute-start | bytes 26120 | tf_op jit(solution)/shard_map/ppermute | solution.py:16
  66.5 16.3 %collective-permute-start.10 = (f32[32,128]{1,0:T(8,128)S(1)}, f32[32,128]{1,0:T(8,128)S(1)}, u32[]{:S(2)}, u32[]{:S(2)}) collective-permute-start(f32[32,128]{1,0:T(8,128)S(1)} %get-tuple-element.68), channel_id=1, source_target_pairs={{0,2},{1,3},{2,0},{3,1},{4,6},{5,7},{6,4},{7,5},{8,10},{9,11},{10,... | collective-permute-start | bytes 49160 | tf_op jit(solution)/shard_map/ppermute | solution.py:16
  67.7 15.1 %collective-permute-start.11 = (f32[32,128]{1,0:T(8,128)S(1)}, f32[32,128]{1,0:T(8,128)S(1)}, u32[]{:S(2)}, u32[]{:S(2)}) collective-permute-start(f32[32,128]{1,0:T(8,128)S(1)} %get-tuple-element.68), channel_id=1, source_target_pairs={{0,3},{1,2},{2,1},{3,0},{4,7},{5,6},{6,5},{7,4},{8,11},{9,10},{10,... | collective-permute-start | bytes 49160 | tf_op jit(solution)/shard_map/ppermute | solution.py:16
  71.0 5.2 %collective-permute-start.15 = (f32[5,64]{1,0:T(8,128)S(1)}, f32[5,64]{1,0:T(8,128)S(1)}, u32[]{:S(2)}, u32[]{:S(2)}) collective-permute-start(f32[5,64]{1,0:T(8,128)S(1)} %pad_maximum_fusion.8), channel_id=1, source_target_pairs={{0,4},{4,0},{8,12},{12,8},{1,5},{5,1},{9,13},{13,9},{2,6},{6,2},{1... | collective-permute-start | bytes 3848 | tf_op jit(solution)/shard_map/ppermute | solution.py:16
  71.1 5.2 %collective-permute-start.16 = (f32[5,64]{1,0:T(8,128)S(1)}, f32[5,64]{1,0:T(8,128)S(1)}, u32[]{:S(2)}, u32[]{:S(2)}) collective-permute-start(f32[5,64]{1,0:T(8,128)S(1)} %pad_maximum_fusion.8), channel_id=1, source_target_pairs={{0,8},{4,12},{8,0},{12,4},{1,9},{5,13},{9,1},{13,5},{2,10},{6,14},... | collective-permute-start | bytes 3848 | tf_op jit(solution)/shard_map/ppermute | solution.py:16
  71.9 5.4 %collective-permute-start.17 = (f32[5,64]{1,0:T(8,128)S(1)}, f32[5,64]{1,0:T(8,128)S(1)}, u32[]{:S(2)}, u32[]{:S(2)}) collective-permute-start(f32[5,64]{1,0:T(8,128)S(1)} %pad_maximum_fusion.8), channel_id=1, source_target_pairs={{0,12},{4,8},{8,4},{12,0},{1,13},{5,9},{9,5},{13,1},{2,14},{6,10},... | collective-permute-start | bytes 3848 | tf_op jit(solution)/shard_map/ppermute | solution.py:16
  76.2 6.6 %collective-permute-start.9 = (f32[32,128]{1,0:T(8,128)S(1)}, f32[32,128]{1,0:T(8,128)S(1)}, u32[]{:S(2)}, u32[]{:S(2)}) collective-permute-start(f32[32,128]{1,0:T(8,128)S(1)} %get-tuple-element.68), channel_id=1, source_target_pairs={{0,1},{1,0},{2,3},{3,2},{4,5},{5,4},{6,7},{7,6},{8,9},{9,8},{10,11... | collective-permute-start | bytes 49160 | tf_op jit(solution)/shard_map/ppermute | solution.py:16
  107.4 1.9 %collective-permute-start.18 = (f32[8,128]{1,0:T(8,128)S(1)}, f32[8,128]{1,0:T(8,128)S(1)}, u32[]{:S(2)}, u32[]{:S(2)}) collective-permute-start(f32[8,128]{1,0:T(8,128)S(1)} %scatter.25), channel_id=1, source_target_pairs={{0,1},{1,0},{2,3},{3,2},{4,5},{5,4},{6,7},{7,6},{8,9},{9,8},{10,11... | collective-permute-start | bytes 12296 | tf_op jit(solution)/shard_map/ppermute | solution.py:16
  107.4 3.9 %collective-permute-start.19 = (f32[8,128]{1,0:T(8,128)S(1)}, f32[8,128]{1,0:T(8,128)S(1)}, u32[]{:S(2)}, u32[]{:S(2)}) collective-permute-start(f32[8,128]{1,0:T(8,128)S(1)} %scatter.25), channel_id=1, source_target_pairs={{0,2},{1,3},{2,0},{3,1},{4,6},{5,7},{6,4},{7,5},{8,10},{9,11},{10,... | collective-permute-start | bytes 12296 | tf_op jit(solution)/shard_map/ppermute | solution.py:16
  108.8 3.0 %collective-permute-start.20 = (f32[8,128]{1,0:T(8,128)S(1)}, f32[8,128]{1,0:T(8,128)S(1)}, u32[]{:S(2)}, u32[]{:S(2)}) collective-permute-start(f32[8,128]{1,0:T(8,128)S(1)} %scatter.25), channel_id=1, source_target_pairs={{0,3},{1,2},{2,1},{3,0},{4,7},{5,6},{6,5},{7,4},{8,11},{9,10},{10,... | collective-permute-start | bytes 12296 | tf_op jit(solution)/shard_map/ppermute | solution.py:16
  111.9 5.2 %collective-permute-start.21 = (f32[8,128]{1,0:T(8,128)S(1)}, f32[8,128]{1,0:T(8,128)S(1)}, u32[]{:S(2)}, u32[]{:S(2)}) collective-permute-start(f32[8,128]{1,0:T(8,128)S(1)} %add_add_fusion.1), channel_id=1, source_target_pairs={{0,4},{4,0},{8,12},{12,8},{1,5},{5,1},{9,13},{13,9},{2,6},{6,2},{1... | collective-permute-start | bytes 12296 | tf_op jit(solution)/shard_map/ppermute | solution.py:16
  111.9 5.3 %collective-permute-start.22 = (f32[8,128]{1,0:T(8,128)S(1)}, f32[8,128]{1,0:T(8,128)S(1)}, u32[]{:S(2)}, u32[]{:S(2)}) collective-permute-start(f32[8,128]{1,0:T(8,128)S(1)} %add_add_fusion.1), channel_id=1, source_target_pairs={{0,8},{4,12},{8,0},{12,4},{1,9},{5,13},{9,1},{13,5},{2,10},{6,14},... | collective-permute-start | bytes 12296 | tf_op jit(solution)/shard_map/ppermute | solution.py:16
  115.6 5.4 %collective-permute-start.23 = (f32[8,128]{1,0:T(8,128)S(1)}, f32[8,128]{1,0:T(8,128)S(1)}, u32[]{:S(2)}, u32[]{:S(2)}) collective-permute-start(f32[8,128]{1,0:T(8,128)S(1)} %add_add_fusion.1), channel_id=1, source_target_pairs={{0,12},{4,8},{8,4},{12,0},{1,13},{5,9},{9,5},{13,1},{2,14},{6,10},... | collective-permute-start | bytes 12296 | tf_op jit(solution)/shard_map/ppermute | solution.py:16
  (63 other events, 388.0 us)

commit v2 on v0

v2 whole, which is shorter than its diff:
```python
import functools
import math

import jax
import jax.numpy as jnp
from jax import lax
from jax.experimental import pallas as pl
from jax.experimental.pallas import tpu as pltpu
from jax.sharding import PartitionSpec as P

SOFTEN = 0.05
EPSILON = 1e-06
KERNEL_SCALE = 0.25 / math.pi
HIGH_PRECISION = lax.Precision.HIGHEST
LANES = 128
TILE_ROWS = 8
VMEM_LIMIT = 16 << 20


def from_peers(value, axis):
    size = lax.axis_size(axis)
    arrived = [
        lax.ppermute(value, axis, [(i, i ^ turn) for i in range(size)]) for turn in range(1, size)
    ]
    return [value] + arrived


def place_of(owner, axis):
    return lax.axis_index(axis) ^ owner


def tree_sum(parts):
    while len(parts) > 1:
        parts = [parts[i] + parts[i + 1] for i in range(0, len(parts), 2)]
    return parts[0]


def device_call(kernel, outputs, scalars, arrays, scratch=()):
    smem = pl.BlockSpec(memory_space=pltpu.SMEM)
    vmem = pl.BlockSpec(memory_space=pltpu.VMEM)
    return pl.pallas_call(
        kernel,
        out_shape=tuple(outputs),
        in_specs=[smem] * len(scalars) + [vmem] * len(arrays),
        out_specs=tuple([vmem] * len(outputs)),
        scratch_shapes=tuple(scratch),
        compiler_params=pltpu.CompilerParams(vmem_limit_bytes=VMEM_LIMIT),
    )(*scalars, *arrays)


def f32(*shape):
    return jax.ShapeDtypeStruct(shape, jnp.float32)


def iota(shape, dimension):
    return lax.broadcasted_iota(jnp.int32, shape, dimension)


def split_three(value):
    first = value.astype(jnp.bfloat16).astype(jnp.float32)
    rest = value - first
    second = rest.astype(jnp.bfloat16).astype(jnp.float32)
    third = (rest - second).astype(jnp.bfloat16).astype(jnp.float32)
    return first, second, third


def lane_row(entries):
    lane = iota((1, LANES), 1)
    row = jnp.zeros((1, LANES), jnp.float32)
    for place, entry in enumerate(entries):
        row = jnp.where(lane == place, entry, row)
    return row


def pack_kernel(counts, points, normals, density, geometry, initial):
    slots, dims, width = points.shape
    used = jnp.where(iota((slots, width), 0) < counts[0], density[...], 0.0)
    initial[...] = used
    geometry[:, 0:dims, :] = points[...]
    geometry[:, dims : 2 * dims, :] = normals[...]
    geometry[:, 2 * dims, :] = used
    geometry[:, 2 * dims + 1, :] = jnp.zeros_like(used)


def write_moments(vector, sums, basis, transfer, message, start):
    slots, rank, _ = basis.shape
    lane = iota((rank, LANES), 1)
    columns = jnp.zeros((rank, LANES), jnp.float32)
    for leaf in range(slots):
        column = jnp.sum(basis[leaf] * vector[leaf : leaf + 1, :], axis=1, keepdims=True)
        columns = jnp.where(lane == leaf, column, columns)
    moments = columns.T
    end = start + slots
    message[start:end, :] = jnp.zeros((slots, LANES), jnp.float32)
    message[start:end, 0:rank] = moments[0:slots]
    box = jnp.zeros((rank, rank), jnp.float32)
    for leaf in range(slots):
        box = box + transfer[leaf] * message[start + leaf : start + leaf + 1, 0:rank]
    message[end : end + TILE_ROWS, :] = jnp.zeros((TILE_ROWS, LANES), jnp.float32)
    column = jnp.broadcast_to(jnp.sum(box, axis=1, keepdims=True), (rank, LANES))
    message[end : end + 1, 0:rank] = column.T[0:1]
    message[end + 1 : end + 2, :] = sums


def first_moments_kernel(counts, initial, basis, transfer, message):
    vector = initial[...]
    square_sum = jnp.sum(vector * vector, keepdims=True)
    in_use = jnp.full((1, 1), counts[0], jnp.int32).astype(jnp.float32)
    write_moments(initial, lane_row([square_sum, in_use]), basis, transfer, message, 0)


def leaf_part(moments, picks, coupling):
    count, rank, _ = coupling.shape
    slots = picks.shape[0] // count
    chosen = jnp.zeros((picks.shape[0], rank), jnp.float32)
    for part in split_three(jnp.concatenate(moments, axis=0)):
        chosen = chosen + jnp.dot(
            picks[...], part.astype(jnp.bfloat16), preferred_element_type=jnp.float32
        )
    local = jnp.zeros((slots, rank), jnp.float32)
    for place in range(count):
        local = local + lax.dot_general(
            chosen[place * slots : (place + 1) * slots],
            coupling[place],
            (((1,), (1,)), ((), ())),
            precision=HIGH_PRECISION,
            preferred_element_type=jnp.float32,
        )
    return local


def first_near_kernel(subs, near_rows, *refs):
    geometry, messages = refs[:subs], refs[subs : 2 * subs]
    picks, coupling, near, local, values, features, squares, fields = refs[2 * subs :]
    slots, height, width = geometry[0].shape
    neighbours = near_rows.shape[1]
    rank = coupling.shape[1]
    row = iota((height, width), 0)
    scale_square = jnp.where(row < 3, -2.0, 0.0)
    ones = jnp.where(row == 7, 1.0, 0.0)
    scale_normal = jnp.where((row >= 3) & (row < 6), -KERNEL_SCALE, 0.0)

    for sub in range(subs):
        rows = geometry[sub]
        at = [rows[:, component, :] for component in range(7)]
        squares[sub * slots : (sub + 1) * slots, :] = at[0] * at[0] + at[1] * at[1] + at[2] * at[2]
        fields[sub * slots : (sub + 1) * slots, :] = at[6]
        inner = (at[0] * at[3] + at[1] * at[4] + at[2] * at[5]) * KERNEL_SCALE
        local[...] = inner

        def source(leaf, carry, rows=rows, sub=sub):
            place = sub * slots + leaf
            plain = rows[leaf]
            square = squares[pl.ds(place, 1), :] + SOFTEN
            distance = jnp.where(row == 6, square, plain * scale_square + ones)
            numerator = jnp.where(row == 6, local[pl.ds(leaf, 1), :], plain * scale_normal)
            for part, value in enumerate((distance, numerator)):
                one, two, three = split_three(value)
                lanes = slice(part * width, (part + 1) * width)
                features[place, 0:16, lanes] = jnp.concatenate([one, two]).astype(jnp.bfloat16)
                features[place, 16:32, lanes] = jnp.concatenate([one, three]).astype(jnp.bfloat16)
            return carry

        lax.fori_loop(0, slots, source, 0, unroll=4)

    own = geometry[0]

    def target(leaf, carry):
        plain = own[leaf]
        shifted = pltpu.roll(plain, 3, 0)
        square = squares[pl.ds(leaf, 1), :]
        value = jnp.where(row < 3, plain, jnp.where(row < 6, shifted, jnp.where(row == 6, 1.0, square)))
        one, two, three = split_three(value)
        left = jnp.concatenate([one, one, two, two, three, one]).T.astype(jnp.bfloat16)
        total = jnp.zeros((width, width), jnp.float32)
        for column in range(neighbours):
            place = near_rows[leaf, column]
            upper, lower = features[place, 0:16, :], features[place, 16:32, :]
            right = jnp.concatenate([upper, upper, lower], axis=0)
            both = jnp.dot(left, right, preferred_element_type=jnp.float32)
            inverse = lax.rsqrt(both[:, 0:width])
            tile = both[:, width : 2 * width] * (inverse * inverse * inverse)
            values[leaf * neighbours + column] = tile
            total = total + tile * fields[pl.ds(place, 1), :]
        near[pl.ds(leaf, 1), :] = jnp.sum(total.T, axis=0, keepdims=True)
        return carry

    lax.fori_loop(0, slots, target, 0)
    local[...] = jnp.zeros_like(local)
    local[:, 0:rank] = leaf_part([ref[0:slots, 0:rank] for ref in messages], picks, coupling)


def second_near_kernel(subs, near_rows, *refs):
    messages = refs[:subs]
    picks, coupling, values, near, local, fields = refs[subs:]
    slots, width = near.shape
    neighbours = near_rows.shape[1]
    rank = coupling.shape[1]
    for sub in range(subs):
        fields[sub * slots : (sub + 1) * slots, :] = messages[sub][0:slots, :]

    def target(leaf, carry):
        total = jnp.zeros((width, width), jnp.float32)
        for column in range(neighbours):
            place = near_rows[leaf, column]
            total = total + values[leaf * neighbours + column] * fields[pl.ds(place, 1), :]
        near[pl.ds(leaf, 1), :] = jnp.sum(total.T, axis=0, keepdims=True)
        return carry

    lax.fori_loop(0, slots, target, 0)
    local[...] = jnp.zeros_like(local)
    local[:, 0:rank] = leaf_part(
        [ref[slots : 2 * slots, 0:rank] for ref in messages], picks, coupling
    )


def surface_sums(boxes):
    return tree_sum(
        [
            tree_sum([ref[at + 1 : at + 2, :] for at in range(0, ref.shape[0], TILE_ROWS)])
            for ref in boxes
        ]
    )


def add_far(counts, box_rows, boxes, near, local, basis, transfer, box_coupling, gather, image):
    slots, rank, width = basis.shape
    height = boxes[0].shape[0]
    for place, ref in enumerate(boxes):
        gather[place * height : (place + 1) * height, :] = ref[...]
    coupled = jnp.zeros((rank, rank), jnp.float32)
    for place in range(box_coupling.shape[0]):
        coupled = coupled + box_coupling[place] * gather[pl.ds(box_rows[place], 1), 0:rank]
    box_local = jnp.broadcast_to(jnp.sum(coupled, axis=1, keepdims=True), (rank, rank))
    for leaf in range(slots):
        local[leaf : leaf + 1, 0:rank] += jnp.sum(
            transfer[leaf] * box_local, axis=0, keepdims=True
        )
    columns = local[...].T
    for leaf in range(slots):
        far = jnp.sum(basis[leaf] * columns[0:rank, leaf : leaf + 1], axis=0, keepdims=True)
        image[leaf : leaf + 1, :] = jnp.where(
            leaf < counts[0], near[leaf : leaf + 1, :] + far, 0.0
        )


def first_image_kernel(patches, counts, box_rows, *refs):
    boxes = refs[:patches]
    near, leaf_local, initial, basis, transfer, box_coupling = refs[patches : patches + 6]
    message, basis_one, numbers, gather, image, local = refs[patches + 6 :]
    slots, _, width = basis.shape
    local[...] = leaf_local[...]
    add_far(
        counts, box_rows, boxes, near, local, basis, transfer, box_coupling, gather, image
    )
    sums = surface_sums(boxes)
    square_sum, unknowns = sums[:, 0:1], width * sums[:, 1:2]
    start_scale = jnp.sqrt(square_sum / unknowns + EPSILON)
    one_one = square_sum / (start_scale * start_scale)
    one = initial[...] / start_scale
    scaled = image[...] / start_scale
    basis_one[...] = one
    message[0:slots, :] = scaled
    numbers[...] = jnp.broadcast_to(lane_row([one_one, unknowns]), numbers.shape)
    partial = lane_row(
        [jnp.sum(one * scaled, keepdims=True), jnp.sum(scaled * scaled, keepdims=True)]
    )
    write_moments(message, partial, basis, transfer, message, slots)


def second_image_kernel(patches, counts, box_rows, *refs):
    boxes = refs[:patches]
    near, leaf_local, message, basis_one, numbers = refs[patches : patches + 5]
    basis, transfer, box_coupling = refs[patches + 5 : patches + 8]
    basis_two, image_two, partial, numbers_out, gather, image, local = refs[patches + 8 :]
    slots = basis.shape[0]
    local[...] = leaf_local[...]
    add_far(
        counts, box_rows, boxes, near, local, basis, transfer, box_coupling, gather, image
    )
    one_one, unknowns = numbers[0:1, 0:1], numbers[0:1, 1:2]
    sums = surface_sums(boxes)
    along, image_sq = sums[:, 0:1], sums[:, 1:2]
    upper_first = (0.5 * one_one + along) / unknowns
    shift = upper_first - 0.5
    residual_sq = image_sq - 2.0 * shift * along + shift * shift * one_one
    lower_first = jnp.sqrt(residual_sq / unknowns + EPSILON)
    one = basis_one[...]
    first = message[0:slots, :]
    two = (first - shift * one) / lower_first
    mapped = (image[...] - shift * first) / lower_first
    basis_two[...] = two
    image_two[...] = mapped
    one_two = (along - shift * one_one) / lower_first
    two_two = residual_sq / (lower_first * lower_first)
    numbers_out[...] = jnp.broadcast_to(
        lane_row([one_one, unknowns, upper_first, lower_first, one_two, two_two]),
        numbers_out.shape,
    )
    partial[...] = jnp.broadcast_to(
        lane_row(
            [
                jnp.sum(one * mapped, keepdims=True),
                jnp.sum(two * mapped, keepdims=True),
                jnp.sum(mapped * mapped, keepdims=True),
            ]
        ),
        partial.shape,
    )


def last_kernel(patches, *refs):
    parts = refs[:patches]
    basis_one, basis_two, image_two, numbers, basis_three, hessenberg = refs[patches:]
    sums = tree_sum([ref[0:1, :] for ref in parts])
    k_one, k_two, k_sq = sums[:, 0:1], sums[:, 1:2], sums[:, 2:3]
    one_one, unknowns, upper_first, lower_first, one_two, two_two = [
        numbers[0:1, place : place + 1] for place in range(6)
    ]
    upper_second = (0.5 * one_two + k_one) / unknowns
    middle_second = (0.5 * two_two + k_two - upper_second * one_two) / unknowns
    shift = middle_second - 0.5
    final_sq = (
        k_sq
        - 2.0 * upper_second * k_one
        - 2.0 * shift * k_two
        + upper_second * upper_second * one_one
        + 2.0 * upper_second * shift * one_two
        + shift * shift * two_two
    )
    lower_second = jnp.sqrt(final_sq / unknowns + EPSILON)
    basis_three[...] = (
        image_two[...] - upper_second * basis_one[...] - shift * basis_two[...]
    ) / lower_second
    row, column = iota(hessenberg.shape, 0), iota(hessenberg.shape, 1)
    matrix = jnp.where(column == 0, upper_first, upper_second)
    matrix = jnp.where(row == 1, jnp.where(column == 0, lower_first, middle_second), matrix)
    hessenberg[...] = jnp.where(row == 2, jnp.where(column == 0, 0.0, lower_second), matrix)


def shards(
    points,
    normals,
    density,
    counts,
    near_list,
    leaf_far,
    leaf_basis,
    leaf_to_box_transfer,
    leaf_coupling,
    box_far,
    box_coupling,
):
    slots, _, width = points.shape
    rank = leaf_basis.shape[1]
    neighbours = near_list.shape[1]
    far_count = leaf_far.shape[1]
    subs, patches = lax.axis_size("sub"), lax.axis_size("patch")
    sources = subs * slots
    patch_start = lax.axis_index("patch") * sources
    rows = f32(slots, width)

    def row_of(leaf):
        leaf = leaf - patch_start
        return place_of(leaf // slots, "sub") * slots + leaf % slots

    near_rows = row_of(near_list)
    picks = (
        row_of(leaf_far).T.reshape(far_count * slots, 1) == jnp.arange(sources)[None, :]
    ).astype(jnp.bfloat16)
    box_rows = TILE_ROWS * (
        place_of(box_far[0] // subs, "patch") * subs + place_of(box_far[0] % subs, "sub")
    )

    def box_parts(parts, start):
        return from_peers(
            jnp.concatenate([part[start : start + TILE_ROWS] for part in parts], axis=0), "patch"
        )

    geometry, initial = device_call(
        pack_kernel, [f32(slots, 8, width), rows], [counts], [points, normals, density]
    )
    geometry = from_peers(geometry, "sub")
    (message,) = device_call(
        first_moments_kernel,
        [f32(slots + TILE_ROWS, LANES)],
        [counts],
        [initial, leaf_basis, leaf_to_box_transfer],
    )
    messages = from_peers(message, "sub")
    boxes = box_parts(messages, slots)
    near, local, values = device_call(
        functools.partial(first_near_kernel, subs),
        [rows, f32(slots, LANES), pltpu.VMEM((slots * neighbours, width, width), jnp.float32)],
        [near_rows],
        [*geometry, *messages, picks, leaf_coupling],
        [
            pltpu.VMEM((sources, 32, 2 * width), jnp.bfloat16),
            pltpu.VMEM((sources, width), jnp.float32),
            pltpu.VMEM((sources, width), jnp.float32),
        ],
    )
    far_scratch = [
        pltpu.VMEM((patches * subs * TILE_ROWS, LANES), jnp.float32),
        pltpu.VMEM((slots, width), jnp.float32),
        pltpu.VMEM((slots, LANES), jnp.float32),
    ]
    message, basis_one, numbers = device_call(
        functools.partial(first_image_kernel, patches),
        [f32(2 * slots + TILE_ROWS, LANES), rows, f32(TILE_ROWS, LANES)],
        [counts, box_rows],
        [*boxes, near, local, initial, leaf_basis, leaf_to_box_transfer, box_coupling],
        far_scratch,
    )
    messages = from_peers(message, "sub")
    boxes = box_parts(messages, 2 * slots)
    near, local = device_call(
        functools.partial(second_near_kernel, subs),
        [rows, f32(slots, LANES)],
        [near_rows],
        [*messages, picks, leaf_coupling, values],
        [pltpu.VMEM((sources, width), jnp.float32)],
    )
    basis_two, image_two, partial, numbers = device_call(
        functools.partial(second_image_kernel, patches),
        [rows, rows, f32(TILE_ROWS, LANES), f32(TILE_ROWS, LANES)],
        [counts, box_rows],
        [
            *boxes,
            near,
            local,
            message,
            basis_one,
            numbers,
            leaf_basis,
            leaf_to_box_transfer,
            box_coupling,
        ],
        far_scratch,
    )
    parts = from_peers(tree_sum(from_peers(partial, "sub")), "patch")
    return device_call(
        functools.partial(last_kernel, patches),
        [rows, f32(3, 2)],
        [],
        [*parts, basis_one, basis_two, image_two, numbers],
    )


def solution(mesh):
    spread = ("groups", "patch", "sub")
    in_specs = (
        P(spread, None, None),
        P(spread, None, None),
        P(spread, None),
        P(spread),
        P(spread, None),
        P(spread, None),
        P(spread, None, None),
        P(spread, None, None),
        P(),
        P(spread, None),
        P(),
    )
    out_specs = (P(spread, None), P("groups", None))
    return jax.shard_map(shards, mesh=mesh, in_specs=in_specs, out_specs=out_specs, check_vma=False)
```

time: 262 us -> 76.1 us (0.29)
  blocking collectives: 183 us -> 0 us
  other arithmetic: 47.3 us -> 1.51 us
  Pallas kernels: 0 us -> 27.6 us
  starting transfers between devices: 0 us -> 22.3 us
  waiting for transfers between devices: 0 us -> 10.9 us
  matrix products: 9.72 us -> 0 us
  between operations: 10.5 us -> 1.55 us
    psum x3 -> x0, blocking collectives: 94.6 us -> none  [the longest x1 34.3 us: shards(): lax.psum((jnp.sum(initial * initial), counts[0].astype(jnp.float32)), ('p...]
    unnamed x2 -> x0, blocking collectives: 59.7 us -> none
    reduce_sum x13 -> x0, other arithmetic: 44.3 us -> none  [the longest x10 42.1 us: near_field(): summed = summed + jnp.sum(block_tile * values[:, column, None, :], axis=2)]
    all_gather x5 -> x0, blocking collectives: 28.7 us -> none  [the longest x2 10.5 us: fetch_rows(): return lax.all_gather(vector, 'sub', axis=0, tiled=True)[near_flat]]
    pallas_call x0 -> x7, Pallas kernels: none -> 27.6 us  [device_call(): pl.pallas_call(kernel, out_shape=tuple(outputs), in_specs=[smem] * len(sc...]
    ppermute x0 -> x21, starting transfers between devices: none -> 22.3 us  [from_peers(): lax.ppermute(value, axis, [(i, i ^ turn) for i in range(size)])]
    ppermute x0 -> x21, waiting for transfers between devices: none -> 10.9 us  [from_peers(): lax.ppermute(value, axis, [(i, i ^ turn) for i in range(size)])]
    dot_general x12 -> x0, matrix products: 9.72 us -> none  [the longest x2 3.47 us: operator(): jnp.einsum('lrp,lp->lr', leaf_basis, vector, precision=HIGH_PRECISION)]
  transfers between devices with their start and end apart: 0 -> 21, of which waited for: 0 -> 7; matrix products, arithmetic and copies ran while one was open for 0% -> 3% of each run, Pallas kernels for 0% -> 30%
where the time goes in v2:
time: 76.1 us; the launch traced here: 75.4 us
  Pallas kernels  27.6 us (36%)
  starting transfers between devices  22.3 us (29%)
  local copies, waits for them, and re-layouts  11.7 us (15%)
  waiting for transfers between devices  10.9 us (14%)
  between operations  1.55 us (2%)
  other arithmetic  1.51 us (2%)
    pallas_call x7, Pallas kernels, device_call(): pl.pallas_call(kernel, out_shape=tuple(outputs), in_specs=[smem] * len(sc...  27.6 us
    ppermute x21, starting transfers between devices, from_peers(): lax.ppermute(value, axis, [(i, i ^ turn) for i in range(size)])  22.3 us
    unnamed x25, local copies, waits for them, and re-layouts  10.9 us
    ppermute x21, waiting for transfers between devices, from_peers(): lax.ppermute(value, axis, [(i, i ^ turn) for i in range(size)])  10.9 us
  transfers between devices with their start and end apart: 21, of which 7 were waited for; matrix products, arithmetic and copies ran while one was open for 3% of the time, Pallas kernels for 30%

profile of v2, /device:TPU:0, one launch (start us, length us, event | category | flops | bytes accessed | tf_op | source)
XLA Modules:
  0.0 75.4 jit_solution(15747222926121629302)
XLA Ops:
  1.3 0.8 %copy.13.points = f32[32,3,128]{2,1,0:T(4,128)S(1)} copy(f32[32,3,128]{2,0,1:T(8,128)} %param.11) | data formatting | bytes 98304 | tf_op args[0]
  2.2 0.8 %copy.14.normals = f32[32,3,128]{2,1,0:T(4,128)S(1)} copy(f32[32,3,128]{2,0,1:T(8,128)} %param.12) | data formatting | bytes 98304 | tf_op args[1]
  3.0 0.7 copy-done.10
  3.8 1.2 %copy-done = f32[32,64,128]{2,1,0:T(8,128)S(1)} copy-done((f32[32,64,128]{2,1,0:T(8,128)S(1)}, f32[32,64,128]{2,1,0:T(8,128)}, u32[]{:S(2)}) %copy-start) | copy-done | bytes 1048600
  5.0 1.2 %copy-done.3 = f32[32,64,64]{2,1,0:T(8,128)S(1)} copy-done((f32[32,64,64]{2,1,0:T(8,128)S(1)}, f32[32,64,64]{2,1,0:T(8,128)}, u32[]{:S(2)}) %copy-start.3) | copy-done | bytes 524312
  7.3 2.5 %collective-permute-start.1 = (f32[40,128]{1,0:T(8,128)S(1)}, f32[40,128]{1,0:T(8,128)S(1)}, u32[]{:S(2)}, u32[]{:S(2)}) collective-permute-start(f32[40,128]{1,0:T(8,128)S(1)} %shard_map.123.refs_4_), channel_id=1, source_target_pairs={{0,2},{1,3},{2,0},{3,1},{4,6},{5,7},{6,4},{7,5},{8,10},{9,11},{10,... | collective-permute-start | bytes 61448 | tf_op jit(solution)/shard_map/ppermute | solution.py:23
  10.1 1.9 %collective-permute-start.7 = (f32[32,8,128]{2,1,0:T(8,128)S(1)}, f32[32,8,128]{2,1,0:T(8,128)S(1)}, u32[]{:S(2)}, u32[]{:S(2)}) collective-permute-start(f32[32,8,128]{2,1,0:T(8,128)S(1)} %get-tuple-element.17.refs_0_), channel_id=1, source_target_pairs={{0,2},{1,3},{2,0},{3,1},{4,6},{5,7},{6,4},{7,5},{8,10},{9,11},{10,... | collective-permute-start | bytes 393224 | tf_op jit(solution)/shard_map/ppermute | solution.py:23
  12.9 0.8 %copy.15 = s32[32,9]{1,0:T(8,128)S(1)} copy(s32[32,9]{0,1:T(8,128)} %param.15) | data formatting | bytes 2304 | tf_op args[4]
  13.8 1.6 %collective-permute-start.3 = (f32[32,128]{1,0:T(8,128)S(1)}, f32[32,128]{1,0:T(8,128)S(1)}, u32[]{:S(2)}, u32[]{:S(2)}) collective-permute-start(f32[32,128]{1,0:T(8,128)S(1)} %pad_maximum_fusion.refs_0_), channel_id=1, source_target_pairs={{0,4},{4,0},{8,12},{12,8},{1,5},{5,1},{9,13},{13,9},{2,6},{6,2},{1... | collective-permute-start | bytes 49160 | tf_op jit(solution)/shard_map/ppermute | solution.py:23
  15.5 2.6 %collective-permute-start.4 = (f32[32,128]{1,0:T(8,128)S(1)}, f32[32,128]{1,0:T(8,128)S(1)}, u32[]{:S(2)}, u32[]{:S(2)}) collective-permute-start(f32[32,128]{1,0:T(8,128)S(1)} %pad_maximum_fusion.refs_0_), channel_id=1, source_target_pairs={{0,8},{4,12},{8,0},{12,4},{1,9},{5,13},{9,1},{13,5},{2,10},{6,14},... | collective-permute-start | bytes 49160 | tf_op jit(solution)/shard_map/ppermute | solution.py:23
  19.5 0.9 %copy-done.6 = f32[8,64,64]{2,1,0:T(8,128)S(1)} copy-done((f32[8,64,64]{2,1,0:T(8,128)S(1)}, f32[8,64,64]{2,1,0:T(8,128)}, u32[]{:S(2)}) %copy-start.6) | copy-done | bytes 131096
  20.4 17.0 %shard_map.124 = (f32[32,128]{1,0:T(8,128)S(1)}, f32[32,128]{1,0:T(8,128)S(1)}, f32[288,128,128]{2,1,0:T(8,128)S(1)}) custom-call(s32[32,9]{1,0:T(8,128)S(1)} %fusion.3.near_rows, f32[32,8,128]{2,1,0:T(8,128)S(1)} %get-tuple-element.17.refs_0_, f32[32,8,128]{2,1,0:T(8,128)S(1)} %collective-permute-done.6.refs_1_, ...), custom_call_target="tpu_custom_call" | custom-call | tf_op jit(solution)/shard_map/pallas_call | solution.py:41
  37.5 1.2 %copy-done.1 = f32[32,64,128]{2,1,0:T(8,128)S(1)} copy-done((f32[32,64,128]{2,1,0:T(8,128)S(1)}, f32[32,64,128]{2,1,0:T(8,128)}, u32[]{:S(2)}) %copy-start.1) | copy-done | bytes 1048600
  38.7 1.2 %copy-done.4 = f32[32,64,64]{2,1,0:T(8,128)S(1)} copy-done((f32[32,64,64]{2,1,0:T(8,128)S(1)}, f32[32,64,64]{2,1,0:T(8,128)}, u32[]{:S(2)}) %copy-start.4) | copy-done | bytes 524312
  39.9 0.9 %copy-done.8 = f32[8,64,64]{2,1,0:T(8,128)S(1)} copy-done((f32[8,64,64]{2,1,0:T(8,128)S(1)}, f32[8,64,64]{2,1,0:T(8,128)}, u32[]{:S(2)}) %copy-start.8) | copy-done | bytes 131096
  40.9 1.9 %shard_map.125 = (f32[72,128]{1,0:T(8,128)S(1)}, f32[32,128]{1,0:T(8,128)S(1)}, f32[8,128]{1,0:T(8,128)S(1)}) custom-call(s32[1]{0:T(128)S(6)} %copy.17.counts, s32[8]{0:T(128)S(1)} %fusion.18.box_rows, f32[32,128]{1,0:T(8,128)S(1)} %pad_maximum_fusion.refs_0_, f32[32,128]{1,0:T(8,128)S(1)} %collective-permute-done.3.refs_1_, ...), custom_call_target="tpu_custom_call" | custom-call | tf_op jit(solution)/shard_map/pallas_call | solution.py:41
  43.0 0.9 %collective-permute-start.10 = (f32[72,128]{1,0:T(8,128)S(1)}, f32[72,128]{1,0:T(8,128)S(1)}, u32[]{:S(2)}, u32[]{:S(2)}) collective-permute-start(f32[72,128]{1,0:T(8,128)S(1)} %get-tuple-element.20.refs_0_.refs_6_), channel_id=1, source_target_pairs={{0,2},{1,3},{2,0},{3,1},{4,6},{5,7},{6,4},{7,5},{8,10},{9,11},{10,... | collective-permute-start | bytes 110600 | tf_op jit(solution)/shard_map/ppermute | solution.py:23
  43.9 0.8 %collective-permute-start.11 = (f32[72,128]{1,0:T(8,128)S(1)}, f32[72,128]{1,0:T(8,128)S(1)}, u32[]{:S(2)}, u32[]{:S(2)}) collective-permute-start(f32[72,128]{1,0:T(8,128)S(1)} %get-tuple-element.20.refs_0_.refs_6_), channel_id=1, source_target_pairs={{0,3},{1,2},{2,1},{3,0},{4,7},{5,6},{6,5},{7,4},{8,11},{9,10},{10,... | collective-permute-start | bytes 110600 | tf_op jit(solution)/shard_map/ppermute | solution.py:23
  44.7 2.3 %collective-permute-done.10.refs_2_ = f32[72,128]{1,0:T(8,128)S(1)} collective-permute-done((f32[72,128]{1,0:T(8,128)S(1)}, f32[72,128]{1,0:T(8,128)S(1)}, u32[]{:S(2)}, u32[]{:S(2)}) %collective-permute-start.10) | collective-permute-done | bytes 36896 | tf_op jit(solution)/shard_map/ppermute | solution.py:23
  47.4 1.8 %collective-permute-start.12 = (f32[32,128]{1,0:T(8,128)S(1)}, f32[32,128]{1,0:T(8,128)S(1)}, u32[]{:S(2)}, u32[]{:S(2)}) collective-permute-start(f32[32,128]{1,0:T(8,128)S(1)} %pad_maximum_fusion.1.refs_0_), channel_id=1, source_target_pairs={{0,4},{4,0},{8,12},{12,8},{1,5},{5,1},{9,13},{13,9},{2,6},{6,2},{1... | collective-permute-start | bytes 49160 | tf_op jit(solution)/shard_map/ppermute | solution.py:23
  49.2 2.5 %collective-permute-start.13 = (f32[32,128]{1,0:T(8,128)S(1)}, f32[32,128]{1,0:T(8,128)S(1)}, u32[]{:S(2)}, u32[]{:S(2)}) collective-permute-start(f32[32,128]{1,0:T(8,128)S(1)} %pad_maximum_fusion.1.refs_0_), channel_id=1, source_target_pairs={{0,8},{4,12},{8,0},{12,4},{1,9},{5,13},{9,1},{13,5},{2,10},{6,14},... | collective-permute-start | bytes 49160 | tf_op jit(solution)/shard_map/ppermute | solution.py:23
  51.8 0.9 %copy-done.7 = f32[8,64,64]{2,1,0:T(8,128)S(1)} copy-done((f32[8,64,64]{2,1,0:T(8,128)S(1)}, f32[8,64,64]{2,1,0:T(8,128)}, u32[]{:S(2)}) %copy-start.7) | copy-done | bytes 131096
  52.7 5.4 %shard_map.126 = (f32[32,128]{1,0:T(8,128)S(1)}, f32[32,128]{1,0:T(8,128)S(1)}) custom-call(s32[32,9]{1,0:T(8,128)S(1)} %fusion.3.near_rows, f32[72,128]{1,0:T(8,128)S(1)} %get-tuple-element.20.refs_0_.refs_6_, f32[72,128]{1,0:T(8,128)S(1)} %collective-permute-done.9.refs_1_, f32[72,128]{1,0:T(8,128)S(1)} %collective-permute-done.10.refs_2_, ...), custom_call_target="tpu_custom_call" | custom-call | tf_op jit(solution)/shard_map/pallas_call | solution.py:41
  58.2 1.5 %shard_map.127 = (f32[32,128]{1,0:T(8,128)S(1)}, f32[32,128]{1,0:T(8,128)S(1)}, f32[8,128]{1,0:T(8,128)S(1)}, f32[8,128]{1,0:T(8,128)S(1)}) custom-call(s32[1]{0:T(128)S(6)} %copy.17.counts, s32[8]{0:T(128)S(1)} %fusion.18.box_rows, f32[32,128]{1,0:T(8,128)S(1)} %pad_maximum_fusion.1.refs_0_, f32[32,128]{1,0:T(8,128)S(1)} %collective-permute-done.12.refs_1_, ...), custom_call_target="tpu_custom_call" | custom-call | tf_op jit(solution)/shard_map/pallas_call | solution.py:41
  59.8 1.2 %collective-permute-start.16 = (f32[8,128]{1,0:T(8,128)S(1)}, f32[8,128]{1,0:T(8,128)S(1)}, u32[]{:S(2)}, u32[]{:S(2)}) collective-permute-start(f32[8,128]{1,0:T(8,128)S(1)} %get-tuple-element.26), channel_id=1, source_target_pairs={{0,2},{1,3},{2,0},{3,1},{4,6},{5,7},{6,4},{7,5},{8,10},{9,11},{10,... | collective-permute-start | bytes 12296 | tf_op jit(solution)/shard_map/ppermute | solution.py:23
  61.0 0.7 collective-permute-start.17
  61.7 1.8 %collective-permute-done.16 = f32[8,128]{1,0:T(8,128)S(1)} collective-permute-done((f32[8,128]{1,0:T(8,128)S(1)}, f32[8,128]{1,0:T(8,128)S(1)}, u32[]{:S(2)}, u32[]{:S(2)}) %collective-permute-start.16) | collective-permute-done | bytes 4128 | tf_op jit(solution)/shard_map/ppermute | solution.py:23
  64.0 0.7 collective-permute-start.18
  64.8 3.6 %collective-permute-start.19 = (f32[8,128]{1,0:T(8,128)S(1)}, f32[8,128]{1,0:T(8,128)S(1)}, u32[]{:S(2)}, u32[]{:S(2)}) collective-permute-start(f32[8,128]{1,0:T(8,128)S(1)} %add_add_fusion.refs_0_), channel_id=1, source_target_pairs={{0,8},{4,12},{8,0},{12,4},{1,9},{5,13},{9,1},{13,5},{2,10},{6,14},... | collective-permute-start | bytes 12296 | tf_op jit(solution)/shard_map/ppermute | solution.py:23
  68.4 1.5 %collective-permute-done.19.refs_2_ = f32[8,128]{1,0:T(8,128)S(1)} collective-permute-done((f32[8,128]{1,0:T(8,128)S(1)}, f32[8,128]{1,0:T(8,128)S(1)}, u32[]{:S(2)}, u32[]{:S(2)}) %collective-permute-start.19) | collective-permute-done | bytes 4128 | tf_op jit(solution)/shard_map/ppermute | solution.py:23
  70.0 3.8 %collective-permute-done.20.refs_3_ = f32[8,128]{1,0:T(8,128)S(1)} collective-permute-done((f32[8,128]{1,0:T(8,128)S(1)}, f32[8,128]{1,0:T(8,128)S(1)}, u32[]{:S(2)}, u32[]{:S(2)}) %collective-permute-start.20) | collective-permute-done | bytes 4128 | tf_op jit(solution)/shard_map/ppermute | solution.py:23
  73.8 1.0 %shard_map.128 = (f32[32,128]{1,0:T(8,128)}, f32[3,2]{1,0:T(4,128)S(1)}) custom-call(f32[8,128]{1,0:T(8,128)S(1)} %add_add_fusion.refs_0_, f32[8,128]{1,0:T(8,128)S(1)} %collective-permute-done.18.refs_1_, f32[8,128]{1,0:T(8,128)S(1)} %collective-permute-done.19.refs_2_, f32[8,128]{1,0:T(8,128)S(1)} %collective-permute-done.20.refs_3_, ...), custom_call_target="tpu_custom_call" | custom-call | tf_op jit(solution)/shard_map/pallas_call | solution.py:41
  (59 shorter events, 5.7 us)
Async XLA Ops:
  0.6 57.6 %copy-start.9 = (f32[8,64,64]{2,1,0:T(8,128)S(1)}, f32[8,64,64]{2,1,0:T(8,128)}, u32[]{:S(2)}) copy-start(f32[8,64,64]{2,1,0:T(8,128)} %refs_11_.1) | copy-start | bytes 393220
  3.0 0.7 copy-start.10
  3.8 1.2 %copy-start = (f32[32,64,128]{2,1,0:T(8,128)S(1)}, f32[32,64,128]{2,1,0:T(8,128)}, u32[]{:S(2)}) copy-start(f32[32,64,128]{2,1,0:T(8,128)} %refs_9_.5) | copy-start | bytes 3145732
  5.0 1.2 %copy-start.3 = (f32[32,64,64]{2,1,0:T(8,128)S(1)}, f32[32,64,64]{2,1,0:T(8,128)}, u32[]{:S(2)}) copy-start(f32[32,64,64]{2,1,0:T(8,128)} %refs_10_.1) | copy-start | bytes 1572868
  6.2 52.0 %copy-start.2 = (f32[32,64,128]{2,1,0:T(8,128)S(1)}, f32[32,64,128]{2,1,0:T(8,128)}, u32[]{:S(2)}) copy-start(f32[32,64,128]{2,1,0:T(8,128)} %refs_9_.5) | copy-start | bytes 3145732
  6.2 52.0 %copy-start.5 = (f32[32,64,64]{2,1,0:T(8,128)S(1)}, f32[32,64,64]{2,1,0:T(8,128)}, u32[]{:S(2)}) copy-start(f32[32,64,64]{2,1,0:T(8,128)} %refs_10_.1) | copy-start | bytes 1572868
  6.9 6.8 %collective-permute-start = (f32[40,128]{1,0:T(8,128)S(1)}, f32[40,128]{1,0:T(8,128)S(1)}, u32[]{:S(2)}, u32[]{:S(2)}) collective-permute-start(f32[40,128]{1,0:T(8,128)S(1)} %shard_map.123.refs_4_), channel_id=1, source_target_pairs={{0,1},{1,0},{2,3},{3,2},{4,5},{5,4},{6,7},{7,6},{8,9},{9,8},{10,11... | collective-permute-start | bytes 61448 | tf_op jit(solution)/shard_map/ppermute | solution.py:23
  7.3 6.5 %collective-permute-start.1 = (f32[40,128]{1,0:T(8,128)S(1)}, f32[40,128]{1,0:T(8,128)S(1)}, u32[]{:S(2)}, u32[]{:S(2)}) collective-permute-start(f32[40,128]{1,0:T(8,128)S(1)} %shard_map.123.refs_4_), channel_id=1, source_target_pairs={{0,2},{1,3},{2,0},{3,1},{4,6},{5,7},{6,4},{7,5},{8,10},{9,11},{10,... | collective-permute-start | bytes 61448 | tf_op jit(solution)/shard_map/ppermute | solution.py:23
  9.8 4.0 %collective-permute-start.2 = (f32[40,128]{1,0:T(8,128)S(1)}, f32[40,128]{1,0:T(8,128)S(1)}, u32[]{:S(2)}, u32[]{:S(2)}) collective-permute-start(f32[40,128]{1,0:T(8,128)S(1)} %shard_map.123.refs_4_), channel_id=1, source_target_pairs={{0,3},{1,2},{2,1},{3,0},{4,7},{5,6},{6,5},{7,4},{8,11},{9,10},{10,... | collective-permute-start | bytes 61448 | tf_op jit(solution)/shard_map/ppermute | solution.py:23
  9.9 8.1 %collective-permute-start.6 = (f32[32,8,128]{2,1,0:T(8,128)S(1)}, f32[32,8,128]{2,1,0:T(8,128)S(1)}, u32[]{:S(2)}, u32[]{:S(2)}) collective-permute-start(f32[32,8,128]{2,1,0:T(8,128)S(1)} %get-tuple-element.17.refs_0_), channel_id=1, source_target_pairs={{0,1},{1,0},{2,3},{3,2},{4,5},{5,4},{6,7},{7,6},{8,9},{9,8},{10,11... | collective-permute-start | bytes 393224 | tf_op jit(solution)/shard_map/ppermute | solution.py:23
  10.1 8.9 %collective-permute-start.7 = (f32[32,8,128]{2,1,0:T(8,128)S(1)}, f32[32,8,128]{2,1,0:T(8,128)S(1)}, u32[]{:S(2)}, u32[]{:S(2)}) collective-permute-start(f32[32,8,128]{2,1,0:T(8,128)S(1)} %get-tuple-element.17.refs_0_), channel_id=1, source_target_pairs={{0,2},{1,3},{2,0},{3,1},{4,6},{5,7},{6,4},{7,5},{8,10},{9,11},{10,... | collective-permute-start | bytes 393224 | tf_op jit(solution)/shard_map/ppermute | solution.py:23
  13.7 5.8 %collective-permute-start.8 = (f32[32,8,128]{2,1,0:T(8,128)S(1)}, f32[32,8,128]{2,1,0:T(8,128)S(1)}, u32[]{:S(2)}, u32[]{:S(2)}) collective-permute-start(f32[32,8,128]{2,1,0:T(8,128)S(1)} %get-tuple-element.17.refs_0_), channel_id=1, source_target_pairs={{0,3},{1,2},{2,1},{3,0},{4,7},{5,6},{6,5},{7,4},{8,11},{9,10},{10,... | collective-permute-start | bytes 393224 | tf_op jit(solution)/shard_map/ppermute | solution.py:23
  13.8 23.6 %collective-permute-start.3 = (f32[32,128]{1,0:T(8,128)S(1)}, f32[32,128]{1,0:T(8,128)S(1)}, u32[]{:S(2)}, u32[]{:S(2)}) collective-permute-start(f32[32,128]{1,0:T(8,128)S(1)} %pad_maximum_fusion.refs_0_), channel_id=1, source_target_pairs={{0,4},{4,0},{8,12},{12,8},{1,5},{5,1},{9,13},{13,9},{2,6},{6,2},{1... | collective-permute-start | bytes 49160 | tf_op jit(solution)/shard_map/ppermute | solution.py:23
  15.5 22.0 %collective-permute-start.4 = (f32[32,128]{1,0:T(8,128)S(1)}, f32[32,128]{1,0:T(8,128)S(1)}, u32[]{:S(2)}, u32[]{:S(2)}) collective-permute-start(f32[32,128]{1,0:T(8,128)S(1)} %pad_maximum_fusion.refs_0_), channel_id=1, source_target_pairs={{0,8},{4,12},{8,0},{12,4},{1,9},{5,13},{9,1},{13,5},{2,10},{6,14},... | collective-permute-start | bytes 49160 | tf_op jit(solution)/shard_map/ppermute | solution.py:23
  18.1 19.4 %collective-permute-start.5 = (f32[32,128]{1,0:T(8,128)S(1)}, f32[32,128]{1,0:T(8,128)S(1)}, u32[]{:S(2)}, u32[]{:S(2)}) collective-permute-start(f32[32,128]{1,0:T(8,128)S(1)} %pad_maximum_fusion.refs_0_), channel_id=1, source_target_pairs={{0,12},{4,8},{8,4},{12,0},{1,13},{5,9},{9,5},{13,1},{2,14},{6,10},... | collective-permute-start | bytes 49160 | tf_op jit(solution)/shard_map/ppermute | solution.py:23
  19.5 1.0 %copy-start.6 = (f32[8,64,64]{2,1,0:T(8,128)S(1)}, f32[8,64,64]{2,1,0:T(8,128)}, u32[]{:S(2)}) copy-start(f32[8,64,64]{2,1,0:T(8,128)} %refs_5_.1) | copy-start | bytes 393220
  37.5 1.2 %copy-start.1 = (f32[32,64,128]{2,1,0:T(8,128)S(1)}, f32[32,64,128]{2,1,0:T(8,128)}, u32[]{:S(2)}) copy-start(f32[32,64,128]{2,1,0:T(8,128)} %refs_9_.5) | copy-start | bytes 3145732
  38.7 1.2 %copy-start.4 = (f32[32,64,64]{2,1,0:T(8,128)S(1)}, f32[32,64,64]{2,1,0:T(8,128)}, u32[]{:S(2)}) copy-start(f32[32,64,64]{2,1,0:T(8,128)} %refs_10_.1) | copy-start | bytes 1572868
  39.9 0.9 %copy-start.8 = (f32[8,64,64]{2,1,0:T(8,128)S(1)}, f32[8,64,64]{2,1,0:T(8,128)}, u32[]{:S(2)}) copy-start(f32[8,64,64]{2,1,0:T(8,128)} %refs_11_.1) | copy-start | bytes 393220
  42.8 1.9 %collective-permute-start.9 = (f32[72,128]{1,0:T(8,128)S(1)}, f32[72,128]{1,0:T(8,128)S(1)}, u32[]{:S(2)}, u32[]{:S(2)}) collective-permute-start(f32[72,128]{1,0:T(8,128)S(1)} %get-tuple-element.20.refs_0_.refs_6_), channel_id=1, source_target_pairs={{0,1},{1,0},{2,3},{3,2},{4,5},{5,4},{6,7},{7,6},{8,9},{9,8},{10,11... | collective-permute-start | bytes 110600 | tf_op jit(solution)/shard_map/ppermute | solution.py:23
  43.0 4.1 %collective-permute-start.10 = (f32[72,128]{1,0:T(8,128)S(1)}, f32[72,128]{1,0:T(8,128)S(1)}, u32[]{:S(2)}, u32[]{:S(2)}) collective-permute-start(f32[72,128]{1,0:T(8,128)S(1)} %get-tuple-element.20.refs_0_.refs_6_), channel_id=1, source_target_pairs={{0,2},{1,3},{2,0},{3,1},{4,6},{5,7},{6,4},{7,5},{8,10},{9,11},{10,... | collective-permute-start | bytes 110600 | tf_op jit(solution)/shard_map/ppermute | solution.py:23
  43.9 3.5 %collective-permute-start.11 = (f32[72,128]{1,0:T(8,128)S(1)}, f32[72,128]{1,0:T(8,128)S(1)}, u32[]{:S(2)}, u32[]{:S(2)}) collective-permute-start(f32[72,128]{1,0:T(8,128)S(1)} %get-tuple-element.20.refs_0_.refs_6_), channel_id=1, source_target_pairs={{0,3},{1,2},{2,1},{3,0},{4,7},{5,6},{6,5},{7,4},{8,11},{9,10},{10,... | collective-permute-start | bytes 110600 | tf_op jit(solution)/shard_map/ppermute | solution.py:23
  47.4 10.8 %collective-permute-start.12 = (f32[32,128]{1,0:T(8,128)S(1)}, f32[32,128]{1,0:T(8,128)S(1)}, u32[]{:S(2)}, u32[]{:S(2)}) collective-permute-start(f32[32,128]{1,0:T(8,128)S(1)} %pad_maximum_fusion.1.refs_0_), channel_id=1, source_target_pairs={{0,4},{4,0},{8,12},{12,8},{1,5},{5,1},{9,13},{13,9},{2,6},{6,2},{1... | collective-permute-start | bytes 49160 | tf_op jit(solution)/shard_map/ppermute | solution.py:23
  49.2 9.0 %collective-permute-start.13 = (f32[32,128]{1,0:T(8,128)S(1)}, f32[32,128]{1,0:T(8,128)S(1)}, u32[]{:S(2)}, u32[]{:S(2)}) collective-permute-start(f32[32,128]{1,0:T(8,128)S(1)} %pad_maximum_fusion.1.refs_0_), channel_id=1, source_target_pairs={{0,8},{4,12},{8,0},{12,4},{1,9},{5,13},{9,1},{13,5},{2,10},{6,14},... | collective-permute-start | bytes 49160 | tf_op jit(solution)/shard_map/ppermute | solution.py:23
  51.7 6.5 %collective-permute-start.14 = (f32[32,128]{1,0:T(8,128)S(1)}, f32[32,128]{1,0:T(8,128)S(1)}, u32[]{:S(2)}, u32[]{:S(2)}) collective-permute-start(f32[32,128]{1,0:T(8,128)S(1)} %pad_maximum_fusion.1.refs_0_), channel_id=1, source_target_pairs={{0,12},{4,8},{8,4},{12,0},{1,13},{5,9},{9,5},{13,1},{2,14},{6,10},... | collective-permute-start | bytes 49160 | tf_op jit(solution)/shard_map/ppermute | solution.py:23
  51.8 0.9 %copy-start.7 = (f32[8,64,64]{2,1,0:T(8,128)S(1)}, f32[8,64,64]{2,1,0:T(8,128)}, u32[]{:S(2)}) copy-start(f32[8,64,64]{2,1,0:T(8,128)} %refs_5_.1) | copy-start | bytes 393220
  59.8 1.9 %collective-permute-start.15 = (f32[8,128]{1,0:T(8,128)S(1)}, f32[8,128]{1,0:T(8,128)S(1)}, u32[]{:S(2)}, u32[]{:S(2)}) collective-permute-start(f32[8,128]{1,0:T(8,128)S(1)} %get-tuple-element.26), channel_id=1, source_target_pairs={{0,1},{1,0},{2,3},{3,2},{4,5},{5,4},{6,7},{7,6},{8,9},{9,8},{10,11... | collective-permute-start | bytes 12296 | tf_op jit(solution)/shard_map/ppermute | solution.py:23
  59.8 3.7 %collective-permute-start.16 = (f32[8,128]{1,0:T(8,128)S(1)}, f32[8,128]{1,0:T(8,128)S(1)}, u32[]{:S(2)}, u32[]{:S(2)}) collective-permute-start(f32[8,128]{1,0:T(8,128)S(1)} %get-tuple-element.26), channel_id=1, source_target_pairs={{0,2},{1,3},{2,0},{3,1},{4,6},{5,7},{6,4},{7,5},{8,10},{9,11},{10,... | collective-permute-start | bytes 12296 | tf_op jit(solution)/shard_map/ppermute | solution.py:23
  61.0 3.0 %collective-permute-start.17 = (f32[8,128]{1,0:T(8,128)S(1)}, f32[8,128]{1,0:T(8,128)S(1)}, u32[]{:S(2)}, u32[]{:S(2)}) collective-permute-start(f32[8,128]{1,0:T(8,128)S(1)} %get-tuple-element.26), channel_id=1, source_target_pairs={{0,3},{1,2},{2,1},{3,0},{4,7},{5,6},{6,5},{7,4},{8,11},{9,10},{10,... | collective-permute-start | bytes 12296 | tf_op jit(solution)/shard_map/ppermute | solution.py:23
  64.0 4.4 %collective-permute-start.18 = (f32[8,128]{1,0:T(8,128)S(1)}, f32[8,128]{1,0:T(8,128)S(1)}, u32[]{:S(2)}, u32[]{:S(2)}) collective-permute-start(f32[8,128]{1,0:T(8,128)S(1)} %add_add_fusion.refs_0_), channel_id=1, source_target_pairs={{0,4},{4,0},{8,12},{12,8},{1,5},{5,1},{9,13},{13,9},{2,6},{6,2},{1... | collective-permute-start | bytes 12296 | tf_op jit(solution)/shard_map/ppermute | solution.py:23
  64.8 5.2 %collective-permute-start.19 = (f32[8,128]{1,0:T(8,128)S(1)}, f32[8,128]{1,0:T(8,128)S(1)}, u32[]{:S(2)}, u32[]{:S(2)}) collective-permute-start(f32[8,128]{1,0:T(8,128)S(1)} %add_add_fusion.refs_0_), channel_id=1, source_target_pairs={{0,8},{4,12},{8,0},{12,4},{1,9},{5,13},{9,1},{13,5},{2,10},{6,14},... | collective-permute-start | bytes 12296 | tf_op jit(solution)/shard_map/ppermute | solution.py:23
  68.4 5.4 %collective-permute-start.20 = (f32[8,128]{1,0:T(8,128)S(1)}, f32[8,128]{1,0:T(8,128)S(1)}, u32[]{:S(2)}, u32[]{:S(2)}) collective-permute-start(f32[8,128]{1,0:T(8,128)S(1)} %add_add_fusion.refs_0_), channel_id=1, source_target_pairs={{0,12},{4,8},{8,4},{12,0},{1,13},{5,9},{9,5},{13,1},{2,14},{6,10},... | collective-permute-start | bytes 12296 | tf_op jit(solution)/shard_map/ppermute | solution.py:23

commit v3 on v2

--- a/solution.py
+++ b/solution.py
@@ -35,17 +35,22 @@
     return parts[0]
 
 
-def device_call(kernel, outputs, scalars, arrays, scratch=()):
+def device_call(kernel, outputs, scalars, arrays, scratch=(), remote=()):
     smem = pl.BlockSpec(memory_space=pltpu.SMEM)
     vmem = pl.BlockSpec(memory_space=pltpu.VMEM)
+    hbm = pl.BlockSpec(memory_space=pltpu.HBM)
     return pl.pallas_call(
         kernel,
         out_shape=tuple(outputs),
-        in_specs=[smem] * len(scalars) + [vmem] * len(arrays),
+        in_specs=[smem] * len(scalars) + [vmem] * len(arrays) + [hbm] * len(remote),
         out_specs=tuple([vmem] * len(outputs)),
         scratch_shapes=tuple(scratch),
         compiler_params=pltpu.CompilerParams(vmem_limit_bytes=VMEM_LIMIT),
-    )(*scalars, *arrays)
+    )(*scalars, *arrays, *remote)
+
+
+def kept(array):
+    return pltpu.VMEM(array.shape, array.dtype)
 
 
 def f32(*shape):
@@ -72,12 +77,21 @@
     return row
 
 
-def pack_kernel(counts, points, normals, density, geometry, initial):
-    slots, dims, width = points.shape
-    used = jnp.where(iota((slots, width), 0) < counts[0], density[...], 0.0)
+def pack_kernel(counts, points, normals, density, geometry, initial, at, arrived):
+    dims, slots, width = points.shape
+    copies = [
+        pltpu.make_async_copy(points, at.at[0:dims], arrived.at[0]),
+        pltpu.make_async_copy(normals, at.at[dims : 2 * dims], arrived.at[1]),
+        pltpu.make_async_copy(density, at.at[2 * dims], arrived.at[2]),
+    ]
+    for copy in copies:
+        copy.start()
+    for copy in copies:
+        copy.wait()
+    for row in range(2 * dims):
+        geometry[:, row, :] = at[row]
+    used = jnp.where(iota((slots, width), 0) < counts[0], at[2 * dims], 0.0)
     initial[...] = used
-    geometry[:, 0:dims, :] = points[...]
-    geometry[:, dims : 2 * dims, :] = normals[...]
     geometry[:, 2 * dims, :] = used
     geometry[:, 2 * dims + 1, :] = jnp.zeros_like(used)
 
@@ -102,11 +116,20 @@
     message[end + 1 : end + 2, :] = sums
 
 
-def first_moments_kernel(counts, initial, basis, transfer, message):
+def first_moments_kernel(counts, initial, *refs):
+    sources, message, held, arrived = refs[:4], refs[4], refs[5:9], refs[9]
+    copies = [
+        pltpu.make_async_copy(source, target, arrived.at[place])
+        for place, (source, target) in enumerate(zip(sources, held))
+    ]
+    for copy in copies:
+        copy.start()
+    for copy in copies:
+        copy.wait()
     vector = initial[...]
     square_sum = jnp.sum(vector * vector, keepdims=True)
     in_use = jnp.full((1, 1), counts[0], jnp.int32).astype(jnp.float32)
-    write_moments(initial, lane_row([square_sum, in_use]), basis, transfer, message, 0)
+    write_moments(initial, lane_row([square_sum, in_use]), held[0], held[1], message, 0)
 
 
 def leaf_part(moments, picks, coupling):
@@ -129,11 +152,11 @@
     return local
 
 
-def first_near_kernel(subs, near_rows, *refs):
+def first_near_kernel(subs, offset, near_list, *refs):
     geometry, messages = refs[:subs], refs[subs : 2 * subs]
     picks, coupling, near, local, values, features, squares, fields = refs[2 * subs :]
     slots, height, width = geometry[0].shape
-    neighbours = near_rows.shape[1]
+    neighbours = near_list.shape[0]
     rank = coupling.shape[1]
     row = iota((height, width), 0)
     scale_square = jnp.where(row < 3, -2.0, 0.0)
@@ -174,7 +197,7 @@
         left = jnp.concatenate([one, one, two, two, three, one]).T.astype(jnp.bfloat16)
         total = jnp.zeros((width, width), jnp.float32)
         for column in range(neighbours):
-            place = near_rows[leaf, column]
+            place = near_list[column, leaf] ^ offset[0]
             upper, lower = features[place, 0:16, :], features[place, 16:32, :]
             right = jnp.concatenate([upper, upper, lower], axis=0)
             both = jnp.dot(left, right, preferred_element_type=jnp.float32)
@@ -185,16 +208,16 @@
         near[pl.ds(leaf, 1), :] = jnp.sum(total.T, axis=0, keepdims=True)
         return carry
 
-    lax.fori_loop(0, slots, target, 0)
+    lax.fori_loop(0, slots, target, 0, unroll=True)
     local[...] = jnp.zeros_like(local)
     local[:, 0:rank] = leaf_part([ref[0:slots, 0:rank] for ref in messages], picks, coupling)
 
 
-def second_near_kernel(subs, near_rows, *refs):
+def second_near_kernel(subs, offset, near_list, *refs):
     messages = refs[:subs]
     picks, coupling, values, near, local, fields = refs[subs:]
     slots, width = near.shape
-    neighbours = near_rows.shape[1]
+    neighbours = near_list.shape[0]
     rank = coupling.shape[1]
     for sub in range(subs):
         fields[sub * slots : (sub + 1) * slots, :] = messages[sub][0:slots, :]
@@ -202,12 +225,12 @@
     def target(leaf, carry):
         total = jnp.zeros((width, width), jnp.float32)
         for column in range(neighbours):
-            place = near_rows[leaf, column]
+            place = near_list[column, leaf] ^ offset[0]
             total = total + values[leaf * neighbours + column] * fields[pl.ds(place, 1), :]
         near[pl.ds(leaf, 1), :] = jnp.sum(total.T, axis=0, keepdims=True)
         return carry
 
-    lax.fori_loop(0, slots, target, 0)
+    lax.fori_loop(0, slots, target, 0, unroll=True)
     local[...] = jnp.zeros_like(local)
     local[:, 0:rank] = leaf_part(
         [ref[slots : 2 * slots, 0:rank] for ref in messages], picks, coupling
@@ -309,10 +332,8 @@
     )
 
 
-def last_kernel(patches, *refs):
-    parts = refs[:patches]
-    basis_one, basis_two, image_two, numbers, basis_three, hessenberg = refs[patches:]
-    sums = tree_sum([ref[0:1, :] for ref in parts])
+def last_kernel(parts, basis_one, basis_two, image_two, numbers, basis_three, hessenberg):
+    sums = jnp.sum(parts[...], axis=0, keepdims=True)
     k_one, k_two, k_sq = sums[:, 0:1], sums[:, 1:2], sums[:, 2:3]
     one_one, unknowns, upper_first, lower_first, one_two, two_two = [
         numbers[0:1, place : place + 1] for place in range(6)
@@ -332,7 +353,7 @@
     basis_three[...] = (
         image_two[...] - upper_second * basis_one[...] - shift * basis_two[...]
     ) / lower_second
-    row, column = iota(hessenberg.shape, 0), iota(hessenberg.shape, 1)
+    column, row = iota(hessenberg.shape, 0), iota(hessenberg.shape, 1)
     matrix = jnp.where(column == 0, upper_first, upper_second)
     matrix = jnp.where(row == 1, jnp.where(column == 0, lower_first, middle_second), matrix)
     hessenberg[...] = jnp.where(row == 2, jnp.where(column == 0, 0.0, lower_second), matrix)
@@ -360,13 +381,11 @@
     patch_start = lax.axis_index("patch") * sources
     rows = f32(slots, width)
 
-    def row_of(leaf):
-        leaf = leaf - patch_start
-        return place_of(leaf // slots, "sub") * slots + leaf % slots
-
-    near_rows = row_of(near_list)
+    offset = patch_start + lax.axis_index("sub") * slots
+    offsets = offset.reshape(1).astype(jnp.int32)
+    near_list = near_list.T
     picks = (
-        row_of(leaf_far).T.reshape(far_count * slots, 1) == jnp.arange(sources)[None, :]
+        leaf_far.T.reshape(far_count * slots, 1) == (jnp.arange(sources) ^ offset)[None, :]
     ).astype(jnp.bfloat16)
     box_rows = TILE_ROWS * (
         place_of(box_far[0] // subs, "patch") * subs + place_of(box_far[0] % subs, "sub")
@@ -378,21 +397,29 @@
         )
 
     geometry, initial = device_call(
-        pack_kernel, [f32(slots, 8, width), rows], [counts], [points, normals, density]
+        pack_kernel,
+        [f32(slots, 8, width), rows],
+        [counts],
+        [],
+        [pltpu.VMEM((7, slots, width), jnp.float32), pltpu.SemaphoreType.DMA((3,))],
+        [points.transpose(1, 0, 2), normals.transpose(1, 0, 2), density],
     )
     geometry = from_peers(geometry, "sub")
-    (message,) = device_call(
+    matrices = [leaf_basis, leaf_to_box_transfer, leaf_coupling, box_coupling]
+    message, leaf_basis, leaf_to_box_transfer, leaf_coupling, box_coupling = device_call(
         first_moments_kernel,
-        [f32(slots + TILE_ROWS, LANES)],
+        [f32(slots + TILE_ROWS, LANES), *[kept(matrix) for matrix in matrices]],
         [counts],
-        [initial, leaf_basis, leaf_to_box_transfer],
+        [initial],
+        [pltpu.SemaphoreType.DMA((4,))],
+        matrices,
     )
     messages = from_peers(message, "sub")
     boxes = box_parts(messages, slots)
     near, local, values = device_call(
         functools.partial(first_near_kernel, subs),
         [rows, f32(slots, LANES), pltpu.VMEM((slots * neighbours, width, width), jnp.float32)],
-        [near_rows],
+        [offsets, near_list],
         [*geometry, *messages, picks, leaf_coupling],
         [
             pltpu.VMEM((sources, 32, 2 * width), jnp.bfloat16),
@@ -417,13 +444,13 @@
     near, local = device_call(
         functools.partial(second_near_kernel, subs),
         [rows, f32(slots, LANES)],
-        [near_rows],
+        [offsets, near_list],
         [*messages, picks, leaf_coupling, values],
         [pltpu.VMEM((sources, width), jnp.float32)],
     )
     basis_two, image_two, partial, numbers = device_call(
         functools.partial(second_image_kernel, patches),
-        [rows, rows, f32(TILE_ROWS, LANES), f32(TILE_ROWS, LANES)],
+        [rows, rows, f32(patches * subs, LANES), f32(TILE_ROWS, LANES)],
         [counts, box_rows],
         [
             *boxes,
@@ -438,13 +465,11 @@
         ],
         far_scratch,
     )
-    parts = from_peers(tree_sum(from_peers(partial, "sub")), "patch")
-    return device_call(
-        functools.partial(last_kernel, patches),
-        [rows, f32(3, 2)],
-        [],
-        [*parts, basis_one, basis_two, image_two, numbers],
-    )
+    parts = lax.all_to_all(partial, ("patch", "sub"), 0, 0, tiled=True)
+    basis_three, hessenberg = device_call(
+        last_kernel, [rows, f32(2, 3)], [], [parts, basis_one, basis_two, image_two, numbers]
+    )
+    return basis_three, hessenberg.T
 
 
 def solution(mesh):

time: 76.1 us -> 59.5 us (0.78)
  Pallas kernels: 27.6 us -> 16.2 us
  blocking collectives: 0 us -> 9.41 us
  starting transfers between devices: 22.3 us -> 16.1 us
  waiting for transfers between devices: 10.9 us -> 6.14 us
  local copies, waits for them, and re-layouts: 11.7 us -> 8.82 us
    pallas_call x7, Pallas kernels: 27.6 us -> 16.2 us  [device_call(): pl.pallas_call(kernel, out_shape=tuple(outputs), in_specs=[smem] * len(sc...]
    all_to_all x0 -> x1, blocking collectives: none -> 9.41 us  [shards(): parts = lax.all_to_all(partial, ('patch', 'sub'), 0, 0, tiled=True)]
    ppermute x21 -> x15, starting transfers between devices: 22.3 us -> 16.1 us  [from_peers(): lax.ppermute(value, axis, [(i, i ^ turn) for i in range(size)])]
    ppermute x21 -> x15, waiting for transfers between devices: 10.9 us -> 6.14 us  [from_peers(): lax.ppermute(value, axis, [(i, i ^ turn) for i in range(size)])]
    unnamed x25 -> x18, local copies, waits for them, and re-layouts: 10.9 us -> 8.04 us
  transfers between devices with their start and end apart: 21 -> 15, of which waited for: 7 -> 5; matrix products, arithmetic and copies ran while one was open for 3% -> 3% of each run, Pallas kernels for 30% -> 18%
where the time goes in v3:
time: 59.5 us; the launch traced here: 58.9 us
  Pallas kernels  16.2 us (27%)
  starting transfers between devices  16.1 us (27%)
  blocking collectives  9.41 us (16%)
  local copies, waits for them, and re-layouts  8.82 us (15%)
  waiting for transfers between devices  6.14 us (10%)
  between operations  1.44 us (2%)
  other arithmetic  0.78 us (1%)
    pallas_call x7, Pallas kernels, device_call(): pl.pallas_call(kernel, out_shape=tuple(outputs), in_specs=[smem] * len(sc...  16.2 us
    ppermute x15, starting transfers between devices, from_peers(): lax.ppermute(value, axis, [(i, i ^ turn) for i in range(size)])  16.1 us
    all_to_all x1, blocking collectives, shards(): parts = lax.all_to_all(partial, ('patch', 'sub'), 0, 0, tiled=True)  9.41 us
    unnamed x18, local copies, waits for them, and re-layouts  8.04 us
    ppermute x15, waiting for transfers between devices, from_peers(): lax.ppermute(value, axis, [(i, i ^ turn) for i in range(size)])  6.14 us
  transfers between devices with their start and end apart: 15, of which 5 were waited for; matrix products, arithmetic and copies ran while one was open for 3% of the time, Pallas kernels for 18%

profile of v3, /device:TPU:0, one launch (start us, length us, event | category | flops | bytes accessed | tf_op | source)
XLA Modules:
  0.0 58.9 jit_solution(16102113903190965102)
XLA Ops:
  1.3 0.8 %copy-done.4 = f32[32,3,128]{2,0,1:T(8,128)S(1)} copy-done((f32[32,3,128]{2,0,1:T(8,128)S(1)}, f32[32,3,128]{2,0,1:T(8,128)}, u32[]{:S(2)}) %copy-start.4) | copy-done | bytes 49176
  2.1 0.8 %copy-done.5 = f32[32,3,128]{2,0,1:T(8,128)S(1)} copy-done((f32[32,3,128]{2,0,1:T(8,128)S(1)}, f32[32,3,128]{2,0,1:T(8,128)}, u32[]{:S(2)}) %copy-start.5) | copy-done | bytes 49176
  2.9 0.7 %copy-done.8 = f32[32,128]{1,0:T(8,128)S(1)} copy-done((f32[32,128]{1,0:T(8,128)S(1)}, f32[32,128]{1,0:T(8,128)}, u32[]{:S(2)}) %copy-start.8) | copy-done | bytes 16408
  3.8 1.2 %copy-done = f32[32,64,128]{2,1,0:T(8,128)S(1)} copy-done((f32[32,64,128]{2,1,0:T(8,128)S(1)}, f32[32,64,128]{2,1,0:T(8,128)}, u32[]{:S(2)}) %copy-start) | copy-done | bytes 1048600
  5.0 1.2 %copy-done.1 = f32[32,64,64]{2,1,0:T(8,128)S(1)} copy-done((f32[32,64,64]{2,1,0:T(8,128)S(1)}, f32[32,64,64]{2,1,0:T(8,128)}, u32[]{:S(2)}) %copy-start.1) | copy-done | bytes 524312
  6.3 0.9 %copy-done.2 = f32[8,64,64]{2,1,0:T(8,128)S(1)} copy-done((f32[8,64,64]{2,1,0:T(8,128)S(1)}, f32[8,64,64]{2,1,0:T(8,128)}, u32[]{:S(2)}) %copy-start.2) | copy-done | bytes 131096
  7.2 0.9 %copy-done.3 = f32[8,64,64]{2,1,0:T(8,128)S(1)} copy-done((f32[8,64,64]{2,1,0:T(8,128)S(1)}, f32[8,64,64]{2,1,0:T(8,128)}, u32[]{:S(2)}) %copy-start.3) | copy-done | bytes 131096
  8.2 0.8 %shard_map.123 = (f32[40,128]{1,0:T(8,128)S(1)}, f32[32,64,128]{2,1,0:T(8,128)S(1)}, f32[32,64,64]{2,1,0:T(8,128)S(1)}, f32[8,64,64]{2,1,0:T(8,128)S(1)}, f32[8,64,64]{2,1,0:T(8,128)S(1)}) custom-call(s32[1]{0:T(128)S(6)} %copy.14.counts, f32[32,128]{1,0:T(8,128)S(1)} %get-tuple-element.23.initial.refs_6_, f32[32,64,128]{2,1,0:T(8,128)S(1)} %copy-done, ...), custom_call_target="tpu_custom_call" | custom-call | tf_op jit(solution)/shard_map/pallas_call | solution.py:42
  9.0 0.5 collective-permute-start
  9.5 2.6 %collective-permute-start.1 = (f32[40,128]{1,0:T(8,128)S(1)}, f32[40,128]{1,0:T(8,128)S(1)}, u32[]{:S(2)}, u32[]{:S(2)}) collective-permute-start(f32[40,128]{1,0:T(8,128)S(1)} %get-tuple-element.24.refs_4_), channel_id=1, source_target_pairs={{0,2},{1,3},{2,0},{3,1},{4,6},{5,7},{6,4},{7,5},{8,10},{9,11},{10,... | collective-permute-start | bytes 61448 | tf_op jit(solution)/shard_map/ppermute | solution.py:23
  12.3 1.9 %collective-permute-start.7 = (f32[32,8,128]{2,1,0:T(8,128)S(1)}, f32[32,8,128]{2,1,0:T(8,128)S(1)}, u32[]{:S(2)}, u32[]{:S(2)}) collective-permute-start(f32[32,8,128]{2,1,0:T(8,128)S(1)} %get-tuple-element.25.refs_0_), channel_id=1, source_target_pairs={{0,2},{1,3},{2,0},{3,1},{4,6},{5,7},{6,4},{7,5},{8,10},{9,11},{10,... | collective-permute-start | bytes 393224 | tf_op jit(solution)/shard_map/ppermute | solution.py:23
  14.3 0.8 %eq.17 = s32[256]{0:T(256)S(1)} reshape(s32[8,32]{1,0:T(8,128)} %bitcast.31) | data formatting | bytes 2048 | tf_op jit(solution)/shard_map/eq | solution.py:388
  15.3 1.6 %collective-permute-start.3 = (f32[32,128]{1,0:T(8,128)S(1)}, f32[32,128]{1,0:T(8,128)S(1)}, u32[]{:S(2)}, u32[]{:S(2)}) collective-permute-start(f32[32,128]{1,0:T(8,128)S(1)} %pad_maximum_fusion.refs_0_), channel_id=1, source_target_pairs={{0,4},{4,0},{8,12},{12,8},{1,5},{5,1},{9,13},{13,9},{2,6},{6,2},{1... | collective-permute-start | bytes 49160 | tf_op jit(solution)/shard_map/ppermute | solution.py:23
  16.9 2.6 %collective-permute-start.4 = (f32[32,128]{1,0:T(8,128)S(1)}, f32[32,128]{1,0:T(8,128)S(1)}, u32[]{:S(2)}, u32[]{:S(2)}) collective-permute-start(f32[32,128]{1,0:T(8,128)S(1)} %pad_maximum_fusion.refs_0_), channel_id=1, source_target_pairs={{0,8},{4,12},{8,0},{12,4},{1,9},{5,13},{9,1},{13,5},{2,10},{6,14},... | collective-permute-start | bytes 49160 | tf_op jit(solution)/shard_map/ppermute | solution.py:23
  19.5 0.2 collective-permute-start.5
  19.8 0.7 %fusion.2.box_rows = s32[8]{0:T(128)S(1)} fusion(s32[1,8]{1,0:T(1,128)} %param.20, s32[]{:T(128)S(6)} %axis_index.33, s32[]{:T(128)S(6)} %axis_index.15), kind=kLoop, calls=%fused_computation.12 | loop fusion | flops 192 | bytes 72 | tf_op jit(solution)/shard_map/mul | solution.py:390
  20.4 0.6 %collective-permute-done.8.refs_3_ = f32[32,8,128]{2,1,0:T(8,128)S(1)} collective-permute-done((f32[32,8,128]{2,1,0:T(8,128)S(1)}, f32[32,8,128]{2,1,0:T(8,128)S(1)}, u32[]{:S(2)}, u32[]{:S(2)}) %collective-permute-start.8) | collective-permute-done | bytes 131104 | tf_op jit(solution)/shard_map/ppermute | solution.py:23
  21.1 0.7 %copy-done.6 = s32[32,9]{0,1:T(8,128)S(1)} copy-done((s32[32,9]{0,1:T(8,128)S(1)}, s32[32,9]{0,1:T(8,128)}, u32[]{:S(2)}) %copy-start.6) | copy-done | bytes 1176
  21.8 8.1 %shard_map.124 = (f32[32,128]{1,0:T(8,128)S(1)}, f32[32,128]{1,0:T(8,128)S(1)}, f32[288,128,128]{2,1,0:T(8,128)S(1)}) custom-call(s32[1]{0:T(128)} %bitcast.3.offset, s32[9,32]{1,0:T(8,128)S(1)} %bitcast.27, f32[32,8,128]{2,1,0:T(8,128)S(1)} %get-tuple-element.25.refs_0_, f32[32,8,128]{2,1,0:T(8,128)S(1)} %collective-permute-done.6.refs_1_, ...), custom_call_target="tpu_custom_call" | custom-call | tf_op jit(solution)/shard_map/pallas_call | solution.py:42
  29.9 1.9 %shard_map.125 = (f32[72,128]{1,0:T(8,128)S(1)}, f32[32,128]{1,0:T(8,128)S(1)}, f32[8,128]{1,0:T(8,128)S(1)}) custom-call(s32[1]{0:T(128)S(6)} %copy.14.counts, s32[8]{0:T(128)S(1)} %fusion.2.box_rows, f32[32,128]{1,0:T(8,128)S(1)} %pad_maximum_fusion.refs_0_, f32[32,128]{1,0:T(8,128)S(1)} %collective-permute-done.3.refs_1_, ...), custom_call_target="tpu_custom_call" | custom-call | tf_op jit(solution)/shard_map/pallas_call | solution.py:42
  31.9 1.3 %collective-permute-start.10 = (f32[72,128]{1,0:T(8,128)S(1)}, f32[72,128]{1,0:T(8,128)S(1)}, u32[]{:S(2)}, u32[]{:S(2)}) collective-permute-start(f32[72,128]{1,0:T(8,128)S(1)} %get-tuple-element.32.refs_0_.refs_6_), channel_id=1, source_target_pairs={{0,2},{1,3},{2,0},{3,1},{4,6},{5,7},{6,4},{7,5},{8,10},{9,11},{10,... | collective-permute-start | bytes 110600 | tf_op jit(solution)/shard_map/ppermute | solution.py:23
  33.2 0.5 collective-permute-start.11
  33.7 2.2 %collective-permute-done.10.refs_2_ = f32[72,128]{1,0:T(8,128)S(1)} collective-permute-done((f32[72,128]{1,0:T(8,128)S(1)}, f32[72,128]{1,0:T(8,128)S(1)}, u32[]{:S(2)}, u32[]{:S(2)}) %collective-permute-start.10) | collective-permute-done | bytes 36896 | tf_op jit(solution)/shard_map/ppermute | solution.py:23
  35.9 1.0 %collective-permute-done.11.refs_3_ = f32[72,128]{1,0:T(8,128)S(1)} collective-permute-done((f32[72,128]{1,0:T(8,128)S(1)}, f32[72,128]{1,0:T(8,128)S(1)}, u32[]{:S(2)}, u32[]{:S(2)}) %collective-permute-start.11) | collective-permute-done | bytes 36896 | tf_op jit(solution)/shard_map/ppermute | solution.py:23
  36.9 1.6 %collective-permute-start.12 = (f32[32,128]{1,0:T(8,128)S(1)}, f32[32,128]{1,0:T(8,128)S(1)}, u32[]{:S(2)}, u32[]{:S(2)}) collective-permute-start(f32[32,128]{1,0:T(8,128)S(1)} %pad_maximum_fusion.1.refs_0_), channel_id=1, source_target_pairs={{0,4},{4,0},{8,12},{12,8},{1,5},{5,1},{9,13},{13,9},{2,6},{6,2},{1... | collective-permute-start | bytes 49160 | tf_op jit(solution)/shard_map/ppermute | solution.py:23
  38.5 2.9 %collective-permute-start.13 = (f32[32,128]{1,0:T(8,128)S(1)}, f32[32,128]{1,0:T(8,128)S(1)}, u32[]{:S(2)}, u32[]{:S(2)}) collective-permute-start(f32[32,128]{1,0:T(8,128)S(1)} %pad_maximum_fusion.1.refs_0_), channel_id=1, source_target_pairs={{0,8},{4,12},{8,0},{12,4},{1,9},{5,13},{9,1},{13,5},{2,10},{6,14},... | collective-permute-start | bytes 49160 | tf_op jit(solution)/shard_map/ppermute | solution.py:23
  41.4 0.7 %copy-done.7 = s32[32,9]{0,1:T(8,128)S(1)} copy-done((s32[32,9]{0,1:T(8,128)S(1)}, s32[32,9]{0,1:T(8,128)}, u32[]{:S(2)}) %copy-start.7) | copy-done | bytes 1176
  42.1 2.6 %shard_map.126 = (f32[32,128]{1,0:T(8,128)S(1)}, f32[32,128]{1,0:T(8,128)S(1)}) custom-call(s32[1]{0:T(128)} %bitcast.3.offset, s32[9,32]{1,0:T(8,128)S(1)} %bitcast.28, f32[72,128]{1,0:T(8,128)S(1)} %get-tuple-element.32.refs_0_.refs_6_, f32[72,128]{1,0:T(8,128)S(1)} %collective-permute-done.9.refs_1_, f32[72,128]{1,0:T(8,128)S(1)} %collective-permute-done.10.refs_2_, ...), custom_call_target="tpu_custom_call" | custom-call | tf_op jit(solution)/shard_map/pallas_call | solution.py:42
  44.7 2.2 %collective-permute-done.14.refs_3_ = f32[32,128]{1,0:T(8,128)S(1)} collective-permute-done((f32[32,128]{1,0:T(8,128)S(1)}, f32[32,128]{1,0:T(8,128)S(1)}, u32[]{:S(2)}, u32[]{:S(2)}) %collective-permute-start.14) | collective-permute-done | bytes 16416 | tf_op jit(solution)/shard_map/ppermute | solution.py:23
  46.9 1.5 %shard_map.127 = (f32[32,128]{1,0:T(8,128)S(1)}, f32[32,128]{1,0:T(8,128)S(1)}, f32[16,128]{1,0:T(8,128)S(1)}, f32[8,128]{1,0:T(8,128)S(1)}) custom-call(s32[1]{0:T(128)S(6)} %copy.14.counts, s32[8]{0:T(128)S(1)} %fusion.2.box_rows, f32[32,128]{1,0:T(8,128)S(1)} %pad_maximum_fusion.1.refs_0_, f32[32,128]{1,0:T(8,128)S(1)} %collective-permute-done.12.refs_1_, ...), custom_call_target="tpu_custom_call" | custom-call | tf_op jit(solution)/shard_map/pallas_call | solution.py:42
  48.5 9.4 %all_to_all.11 = f32[16,1,128]{2,1,0:T(1,128)S(1)} all-to-all(f32[16,1,128]{2,1,0:T(1,128)S(1)} %bitcast.30), channel_id=1, replica_groups=mesh['groups'=2,'patch'=4,'sub'=4] {'patch','sub'}, dimensions={0} | all-to-all | bytes 16384 | tf_op jit(solution)/shard_map/all_to_all | solution.py:468
  57.9 1.0 %shard_map.128 = (f32[32,128]{1,0:T(8,128)}, f32[2,3]{1,0:T(2,128)}) custom-call(f32[16,128]{1,0:T(8,128)S(1)} %bitcast.29, f32[32,128]{1,0:T(8,128)S(1)} %get-tuple-element.36.refs_7_.basis_one, f32[32,128]{1,0:T(8,128)S(1)} %get-tuple-element.39.basis_two, f32[32,128]{1,0:T(8,128)S(1)} %get-tuple-element.40.image_two, f32[8,128]{1,0:T(8,128)S(1)} %get-tuple-element.41.numbers), custom_call_target="tpu_custom_call" | custom-call | tf_op jit(solution)/shard_map/pallas_call | solution.py:42
  (38 shorter events, 0.9 us)
Async XLA Ops:
  1.3 0.8 %copy-start.4 = (f32[32,3,128]{2,0,1:T(8,128)S(1)}, f32[32,3,128]{2,0,1:T(8,128)}, u32[]{:S(2)}) copy-start(f32[32,3,128]{2,0,1:T(8,128)} %param.11) | copy-start | bytes 147460
  2.1 0.8 %copy-start.5 = (f32[32,3,128]{2,0,1:T(8,128)S(1)}, f32[32,3,128]{2,0,1:T(8,128)}, u32[]{:S(2)}) copy-start(f32[32,3,128]{2,0,1:T(8,128)} %param.12) | copy-start | bytes 147460
  2.9 0.7 %copy-start.8 = (f32[32,128]{1,0:T(8,128)S(1)}, f32[32,128]{1,0:T(8,128)}, u32[]{:S(2)}) copy-start(f32[32,128]{1,0:T(8,128)} %density.1) | copy-start | bytes 49156
  3.8 1.2 %copy-start = (f32[32,64,128]{2,1,0:T(8,128)S(1)}, f32[32,64,128]{2,1,0:T(8,128)}, u32[]{:S(2)}) copy-start(f32[32,64,128]{2,1,0:T(8,128)} %refs_0_.1) | copy-start | bytes 3145732
  5.0 1.2 %copy-start.1 = (f32[32,64,64]{2,1,0:T(8,128)S(1)}, f32[32,64,64]{2,1,0:T(8,128)}, u32[]{:S(2)}) copy-start(f32[32,64,64]{2,1,0:T(8,128)} %refs_1_.1) | copy-start | bytes 1572868
  6.3 0.9 %copy-start.2 = (f32[8,64,64]{2,1,0:T(8,128)S(1)}, f32[8,64,64]{2,1,0:T(8,128)}, u32[]{:S(2)}) copy-start(f32[8,64,64]{2,1,0:T(8,128)} %refs_2_.1) | copy-start | bytes 393220
  7.2 0.9 %copy-start.3 = (f32[8,64,64]{2,1,0:T(8,128)S(1)}, f32[8,64,64]{2,1,0:T(8,128)}, u32[]{:S(2)}) copy-start(f32[8,64,64]{2,1,0:T(8,128)} %refs_3_.1) | copy-start | bytes 393220
  9.0 6.1 %collective-permute-start = (f32[40,128]{1,0:T(8,128)S(1)}, f32[40,128]{1,0:T(8,128)S(1)}, u32[]{:S(2)}, u32[]{:S(2)}) collective-permute-start(f32[40,128]{1,0:T(8,128)S(1)} %get-tuple-element.24.refs_4_), channel_id=1, source_target_pairs={{0,1},{1,0},{2,3},{3,2},{4,5},{5,4},{6,7},{7,6},{8,9},{9,8},{10,11... | collective-permute-start | bytes 61448 | tf_op jit(solution)/shard_map/ppermute | solution.py:23
  9.5 5.7 %collective-permute-start.1 = (f32[40,128]{1,0:T(8,128)S(1)}, f32[40,128]{1,0:T(8,128)S(1)}, u32[]{:S(2)}, u32[]{:S(2)}) collective-permute-start(f32[40,128]{1,0:T(8,128)S(1)} %get-tuple-element.24.refs_4_), channel_id=1, source_target_pairs={{0,2},{1,3},{2,0},{3,1},{4,6},{5,7},{6,4},{7,5},{8,10},{9,11},{10,... | collective-permute-start | bytes 61448 | tf_op jit(solution)/shard_map/ppermute | solution.py:23
  12.1 3.2 %collective-permute-start.2 = (f32[40,128]{1,0:T(8,128)S(1)}, f32[40,128]{1,0:T(8,128)S(1)}, u32[]{:S(2)}, u32[]{:S(2)}) collective-permute-start(f32[40,128]{1,0:T(8,128)S(1)} %get-tuple-element.24.refs_4_), channel_id=1, source_target_pairs={{0,3},{1,2},{2,1},{3,0},{4,7},{5,6},{6,5},{7,4},{8,11},{9,10},{10,... | collective-permute-start | bytes 61448 | tf_op jit(solution)/shard_map/ppermute | solution.py:23
  12.2 7.4 %collective-permute-start.6 = (f32[32,8,128]{2,1,0:T(8,128)S(1)}, f32[32,8,128]{2,1,0:T(8,128)S(1)}, u32[]{:S(2)}, u32[]{:S(2)}) collective-permute-start(f32[32,8,128]{2,1,0:T(8,128)S(1)} %get-tuple-element.25.refs_0_), channel_id=1, source_target_pairs={{0,1},{1,0},{2,3},{3,2},{4,5},{5,4},{6,7},{7,6},{8,9},{9,8},{10,11... | collective-permute-start | bytes 393224 | tf_op jit(solution)/shard_map/ppermute | solution.py:23
  12.3 8.1 %collective-permute-start.7 = (f32[32,8,128]{2,1,0:T(8,128)S(1)}, f32[32,8,128]{2,1,0:T(8,128)S(1)}, u32[]{:S(2)}, u32[]{:S(2)}) collective-permute-start(f32[32,8,128]{2,1,0:T(8,128)S(1)} %get-tuple-element.25.refs_0_), channel_id=1, source_target_pairs={{0,2},{1,3},{2,0},{3,1},{4,6},{5,7},{6,4},{7,5},{8,10},{9,11},{10,... | collective-permute-start | bytes 393224 | tf_op jit(solution)/shard_map/ppermute | solution.py:23
  15.1 5.9 %collective-permute-start.8 = (f32[32,8,128]{2,1,0:T(8,128)S(1)}, f32[32,8,128]{2,1,0:T(8,128)S(1)}, u32[]{:S(2)}, u32[]{:S(2)}) collective-permute-start(f32[32,8,128]{2,1,0:T(8,128)S(1)} %get-tuple-element.25.refs_0_), channel_id=1, source_target_pairs={{0,3},{1,2},{2,1},{3,0},{4,7},{5,6},{6,5},{7,4},{8,11},{9,10},{10,... | collective-permute-start | bytes 393224 | tf_op jit(solution)/shard_map/ppermute | solution.py:23
  15.3 14.5 %collective-permute-start.3 = (f32[32,128]{1,0:T(8,128)S(1)}, f32[32,128]{1,0:T(8,128)S(1)}, u32[]{:S(2)}, u32[]{:S(2)}) collective-permute-start(f32[32,128]{1,0:T(8,128)S(1)} %pad_maximum_fusion.refs_0_), channel_id=1, source_target_pairs={{0,4},{4,0},{8,12},{12,8},{1,5},{5,1},{9,13},{13,9},{2,6},{6,2},{1... | collective-permute-start | bytes 49160 | tf_op jit(solution)/shard_map/ppermute | solution.py:23
  16.9 12.9 %collective-permute-start.4 = (f32[32,128]{1,0:T(8,128)S(1)}, f32[32,128]{1,0:T(8,128)S(1)}, u32[]{:S(2)}, u32[]{:S(2)}) collective-permute-start(f32[32,128]{1,0:T(8,128)S(1)} %pad_maximum_fusion.refs_0_), channel_id=1, source_target_pairs={{0,8},{4,12},{8,0},{12,4},{1,9},{5,13},{9,1},{13,5},{2,10},{6,14},... | collective-permute-start | bytes 49160 | tf_op jit(solution)/shard_map/ppermute | solution.py:23
  19.5 10.3 %collective-permute-start.5 = (f32[32,128]{1,0:T(8,128)S(1)}, f32[32,128]{1,0:T(8,128)S(1)}, u32[]{:S(2)}, u32[]{:S(2)}) collective-permute-start(f32[32,128]{1,0:T(8,128)S(1)} %pad_maximum_fusion.refs_0_), channel_id=1, source_target_pairs={{0,12},{4,8},{8,4},{12,0},{1,13},{5,9},{9,5},{13,1},{2,14},{6,10},... | collective-permute-start | bytes 49160 | tf_op jit(solution)/shard_map/ppermute | solution.py:23
  21.1 0.7 %copy-start.6 = (s32[32,9]{0,1:T(8,128)S(1)}, s32[32,9]{0,1:T(8,128)}, u32[]{:S(2)}) copy-start(s32[32,9]{0,1:T(8,128)} %param.15) | copy-start | bytes 3460
  31.8 1.9 %collective-permute-start.9 = (f32[72,128]{1,0:T(8,128)S(1)}, f32[72,128]{1,0:T(8,128)S(1)}, u32[]{:S(2)}, u32[]{:S(2)}) collective-permute-start(f32[72,128]{1,0:T(8,128)S(1)} %get-tuple-element.32.refs_0_.refs_6_), channel_id=1, source_target_pairs={{0,1},{1,0},{2,3},{3,2},{4,5},{5,4},{6,7},{7,6},{8,9},{9,8},{10,11... | collective-permute-start | bytes 110600 | tf_op jit(solution)/shard_map/ppermute | solution.py:23
  31.9 4.0 %collective-permute-start.10 = (f32[72,128]{1,0:T(8,128)S(1)}, f32[72,128]{1,0:T(8,128)S(1)}, u32[]{:S(2)}, u32[]{:S(2)}) collective-permute-start(f32[72,128]{1,0:T(8,128)S(1)} %get-tuple-element.32.refs_0_.refs_6_), channel_id=1, source_target_pairs={{0,2},{1,3},{2,0},{3,1},{4,6},{5,7},{6,4},{7,5},{8,10},{9,11},{10,... | collective-permute-start | bytes 110600 | tf_op jit(solution)/shard_map/ppermute | solution.py:23
  33.2 3.7 %collective-permute-start.11 = (f32[72,128]{1,0:T(8,128)S(1)}, f32[72,128]{1,0:T(8,128)S(1)}, u32[]{:S(2)}, u32[]{:S(2)}) collective-permute-start(f32[72,128]{1,0:T(8,128)S(1)} %get-tuple-element.32.refs_0_.refs_6_), channel_id=1, source_target_pairs={{0,3},{1,2},{2,1},{3,0},{4,7},{5,6},{6,5},{7,4},{8,11},{9,10},{10,... | collective-permute-start | bytes 110600 | tf_op jit(solution)/shard_map/ppermute | solution.py:23
  36.9 7.8 %collective-permute-start.12 = (f32[32,128]{1,0:T(8,128)S(1)}, f32[32,128]{1,0:T(8,128)S(1)}, u32[]{:S(2)}, u32[]{:S(2)}) collective-permute-start(f32[32,128]{1,0:T(8,128)S(1)} %pad_maximum_fusion.1.refs_0_), channel_id=1, source_target_pairs={{0,4},{4,0},{8,12},{12,8},{1,5},{5,1},{9,13},{13,9},{2,6},{6,2},{1... | collective-permute-start | bytes 49160 | tf_op jit(solution)/shard_map/ppermute | solution.py:23
  38.5 6.2 %collective-permute-start.13 = (f32[32,128]{1,0:T(8,128)S(1)}, f32[32,128]{1,0:T(8,128)S(1)}, u32[]{:S(2)}, u32[]{:S(2)}) collective-permute-start(f32[32,128]{1,0:T(8,128)S(1)} %pad_maximum_fusion.1.refs_0_), channel_id=1, source_target_pairs={{0,8},{4,12},{8,0},{12,4},{1,9},{5,13},{9,1},{13,5},{2,10},{6,14},... | collective-permute-start | bytes 49160 | tf_op jit(solution)/shard_map/ppermute | solution.py:23
  41.4 5.5 %collective-permute-start.14 = (f32[32,128]{1,0:T(8,128)S(1)}, f32[32,128]{1,0:T(8,128)S(1)}, u32[]{:S(2)}, u32[]{:S(2)}) collective-permute-start(f32[32,128]{1,0:T(8,128)S(1)} %pad_maximum_fusion.1.refs_0_), channel_id=1, source_target_pairs={{0,12},{4,8},{8,4},{12,0},{1,13},{5,9},{9,5},{13,1},{2,14},{6,10},... | collective-permute-start | bytes 49160 | tf_op jit(solution)/shard_map/ppermute | solution.py:23
  41.4 0.7 %copy-start.7 = (s32[32,9]{0,1:T(8,128)S(1)}, s32[32,9]{0,1:T(8,128)}, u32[]{:S(2)}) copy-start(s32[32,9]{0,1:T(8,128)} %param.15) | copy-start | bytes 3460

commit v4 on v3

--- a/solution.py
+++ b/solution.py
@@ -23,10 +23,6 @@
         lax.ppermute(value, axis, [(i, i ^ turn) for i in range(size)]) for turn in range(1, size)
     ]
     return [value] + arrived
-
-
-def place_of(owner, axis):
-    return lax.axis_index(axis) ^ owner
 
 
 def tree_sum(parts):
@@ -46,7 +42,11 @@
         out_specs=tuple([vmem] * len(outputs)),
         scratch_shapes=tuple(scratch),
         compiler_params=pltpu.CompilerParams(vmem_limit_bytes=VMEM_LIMIT),
-    )(*scalars, *arrays, *remote)
+    )(
+        *scalars,
+        *arrays,
+        *[pltpu.with_memory_space_constraint(array, pltpu.HBM) for array in remote],
+    )
 
 
 def kept(array):
@@ -75,25 +75,6 @@
     for place, entry in enumerate(entries):
         row = jnp.where(lane == place, entry, row)
     return row
-
-
-def pack_kernel(counts, points, normals, density, geometry, initial, at, arrived):
-    dims, slots, width = points.shape
-    copies = [
-        pltpu.make_async_copy(points, at.at[0:dims], arrived.at[0]),
-        pltpu.make_async_copy(normals, at.at[dims : 2 * dims], arrived.at[1]),
-        pltpu.make_async_copy(density, at.at[2 * dims], arrived.at[2]),
-    ]
-    for copy in copies:
-        copy.start()
-    for copy in copies:
-        copy.wait()
-    for row in range(2 * dims):
-        geometry[:, row, :] = at[row]
-    used = jnp.where(iota((slots, width), 0) < counts[0], at[2 * dims], 0.0)
-    initial[...] = used
-    geometry[:, 2 * dims, :] = used
-    geometry[:, 2 * dims + 1, :] = jnp.zeros_like(used)
 
 
 def write_moments(vector, sums, basis, transfer, message, start):
@@ -116,19 +97,29 @@
     message[end + 1 : end + 2, :] = sums
 
 
-def first_moments_kernel(counts, initial, *refs):
-    sources, message, held, arrived = refs[:4], refs[4], refs[5:9], refs[9]
+def start_kernel(counts, *refs):
+    sources, (geometry, initial, message), held = refs[:7], refs[7:10], refs[10:14]
+    at, arrived = refs[14:]
+    dims, slots, width = sources[0].shape
+    targets = [at.at[0:dims], at.at[dims : 2 * dims], at.at[2 * dims], *held]
     copies = [
         pltpu.make_async_copy(source, target, arrived.at[place])
-        for place, (source, target) in enumerate(zip(sources, held))
+        for place, (source, target) in enumerate(zip(sources, targets))
     ]
     for copy in copies:
         copy.start()
-    for copy in copies:
+    for copy in copies[:3]:
         copy.wait()
-    vector = initial[...]
+    for row in range(2 * dims):
+        geometry[:, row, :] = at[row]
+    vector = jnp.where(iota((slots, width), 0) < counts[0], at[2 * dims], 0.0)
+    initial[...] = vector
+    geometry[:, 2 * dims, :] = vector
+    geometry[:, 2 * dims + 1, :] = jnp.zeros_like(vector)
     square_sum = jnp.sum(vector * vector, keepdims=True)
     in_use = jnp.full((1, 1), counts[0], jnp.int32).astype(jnp.float32)
+    for copy in copies[3:]:
+        copy.wait()
     write_moments(initial, lane_row([square_sum, in_use]), held[0], held[1], message, 0)
 
 
@@ -152,9 +143,12 @@
     return local
 
 
-def first_near_kernel(subs, offset, near_list, *refs):
+def first_near_kernel(subs, box, *refs):
     geometry, messages = refs[:subs], refs[subs : 2 * subs]
-    picks, coupling, near, local, values, features, squares, fields = refs[2 * subs :]
+    picks, coupling, near_source, near, local, values = refs[2 * subs : 2 * subs + 6]
+    features, squares, fields, near_list, arrived = refs[2 * subs + 6 :]
+    copy = pltpu.make_async_copy(near_source, near_list, arrived)
+    copy.start()
     slots, height, width = geometry[0].shape
     neighbours = near_list.shape[0]
     rank = coupling.shape[1]
@@ -197,7 +191,7 @@
         left = jnp.concatenate([one, one, two, two, three, one]).T.astype(jnp.bfloat16)
         total = jnp.zeros((width, width), jnp.float32)
         for column in range(neighbours):
-            place = near_list[column, leaf] ^ offset[0]
+            place = near_list[column, leaf] ^ (box[0] * slots)
             upper, lower = features[place, 0:16, :], features[place, 16:32, :]
             right = jnp.concatenate([upper, upper, lower], axis=0)
             both = jnp.dot(left, right, preferred_element_type=jnp.float32)
@@ -208,14 +202,17 @@
         near[pl.ds(leaf, 1), :] = jnp.sum(total.T, axis=0, keepdims=True)
         return carry
 
+    copy.wait()
     lax.fori_loop(0, slots, target, 0, unroll=True)
     local[...] = jnp.zeros_like(local)
     local[:, 0:rank] = leaf_part([ref[0:slots, 0:rank] for ref in messages], picks, coupling)
 
 
-def second_near_kernel(subs, offset, near_list, *refs):
+def second_near_kernel(subs, box, *refs):
     messages = refs[:subs]
-    picks, coupling, values, near, local, fields = refs[subs:]
+    picks, coupling, values, near_source, near, local, fields, near_list, arrived = refs[subs:]
+    copy = pltpu.make_async_copy(near_source, near_list, arrived)
+    copy.start()
     slots, width = near.shape
     neighbours = near_list.shape[0]
     rank = coupling.shape[1]
@@ -225,16 +222,17 @@
     def target(leaf, carry):
         total = jnp.zeros((width, width), jnp.float32)
         for column in range(neighbours):
-            place = near_list[column, leaf] ^ offset[0]
+            place = near_list[column, leaf] ^ (box[0] * slots)
             total = total + values[leaf * neighbours + column] * fields[pl.ds(place, 1), :]
         near[pl.ds(leaf, 1), :] = jnp.sum(total.T, axis=0, keepdims=True)
         return carry
 
-    lax.fori_loop(0, slots, target, 0, unroll=True)
     local[...] = jnp.zeros_like(local)
     local[:, 0:rank] = leaf_part(
         [ref[slots : 2 * slots, 0:rank] for ref in messages], picks, coupling
     )
+    copy.wait()
+    lax.fori_loop(0, slots, target, 0, unroll=True)
 
 
 def surface_sums(boxes):
@@ -246,14 +244,15 @@
     )
 
 
-def add_far(counts, box_rows, boxes, near, local, basis, transfer, box_coupling, gather, image):
+def add_far(counts, box, box_far, boxes, near, local, basis, transfer, box_coupling, gather, image):
     slots, rank, width = basis.shape
     height = boxes[0].shape[0]
     for place, ref in enumerate(boxes):
         gather[place * height : (place + 1) * height, :] = ref[...]
     coupled = jnp.zeros((rank, rank), jnp.float32)
     for place in range(box_coupling.shape[0]):
-        coupled = coupled + box_coupling[place] * gather[pl.ds(box_rows[place], 1), 0:rank]
+        row = (box_far[0, place] ^ box[0]) * TILE_ROWS
+        coupled = coupled + box_coupling[place] * gather[pl.ds(row, 1), 0:rank]
     box_local = jnp.broadcast_to(jnp.sum(coupled, axis=1, keepdims=True), (rank, rank))
     for leaf in range(slots):
         local[leaf : leaf + 1, 0:rank] += jnp.sum(
@@ -267,14 +266,14 @@
         )
 
 
-def first_image_kernel(patches, counts, box_rows, *refs):
+def first_image_kernel(patches, counts, box, box_far, *refs):
     boxes = refs[:patches]
     near, leaf_local, initial, basis, transfer, box_coupling = refs[patches : patches + 6]
     message, basis_one, numbers, gather, image, local = refs[patches + 6 :]
     slots, _, width = basis.shape
     local[...] = leaf_local[...]
     add_far(
-        counts, box_rows, boxes, near, local, basis, transfer, box_coupling, gather, image
+        counts, box, box_far, boxes, near, local, basis, transfer, box_coupling, gather, image
     )
     sums = surface_sums(boxes)
     square_sum, unknowns = sums[:, 0:1], width * sums[:, 1:2]
@@ -291,7 +290,7 @@
     write_moments(message, partial, basis, transfer, message, slots)
 
 
-def second_image_kernel(patches, counts, box_rows, *refs):
+def second_image_kernel(patches, counts, box, box_far, *refs):
     boxes = refs[:patches]
     near, leaf_local, message, basis_one, numbers = refs[patches : patches + 5]
     basis, transfer, box_coupling = refs[patches + 5 : patches + 8]
@@ -299,7 +298,7 @@
     slots = basis.shape[0]
     local[...] = leaf_local[...]
     add_far(
-        counts, box_rows, boxes, near, local, basis, transfer, box_coupling, gather, image
+        counts, box, box_far, boxes, near, local, basis, transfer, box_coupling, gather, image
     )
     one_one, unknowns = numbers[0:1, 0:1], numbers[0:1, 1:2]
     sums = surface_sums(boxes)
@@ -373,59 +372,57 @@
     box_coupling,
 ):
     slots, _, width = points.shape
-    rank = leaf_basis.shape[1]
     neighbours = near_list.shape[1]
     far_count = leaf_far.shape[1]
     subs, patches = lax.axis_size("sub"), lax.axis_size("patch")
     sources = subs * slots
+    rows = f32(slots, width)
+    this_box = lax.axis_index("patch") * subs + lax.axis_index("sub")
+    box = this_box.astype(jnp.int32).reshape(1)
     patch_start = lax.axis_index("patch") * sources
-    rows = f32(slots, width)
-
-    offset = patch_start + lax.axis_index("sub") * slots
-    offsets = offset.reshape(1).astype(jnp.int32)
-    near_list = near_list.T
-    picks = (
-        leaf_far.T.reshape(far_count * slots, 1) == (jnp.arange(sources) ^ offset)[None, :]
-    ).astype(jnp.bfloat16)
-    box_rows = TILE_ROWS * (
-        place_of(box_far[0] // subs, "patch") * subs + place_of(box_far[0] % subs, "sub")
-    )
+    leaves = (jnp.arange(sources) + patch_start) ^ (lax.axis_index("sub") * slots)
+    picks = (leaf_far.T.reshape(far_count * slots, 1) == leaves[None, :]).astype(jnp.bfloat16)
 
     def box_parts(parts, start):
         return from_peers(
             jnp.concatenate([part[start : start + TILE_ROWS] for part in parts], axis=0), "patch"
         )
 
-    geometry, initial = device_call(
-        pack_kernel,
-        [f32(slots, 8, width), rows],
+    matrices = [leaf_basis, leaf_to_box_transfer, leaf_coupling, box_coupling]
+    geometry, initial, message, *matrices = device_call(
+        start_kernel,
+        [
+            f32(slots, 8, width),
+            rows,
+            f32(slots + TILE_ROWS, LANES),
+            *[kept(matrix) for matrix in matrices],
+        ],
         [counts],
         [],
-        [pltpu.VMEM((7, slots, width), jnp.float32), pltpu.SemaphoreType.DMA((3,))],
-        [points.transpose(1, 0, 2), normals.transpose(1, 0, 2), density],
-    )
+        [pltpu.VMEM((7, slots, width), jnp.float32), pltpu.SemaphoreType.DMA((7,))],
+        [points.transpose(1, 0, 2), normals.transpose(1, 0, 2), density, *matrices],
+    )
+    leaf_basis, leaf_to_box_transfer, leaf_coupling, box_coupling = matrices
+    near_list = near_list.T
+    list_scratch = [
+        pltpu.SMEM(near_list.shape, jnp.int32),
+        pltpu.SemaphoreType.DMA,
+    ]
     geometry = from_peers(geometry, "sub")
-    matrices = [leaf_basis, leaf_to_box_transfer, leaf_coupling, box_coupling]
-    message, leaf_basis, leaf_to_box_transfer, leaf_coupling, box_coupling = device_call(
-        first_moments_kernel,
-        [f32(slots + TILE_ROWS, LANES), *[kept(matrix) for matrix in matrices]],
-        [counts],
-        [initial],
-        [pltpu.SemaphoreType.DMA((4,))],
-        matrices,
-    )
     messages = from_peers(message, "sub")
     boxes = box_parts(messages, slots)
     near, local, values = device_call(
         functools.partial(first_near_kernel, subs),
         [rows, f32(slots, LANES), pltpu.VMEM((slots * neighbours, width, width), jnp.float32)],
-        [offsets, near_list],
+        [box],
         [*geometry, *messages, picks, leaf_coupling],
         [
             pltpu.VMEM((sources, 32, 2 * width), jnp.bfloat16),
             pltpu.VMEM((sources, width), jnp.float32),
             pltpu.VMEM((sources, width), jnp.float32),
+            *list_scratch,
         ],
+        [near_list],
     )
     far_scratch = [
         pltpu.VMEM((patches * subs * TILE_ROWS, LANES), jnp.float32),
@@ -435,7 +432,7 @@
     message, basis_one, numbers = device_call(
         functools.partial(first_image_kernel, patches),
         [f32(2 * slots + TILE_ROWS, LANES), rows, f32(TILE_ROWS, LANES)],
-        [counts, box_rows],
+        [counts, box, box_far],
         [*boxes, near, local, initial, leaf_basis, leaf_to_box_transfer, box_coupling],
         far_scratch,
     )
@@ -444,14 +441,15 @@
     near, local = device_call(
         functools.partial(second_near_kernel, subs),
         [rows, f32(slots, LANES)],
-        [offsets, near_list],
+        [box],
         [*messages, picks, leaf_coupling, values],
-        [pltpu.VMEM((sources, width), jnp.float32)],
+        [pltpu.VMEM((sources, width), jnp.float32), *list_scratch],
+        [near_list],
     )
     basis_two, image_two, partial, numbers = device_call(
         functools.partial(second_image_kernel, patches),
         [rows, rows, f32(patches * subs, LANES), f32(TILE_ROWS, LANES)],
-        [counts, box_rows],
+        [counts, box, box_far],
         [
             *boxes,
             near,

time: 59.5 us -> 52.7 us (0.89)
  local copies, waits for them, and re-layouts: 8.82 us -> 1.43 us
  waiting for transfers between devices: 6.14 us -> 7.93 us
  other arithmetic: 0.78 us -> 0.11 us
    unnamed x18 -> x2, local copies, waits for them, and re-layouts: 8.04 us -> 0.65 us
    ppermute x15, waiting for transfers between devices: 6.14 us -> 7.93 us  [from_peers(): lax.ppermute(value, axis, [(i, i ^ turn) for i in range(size)])]
    mul x1 -> x0, other arithmetic: 0.67 us -> none  [shards(): TILE_ROWS * (place_of(box_far[0] // subs, 'patch') * subs + place_of(box_...]
    pallas_call x7 -> x6, Pallas kernels: 16.2 us -> 16.6 us  [device_call(): pl.pallas_call(kernel, out_shape=tuple(outputs), in_specs=[smem] * len(sc...]
  transfers between devices with their start and end apart: 15 -> 15, of which waited for: 5 -> 5; matrix products, arithmetic and copies ran while one was open for 3% -> 2% of each run, Pallas kernels for 18% -> 19%
where the time goes in v4:
time: 52.7 us; the launch traced here: 52.4 us
  Pallas kernels  16.6 us (31%)
  starting transfers between devices  16 us (30%)
  blocking collectives  8.98 us (17%)
  waiting for transfers between devices  7.93 us (15%)
  between operations  1.44 us (3%)
  local copies, waits for them, and re-layouts  1.43 us (3%)
    pallas_call x6, Pallas kernels, device_call(): pl.pallas_call(kernel, out_shape=tuple(outputs), in_specs=[smem] * len(sc...  16.6 us
    ppermute x15, starting transfers between devices, from_peers(): lax.ppermute(value, axis, [(i, i ^ turn) for i in range(size)])  16 us
    all_to_all x1, blocking collectives, shards(): parts = lax.all_to_all(partial, ('patch', 'sub'), 0, 0, tiled=True)  8.98 us
    ppermute x15, waiting for transfers between devices, from_peers(): lax.ppermute(value, axis, [(i, i ^ turn) for i in range(size)])  7.93 us
  transfers between devices with their start and end apart: 15, of which 5 were waited for; matrix products, arithmetic and copies ran while one was open for 2% of the time, Pallas kernels for 19%

profile of v4, /device:TPU:0, one launch (start us, length us, event | category | flops | bytes accessed | tf_op | source)
XLA Modules:
  0.0 52.4 jit_solution(12269870463560600593)
XLA Ops:
  1.3 2.4 %shard_map.122 = (f32[32,8,128]{2,1,0:T(8,128)S(1)}, f32[32,128]{1,0:T(8,128)S(1)}, f32[40,128]{1,0:T(8,128)S(1)}, f32[32,64,128]{2,1,0:T(8,128)S(1)}, f32[32,64...) custom-call(s32[1]{0:T(128)S(6)} %copy.14.counts, f32[3,32,128]{2,1,0:T(8,128)} %bitcast.12, ...), custom_call_target="tpu_custom_call" | custom-call | tf_op jit(solution)/shard_map/pallas_call | solution.py:38
  3.7 0.5 collective-permute-start
  4.2 2.6 %collective-permute-start.1 = (f32[40,128]{1,0:T(8,128)S(1)}, f32[40,128]{1,0:T(8,128)S(1)}, u32[]{:S(2)}, u32[]{:S(2)}) collective-permute-start(f32[40,128]{1,0:T(8,128)S(1)} %get-tuple-element.23.refs_4_), channel_id=1, source_target_pairs={{0,2},{1,3},{2,0},{3,1},{4,6},{5,7},{6,4},{7,5},{8,10},{9,11},{10,... | collective-permute-start | bytes 61448 | tf_op jit(solution)/shard_map/ppermute | solution.py:23
  6.8 0.1 collective-permute-start.2
  6.9 0.1 collective-permute-start.6
  7.0 1.9 %collective-permute-start.7 = (f32[32,8,128]{2,1,0:T(8,128)S(1)}, f32[32,8,128]{2,1,0:T(8,128)S(1)}, u32[]{:S(2)}, u32[]{:S(2)}) collective-permute-start(f32[32,8,128]{2,1,0:T(8,128)S(1)} %get-tuple-element.24.refs_0_), channel_id=1, source_target_pairs={{0,2},{1,3},{2,0},{3,1},{4,6},{5,7},{6,4},{7,5},{8,10},{9,11},{10,... | collective-permute-start | bytes 393224 | tf_op jit(solution)/shard_map/ppermute | solution.py:23
  8.9 0.8 %eq.15 = s32[256]{0:T(256)S(1)} reshape(s32[8,32]{1,0:T(8,128)} %bitcast.16) | data formatting | bytes 2048 | tf_op jit(solution)/shard_map/eq | solution.py:384
  9.7 0.0 collective-permute-start.8
  9.7 0.2 collective-permute-done.2.refs_7_
  10.0 1.6 %collective-permute-start.3 = (f32[32,128]{1,0:T(8,128)S(1)}, f32[32,128]{1,0:T(8,128)S(1)}, u32[]{:S(2)}, u32[]{:S(2)}) collective-permute-start(f32[32,128]{1,0:T(8,128)S(1)} %pad_maximum_fusion.refs_0_), channel_id=1, source_target_pairs={{0,4},{4,0},{8,12},{12,8},{1,5},{5,1},{9,13},{13,9},{2,6},{6,2},{1... | collective-permute-start | bytes 49160 | tf_op jit(solution)/shard_map/ppermute | solution.py:23
  11.6 2.6 %collective-permute-start.4 = (f32[32,128]{1,0:T(8,128)S(1)}, f32[32,128]{1,0:T(8,128)S(1)}, u32[]{:S(2)}, u32[]{:S(2)}) collective-permute-start(f32[32,128]{1,0:T(8,128)S(1)} %pad_maximum_fusion.refs_0_), channel_id=1, source_target_pairs={{0,8},{4,12},{8,0},{12,4},{1,9},{5,13},{9,1},{13,5},{2,10},{6,14},... | collective-permute-start | bytes 49160 | tf_op jit(solution)/shard_map/ppermute | solution.py:23
  14.2 0.2 collective-permute-start.5
  14.4 0.1 compare_convert_fusion.refs_8_.refs_4_
  14.5 0.0 collective-permute-done.7.refs_2_
  14.5 1.0 %collective-permute-done.8.refs_3_ = f32[32,8,128]{2,1,0:T(8,128)S(1)} collective-permute-done((f32[32,8,128]{2,1,0:T(8,128)S(1)}, f32[32,8,128]{2,1,0:T(8,128)S(1)}, u32[]{:S(2)}, u32[]{:S(2)}) %collective-permute-start.8) | collective-permute-done | bytes 131104 | tf_op jit(solution)/shard_map/ppermute | solution.py:23
  15.5 7.4 %shard_map.123 = (f32[32,128]{1,0:T(8,128)S(1)}, f32[32,128]{1,0:T(8,128)S(1)}, f32[288,128,128]{2,1,0:T(8,128)S(1)}) custom-call(s32[1]{0:T(128)} %bitcast.box, f32[32,8,128]{2,1,0:T(8,128)S(1)} %get-tuple-element.24.refs_0_, f32[32,8,128]{2,1,0:T(8,128)S(1)} %collective-permute-done.6.refs_1_, f32[32,8,128]{2,1,0:T(8,128)S(1)} %collective-permute-done.7.refs_2_, ...), custom_call_target="tpu_custom_call" | custom-call | tf_op jit(solution)/shard_map/pallas_call | solution.py:38
  22.9 0.0 collective-permute-done.3.refs_1_
  23.0 0.0 copy-start
  23.0 0.6 %copy-done = s32[1,8]{1,0:T(1,128)S(1)} copy-done((s32[1,8]{1,0:T(1,128)S(1)}, s32[1,8]{1,0:T(1,128)}, u32[]{:S(2)}) %copy-start) | copy-done | bytes 56
  23.6 1.9 %shard_map.124 = (f32[72,128]{1,0:T(8,128)S(1)}, f32[32,128]{1,0:T(8,128)S(1)}, f32[8,128]{1,0:T(8,128)S(1)}) custom-call(s32[1]{0:T(128)S(6)} %copy.14.counts, s32[1]{0:T(128)} %bitcast.box, s32[1,8]{1,0:T(1,128)S(1)} %copy-done, f32[32,128]{1,0:T(8,128)S(1)} %pad_maximum_fusion.refs_0_, f32[32,128]{1,0:T(8,128)S(1)} %collective-permute-done.3.refs_1_, ...), custom_call_target="tpu_custom_call" | custom-call | tf_op jit(solution)/shard_map/pallas_call | solution.py:38
  25.5 0.2 collective-permute-start.9
  25.7 1.8 %collective-permute-start.10 = (f32[72,128]{1,0:T(8,128)S(1)}, f32[72,128]{1,0:T(8,128)S(1)}, u32[]{:S(2)}, u32[]{:S(2)}) collective-permute-start(f32[72,128]{1,0:T(8,128)S(1)} %get-tuple-element.32.refs_0_.refs_6_), channel_id=1, source_target_pairs={{0,2},{1,3},{2,0},{3,1},{4,6},{5,7},{6,4},{7,5},{8,10},{9,11},{10,... | collective-permute-start | bytes 110600 | tf_op jit(solution)/shard_map/ppermute | solution.py:23
  27.5 2.2 %collective-permute-done.10.refs_2_ = f32[72,128]{1,0:T(8,128)S(1)} collective-permute-done((f32[72,128]{1,0:T(8,128)S(1)}, f32[72,128]{1,0:T(8,128)S(1)}, u32[]{:S(2)}, u32[]{:S(2)}) %collective-permute-start.10) | collective-permute-done | bytes 36896 | tf_op jit(solution)/shard_map/ppermute | solution.py:23
  29.7 1.5 %collective-permute-done.11.refs_3_ = f32[72,128]{1,0:T(8,128)S(1)} collective-permute-done((f32[72,128]{1,0:T(8,128)S(1)}, f32[72,128]{1,0:T(8,128)S(1)}, u32[]{:S(2)}, u32[]{:S(2)}) %collective-permute-start.11) | collective-permute-done | bytes 36896 | tf_op jit(solution)/shard_map/ppermute | solution.py:23
  31.2 1.3 %collective-permute-start.12 = (f32[32,128]{1,0:T(8,128)S(1)}, f32[32,128]{1,0:T(8,128)S(1)}, u32[]{:S(2)}, u32[]{:S(2)}) collective-permute-start(f32[32,128]{1,0:T(8,128)S(1)} %pad_maximum_fusion.1.refs_0_), channel_id=1, source_target_pairs={{0,4},{4,0},{8,12},{12,8},{1,5},{5,1},{9,13},{13,9},{2,6},{6,2},{1... | collective-permute-start | bytes 49160 | tf_op jit(solution)/shard_map/ppermute | solution.py:23
  32.5 2.9 %collective-permute-start.13 = (f32[32,128]{1,0:T(8,128)S(1)}, f32[32,128]{1,0:T(8,128)S(1)}, u32[]{:S(2)}, u32[]{:S(2)}) collective-permute-start(f32[32,128]{1,0:T(8,128)S(1)} %pad_maximum_fusion.1.refs_0_), channel_id=1, source_target_pairs={{0,8},{4,12},{8,0},{12,4},{1,9},{5,13},{9,1},{13,5},{2,10},{6,14},... | collective-permute-start | bytes 49160 | tf_op jit(solution)/shard_map/ppermute | solution.py:23
  35.4 0.2 collective-permute-start.14
  35.6 2.3 %shard_map.125 = (f32[32,128]{1,0:T(8,128)S(1)}, f32[32,128]{1,0:T(8,128)S(1)}) custom-call(s32[1]{0:T(128)} %bitcast.box, f32[72,128]{1,0:T(8,128)S(1)} %get-tuple-element.32.refs_0_.refs_6_, f32[72,128]{1,0:T(8,128)S(1)} %collective-permute-done.9.refs_1_, f32[72,128]{1,0:T(8,128)S(1)} %collective-permute-done.10.refs_2_, ...), custom_call_target="tpu_custom_call" | custom-call | tf_op jit(solution)/shard_map/pallas_call | solution.py:38
  37.9 3.0 %collective-permute-done.14.refs_3_ = f32[32,128]{1,0:T(8,128)S(1)} collective-permute-done((f32[32,128]{1,0:T(8,128)S(1)}, f32[32,128]{1,0:T(8,128)S(1)}, u32[]{:S(2)}, u32[]{:S(2)}) %collective-permute-start.14) | collective-permute-done | bytes 16416 | tf_op jit(solution)/shard_map/ppermute | solution.py:23
  40.9 1.5 %shard_map.126 = (f32[32,128]{1,0:T(8,128)S(1)}, f32[32,128]{1,0:T(8,128)S(1)}, f32[16,128]{1,0:T(8,128)S(1)}, f32[8,128]{1,0:T(8,128)S(1)}) custom-call(s32[1]{0:T(128)S(6)} %copy.14.counts, s32[1]{0:T(128)} %bitcast.box, s32[1,8]{1,0:T(1,128)S(1)} %copy-done, f32[32,128]{1,0:T(8,128)S(1)} %pad_maximum_fusion.1.refs_0_, ...), custom_call_target="tpu_custom_call" | custom-call | tf_op jit(solution)/shard_map/pallas_call | solution.py:38
  42.4 9.0 %all_to_all.11 = f32[16,1,128]{2,1,0:T(1,128)S(1)} all-to-all(f32[16,1,128]{2,1,0:T(1,128)S(1)} %bitcast.11), channel_id=1, replica_groups=mesh['groups'=2,'patch'=4,'sub'=4] {'patch','sub'}, dimensions={0} | all-to-all | bytes 16384 | tf_op jit(solution)/shard_map/all_to_all | solution.py:466
  51.4 1.0 %shard_map.127 = (f32[32,128]{1,0:T(8,128)}, f32[2,3]{1,0:T(2,128)}) custom-call(f32[16,128]{1,0:T(8,128)S(1)} %bitcast.10, f32[32,128]{1,0:T(8,128)S(1)} %get-tuple-element.36.refs_7_.basis_one, f32[32,128]{1,0:T(8,128)S(1)} %get-tuple-element.39.basis_two, f32[32,128]{1,0:T(8,128)S(1)} %get-tuple-element.40.image_two, f32[8,128]{1,0:T(8,128)S(1)} %get-tuple-element.41.numbers), custom_call_target="tpu_custom_call" | custom-call | tf_op jit(solution)/shard_map/pallas_call | solution.py:38
  (20 shorter events, 0.1 us)
Async XLA Ops:
  3.7 6.0 %collective-permute-start = (f32[40,128]{1,0:T(8,128)S(1)}, f32[40,128]{1,0:T(8,128)S(1)}, u32[]{:S(2)}, u32[]{:S(2)}) collective-permute-start(f32[40,128]{1,0:T(8,128)S(1)} %get-tuple-element.23.refs_4_), channel_id=1, source_target_pairs={{0,1},{1,0},{2,3},{3,2},{4,5},{5,4},{6,7},{7,6},{8,9},{9,8},{10,11... | collective-permute-start | bytes 61448 | tf_op jit(solution)/shard_map/ppermute | solution.py:23
  4.2 5.5 %collective-permute-start.1 = (f32[40,128]{1,0:T(8,128)S(1)}, f32[40,128]{1,0:T(8,128)S(1)}, u32[]{:S(2)}, u32[]{:S(2)}) collective-permute-start(f32[40,128]{1,0:T(8,128)S(1)} %get-tuple-element.23.refs_4_), channel_id=1, source_target_pairs={{0,2},{1,3},{2,0},{3,1},{4,6},{5,7},{6,4},{7,5},{8,10},{9,11},{10,... | collective-permute-start | bytes 61448 | tf_op jit(solution)/shard_map/ppermute | solution.py:23
  6.8 3.2 %collective-permute-start.2 = (f32[40,128]{1,0:T(8,128)S(1)}, f32[40,128]{1,0:T(8,128)S(1)}, u32[]{:S(2)}, u32[]{:S(2)}) collective-permute-start(f32[40,128]{1,0:T(8,128)S(1)} %get-tuple-element.23.refs_4_), channel_id=1, source_target_pairs={{0,3},{1,2},{2,1},{3,0},{4,7},{5,6},{6,5},{7,4},{8,11},{9,10},{10,... | collective-permute-start | bytes 61448 | tf_op jit(solution)/shard_map/ppermute | solution.py:23
  6.9 7.3 %collective-permute-start.6 = (f32[32,8,128]{2,1,0:T(8,128)S(1)}, f32[32,8,128]{2,1,0:T(8,128)S(1)}, u32[]{:S(2)}, u32[]{:S(2)}) collective-permute-start(f32[32,8,128]{2,1,0:T(8,128)S(1)} %get-tuple-element.24.refs_0_), channel_id=1, source_target_pairs={{0,1},{1,0},{2,3},{3,2},{4,5},{5,4},{6,7},{7,6},{8,9},{9,8},{10,11... | collective-permute-start | bytes 393224 | tf_op jit(solution)/shard_map/ppermute | solution.py:23
  7.0 7.5 %collective-permute-start.7 = (f32[32,8,128]{2,1,0:T(8,128)S(1)}, f32[32,8,128]{2,1,0:T(8,128)S(1)}, u32[]{:S(2)}, u32[]{:S(2)}) collective-permute-start(f32[32,8,128]{2,1,0:T(8,128)S(1)} %get-tuple-element.24.refs_0_), channel_id=1, source_target_pairs={{0,2},{1,3},{2,0},{3,1},{4,6},{5,7},{6,4},{7,5},{8,10},{9,11},{10,... | collective-permute-start | bytes 393224 | tf_op jit(solution)/shard_map/ppermute | solution.py:23
  9.7 5.8 %collective-permute-start.8 = (f32[32,8,128]{2,1,0:T(8,128)S(1)}, f32[32,8,128]{2,1,0:T(8,128)S(1)}, u32[]{:S(2)}, u32[]{:S(2)}) collective-permute-start(f32[32,8,128]{2,1,0:T(8,128)S(1)} %get-tuple-element.24.refs_0_), channel_id=1, source_target_pairs={{0,3},{1,2},{2,1},{3,0},{4,7},{5,6},{6,5},{7,4},{8,11},{9,10},{10,... | collective-permute-start | bytes 393224 | tf_op jit(solution)/shard_map/ppermute | solution.py:23
  10.0 12.9 %collective-permute-start.3 = (f32[32,128]{1,0:T(8,128)S(1)}, f32[32,128]{1,0:T(8,128)S(1)}, u32[]{:S(2)}, u32[]{:S(2)}) collective-permute-start(f32[32,128]{1,0:T(8,128)S(1)} %pad_maximum_fusion.refs_0_), channel_id=1, source_target_pairs={{0,4},{4,0},{8,12},{12,8},{1,5},{5,1},{9,13},{13,9},{2,6},{6,2},{1... | collective-permute-start | bytes 49160 | tf_op jit(solution)/shard_map/ppermute | solution.py:23
  11.6 11.4 %collective-permute-start.4 = (f32[32,128]{1,0:T(8,128)S(1)}, f32[32,128]{1,0:T(8,128)S(1)}, u32[]{:S(2)}, u32[]{:S(2)}) collective-permute-start(f32[32,128]{1,0:T(8,128)S(1)} %pad_maximum_fusion.refs_0_), channel_id=1, source_target_pairs={{0,8},{4,12},{8,0},{12,4},{1,9},{5,13},{9,1},{13,5},{2,10},{6,14},... | collective-permute-start | bytes 49160 | tf_op jit(solution)/shard_map/ppermute | solution.py:23
  14.2 8.8 %collective-permute-start.5 = (f32[32,128]{1,0:T(8,128)S(1)}, f32[32,128]{1,0:T(8,128)S(1)}, u32[]{:S(2)}, u32[]{:S(2)}) collective-permute-start(f32[32,128]{1,0:T(8,128)S(1)} %pad_maximum_fusion.refs_0_), channel_id=1, source_target_pairs={{0,12},{4,8},{8,4},{12,0},{1,13},{5,9},{9,5},{13,1},{2,14},{6,10},... | collective-permute-start | bytes 49160 | tf_op jit(solution)/shard_map/ppermute | solution.py:23
  23.0 0.7 %copy-start = (s32[1,8]{1,0:T(1,128)S(1)}, s32[1,8]{1,0:T(1,128)}, u32[]{:S(2)}) copy-start(s32[1,8]{1,0:T(1,128)} %box_far.3) | copy-start | bytes 100
  25.5 1.9 %collective-permute-start.9 = (f32[72,128]{1,0:T(8,128)S(1)}, f32[72,128]{1,0:T(8,128)S(1)}, u32[]{:S(2)}, u32[]{:S(2)}) collective-permute-start(f32[72,128]{1,0:T(8,128)S(1)} %get-tuple-element.32.refs_0_.refs_6_), channel_id=1, source_target_pairs={{0,1},{1,0},{2,3},{3,2},{4,5},{5,4},{6,7},{7,6},{8,9},{9,8},{10,11... | collective-permute-start | bytes 110600 | tf_op jit(solution)/shard_map/ppermute | solution.py:23
  25.7 4.0 %collective-permute-start.10 = (f32[72,128]{1,0:T(8,128)S(1)}, f32[72,128]{1,0:T(8,128)S(1)}, u32[]{:S(2)}, u32[]{:S(2)}) collective-permute-start(f32[72,128]{1,0:T(8,128)S(1)} %get-tuple-element.32.refs_0_.refs_6_), channel_id=1, source_target_pairs={{0,2},{1,3},{2,0},{3,1},{4,6},{5,7},{6,4},{7,5},{8,10},{9,11},{10,... | collective-permute-start | bytes 110600 | tf_op jit(solution)/shard_map/ppermute | solution.py:23
  27.5 3.7 %collective-permute-start.11 = (f32[72,128]{1,0:T(8,128)S(1)}, f32[72,128]{1,0:T(8,128)S(1)}, u32[]{:S(2)}, u32[]{:S(2)}) collective-permute-start(f32[72,128]{1,0:T(8,128)S(1)} %get-tuple-element.32.refs_0_.refs_6_), channel_id=1, source_target_pairs={{0,3},{1,2},{2,1},{3,0},{4,7},{5,6},{6,5},{7,4},{8,11},{9,10},{10,... | collective-permute-start | bytes 110600 | tf_op jit(solution)/shard_map/ppermute | solution.py:23
  31.2 6.7 %collective-permute-start.12 = (f32[32,128]{1,0:T(8,128)S(1)}, f32[32,128]{1,0:T(8,128)S(1)}, u32[]{:S(2)}, u32[]{:S(2)}) collective-permute-start(f32[32,128]{1,0:T(8,128)S(1)} %pad_maximum_fusion.1.refs_0_), channel_id=1, source_target_pairs={{0,4},{4,0},{8,12},{12,8},{1,5},{5,1},{9,13},{13,9},{2,6},{6,2},{1... | collective-permute-start | bytes 49160 | tf_op jit(solution)/shard_map/ppermute | solution.py:23
  32.5 5.4 %collective-permute-start.13 = (f32[32,128]{1,0:T(8,128)S(1)}, f32[32,128]{1,0:T(8,128)S(1)}, u32[]{:S(2)}, u32[]{:S(2)}) collective-permute-start(f32[32,128]{1,0:T(8,128)S(1)} %pad_maximum_fusion.1.refs_0_), channel_id=1, source_target_pairs={{0,8},{4,12},{8,0},{12,4},{1,9},{5,13},{9,1},{13,5},{2,10},{6,14},... | collective-permute-start | bytes 49160 | tf_op jit(solution)/shard_map/ppermute | solution.py:23
  35.4 5.5 %collective-permute-start.14 = (f32[32,128]{1,0:T(8,128)S(1)}, f32[32,128]{1,0:T(8,128)S(1)}, u32[]{:S(2)}, u32[]{:S(2)}) collective-permute-start(f32[32,128]{1,0:T(8,128)S(1)} %pad_maximum_fusion.1.refs_0_), channel_id=1, source_target_pairs={{0,12},{4,8},{8,4},{12,0},{1,13},{5,9},{9,5},{13,1},{2,14},{6,10},... | collective-permute-start | bytes 49160 | tf_op jit(solution)/shard_map/ppermute | solution.py:23

commit v5 on v4

v5 whole, which is shorter than its diff:
```python
import functools
import math

import jax
import jax.numpy as jnp
from jax import lax
from jax.experimental import pallas as pl
from jax.experimental.pallas import tpu as pltpu
from jax.sharding import PartitionSpec as P

SOFTEN = 0.05
EPSILON = 1e-06
KERNEL_SCALE = 0.25 / math.pi
HIGH_PRECISION = lax.Precision.HIGHEST
LANES = 128
TILE_ROWS = 8
VMEM_LIMIT = 16 << 20


def from_peers(value, axis):
    size = lax.axis_size(axis)
    arrived = [
        lax.ppermute(value, axis, [(i, i ^ turn) for i in range(size)]) for turn in range(1, size)
    ]
    return [value] + arrived


def tree_sum(parts):
    while len(parts) > 1:
        parts = [parts[i] + parts[i + 1] for i in range(0, len(parts), 2)]
    return parts[0]


def device_call(kernel, outputs, scalars, arrays, scratch=(), remote=()):
    smem = pl.BlockSpec(memory_space=pltpu.SMEM)
    vmem = pl.BlockSpec(memory_space=pltpu.VMEM)
    hbm = pl.BlockSpec(memory_space=pltpu.HBM)
    return pl.pallas_call(
        kernel,
        out_shape=tuple(outputs),
        in_specs=[smem] * len(scalars) + [vmem] * len(arrays) + [hbm] * len(remote),
        out_specs=tuple([vmem] * len(outputs)),
        scratch_shapes=tuple(scratch),
        compiler_params=pltpu.CompilerParams(vmem_limit_bytes=VMEM_LIMIT),
    )(
        *scalars,
        *arrays,
        *[pltpu.with_memory_space_constraint(array, pltpu.HBM) for array in remote],
    )


def kept(array):
    return pltpu.VMEM(array.shape, array.dtype)


def f32(*shape):
    return jax.ShapeDtypeStruct(shape, jnp.float32)


def iota(shape, dimension):
    return lax.broadcasted_iota(jnp.int32, shape, dimension)


def split_three(value):
    first = value.astype(jnp.bfloat16).astype(jnp.float32)
    rest = value - first
    second = rest.astype(jnp.bfloat16).astype(jnp.float32)
    third = (rest - second).astype(jnp.bfloat16).astype(jnp.float32)
    return first, second, third


def lane_row(entries):
    lane = iota((1, LANES), 1)
    row = jnp.zeros((1, LANES), jnp.float32)
    for place, entry in enumerate(entries):
        row = jnp.where(lane == place, entry, row)
    return row


def copy_all(pairs, arrived):
    copies = [
        pltpu.make_async_copy(source, target, arrived.at[place])
        for place, (source, target) in enumerate(pairs)
    ]
    for copy in copies:
        copy.start()
    return copies


def start_kernel(counts, points, normals, density, geometry, initial, at, arrived):
    dims, slots, width = points.shape
    targets = [at.at[0:dims], at.at[dims : 2 * dims], at.at[2 * dims]]
    for copy in copy_all(zip((points, normals, density), targets), arrived):
        copy.wait()
    for row in range(2 * dims):
        geometry[:, row, :] = at[row]
    vector = jnp.where(iota((slots, width), 0) < counts[0], at[2 * dims], 0.0)
    initial[...] = vector
    geometry[:, 2 * dims, :] = vector
    geometry[:, 2 * dims + 1, :] = jnp.zeros_like(vector)


def write_moments(vector, basis, message, start):
    slots, rank, _ = basis.shape
    lane = iota((rank, LANES), 1)
    columns = jnp.zeros((rank, LANES), jnp.float32)
    for leaf in range(slots):
        column = jnp.sum(basis[leaf] * vector[leaf : leaf + 1, :], axis=1, keepdims=True)
        columns = jnp.where(lane == leaf, column, columns)
    message[start : start + slots, :] = jnp.zeros((slots, LANES), jnp.float32)
    message[start : start + slots, 0:rank] = columns.T[0:slots]


def box_moments(vector, box_basis):
    slots, rank, width = box_basis.shape
    total = jnp.zeros((rank, width), jnp.float32)
    for leaf in range(slots):
        total = total + box_basis[leaf] * vector[leaf : leaf + 1, :]
    column = jnp.sum(total, axis=1, keepdims=True)
    diagonal = iota((rank, LANES), 0) == iota((rank, LANES), 1)
    return jnp.sum(jnp.where(diagonal, column, 0.0), axis=0, keepdims=True)


def six_products(left, right, contract):
    one, two, three = [part.astype(jnp.bfloat16) for part in split_three(right)]
    parts = jnp.concatenate(split_three(left)).astype(jnp.bfloat16)
    rows = left.shape[0]

    def product(count, other):
        return lax.dot_general(
            parts[0 : count * rows],
            other,
            (contract, ((), ())),
            preferred_element_type=jnp.float32,
        )

    first, second, third = product(3, one), product(2, two), product(1, three)
    return first[0:rows] + (
        (first[rows : 2 * rows] + second[0:rows])
        + (first[2 * rows : 3 * rows] + second[rows : 2 * rows] + third)
    )


def basis_kernel(counts, box_far, initial, *refs):
    sources, message, box_basis, (basis, leaf_coupling, box_coupling) = (
        refs[:4],
        refs[4],
        refs[5],
        refs[6:9],
    )
    transfer, arrived = refs[9:]
    slots, rank, _ = basis.shape
    targets = (basis, transfer, leaf_coupling, box_coupling)
    copies = copy_all(zip(sources, targets), arrived)
    for copy in copies:
        copy.wait()
    gram = jnp.zeros((rank, rank), jnp.float32)
    for leaf in range(slots):
        product = jnp.dot(
            transfer[leaf],
            basis[leaf],
            precision=HIGH_PRECISION,
            preferred_element_type=jnp.float32,
        )
        product = jnp.where(leaf < counts[0], product, 0.0)
        box_basis[leaf] = product
        gram = gram + six_products(product, product, ((1,), (1,)))
    write_moments(initial, basis, message, 0)
    vector = initial[...]
    entries = [jnp.sum(vector * vector, keepdims=True)] + [
        jnp.full((1, 1), value, jnp.int32).astype(jnp.float32)
        for value in [counts[0]] + [box_far[0, place] for place in range(box_far.shape[1])]
    ]
    message[slots : slots + TILE_ROWS, :] = jnp.zeros((TILE_ROWS, LANES), jnp.float32)
    message[slots : slots + 1, :] = box_moments(initial, box_basis)
    message[slots + 1 : slots + 2, :] = lane_row(entries)
    start, half = slots + TILE_ROWS, rank // 2
    message[start : start + half, 0:rank] = gram[0:half]
    message[start : start + half, rank : 2 * rank] = gram[half:rank]


def leaf_part(moments, picks, coupling):
    count, rank, _ = coupling.shape
    slots = picks.shape[0] // count
    chosen = jnp.zeros((picks.shape[0], rank), jnp.float32)
    for part in split_three(jnp.concatenate(moments, axis=0)):
        chosen = chosen + jnp.dot(
            picks[...], part.astype(jnp.bfloat16), preferred_element_type=jnp.float32
        )
    local = jnp.zeros((slots, rank), jnp.float32)
    for place in range(count):
        local = local + lax.dot_general(
            chosen[place * slots : (place + 1) * slots],
            coupling[place],
            (((1,), (1,)), ((), ())),
            precision=HIGH_PRECISION,
            preferred_element_type=jnp.float32,
        )
    return local


def add_leaf_far(counts, moments, picks, coupling, basis, near):
    slots, rank, width = basis.shape
    local = leaf_part(moments, picks, coupling)
    columns = jnp.concatenate([local, jnp.zeros((slots, LANES - rank), jnp.float32)], axis=1).T
    for leaf in range(slots):
        far = jnp.sum(basis[leaf] * columns[0:rank, leaf : leaf + 1], axis=0, keepdims=True)
        near[leaf : leaf + 1, :] = jnp.where(
            leaf < counts[0], near[leaf : leaf + 1, :] + far, 0.0
        )


def first_near_kernel(subs, box, counts, *refs):
    geometry, messages = refs[:subs], refs[subs : 2 * subs]
    picks, coupling, basis, near_source, near, values = refs[2 * subs : 2 * subs + 6]
    features, squares, fields, inner, near_list, arrived = refs[2 * subs + 6 :]
    copy = pltpu.make_async_copy(near_source, near_list, arrived)
    copy.start()
    slots, height, width = geometry[0].shape
    neighbours = near_list.shape[0]
    rank = coupling.shape[1]
    row = iota((height, width), 0)
    scale_square = jnp.where(row < 3, -2.0, 0.0)
    ones = jnp.where(row == 7, 1.0, 0.0)
    scale_normal = jnp.where((row >= 3) & (row < 6), -KERNEL_SCALE, 0.0)

    for sub in range(subs):
        rows = geometry[sub]
        at = [rows[:, component, :] for component in range(7)]
        squares[sub * slots : (sub + 1) * slots, :] = at[0] * at[0] + at[1] * at[1] + at[2] * at[2]
        fields[sub * slots : (sub + 1) * slots, :] = at[6]
        inner[...] = (at[0] * at[3] + at[1] * at[4] + at[2] * at[5]) * KERNEL_SCALE

        def source(leaf, carry, rows=rows, sub=sub):
            place = sub * slots + leaf
            plain = rows[leaf]
            square = squares[pl.ds(place, 1), :] + SOFTEN
            distance = jnp.where(row == 6, square, plain * scale_square + ones)
            numerator = jnp.where(row == 6, inner[pl.ds(leaf, 1), :], plain * scale_normal)
            for part, value in enumerate((distance, numerator)):
                one, two, three = split_three(value)
                lanes = slice(part * width, (part + 1) * width)
                features[place, 0:16, lanes] = jnp.concatenate([one, two]).astype(jnp.bfloat16)
                features[place, 16:32, lanes] = jnp.concatenate([one, three]).astype(jnp.bfloat16)
            return carry

        lax.fori_loop(0, slots, source, 0, unroll=4)

    own = geometry[0]

    def target(leaf, carry):
        plain = own[leaf]
        shifted = pltpu.roll(plain, 3, 0)
        square = squares[pl.ds(leaf, 1), :]
        value = jnp.where(row < 3, plain, jnp.where(row < 6, shifted, jnp.where(row == 6, 1.0, square)))
        one, two, three = split_three(value)
        left = jnp.concatenate([one, one, two, two, three, one]).T.astype(jnp.bfloat16)
        total = jnp.zeros((width, width), jnp.float32)
        for column in range(neighbours):
            place = near_list[column, leaf] ^ (box[0] * slots)
            upper, lower = features[place, 0:16, :], features[place, 16:32, :]
            right = jnp.concatenate([upper, upper, lower], axis=0)
            both = jnp.dot(left, right, preferred_element_type=jnp.float32)
            inverse = lax.rsqrt(both[:, 0:width])
            tile = both[:, width : 2 * width] * (inverse * inverse * inverse)
            values[leaf * neighbours + column] = tile
            total = total + tile * fields[pl.ds(place, 1), :]
        near[pl.ds(leaf, 1), :] = jnp.sum(total.T, axis=0, keepdims=True)
        return carry

    copy.wait()
    lax.fori_loop(0, slots, target, 0, unroll=True)
    moments = [ref[0:slots, 0:rank] for ref in messages]
    add_leaf_far(counts, moments, picks, coupling, basis, near)


def box_images(box_basis, coefficients, image):
    slots, rank, width = box_basis.shape
    spread = jnp.broadcast_to(coefficients, (rank, width))
    for leaf in range(slots):
        image[leaf : leaf + 1, :] += jnp.sum(box_basis[leaf] * spread, axis=0, keepdims=True)


def first_image_kernel(patches, span, box, box_far, *refs):
    boxes = refs[:patches]
    part, initial, basis, box_basis, box_coupling = refs[patches : patches + 5]
    message, basis_one, numbers, gather, image = refs[patches + 5 :]
    slots, rank, width = basis.shape
    height = boxes[0].shape[0]
    for place, ref in enumerate(boxes):
        gather[place * height : (place + 1) * height, :] = ref[...]
    coupled = jnp.zeros((rank, rank), jnp.float32)
    for place in range(box_coupling.shape[0]):
        row = (box_far[0, place] ^ box[0]) * span
        coupled = coupled + box_coupling[place] * gather[pl.ds(row, 1), 0:rank]
    image[...] = part[...]
    box_images(box_basis, jnp.sum(coupled, axis=1, keepdims=True), image)
    sums = tree_sum(
        [
            tree_sum([ref[at + 1 : at + 2, :] for at in range(0, height, span)])
            for ref in boxes
        ]
    )
    square_sum, unknowns = sums[:, 0:1], width * sums[:, 1:2]
    start_scale = jnp.sqrt(square_sum / unknowns + EPSILON)
    one_one = square_sum / (start_scale * start_scale)
    basis_one[...] = initial[...] / start_scale
    message[0:slots, :] = image[...] / start_scale
    numbers[...] = jnp.broadcast_to(lane_row([one_one, unknowns, start_scale]), numbers.shape)
    write_moments(message, basis, message, slots)


def second_near_kernel(subs, box, counts, *refs):
    messages = refs[:subs]
    picks, coupling, basis, box_basis, basis_one, values, near_source = refs[subs : subs + 7]
    part, shares, fields, near_list, arrived = refs[subs + 7 :]
    copy = pltpu.make_async_copy(near_source, near_list, arrived)
    copy.start()
    slots, width = part.shape
    neighbours = near_list.shape[0]
    rank = coupling.shape[1]
    for sub in range(subs):
        fields[sub * slots : (sub + 1) * slots, :] = messages[sub][0:slots, :]

    def target(leaf, carry):
        total = jnp.zeros((width, width), jnp.float32)
        for column in range(neighbours):
            place = near_list[column, leaf] ^ (box[0] * slots)
            total = total + values[leaf * neighbours + column] * fields[pl.ds(place, 1), :]
        part[pl.ds(leaf, 1), :] = jnp.sum(total.T, axis=0, keepdims=True)
        return carry

    copy.wait()
    lax.fori_loop(0, slots, target, 0, unroll=True)
    moments = [ref[slots : 2 * slots, 0:rank] for ref in messages]
    add_leaf_far(counts, moments, picks, coupling, basis, part)
    first, one, second = messages[0][0:slots, :], basis_one[...], part[...]
    products = [one * first, first * first, one * second, first * second, second * second]
    sums = lane_row([jnp.sum(product, keepdims=True) for product in products])
    lane = iota((1, LANES), 1)
    both = jnp.where(
        lane < rank,
        box_moments(messages[0], box_basis),
        pltpu.roll(box_moments(part, box_basis), rank, 1),
    )
    shares[...] = jnp.where(iota(shares.shape, 0) % 2 == 0, both, sums)


def last_kernel(patches, span, box, *refs):
    boxes, (shares, message, basis_one, part, numbers) = refs[:patches], refs[patches : patches + 5]
    box_basis, box_coupling = refs[patches + 5 : patches + 7]
    basis_three, hessenberg, gather, starts, lists, pairs, image = refs[patches + 7 :]
    slots, rank, width = box_basis.shape
    height = boxes[0].shape[0]
    count = patches * (height // span)
    for place, ref in enumerate(boxes):
        gather[place * height : (place + 1) * height, :] = ref[...]
    for other in range(count):
        row = (box[0] ^ other) * span
        starts[other : other + 1, :] = gather[pl.ds(row, 1), :]
        lists[other : other + 1, :] = gather[pl.ds(row + 1, 1), :]
        pairs[other : other + 1, :] = shares[2 * other : 2 * other + 1, :]
        pairs[count + other : count + other + 1, :] = shares[2 * other + 1 : 2 * other + 2, :]
    first_box, second_box = pairs[0:count, 0:rank], pairs[0:count, rank : 2 * rank]
    parts = [part.astype(jnp.bfloat16) for part in split_three(first_box)]
    lane = iota((count, count), 1).astype(jnp.float32)
    box_local = jnp.zeros((count, rank), jnp.float32)
    for place in range(box_coupling.shape[0]):
        pick = jnp.where(lists[:, 2 + place : 3 + place] == lane, 1.0, 0.0).astype(jnp.bfloat16)
        chosen = jnp.zeros((count, rank), jnp.float32)
        for split in parts:
            chosen = chosen + jnp.dot(pick, split, preferred_element_type=jnp.float32)
        box_local = box_local + lax.dot_general(
            chosen,
            box_coupling[place],
            (((1,), (1,)), ((), ())),
            precision=HIGH_PRECISION,
            preferred_element_type=jnp.float32,
        )
    twice = jnp.concatenate([box_local, box_local], axis=1)
    columns = twice.T
    half = rank // 2
    low = iota((half, 2 * rank), 1) < rank
    quadratic = jnp.zeros((half, 2 * rank), jnp.float32)
    for other in range(count):
        row = (box[0] ^ other) * span + TILE_ROWS
        column = jnp.where(
            low, columns[0:half, other : other + 1], columns[half:rank, other : other + 1]
        )
        quadratic = quadratic + gather[pl.ds(row, half), :] * twice[other : other + 1, :] * column
    one_one, unknowns, start_scale = [numbers[0:1, place : place + 1] for place in range(3)]
    sums = jnp.sum(pairs[count : 2 * count, :], axis=0, keepdims=True)
    along, image_sq, one_part, first_part, part_sq = [
        sums[:, place : place + 1] for place in range(5)
    ]
    one_second = (
        one_part + jnp.sum(starts[:, 0:rank] * box_local, keepdims=True) / start_scale
    )
    first_second = first_part + jnp.sum(first_box * box_local, keepdims=True)
    second_sq = (
        part_sq
        + 2.0 * jnp.sum(second_box * box_local, keepdims=True)
        + jnp.sum(quadratic, keepdims=True)
    )
    upper_first = (0.5 * one_one + along) / unknowns
    shift = upper_first - 0.5
    residual_sq = image_sq - 2.0 * shift * along + shift * shift * one_one
    lower_first = jnp.sqrt(residual_sq / unknowns + EPSILON)
    one_two = (along - shift * one_one) / lower_first
    two_two = residual_sq / (lower_first * lower_first)
    k_one = (one_second - shift * along) / lower_first
    k_two = (
        (first_second - shift * image_sq) - shift * (one_second - shift * along)
    ) / (lower_first * lower_first)
    k_sq = (second_sq - 2.0 * shift * first_second + shift * shift * image_sq) / (
        lower_first * lower_first
    )
    upper_second = (0.5 * one_two + k_one) / unknowns
    middle_second = (0.5 * two_two + k_two - upper_second * one_two) / unknowns
    turn = middle_second - 0.5
    final_sq = (
        k_sq
        - 2.0 * upper_second * k_one
        - 2.0 * turn * k_two
        + upper_second * upper_second * one_one
        + 2.0 * upper_second * turn * one_two
        + turn * turn * two_two
    )
    lower_second = jnp.sqrt(final_sq / unknowns + EPSILON)
    image[...] = part[...]
    own = jnp.where(iota((rank, count), 1) == box[0], columns[0:rank], 0.0)
    box_images(box_basis, jnp.sum(own, axis=1, keepdims=True), image)
    one, first = basis_one[...], message[0:slots, :]
    two = (first - shift * one) / lower_first
    mapped = (image[...] - shift * first) / lower_first
    basis_three[...] = (mapped - upper_second * one - turn * two) / lower_second
    column, row = iota(hessenberg.shape, 0), iota(hessenberg.shape, 1)
    matrix = jnp.where(column == 0, upper_first, upper_second)
    matrix = jnp.where(row == 1, jnp.where(column == 0, lower_first, middle_second), matrix)
    hessenberg[...] = jnp.where(row == 2, jnp.where(column == 0, 0.0, lower_second), matrix)


def shards(
    points,
    normals,
    density,
    counts,
    near_list,
    leaf_far,
    leaf_basis,
    leaf_to_box_transfer,
    leaf_coupling,
    box_far,
    box_coupling,
):
    slots, _, width = points.shape
    neighbours = near_list.shape[1]
    far_count = leaf_far.shape[1]
    subs, patches = lax.axis_size("sub"), lax.axis_size("patch")
    sources = subs * slots
    rows = f32(slots, width)
    this_box = lax.axis_index("patch") * subs + lax.axis_index("sub")
    box = this_box.astype(jnp.int32).reshape(1)
    patch_start = lax.axis_index("patch") * sources
    leaves = (jnp.arange(sources) + patch_start) ^ (lax.axis_index("sub") * slots)
    picks = (leaf_far.T.reshape(far_count * slots, 1) == leaves[None, :]).astype(jnp.bfloat16)

    rank = leaf_basis.shape[1]
    span = TILE_ROWS + rank // 2
    near_list = near_list.T
    list_scratch = [pltpu.SMEM(near_list.shape, jnp.int32), pltpu.SemaphoreType.DMA]
    block = pltpu.VMEM((sources, width), jnp.float32)

    geometry, initial = device_call(
        start_kernel,
        [f32(slots, 8, width), rows],
        [counts],
        [],
        [pltpu.VMEM((7, slots, width), jnp.float32), pltpu.SemaphoreType.DMA((3,))],
        [points.transpose(1, 0, 2), normals.transpose(1, 0, 2), density],
    )
    geometry = from_peers(geometry, "sub")
    message, box_basis, leaf_basis, leaf_coupling, box_coupling = device_call(
        basis_kernel,
        [
            f32(slots + span, LANES),
            kept(leaf_basis),
            kept(leaf_basis),
            kept(leaf_coupling),
            kept(box_coupling),
        ],
        [counts, box_far],
        [initial],
        [
            pltpu.VMEM(leaf_to_box_transfer.shape, jnp.float32),
            pltpu.SemaphoreType.DMA((4,)),
        ],
        [leaf_basis, leaf_to_box_transfer, leaf_coupling, box_coupling],
    )
    messages = from_peers(message, "sub")
    boxes = from_peers(
        jnp.concatenate([part[slots : slots + span] for part in messages], axis=0), "patch"
    )
    gather = pltpu.VMEM((patches * subs * span, LANES), jnp.float32)
    part, values = device_call(
        functools.partial(first_near_kernel, subs),
        [rows, pltpu.VMEM((slots * neighbours, width, width), jnp.float32)],
        [box, counts],
        [*geometry, *messages, picks, leaf_coupling, leaf_basis],
        [
            pltpu.VMEM((sources, 32, 2 * width), jnp.bfloat16),
            block,
            block,
            pltpu.VMEM((slots, width), jnp.float32),
            *list_scratch,
        ],
        [near_list],
    )
    message, basis_one, numbers = device_call(
        functools.partial(first_image_kernel, patches, span),
        [f32(2 * slots, LANES), rows, f32(TILE_ROWS, LANES)],
        [box, box_far],
        [*boxes, part, initial, leaf_basis, box_basis, box_coupling],
        [gather, pltpu.VMEM((slots, width), jnp.float32)],
    )
    messages = from_peers(message, "sub")
    part, shares = device_call(
        functools.partial(second_near_kernel, subs),
        [rows, f32(2 * patches * subs, LANES)],
        [box, counts],
        [*messages, picks, leaf_coupling, leaf_basis, box_basis, basis_one, values],
        [block, *list_scratch],
        [near_list],
    )
    shares = lax.all_to_all(shares, ("patch", "sub"), 0, 0, tiled=True)
    basis_three, hessenberg = device_call(
        functools.partial(last_kernel, patches, span),
        [rows, f32(2, 3)],
        [box],
        [*boxes, shares, message, basis_one, part, numbers, box_basis, box_coupling],
        [
            gather,
            pltpu.VMEM((patches * subs, LANES), jnp.float32),
            pltpu.VMEM((patches * subs, LANES), jnp.float32),
            pltpu.VMEM((2 * patches * subs, LANES), jnp.float32),
            pltpu.VMEM((slots, width), jnp.float32),
        ],
    )
    return basis_three, hessenberg.T


def solution(mesh):
    spread = ("groups", "patch", "sub")
    in_specs = (
        P(spread, None, None),
        P(spread, None, None),
        P(spread, None),
        P(spread),
        P(spread, None),
        P(spread, None),
        P(spread, None, None),
        P(spread, None, None),
        P(),
        P(spread, None),
        P(),
    )
    out_specs = (P(spread, None), P("groups", None))
    return jax.shard_map(shards, mesh=mesh, in_specs=in_specs, out_specs=out_specs, check_vma=False)
```

time: 52.7 us -> 57.3 us (1.087)
  waiting for transfers between devices: 7.93 us -> 3.04 us
  local copies, waits for them, and re-layouts: 1.43 us -> 6.29 us
  Pallas kernels: 16.6 us -> 21.4 us
  starting transfers between devices: 16 us -> 11.9 us
  blocking collectives: 8.98 us -> 11.3 us
  other arithmetic: 0.11 us -> 1.31 us
    ppermute x15 -> x12, waiting for transfers between devices: 7.93 us -> 3.04 us  [from_peers(): lax.ppermute(value, axis, [(i, i ^ turn) for i in range(size)])]
    pallas_call x6, Pallas kernels: 16.6 us -> 21.4 us  [device_call(): pl.pallas_call(kernel, out_shape=tuple(outputs), in_specs=[smem] * len(sc...]
    unnamed x2 -> x20, local copies, waits for them, and re-layouts: 0.65 us -> 4.95 us
    ppermute x15 -> x12, starting transfers between devices: 16 us -> 11.9 us  [from_peers(): lax.ppermute(value, axis, [(i, i ^ turn) for i in range(size)])]
    all_to_all x1, blocking collectives: 8.98 us -> 11.3 us  [shards(): shares = lax.all_to_all(shares, ('patch', 'sub'), 0, 0, tiled=True)]
    convert_element_type x1, other arithmetic: 0.1 us -> 0.79 us  [shards(): (leaf_far.T.reshape(far_count * slots, 1) == leaves[None, :]).astype(jnp....]
  transfers between devices with their start and end apart: 15 -> 12, of which waited for: 5 -> 2; matrix products, arithmetic and copies ran while one was open for 2% -> 5% of each run, Pallas kernels for 19% -> 14%
where the time goes in v5:
time: 57.3 us; the launch traced here: 56.6 us
  Pallas kernels  21.4 us (37%)
  starting transfers between devices  11.9 us (21%)
  blocking collectives  11.3 us (20%)
  local copies, waits for them, and re-layouts  6.29 us (11%)
  waiting for transfers between devices  3.04 us (5%)
  between operations  1.47 us (3%)
  other arithmetic  1.31 us (2%)
    pallas_call x6, Pallas kernels, device_call(): pl.pallas_call(kernel, out_shape=tuple(outputs), in_specs=[smem] * len(sc...  21.4 us
    ppermute x12, starting transfers between devices, from_peers(): lax.ppermute(value, axis, [(i, i ^ turn) for i in range(size)])  11.9 us
    all_to_all x1, blocking collectives, shards(): shares = lax.all_to_all(shares, ('patch', 'sub'), 0, 0, tiled=True)  11.3 us
    unnamed x20, local copies, waits for them, and re-layouts  4.95 us
    ppermute x12, waiting for transfers between devices, from_peers(): lax.ppermute(value, axis, [(i, i ^ turn) for i in range(size)])  3.04 us
    eq x1, local copies, waits for them, and re-layouts, shards(): leaf_far.T.reshape(far_count * slots, 1) == leaves[None, :]  1.33 us
  transfers between devices with their start and end apart: 12, of which 2 were waited for; matrix products, arithmetic and copies ran while one was open for 5% of the time, Pallas kernels for 14%

profile of v5, /device:TPU:0, one launch (start us, length us, event | category | flops | bytes accessed | tf_op | source)
XLA Modules:
  0.0 56.6 jit_solution(12957671480012913411)
XLA Ops:
  1.3 0.9 %shard_map.122 = (f32[32,8,128]{2,1,0:T(8,128)S(1)}, f32[32,128]{1,0:T(8,128)S(1)}) custom-call(s32[1]{0:T(128)S(6)} %copy.13.counts, f32[3,32,128]{2,1,0:T(8,128)} %bitcast.10, f32[3,32,128]{2,1,0:T(8,128)} %bitcast.11, f32[32,128]{1,0:T(8,128)} %density.1), custom_call_target="tpu_custom_call" | custom-call | tf_op jit(solution)/shard_map/pallas_call | solution.py:38
  2.2 0.0 copy-start.8
  2.2 0.6 %copy-done.8 = s32[1,8]{1,0:T(1,128)S(1)} copy-done((s32[1,8]{1,0:T(1,128)S(1)}, s32[1,8]{1,0:T(1,128)}, u32[]{:S(2)}) %copy-start.8) | copy-done | bytes 56
  2.9 5.2 %shard_map.123 = (f32[72,128]{1,0:T(8,128)S(1)}, f32[32,64,128]{2,1,0:T(8,128)S(1)}, f32[32,64,128]{2,1,0:T(8,128)S(1)}, f32[8,64,64]{2,1,0:T(8,128)S(1)}, f32[8,64,64]{2,1,0:T(8,128)S(1)}) custom-call(s32[1]{0:T(128)S(6)} %copy.13.counts, s32[1,8]{1,0:T(1,128)S(1)} %copy-done.8, f32[32,128]{1,0:T(8,128)S(1)} %get-tuple-element.18.initial.refs_5_, ...), custom_call_target="tpu_custom_call" | custom-call | tf_op jit(solution)/shard_map/pallas_call | solution.py:38
  8.0 0.5 collective-permute-start
  8.6 2.6 %collective-permute-start.1 = (f32[72,128]{1,0:T(8,128)S(1)}, f32[72,128]{1,0:T(8,128)S(1)}, u32[]{:S(2)}, u32[]{:S(2)}) collective-permute-start(f32[72,128]{1,0:T(8,128)S(1)} %get-tuple-element.19.refs_4_), channel_id=1, source_target_pairs={{0,2},{1,3},{2,0},{3,1},{4,6},{5,7},{6,4},{7,5},{8,10},{9,11},{10,... | collective-permute-start | bytes 110600 | tf_op jit(solution)/shard_map/ppermute | solution.py:23
  11.1 0.1 collective-permute-start.2
  11.2 0.1 collective-permute-start.6
  11.3 1.9 %collective-permute-start.7 = (f32[32,8,128]{2,1,0:T(8,128)S(1)}, f32[32,8,128]{2,1,0:T(8,128)S(1)}, u32[]{:S(2)}, u32[]{:S(2)}) collective-permute-start(f32[32,8,128]{2,1,0:T(8,128)S(1)} %get-tuple-element.20.refs_0_), channel_id=1, source_target_pairs={{0,2},{1,3},{2,0},{3,1},{4,6},{5,7},{6,4},{7,5},{8,10},{9,11},{10,... | collective-permute-start | bytes 393224 | tf_op jit(solution)/shard_map/ppermute | solution.py:23
  13.3 0.5 add_xor_fusion
  13.8 1.3 %eq.15 = s32[256]{0:T(256)} reshape(s32[8,32]{1,0:T(8,128)} %bitcast.14) | data formatting | bytes 2048 | tf_op jit(solution)/shard_map/eq | solution.py:466
  15.2 0.5 copy-done.2
  15.7 0.0 copy-done.4
  15.8 1.6 %collective-permute-start.3 = (f32[160,128]{1,0:T(8,128)S(1)}, f32[160,128]{1,0:T(8,128)S(1)}, u32[]{:S(2)}, u32[]{:S(2)}) collective-permute-start(f32[160,128]{1,0:T(8,128)S(1)} %pad_maximum_fusion.refs_0_), channel_id=1, source_target_pairs={{0,4},{4,0},{8,12},{12,8},{1,5},{5,1},{9,13},{13,9},{2,6},{6,2},{1... | collective-permute-start | bytes 245768 | tf_op jit(solution)/shard_map/ppermute | solution.py:23
  17.4 2.6 %collective-permute-start.4 = (f32[160,128]{1,0:T(8,128)S(1)}, f32[160,128]{1,0:T(8,128)S(1)}, u32[]{:S(2)}, u32[]{:S(2)}) collective-permute-start(f32[160,128]{1,0:T(8,128)S(1)} %pad_maximum_fusion.refs_0_), channel_id=1, source_target_pairs={{0,8},{4,12},{8,0},{12,4},{1,9},{5,13},{9,1},{13,5},{2,10},{6,14},... | collective-permute-start | bytes 245768 | tf_op jit(solution)/shard_map/ppermute | solution.py:23
  20.0 0.2 collective-permute-start.5
  20.3 0.8 %compare_convert_fusion.refs_8_.refs_4_ = bf16[256,128]{1,0:T(8,128)(2,1)S(1)} fusion(s32[128]{0:T(128)} %add_xor_fusion, s32[256]{0:T(256)} %eq.15), kind=kLoop, calls=%fused_computation | loop fusion | flops 65536 | bytes 67072 | tf_op jit(solution)/shard_map/convert_element_type | solution.py:466
  21.1 0.8 %copy-done.1 = f32[72,128]{1,0:T(8,128)S(1)} copy-done((f32[72,128]{1,0:T(8,128)S(1)}, f32[72,128]{1,0:T(8,128)}, u32[]{:S(2)}) %copy-start.1) | copy-done | bytes 36888
  21.9 0.8 %copy-done.3 = f32[72,128]{1,0:T(8,128)S(1)} copy-done((f32[72,128]{1,0:T(8,128)S(1)}, f32[72,128]{1,0:T(8,128)}, u32[]{:S(2)}) %copy-start.3) | copy-done | bytes 36888
  22.6 0.8 %copy-done.5 = f32[72,128]{1,0:T(8,128)S(1)} copy-done((f32[72,128]{1,0:T(8,128)S(1)}, f32[72,128]{1,0:T(8,128)}, u32[]{:S(2)}) %copy-start.5) | copy-done | bytes 36888
  23.4 0.8 %copy-done.7 = f32[72,128]{1,0:T(8,128)S(1)} copy-done((f32[72,128]{1,0:T(8,128)S(1)}, f32[72,128]{1,0:T(8,128)}, u32[]{:S(2)}) %copy-start.7) | copy-done | bytes 36888
  24.2 8.1 %shard_map.124 = (f32[32,128]{1,0:T(8,128)S(1)}, f32[288,128,128]{2,1,0:T(8,128)S(1)}) custom-call(s32[1]{0:T(128)} %bitcast.box, s32[1]{0:T(128)S(6)} %copy.13.counts, f32[32,8,128]{2,1,0:T(8,128)S(1)} %get-tuple-element.20.refs_0_, f32[32,8,128]{2,1,0:T(8,128)S(1)} %collective-permute-done.6.refs_1_, f32[32,8,128]{2,1,0:T(8,128)S(1)} %collective-permute-done.7.refs_2_, ...), custom_call_target="tpu_custom_call" | custom-call | tf_op jit(solution)/shard_map/pallas_call | solution.py:38
  32.3 0.0 copy-start.9
  32.3 0.6 %copy-done.9 = s32[1,8]{1,0:T(1,128)S(1)} copy-done((s32[1,8]{1,0:T(1,128)S(1)}, s32[1,8]{1,0:T(1,128)}, u32[]{:S(2)}) %copy-start.9) | copy-done | bytes 56
  33.0 1.1 %shard_map.125 = (f32[64,128]{1,0:T(8,128)S(1)}, f32[32,128]{1,0:T(8,128)S(1)}, f32[8,128]{1,0:T(8,128)S(1)}) custom-call(s32[1]{0:T(128)} %bitcast.box, s32[1,8]{1,0:T(1,128)S(1)} %copy-done.9, f32[160,128]{1,0:T(8,128)S(1)} %pad_maximum_fusion.refs_0_, f32[160,128]{1,0:T(8,128)S(1)} %collective-permute-done.3.refs_1_, ...), custom_call_target="tpu_custom_call" | custom-call | tf_op jit(solution)/shard_map/pallas_call | solution.py:38
  34.1 1.5 %collective-permute-start.10 = (f32[64,128]{1,0:T(8,128)S(1)}, f32[64,128]{1,0:T(8,128)S(1)}, u32[]{:S(2)}, u32[]{:S(2)}) collective-permute-start(f32[64,128]{1,0:T(8,128)S(1)} %get-tuple-element.26.refs_0_.refs_5_), channel_id=1, source_target_pairs={{0,2},{1,3},{2,0},{3,1},{4,6},{5,7},{6,4},{7,5},{8,10},{9,11},{10,... | collective-permute-start | bytes 98312 | tf_op jit(solution)/shard_map/ppermute | solution.py:23
  35.6 0.6 %collective-permute-start.9 = (f32[64,128]{1,0:T(8,128)S(1)}, f32[64,128]{1,0:T(8,128)S(1)}, u32[]{:S(2)}, u32[]{:S(2)}) collective-permute-start(f32[64,128]{1,0:T(8,128)S(1)} %get-tuple-element.26.refs_0_.refs_5_), channel_id=1, source_target_pairs={{0,1},{1,0},{2,3},{3,2},{4,5},{5,4},{6,7},{7,6},{8,9},{9,8},{10,11... | collective-permute-start | bytes 98312 | tf_op jit(solution)/shard_map/ppermute | solution.py:23
  36.2 1.8 %collective-permute-done.10.refs_2_ = f32[64,128]{1,0:T(8,128)S(1)} collective-permute-done((f32[64,128]{1,0:T(8,128)S(1)}, f32[64,128]{1,0:T(8,128)S(1)}, u32[]{:S(2)}, u32[]{:S(2)}) %collective-permute-start.10) | collective-permute-done | bytes 32800 | tf_op jit(solution)/shard_map/ppermute | solution.py:23
  38.0 1.2 %collective-permute-done.11.refs_3_ = f32[64,128]{1,0:T(8,128)S(1)} collective-permute-done((f32[64,128]{1,0:T(8,128)S(1)}, f32[64,128]{1,0:T(8,128)S(1)}, u32[]{:S(2)}, u32[]{:S(2)}) %collective-permute-start.11) | collective-permute-done | bytes 32800 | tf_op jit(solution)/shard_map/ppermute | solution.py:23
  39.3 3.2 %shard_map.126 = (f32[32,128]{1,0:T(8,128)S(1)}, f32[32,128]{1,0:T(8,128)S(1)}) custom-call(s32[1]{0:T(128)} %bitcast.box, s32[1]{0:T(128)S(6)} %copy.13.counts, f32[64,128]{1,0:T(8,128)S(1)} %get-tuple-element.26.refs_0_.refs_5_, f32[64,128]{1,0:T(8,128)S(1)} %collective-permute-done.9.refs_1_, f32[64,128]{1,0:T(8,128)S(1)} %collective-permute-done.10.refs_2_, ...), custom_call_target="tpu_custom_call" | custom-call | tf_op jit(solution)/shard_map/pallas_call | solution.py:38
  42.5 11.3 %all_to_all.11 = f32[16,2,128]{2,1,0:T(2,128)S(1)} all-to-all(f32[16,2,128]{2,1,0:T(2,128)S(1)} %bitcast.9), channel_id=1, replica_groups=mesh['groups'=2,'patch'=4,'sub'=4] {'patch','sub'}, dimensions={0} | all-to-all | bytes 32768 | tf_op jit(solution)/shard_map/all_to_all | solution.py:535
  53.8 2.9 %shard_map.127 = (f32[32,128]{1,0:T(8,128)}, f32[2,3]{1,0:T(2,128)}) custom-call(s32[1]{0:T(128)} %bitcast.box, f32[160,128]{1,0:T(8,128)S(1)} %pad_maximum_fusion.refs_0_, f32[160,128]{1,0:T(8,128)S(1)} %collective-permute-done.3.refs_1_, f32[160,128]{1,0:T(8,128)S(1)} %collective-permute-done.4.refs_2_, f32[160,128]{1,0:T(8,128)S(1)} %collective-permute-done.5.refs_3_, ...), custom_call_target="tpu_custom_call" | custom-call | tf_op jit(solution)/shard_map/pallas_call | solution.py:38
  (27 shorter events, 0.1 us)
Async XLA Ops:
  2.2 0.7 %copy-start.8 = (s32[1,8]{1,0:T(1,128)S(1)}, s32[1,8]{1,0:T(1,128)}, u32[]{:S(2)}) copy-start(s32[1,8]{1,0:T(1,128)} %box_far.3) | copy-start | bytes 100
  8.0 7.1 %copy-start = (f32[72,128]{1,0:T(8,128)}, f32[72,128]{1,0:T(8,128)S(1)}, u32[]{:S(2)}) copy-start(f32[72,128]{1,0:T(8,128)S(1)} %get-tuple-element.19.refs_4_) | copy-start | bytes 110596
  8.0 7.1 %collective-permute-start = (f32[72,128]{1,0:T(8,128)S(1)}, f32[72,128]{1,0:T(8,128)S(1)}, u32[]{:S(2)}, u32[]{:S(2)}) collective-permute-start(f32[72,128]{1,0:T(8,128)S(1)} %get-tuple-element.19.refs_4_), channel_id=1, source_target_pairs={{0,1},{1,0},{2,3},{3,2},{4,5},{5,4},{6,7},{7,6},{8,9},{9,8},{10,11... | collective-permute-start | bytes 110600 | tf_op jit(solution)/shard_map/ppermute | solution.py:23
  8.6 6.6 %collective-permute-start.1 = (f32[72,128]{1,0:T(8,128)S(1)}, f32[72,128]{1,0:T(8,128)S(1)}, u32[]{:S(2)}, u32[]{:S(2)}) collective-permute-start(f32[72,128]{1,0:T(8,128)S(1)} %get-tuple-element.19.refs_4_), channel_id=1, source_target_pairs={{0,2},{1,3},{2,0},{3,1},{4,6},{5,7},{6,4},{7,5},{8,10},{9,11},{10,... | collective-permute-start | bytes 110600 | tf_op jit(solution)/shard_map/ppermute | solution.py:23
  11.1 4.0 %collective-permute-start.2 = (f32[72,128]{1,0:T(8,128)S(1)}, f32[72,128]{1,0:T(8,128)S(1)}, u32[]{:S(2)}, u32[]{:S(2)}) collective-permute-start(f32[72,128]{1,0:T(8,128)S(1)} %get-tuple-element.19.refs_4_), channel_id=1, source_target_pairs={{0,3},{1,2},{2,1},{3,0},{4,7},{5,6},{6,5},{7,4},{8,11},{9,10},{10,... | collective-permute-start | bytes 110600 | tf_op jit(solution)/shard_map/ppermute | solution.py:23
  11.2 8.8 %collective-permute-start.6 = (f32[32,8,128]{2,1,0:T(8,128)S(1)}, f32[32,8,128]{2,1,0:T(8,128)S(1)}, u32[]{:S(2)}, u32[]{:S(2)}) collective-permute-start(f32[32,8,128]{2,1,0:T(8,128)S(1)} %get-tuple-element.20.refs_0_), channel_id=1, source_target_pairs={{0,1},{1,0},{2,3},{3,2},{4,5},{5,4},{6,7},{7,6},{8,9},{9,8},{10,11... | collective-permute-start | bytes 393224 | tf_op jit(solution)/shard_map/ppermute | solution.py:23
  11.3 9.7 %collective-permute-start.7 = (f32[32,8,128]{2,1,0:T(8,128)S(1)}, f32[32,8,128]{2,1,0:T(8,128)S(1)}, u32[]{:S(2)}, u32[]{:S(2)}) collective-permute-start(f32[32,8,128]{2,1,0:T(8,128)S(1)} %get-tuple-element.20.refs_0_), channel_id=1, source_target_pairs={{0,2},{1,3},{2,0},{3,1},{4,6},{5,7},{6,4},{7,5},{8,10},{9,11},{10,... | collective-permute-start | bytes 393224 | tf_op jit(solution)/shard_map/ppermute | solution.py:23
  15.1 0.6 %copy-start.2 = (f32[72,128]{1,0:T(8,128)}, f32[72,128]{1,0:T(8,128)S(1)}, u32[]{:S(2)}) copy-start(f32[72,128]{1,0:T(8,128)S(1)} %collective-permute-done.refs_5_) | copy-start | bytes 110596
  15.1 6.0 %collective-permute-start.8 = (f32[32,8,128]{2,1,0:T(8,128)S(1)}, f32[32,8,128]{2,1,0:T(8,128)S(1)}, u32[]{:S(2)}, u32[]{:S(2)}) collective-permute-start(f32[32,8,128]{2,1,0:T(8,128)S(1)} %get-tuple-element.20.refs_0_), channel_id=1, source_target_pairs={{0,3},{1,2},{2,1},{3,0},{4,7},{5,6},{6,5},{7,4},{8,11},{9,10},{10,... | collective-permute-start | bytes 393224 | tf_op jit(solution)/shard_map/ppermute | solution.py:23
  15.1 0.6 %copy-start.4 = (f32[72,128]{1,0:T(8,128)}, f32[72,128]{1,0:T(8,128)S(1)}, u32[]{:S(2)}) copy-start(f32[72,128]{1,0:T(8,128)S(1)} %collective-permute-done.1.refs_6_) | copy-start | bytes 110596
  15.8 4.3 %copy-start.6 = (f32[72,128]{1,0:T(8,128)}, f32[72,128]{1,0:T(8,128)S(1)}, u32[]{:S(2)}) copy-start(f32[72,128]{1,0:T(8,128)S(1)} %collective-permute-done.2.refs_7_) | copy-start | bytes 110596
  15.8 16.5 %collective-permute-start.3 = (f32[160,128]{1,0:T(8,128)S(1)}, f32[160,128]{1,0:T(8,128)S(1)}, u32[]{:S(2)}, u32[]{:S(2)}) collective-permute-start(f32[160,128]{1,0:T(8,128)S(1)} %pad_maximum_fusion.refs_0_), channel_id=1, source_target_pairs={{0,4},{4,0},{8,12},{12,8},{1,5},{5,1},{9,13},{13,9},{2,6},{6,2},{1... | collective-permute-start | bytes 245768 | tf_op jit(solution)/shard_map/ppermute | solution.py:23
  17.4 14.8 %collective-permute-start.4 = (f32[160,128]{1,0:T(8,128)S(1)}, f32[160,128]{1,0:T(8,128)S(1)}, u32[]{:S(2)}, u32[]{:S(2)}) collective-permute-start(f32[160,128]{1,0:T(8,128)S(1)} %pad_maximum_fusion.refs_0_), channel_id=1, source_target_pairs={{0,8},{4,12},{8,0},{12,4},{1,9},{5,13},{9,1},{13,5},{2,10},{6,14},... | collective-permute-start | bytes 245768 | tf_op jit(solution)/shard_map/ppermute | solution.py:23
  20.0 12.3 %collective-permute-start.5 = (f32[160,128]{1,0:T(8,128)S(1)}, f32[160,128]{1,0:T(8,128)S(1)}, u32[]{:S(2)}, u32[]{:S(2)}) collective-permute-start(f32[160,128]{1,0:T(8,128)S(1)} %pad_maximum_fusion.refs_0_), channel_id=1, source_target_pairs={{0,12},{4,8},{8,4},{12,0},{1,13},{5,9},{9,5},{13,1},{2,14},{6,10},... | collective-permute-start | bytes 245768 | tf_op jit(solution)/shard_map/ppermute | solution.py:23
  21.1 0.8 %copy-start.1 = (f32[72,128]{1,0:T(8,128)S(1)}, f32[72,128]{1,0:T(8,128)}, u32[]{:S(2)}) copy-start(f32[72,128]{1,0:T(8,128)} %copy-done) | copy-start | bytes 110596
  21.9 0.8 %copy-start.3 = (f32[72,128]{1,0:T(8,128)S(1)}, f32[72,128]{1,0:T(8,128)}, u32[]{:S(2)}) copy-start(f32[72,128]{1,0:T(8,128)} %copy-done.2) | copy-start | bytes 110596
  22.6 0.8 %copy-start.5 = (f32[72,128]{1,0:T(8,128)S(1)}, f32[72,128]{1,0:T(8,128)}, u32[]{:S(2)}) copy-start(f32[72,128]{1,0:T(8,128)} %copy-done.4) | copy-start | bytes 110596
  23.4 0.8 %copy-start.7 = (f32[72,128]{1,0:T(8,128)S(1)}, f32[72,128]{1,0:T(8,128)}, u32[]{:S(2)}) copy-start(f32[72,128]{1,0:T(8,128)} %copy-done.6) | copy-start | bytes 110596
  32.3 0.7 %copy-start.9 = (s32[1,8]{1,0:T(1,128)S(1)}, s32[1,8]{1,0:T(1,128)}, u32[]{:S(2)}) copy-start(s32[1,8]{1,0:T(1,128)} %box_far.3) | copy-start | bytes 100
  34.1 4.0 %collective-permute-start.10 = (f32[64,128]{1,0:T(8,128)S(1)}, f32[64,128]{1,0:T(8,128)S(1)}, u32[]{:S(2)}, u32[]{:S(2)}) collective-permute-start(f32[64,128]{1,0:T(8,128)S(1)} %get-tuple-element.26.refs_0_.refs_5_), channel_id=1, source_target_pairs={{0,2},{1,3},{2,0},{3,1},{4,6},{5,7},{6,4},{7,5},{8,10},{9,11},{10,... | collective-permute-start | bytes 98312 | tf_op jit(solution)/shard_map/ppermute | solution.py:23
  35.6 3.7 %collective-permute-start.11 = (f32[64,128]{1,0:T(8,128)S(1)}, f32[64,128]{1,0:T(8,128)S(1)}, u32[]{:S(2)}, u32[]{:S(2)}) collective-permute-start(f32[64,128]{1,0:T(8,128)S(1)} %get-tuple-element.26.refs_0_.refs_5_), channel_id=1, source_target_pairs={{0,3},{1,2},{2,1},{3,0},{4,7},{5,6},{6,5},{7,4},{8,11},{9,10},{10,... | collective-permute-start | bytes 98312 | tf_op jit(solution)/shard_map/ppermute | solution.py:23
  35.6 3.7 %collective-permute-start.9 = (f32[64,128]{1,0:T(8,128)S(1)}, f32[64,128]{1,0:T(8,128)S(1)}, u32[]{:S(2)}, u32[]{:S(2)}) collective-permute-start(f32[64,128]{1,0:T(8,128)S(1)} %get-tuple-element.26.refs_0_.refs_5_), channel_id=1, source_target_pairs={{0,1},{1,0},{2,3},{3,2},{4,5},{5,4},{6,7},{7,6},{8,9},{9,8},{10,11... | collective-permute-start | bytes 98312 | tf_op jit(solution)/shard_map/ppermute | solution.py:23

commit v6 on v5

--- a/solution.py
+++ b/solution.py
@@ -87,19 +87,6 @@
     return copies
 
 
-def start_kernel(counts, points, normals, density, geometry, initial, at, arrived):
-    dims, slots, width = points.shape
-    targets = [at.at[0:dims], at.at[dims : 2 * dims], at.at[2 * dims]]
-    for copy in copy_all(zip((points, normals, density), targets), arrived):
-        copy.wait()
-    for row in range(2 * dims):
-        geometry[:, row, :] = at[row]
-    vector = jnp.where(iota((slots, width), 0) < counts[0], at[2 * dims], 0.0)
-    initial[...] = vector
-    geometry[:, 2 * dims, :] = vector
-    geometry[:, 2 * dims + 1, :] = jnp.zeros_like(vector)
-
-
 def write_moments(vector, basis, message, start):
     slots, rank, _ = basis.shape
     lane = iota((rank, LANES), 1)
@@ -141,18 +128,30 @@
     )
 
 
-def basis_kernel(counts, box_far, initial, *refs):
-    sources, message, box_basis, (basis, leaf_coupling, box_coupling) = (
-        refs[:4],
-        refs[4],
-        refs[5],
-        refs[6:9],
-    )
-    transfer, arrived = refs[9:]
-    slots, rank, _ = basis.shape
-    targets = (basis, transfer, leaf_coupling, box_coupling)
+def start_kernel(counts, box_far, *refs):
+    sources, (geometry, initial, message, box_basis) = refs[:7], refs[7:11]
+    basis, leaf_coupling, box_coupling = refs[11:14]
+    at, transfer, arrived = refs[14:]
+    dims, slots, width = sources[0].shape
+    rank = basis.shape[1]
+    targets = [at.at[0:dims], at.at[dims : 2 * dims], at.at[2 * dims]]
+    targets += [transfer, basis, leaf_coupling, box_coupling]
     copies = copy_all(zip(sources, targets), arrived)
-    for copy in copies:
+    for copy in copies[:3]:
+        copy.wait()
+    for row in range(2 * dims):
+        geometry[:, row, :] = at[row]
+    vector = jnp.where(iota((slots, width), 0) < counts[0], at[2 * dims], 0.0)
+    initial[...] = vector
+    geometry[:, 2 * dims, :] = vector
+    geometry[:, 2 * dims + 1, :] = jnp.zeros_like(vector)
+    entries = [jnp.sum(vector * vector, keepdims=True)] + [
+        jnp.full((1, 1), value, jnp.int32).astype(jnp.float32)
+        for value in [counts[0]] + [box_far[place] for place in range(box_far.shape[0])]
+    ]
+    message[slots : slots + TILE_ROWS, :] = jnp.zeros((TILE_ROWS, LANES), jnp.float32)
+    message[slots + 1 : slots + 2, :] = lane_row(entries)
+    for copy in copies[3:]:
         copy.wait()
     gram = jnp.zeros((rank, rank), jnp.float32)
     for leaf in range(slots):
@@ -166,14 +165,7 @@
         box_basis[leaf] = product
         gram = gram + six_products(product, product, ((1,), (1,)))
     write_moments(initial, basis, message, 0)
-    vector = initial[...]
-    entries = [jnp.sum(vector * vector, keepdims=True)] + [
-        jnp.full((1, 1), value, jnp.int32).astype(jnp.float32)
-        for value in [counts[0]] + [box_far[0, place] for place in range(box_far.shape[1])]
-    ]
-    message[slots : slots + TILE_ROWS, :] = jnp.zeros((TILE_ROWS, LANES), jnp.float32)
     message[slots : slots + 1, :] = box_moments(initial, box_basis)
-    message[slots + 1 : slots + 2, :] = lane_row(entries)
     start, half = slots + TILE_ROWS, rank // 2
     message[start : start + half, 0:rank] = gram[0:half]
     message[start : start + half, rank : 2 * rank] = gram[half:rank]
@@ -212,10 +204,9 @@
 
 def first_near_kernel(subs, box, counts, *refs):
     geometry, messages = refs[:subs], refs[subs : 2 * subs]
-    picks, coupling, basis, near_source, near, values = refs[2 * subs : 2 * subs + 6]
-    features, squares, fields, inner, near_list, arrived = refs[2 * subs + 6 :]
-    copy = pltpu.make_async_copy(near_source, near_list, arrived)
-    copy.start()
+    coupling, basis, near_source, far_source, near, values, picks = refs[2 * subs : 2 * subs + 7]
+    features, squares, fields, inner, near_list, far_list, arrived = refs[2 * subs + 7 :]
+    copies = copy_all([(near_source, near_list), (far_source, far_list)], arrived)
     slots, height, width = geometry[0].shape
     neighbours = near_list.shape[0]
     rank = coupling.shape[1]
@@ -268,7 +259,17 @@
         near[pl.ds(leaf, 1), :] = jnp.sum(total.T, axis=0, keepdims=True)
         return carry
 
-    copy.wait()
+    for copy in copies:
+        copy.wait()
+    far_count, sources = far_list.shape[0], subs * slots
+    far_rows = far_list[...].astype(jnp.float32)
+    far_rows = jnp.concatenate(
+        [far_rows, jnp.zeros((far_count, LANES - slots), jnp.float32)], axis=1
+    ).T
+    leaves = (iota((slots, sources), 1) ^ (box[0] * slots)).astype(jnp.float32)
+    for place in range(far_count):
+        chosen = jnp.where(far_rows[0:slots, place : place + 1] == leaves, 1.0, 0.0)
+        picks[place * slots : (place + 1) * slots, :] = chosen.astype(jnp.bfloat16)
     lax.fori_loop(0, slots, target, 0, unroll=True)
     moments = [ref[0:slots, 0:rank] for ref in messages]
     add_leaf_far(counts, moments, picks, coupling, basis, near)
@@ -291,7 +292,7 @@
         gather[place * height : (place + 1) * height, :] = ref[...]
     coupled = jnp.zeros((rank, rank), jnp.float32)
     for place in range(box_coupling.shape[0]):
-        row = (box_far[0, place] ^ box[0]) * span
+        row = (box_far[place] ^ box[0]) * span
         coupled = coupled + box_coupling[place] * gather[pl.ds(row, 1), 0:rank]
     image[...] = part[...]
     box_images(box_basis, jnp.sum(coupled, axis=1, keepdims=True), image)
@@ -461,28 +462,19 @@
     rows = f32(slots, width)
     this_box = lax.axis_index("patch") * subs + lax.axis_index("sub")
     box = this_box.astype(jnp.int32).reshape(1)
-    patch_start = lax.axis_index("patch") * sources
-    leaves = (jnp.arange(sources) + patch_start) ^ (lax.axis_index("sub") * slots)
-    picks = (leaf_far.T.reshape(far_count * slots, 1) == leaves[None, :]).astype(jnp.bfloat16)
-
+    box_far = box_far.reshape(-1)
+    far_list = leaf_far.T
     rank = leaf_basis.shape[1]
     span = TILE_ROWS + rank // 2
     near_list = near_list.T
     list_scratch = [pltpu.SMEM(near_list.shape, jnp.int32), pltpu.SemaphoreType.DMA]
     block = pltpu.VMEM((sources, width), jnp.float32)
 
-    geometry, initial = device_call(
+    geometry, initial, message, box_basis, *matrices = device_call(
         start_kernel,
-        [f32(slots, 8, width), rows],
-        [counts],
-        [],
-        [pltpu.VMEM((7, slots, width), jnp.float32), pltpu.SemaphoreType.DMA((3,))],
-        [points.transpose(1, 0, 2), normals.transpose(1, 0, 2), density],
-    )
-    geometry = from_peers(geometry, "sub")
-    message, box_basis, leaf_basis, leaf_coupling, box_coupling = device_call(
-        basis_kernel,
-        [
+        [
+            f32(slots, 8, width),
+            rows,
             f32(slots + span, LANES),
             kept(leaf_basis),
             kept(leaf_basis),
@@ -490,31 +482,48 @@
             kept(box_coupling),
         ],
         [counts, box_far],
-        [initial],
-        [
+        [],
+        [
+            pltpu.VMEM((7, slots, width), jnp.float32),
             pltpu.VMEM(leaf_to_box_transfer.shape, jnp.float32),
-            pltpu.SemaphoreType.DMA((4,)),
+            pltpu.SemaphoreType.DMA((7,)),
         ],
-        [leaf_basis, leaf_to_box_transfer, leaf_coupling, box_coupling],
-    )
+        [
+            points.transpose(1, 0, 2),
+            normals.transpose(1, 0, 2),
+            density,
+            leaf_to_box_transfer,
+            leaf_basis,
+            leaf_coupling,
+            box_coupling,
+        ],
+    )
+    leaf_basis, leaf_coupling, box_coupling = matrices
+    geometry = from_peers(geometry, "sub")
     messages = from_peers(message, "sub")
     boxes = from_peers(
         jnp.concatenate([part[slots : slots + span] for part in messages], axis=0), "patch"
     )
     gather = pltpu.VMEM((patches * subs * span, LANES), jnp.float32)
-    part, values = device_call(
+    part, values, picks = device_call(
         functools.partial(first_near_kernel, subs),
-        [rows, pltpu.VMEM((slots * neighbours, width, width), jnp.float32)],
+        [
+            rows,
+            pltpu.VMEM((slots * neighbours, width, width), jnp.float32),
+            pltpu.VMEM((far_count * slots, sources), jnp.bfloat16),
+        ],
         [box, counts],
-        [*geometry, *messages, picks, leaf_coupling, leaf_basis],
+        [*geometry, *messages, leaf_coupling, leaf_basis],
         [
             pltpu.VMEM((sources, 32, 2 * width), jnp.bfloat16),
             block,
             block,
             pltpu.VMEM((slots, width), jnp.float32),
-            *list_scratch,
+            pltpu.SMEM(near_list.shape, jnp.int32),
+            pltpu.VMEM(far_list.shape, jnp.int32),
+            pltpu.SemaphoreType.DMA((2,)),
         ],
-        [near_list],
+        [near_list, far_list],
     )
     message, basis_one, numbers = device_call(
         functools.partial(first_image_kernel, patches, span),

time: 57.3 us -> 54.7 us (0.955)
  local copies, waits for them, and re-layouts: 6.29 us -> 4.77 us
  other arithmetic: 1.31 us -> 0.01 us
  waiting for transfers between devices: 3.04 us -> 4.04 us
  Pallas kernels: 21.4 us -> 20.7 us
    eq x1 -> x0, local copies, waits for them, and re-layouts: 1.33 us -> none  [shards(): leaf_far.T.reshape(far_count * slots, 1) == leaves[None, :]]
    ppermute x12, waiting for transfers between devices: 3.04 us -> 4.04 us  [from_peers(): lax.ppermute(value, axis, [(i, i ^ turn) for i in range(size)])]
    convert_element_type x1 -> x0, other arithmetic: 0.79 us -> none  [shards(): (leaf_far.T.reshape(far_count * slots, 1) == leaves[None, :]).astype(jnp....]
    pallas_call x6 -> x5, Pallas kernels: 21.4 us -> 20.7 us  [device_call(): pl.pallas_call(kernel, out_shape=tuple(outputs), in_specs=[smem] * len(sc...]
    unnamed x20 -> x16, local copies, waits for them, and re-layouts: 4.95 us -> 4.76 us
  transfers between devices with their start and end apart: 12 -> 12, of which waited for: 2 -> 4; matrix products, arithmetic and copies ran while one was open for 5% -> 0% of each run, Pallas kernels for 14% -> 15%
where the time goes in v6:
time: 54.7 us; the launch traced here: 54.3 us
  Pallas kernels  20.7 us (38%)
  starting transfers between devices  11.7 us (21%)
  blocking collectives  11.7 us (21%)
  local copies, waits for them, and re-layouts  4.77 us (9%)
  waiting for transfers between devices  4.04 us (7%)
  between operations  1.41 us (3%)
    pallas_call x5, Pallas kernels, device_call(): pl.pallas_call(kernel, out_shape=tuple(outputs), in_specs=[smem] * len(sc...  20.7 us
    all_to_all x1, blocking collectives, shards(): shares = lax.all_to_all(shares, ('patch', 'sub'), 0, 0, tiled=True)  11.7 us
    ppermute x12, starting transfers between devices, from_peers(): lax.ppermute(value, axis, [(i, i ^ turn) for i in range(size)])  11.7 us
    unnamed x16, local copies, waits for them, and re-layouts  4.76 us
    ppermute x12, waiting for transfers between devices, from_peers(): lax.ppermute(value, axis, [(i, i ^ turn) for i in range(size)])  4.04 us
  transfers between devices with their start and end apart: 12, of which 4 were waited for; matrix products, arithmetic and copies ran while one was open for 0% of the time, Pallas kernels for 15%

profile of v6, /device:TPU:0, one launch (start us, length us, event | category | flops | bytes accessed | tf_op | source)
XLA Modules:
  0.0 54.3 jit_solution(861680533700469498)
XLA Ops:
  1.3 0.0 copy-start.6
  1.3 0.6 %copy-done.6 = s32[1,8]{1,0:T(1,128)S(1)} copy-done((s32[1,8]{1,0:T(1,128)S(1)}, s32[1,8]{1,0:T(1,128)}, u32[]{:S(2)}) %copy-start.6) | copy-done | bytes 56
  1.9 5.3 %shard_map.122 = (f32[32,8,128]{2,1,0:T(8,128)S(1)}, f32[32,128]{1,0:T(8,128)S(1)}, f32[72,128]{1,0:T(8,128)S(1)}, f32[32,64,128]{2,1,0:T(8,128)S(1)}, f32[32,64...) custom-call(s32[1]{0:T(128)S(6)} %copy.13.counts, s32[8]{0:T(128)S(1)} %bitcast.11, ...), custom_call_target="tpu_custom_call" | custom-call | tf_op jit(solution)/shard_map/pallas_call | solution.py:38
  7.2 0.0 copy-start.4
  7.2 0.6 %copy-done.4 = f32[32,128]{1,0:T(8,128)} copy-done((f32[32,128]{1,0:T(8,128)}, f32[32,128]{1,0:T(8,128)S(1)}, u32[]{:S(2)}) %copy-start.4) | copy-done | bytes 16408
  7.8 0.5 collective-permute-start
  8.3 2.5 %collective-permute-start.1 = (f32[72,128]{1,0:T(8,128)S(1)}, f32[72,128]{1,0:T(8,128)S(1)}, u32[]{:S(2)}, u32[]{:S(2)}) collective-permute-start(f32[72,128]{1,0:T(8,128)S(1)} %get-tuple-element.19.refs_4_), channel_id=1, source_target_pairs={{0,2},{1,3},{2,0},{3,1},{4,6},{5,7},{6,4},{7,5},{8,10},{9,11},{10,... | collective-permute-start | bytes 110600 | tf_op jit(solution)/shard_map/ppermute | solution.py:23
  10.7 0.1 collective-permute-start.2
  10.9 0.1 collective-permute-start.6
  11.0 1.9 %collective-permute-start.7 = (f32[32,8,128]{2,1,0:T(8,128)S(1)}, f32[32,8,128]{2,1,0:T(8,128)S(1)}, u32[]{:S(2)}, u32[]{:S(2)}) collective-permute-start(f32[32,8,128]{2,1,0:T(8,128)S(1)} %get-tuple-element.20.refs_0_), channel_id=1, source_target_pairs={{0,2},{1,3},{2,0},{3,1},{4,6},{5,7},{6,4},{7,5},{8,10},{9,11},{10,... | collective-permute-start | bytes 393224 | tf_op jit(solution)/shard_map/ppermute | solution.py:23
  12.9 0.0 collective-permute-done.1.refs_6_
  13.0 1.2 %collective-permute-done.2.refs_7_ = f32[72,128]{1,0:T(8,128)S(1)} collective-permute-done((f32[72,128]{1,0:T(8,128)S(1)}, f32[72,128]{1,0:T(8,128)S(1)}, u32[]{:S(2)}, u32[]{:S(2)}) %collective-permute-start.2) | collective-permute-done | bytes 36896 | tf_op jit(solution)/shard_map/ppermute | solution.py:23
  14.1 0.6 %copy-done.2 = f32[72,128]{1,0:T(8,128)} copy-done((f32[72,128]{1,0:T(8,128)}, f32[72,128]{1,0:T(8,128)S(1)}, u32[]{:S(2)}) %copy-start.2) | copy-done | bytes 36888
  14.8 1.6 %collective-permute-start.3 = (f32[160,128]{1,0:T(8,128)S(1)}, f32[160,128]{1,0:T(8,128)S(1)}, u32[]{:S(2)}, u32[]{:S(2)}) collective-permute-start(f32[160,128]{1,0:T(8,128)S(1)} %pad_maximum_fusion.refs_0_), channel_id=1, source_target_pairs={{0,4},{4,0},{8,12},{12,8},{1,5},{5,1},{9,13},{13,9},{2,6},{6,2},{1... | collective-permute-start | bytes 245768 | tf_op jit(solution)/shard_map/ppermute | solution.py:23
  16.3 2.6 %collective-permute-start.4 = (f32[160,128]{1,0:T(8,128)S(1)}, f32[160,128]{1,0:T(8,128)S(1)}, u32[]{:S(2)}, u32[]{:S(2)}) collective-permute-start(f32[160,128]{1,0:T(8,128)S(1)} %pad_maximum_fusion.refs_0_), channel_id=1, source_target_pairs={{0,8},{4,12},{8,0},{12,4},{1,9},{5,13},{9,1},{13,5},{2,10},{6,14},... | collective-permute-start | bytes 245768 | tf_op jit(solution)/shard_map/ppermute | solution.py:23
  18.9 0.2 collective-permute-start.5
  19.1 0.7 %collective-permute-done.8.refs_3_ = f32[32,8,128]{2,1,0:T(8,128)S(1)} collective-permute-done((f32[32,8,128]{2,1,0:T(8,128)S(1)}, f32[32,8,128]{2,1,0:T(8,128)S(1)}, u32[]{:S(2)}, u32[]{:S(2)}) %collective-permute-start.8) | collective-permute-done | bytes 131104 | tf_op jit(solution)/shard_map/ppermute | solution.py:23
  19.8 0.8 %copy-done.1 = f32[72,128]{1,0:T(8,128)S(1)} copy-done((f32[72,128]{1,0:T(8,128)S(1)}, f32[72,128]{1,0:T(8,128)}, u32[]{:S(2)}) %copy-start.1) | copy-done | bytes 36888
  20.6 0.8 %copy-done.3 = f32[72,128]{1,0:T(8,128)S(1)} copy-done((f32[72,128]{1,0:T(8,128)S(1)}, f32[72,128]{1,0:T(8,128)}, u32[]{:S(2)}) %copy-start.3) | copy-done | bytes 36888
  21.4 8.1 %shard_map.123 = (f32[32,128]{1,0:T(8,128)S(1)}, f32[288,128,128]{2,1,0:T(8,128)S(1)}, bf16[256,128]{1,0:T(8,128)(2,1)S(1)}) custom-call(s32[1]{0:T(128)} %bitcast.box, s32[1]{0:T(128)S(6)} %copy.13.counts, f32[32,8,128]{2,1,0:T(8,128)S(1)} %get-tuple-element.20.refs_0_, f32[32,8,128]{2,1,0:T(8,128)S(1)} %collective-permute-done.6.refs_1_, ...), custom_call_target="tpu_custom_call" | custom-call | tf_op jit(solution)/shard_map/pallas_call | solution.py:38
  29.5 0.0 copy-start.5
  29.6 0.7 %copy-done.5 = f32[32,128]{1,0:T(8,128)S(1)} copy-done((f32[32,128]{1,0:T(8,128)S(1)}, f32[32,128]{1,0:T(8,128)}, u32[]{:S(2)}) %copy-start.5) | copy-done | bytes 16408
  30.3 0.7 %copy-done.7 = s32[1,8]{1,0:T(1,128)S(1)} copy-done((s32[1,8]{1,0:T(1,128)S(1)}, s32[1,8]{1,0:T(1,128)}, u32[]{:S(2)}) %copy-start.7) | copy-done | bytes 56
  30.9 1.1 %shard_map.124 = (f32[64,128]{1,0:T(8,128)S(1)}, f32[32,128]{1,0:T(8,128)S(1)}, f32[8,128]{1,0:T(8,128)S(1)}) custom-call(s32[1]{0:T(128)} %bitcast.box, s32[8]{0:T(128)S(1)} %bitcast.12, f32[160,128]{1,0:T(8,128)S(1)} %pad_maximum_fusion.refs_0_, f32[160,128]{1,0:T(8,128)S(1)} %collective-permute-done.3.refs_1_, ...), custom_call_target="tpu_custom_call" | custom-call | tf_op jit(solution)/shard_map/pallas_call | solution.py:38
  32.0 0.9 %collective-permute-start.10 = (f32[64,128]{1,0:T(8,128)S(1)}, f32[64,128]{1,0:T(8,128)S(1)}, u32[]{:S(2)}, u32[]{:S(2)}) collective-permute-start(f32[64,128]{1,0:T(8,128)S(1)} %get-tuple-element.27.refs_0_.refs_5_), channel_id=1, source_target_pairs={{0,2},{1,3},{2,0},{3,1},{4,6},{5,7},{6,4},{7,5},{8,10},{9,11},{10,... | collective-permute-start | bytes 98312 | tf_op jit(solution)/shard_map/ppermute | solution.py:23
  32.9 0.6 %collective-permute-start.11 = (f32[64,128]{1,0:T(8,128)S(1)}, f32[64,128]{1,0:T(8,128)S(1)}, u32[]{:S(2)}, u32[]{:S(2)}) collective-permute-start(f32[64,128]{1,0:T(8,128)S(1)} %get-tuple-element.27.refs_0_.refs_5_), channel_id=1, source_target_pairs={{0,3},{1,2},{2,1},{3,0},{4,7},{5,6},{6,5},{7,4},{8,11},{9,10},{10,... | collective-permute-start | bytes 98312 | tf_op jit(solution)/shard_map/ppermute | solution.py:23
  33.6 0.6 %collective-permute-start.9 = (f32[64,128]{1,0:T(8,128)S(1)}, f32[64,128]{1,0:T(8,128)S(1)}, u32[]{:S(2)}, u32[]{:S(2)}) collective-permute-start(f32[64,128]{1,0:T(8,128)S(1)} %get-tuple-element.27.refs_0_.refs_5_), channel_id=1, source_target_pairs={{0,1},{1,0},{2,3},{3,2},{4,5},{5,4},{6,7},{7,6},{8,9},{9,8},{10,11... | collective-permute-start | bytes 98312 | tf_op jit(solution)/shard_map/ppermute | solution.py:23
  34.2 1.8 %collective-permute-done.10.refs_2_ = f32[64,128]{1,0:T(8,128)S(1)} collective-permute-done((f32[64,128]{1,0:T(8,128)S(1)}, f32[64,128]{1,0:T(8,128)S(1)}, u32[]{:S(2)}, u32[]{:S(2)}) %collective-permute-start.10) | collective-permute-done | bytes 32800 | tf_op jit(solution)/shard_map/ppermute | solution.py:23
  36.1 0.3 collective-permute-done.11.refs_3_
  36.4 3.3 %shard_map.125 = (f32[32,128]{1,0:T(8,128)S(1)}, f32[32,128]{1,0:T(8,128)S(1)}) custom-call(s32[1]{0:T(128)} %bitcast.box, s32[1]{0:T(128)S(6)} %copy.13.counts, f32[64,128]{1,0:T(8,128)S(1)} %get-tuple-element.27.refs_0_.refs_5_, f32[64,128]{1,0:T(8,128)S(1)} %collective-permute-done.9.refs_1_, f32[64,128]{1,0:T(8,128)S(1)} %collective-permute-done.10.refs_2_, ...), custom_call_target="tpu_custom_call" | custom-call | tf_op jit(solution)/shard_map/pallas_call | solution.py:38
  39.7 11.7 %all_to_all.11 = f32[16,2,128]{2,1,0:T(2,128)S(1)} all-to-all(f32[16,2,128]{2,1,0:T(2,128)S(1)} %bitcast.10), channel_id=1, replica_groups=mesh['groups'=2,'patch'=4,'sub'=4] {'patch','sub'}, dimensions={0} | all-to-all | bytes 32768 | tf_op jit(solution)/shard_map/all_to_all | solution.py:544
  51.4 2.9 %shard_map.126 = (f32[32,128]{1,0:T(8,128)}, f32[2,3]{1,0:T(2,128)}) custom-call(s32[1]{0:T(128)} %bitcast.box, f32[160,128]{1,0:T(8,128)S(1)} %pad_maximum_fusion.refs_0_, f32[160,128]{1,0:T(8,128)S(1)} %collective-permute-done.3.refs_1_, f32[160,128]{1,0:T(8,128)S(1)} %collective-permute-done.4.refs_2_, f32[160,128]{1,0:T(8,128)S(1)} %collective-permute-done.5.refs_3_, ...), custom_call_target="tpu_custom_call" | custom-call | tf_op jit(solution)/shard_map/pallas_call | solution.py:38
  (19 shorter events, 0.1 us)
Async XLA Ops:
  1.3 0.7 %copy-start.6 = (s32[1,8]{1,0:T(1,128)S(1)}, s32[1,8]{1,0:T(1,128)}, u32[]{:S(2)}) copy-start(s32[1,8]{1,0:T(1,128)} %param.20) | copy-start | bytes 100
  7.2 0.6 %copy-start.4 = (f32[32,128]{1,0:T(8,128)}, f32[32,128]{1,0:T(8,128)S(1)}, u32[]{:S(2)}) copy-start(f32[32,128]{1,0:T(8,128)S(1)} %get-tuple-element.24.refs_5_) | copy-start | bytes 49156
  7.8 5.1 %collective-permute-start = (f32[72,128]{1,0:T(8,128)S(1)}, f32[72,128]{1,0:T(8,128)S(1)}, u32[]{:S(2)}, u32[]{:S(2)}) collective-permute-start(f32[72,128]{1,0:T(8,128)S(1)} %get-tuple-element.19.refs_4_), channel_id=1, source_target_pairs={{0,1},{1,0},{2,3},{3,2},{4,5},{5,4},{6,7},{7,6},{8,9},{9,8},{10,11... | collective-permute-start | bytes 110600 | tf_op jit(solution)/shard_map/ppermute | solution.py:23
  8.3 4.7 %collective-permute-start.1 = (f32[72,128]{1,0:T(8,128)S(1)}, f32[72,128]{1,0:T(8,128)S(1)}, u32[]{:S(2)}, u32[]{:S(2)}) collective-permute-start(f32[72,128]{1,0:T(8,128)S(1)} %get-tuple-element.19.refs_4_), channel_id=1, source_target_pairs={{0,2},{1,3},{2,0},{3,1},{4,6},{5,7},{6,4},{7,5},{8,10},{9,11},{10,... | collective-permute-start | bytes 110600 | tf_op jit(solution)/shard_map/ppermute | solution.py:23
  10.7 3.4 %collective-permute-start.2 = (f32[72,128]{1,0:T(8,128)S(1)}, f32[72,128]{1,0:T(8,128)S(1)}, u32[]{:S(2)}, u32[]{:S(2)}) collective-permute-start(f32[72,128]{1,0:T(8,128)S(1)} %get-tuple-element.19.refs_4_), channel_id=1, source_target_pairs={{0,3},{1,2},{2,1},{3,0},{4,7},{5,6},{6,5},{7,4},{8,11},{9,10},{10,... | collective-permute-start | bytes 110600 | tf_op jit(solution)/shard_map/ppermute | solution.py:23
  10.9 8.0 %collective-permute-start.6 = (f32[32,8,128]{2,1,0:T(8,128)S(1)}, f32[32,8,128]{2,1,0:T(8,128)S(1)}, u32[]{:S(2)}, u32[]{:S(2)}) collective-permute-start(f32[32,8,128]{2,1,0:T(8,128)S(1)} %get-tuple-element.20.refs_0_), channel_id=1, source_target_pairs={{0,1},{1,0},{2,3},{3,2},{4,5},{5,4},{6,7},{7,6},{8,9},{9,8},{10,11... | collective-permute-start | bytes 393224 | tf_op jit(solution)/shard_map/ppermute | solution.py:23
  11.0 8.2 %collective-permute-start.7 = (f32[32,8,128]{2,1,0:T(8,128)S(1)}, f32[32,8,128]{2,1,0:T(8,128)S(1)}, u32[]{:S(2)}, u32[]{:S(2)}) collective-permute-start(f32[32,8,128]{2,1,0:T(8,128)S(1)} %get-tuple-element.20.refs_0_), channel_id=1, source_target_pairs={{0,2},{1,3},{2,0},{3,1},{4,6},{5,7},{6,4},{7,5},{8,10},{9,11},{10,... | collective-permute-start | bytes 393224 | tf_op jit(solution)/shard_map/ppermute | solution.py:23
  12.9 6.9 %collective-permute-start.8 = (f32[32,8,128]{2,1,0:T(8,128)S(1)}, f32[32,8,128]{2,1,0:T(8,128)S(1)}, u32[]{:S(2)}, u32[]{:S(2)}) collective-permute-start(f32[32,8,128]{2,1,0:T(8,128)S(1)} %get-tuple-element.20.refs_0_), channel_id=1, source_target_pairs={{0,3},{1,2},{2,1},{3,0},{4,7},{5,6},{6,5},{7,4},{8,11},{9,10},{10,... | collective-permute-start | bytes 393224 | tf_op jit(solution)/shard_map/ppermute | solution.py:23
  12.9 1.2 %copy-start = (f32[72,128]{1,0:T(8,128)}, f32[72,128]{1,0:T(8,128)S(1)}, u32[]{:S(2)}) copy-start(f32[72,128]{1,0:T(8,128)S(1)} %collective-permute-done.1.refs_6_) | copy-start | bytes 110596
  14.1 0.6 %copy-start.2 = (f32[72,128]{1,0:T(8,128)}, f32[72,128]{1,0:T(8,128)S(1)}, u32[]{:S(2)}) copy-start(f32[72,128]{1,0:T(8,128)S(1)} %collective-permute-done.2.refs_7_) | copy-start | bytes 110596
  14.8 14.8 %collective-permute-start.3 = (f32[160,128]{1,0:T(8,128)S(1)}, f32[160,128]{1,0:T(8,128)S(1)}, u32[]{:S(2)}, u32[]{:S(2)}) collective-permute-start(f32[160,128]{1,0:T(8,128)S(1)} %pad_maximum_fusion.refs_0_), channel_id=1, source_target_pairs={{0,4},{4,0},{8,12},{12,8},{1,5},{5,1},{9,13},{13,9},{2,6},{6,2},{1... | collective-permute-start | bytes 245768 | tf_op jit(solution)/shard_map/ppermute | solution.py:23
  16.3 13.2 %collective-permute-start.4 = (f32[160,128]{1,0:T(8,128)S(1)}, f32[160,128]{1,0:T(8,128)S(1)}, u32[]{:S(2)}, u32[]{:S(2)}) collective-permute-start(f32[160,128]{1,0:T(8,128)S(1)} %pad_maximum_fusion.refs_0_), channel_id=1, source_target_pairs={{0,8},{4,12},{8,0},{12,4},{1,9},{5,13},{9,1},{13,5},{2,10},{6,14},... | collective-permute-start | bytes 245768 | tf_op jit(solution)/shard_map/ppermute | solution.py:23
  18.9 10.6 %collective-permute-start.5 = (f32[160,128]{1,0:T(8,128)S(1)}, f32[160,128]{1,0:T(8,128)S(1)}, u32[]{:S(2)}, u32[]{:S(2)}) collective-permute-start(f32[160,128]{1,0:T(8,128)S(1)} %pad_maximum_fusion.refs_0_), channel_id=1, source_target_pairs={{0,12},{4,8},{8,4},{12,0},{1,13},{5,9},{9,5},{13,1},{2,14},{6,10},... | collective-permute-start | bytes 245768 | tf_op jit(solution)/shard_map/ppermute | solution.py:23
  19.8 0.8 %copy-start.1 = (f32[72,128]{1,0:T(8,128)S(1)}, f32[72,128]{1,0:T(8,128)}, u32[]{:S(2)}) copy-start(f32[72,128]{1,0:T(8,128)} %copy-done) | copy-start | bytes 110596
  20.6 0.8 %copy-start.3 = (f32[72,128]{1,0:T(8,128)S(1)}, f32[72,128]{1,0:T(8,128)}, u32[]{:S(2)}) copy-start(f32[72,128]{1,0:T(8,128)} %copy-done.2) | copy-start | bytes 110596
  29.5 0.7 %copy-start.5 = (f32[32,128]{1,0:T(8,128)S(1)}, f32[32,128]{1,0:T(8,128)}, u32[]{:S(2)}) copy-start(f32[32,128]{1,0:T(8,128)} %copy-done.4) | copy-start | bytes 49156
  30.3 0.7 %copy-start.7 = (s32[1,8]{1,0:T(1,128)S(1)}, s32[1,8]{1,0:T(1,128)}, u32[]{:S(2)}) copy-start(s32[1,8]{1,0:T(1,128)} %param.20) | copy-start | bytes 100
  32.0 4.0 %collective-permute-start.10 = (f32[64,128]{1,0:T(8,128)S(1)}, f32[64,128]{1,0:T(8,128)S(1)}, u32[]{:S(2)}, u32[]{:S(2)}) collective-permute-start(f32[64,128]{1,0:T(8,128)S(1)} %get-tuple-element.27.refs_0_.refs_5_), channel_id=1, source_target_pairs={{0,2},{1,3},{2,0},{3,1},{4,6},{5,7},{6,4},{7,5},{8,10},{9,11},{10,... | collective-permute-start | bytes 98312 | tf_op jit(solution)/shard_map/ppermute | solution.py:23
  32.9 3.5 %collective-permute-start.11 = (f32[64,128]{1,0:T(8,128)S(1)}, f32[64,128]{1,0:T(8,128)S(1)}, u32[]{:S(2)}, u32[]{:S(2)}) collective-permute-start(f32[64,128]{1,0:T(8,128)S(1)} %get-tuple-element.27.refs_0_.refs_5_), channel_id=1, source_target_pairs={{0,3},{1,2},{2,1},{3,0},{4,7},{5,6},{6,5},{7,4},{8,11},{9,10},{10,... | collective-permute-start | bytes 98312 | tf_op jit(solution)/shard_map/ppermute | solution.py:23
  33.6 2.8 %collective-permute-start.9 = (f32[64,128]{1,0:T(8,128)S(1)}, f32[64,128]{1,0:T(8,128)S(1)}, u32[]{:S(2)}, u32[]{:S(2)}) collective-permute-start(f32[64,128]{1,0:T(8,128)S(1)} %get-tuple-element.27.refs_0_.refs_5_), channel_id=1, source_target_pairs={{0,1},{1,0},{2,3},{3,2},{4,5},{5,4},{6,7},{7,6},{8,9},{9,8},{10,11... | collective-permute-start | bytes 98312 | tf_op jit(solution)/shard_map/ppermute | solution.py:23

commit v7 on v6

--- a/solution.py
+++ b/solution.py
@@ -44,13 +44,13 @@
         compiler_params=pltpu.CompilerParams(vmem_limit_bytes=VMEM_LIMIT),
     )(
         *scalars,
-        *arrays,
+        *[pltpu.with_memory_space_constraint(array, pltpu.VMEM) for array in arrays],
         *[pltpu.with_memory_space_constraint(array, pltpu.HBM) for array in remote],
     )
 
 
-def kept(array):
-    return pltpu.VMEM(array.shape, array.dtype)
+def kept(*shape, dtype=jnp.float32):
+    return pltpu.VMEM(shape, dtype)
 
 
 def f32(*shape):
@@ -108,36 +108,16 @@
     return jnp.sum(jnp.where(diagonal, column, 0.0), axis=0, keepdims=True)
 
 
-def six_products(left, right, contract):
-    one, two, three = [part.astype(jnp.bfloat16) for part in split_three(right)]
-    parts = jnp.concatenate(split_three(left)).astype(jnp.bfloat16)
-    rows = left.shape[0]
-
-    def product(count, other):
-        return lax.dot_general(
-            parts[0 : count * rows],
-            other,
-            (contract, ((), ())),
-            preferred_element_type=jnp.float32,
-        )
-
-    first, second, third = product(3, one), product(2, two), product(1, three)
-    return first[0:rows] + (
-        (first[rows : 2 * rows] + second[0:rows])
-        + (first[2 * rows : 3 * rows] + second[rows : 2 * rows] + third)
-    )
-
-
-def start_kernel(counts, box_far, *refs):
-    sources, (geometry, initial, message, box_basis) = refs[:7], refs[7:11]
-    basis, leaf_coupling, box_coupling = refs[11:14]
-    at, transfer, arrived = refs[14:]
+def start_kernel(counts, *refs):
+    sources, (geometry, initial, message, box_basis) = refs[:8], refs[8:12]
+    basis, leaf_coupling, box_coupling = refs[12:15]
+    at, box_far, transfer, parts, arrived = refs[15:]
     dims, slots, width = sources[0].shape
     rank = basis.shape[1]
-    targets = [at.at[0:dims], at.at[dims : 2 * dims], at.at[2 * dims]]
+    targets = [at.at[0:dims], at.at[dims : 2 * dims], at.at[2 * dims], box_far]
     targets += [transfer, basis, leaf_coupling, box_coupling]
     copies = copy_all(zip(sources, targets), arrived)
-    for copy in copies[:3]:
+    for copy in copies[:4]:
         copy.wait()
     for row in range(2 * dims):
         geometry[:, row, :] = at[row]
@@ -147,13 +127,12 @@
     geometry[:, 2 * dims + 1, :] = jnp.zeros_like(vector)
     entries = [jnp.sum(vector * vector, keepdims=True)] + [
         jnp.full((1, 1), value, jnp.int32).astype(jnp.float32)
-        for value in [counts[0]] + [box_far[place] for place in range(box_far.shape[0])]
+        for value in [counts[0]] + [box_far[0, place] for place in range(box_far.shape[1])]
     ]
     message[slots : slots + TILE_ROWS, :] = jnp.zeros((TILE_ROWS, LANES), jnp.float32)
     message[slots + 1 : slots + 2, :] = lane_row(entries)
-    for copy in copies[3:]:
+    for copy in copies[4:6]:
         copy.wait()
-    gram = jnp.zeros((rank, rank), jnp.float32)
     for leaf in range(slots):
         product = jnp.dot(
             transfer[leaf],
@@ -163,12 +142,22 @@
         )
         product = jnp.where(leaf < counts[0], product, 0.0)
         box_basis[leaf] = product
-        gram = gram + six_products(product, product, ((1,), (1,)))
+        split = jnp.concatenate(split_three(product)).astype(jnp.bfloat16)
+        parts[:, leaf * width : (leaf + 1) * width] = split
     write_moments(initial, basis, message, 0)
     message[slots : slots + 1, :] = box_moments(initial, box_basis)
+    products = lax.dot_general(
+        parts[...], parts[...], (((1,), (1,)), ((), ())), preferred_element_type=jnp.float32
+    )
+    mixed = products[rank : 2 * rank, 0:rank] + products[2 * rank : 3 * rank, 0:rank]
+    gram = products[0:rank, 0:rank] + (
+        mixed + mixed.T + products[rank : 2 * rank, rank : 2 * rank]
+    )
     start, half = slots + TILE_ROWS, rank // 2
     message[start : start + half, 0:rank] = gram[0:half]
     message[start : start + half, rank : 2 * rank] = gram[half:rank]
+    for copy in copies[6:]:
+        copy.wait()
 
 
 def leaf_part(moments, picks, coupling):
@@ -191,10 +180,14 @@
     return local
 
 
-def add_leaf_far(counts, moments, picks, coupling, basis, near):
+def wide_transpose(rows):
+    count, lanes = rows.shape
+    return jnp.concatenate([rows, jnp.zeros((count, LANES - lanes), rows.dtype)], axis=1).T
+
+
+def add_leaf_far(counts, local, basis, near):
     slots, rank, width = basis.shape
-    local = leaf_part(moments, picks, coupling)
-    columns = jnp.concatenate([local, jnp.zeros((slots, LANES - rank), jnp.float32)], axis=1).T
+    columns = wide_transpose(local)
     for leaf in range(slots):
         far = jnp.sum(basis[leaf] * columns[0:rank, leaf : leaf + 1], axis=0, keepdims=True)
         near[leaf : leaf + 1, :] = jnp.where(
@@ -262,17 +255,14 @@
     for copy in copies:
         copy.wait()
     far_count, sources = far_list.shape[0], subs * slots
-    far_rows = far_list[...].astype(jnp.float32)
-    far_rows = jnp.concatenate(
-        [far_rows, jnp.zeros((far_count, LANES - slots), jnp.float32)], axis=1
-    ).T
+    far_rows = wide_transpose(far_list[...].astype(jnp.float32))
     leaves = (iota((slots, sources), 1) ^ (box[0] * slots)).astype(jnp.float32)
     for place in range(far_count):
         chosen = jnp.where(far_rows[0:slots, place : place + 1] == leaves, 1.0, 0.0)
         picks[place * slots : (place + 1) * slots, :] = chosen.astype(jnp.bfloat16)
+    local = leaf_part([ref[0:slots, 0:rank] for ref in messages], picks, coupling)
     lax.fori_loop(0, slots, target, 0, unroll=True)
-    moments = [ref[0:slots, 0:rank] for ref in messages]
-    add_leaf_far(counts, moments, picks, coupling, basis, near)
+    add_leaf_far(counts, local, basis, near)
 
 
 def box_images(box_basis, coefficients, image):
@@ -282,18 +272,22 @@
         image[leaf : leaf + 1, :] += jnp.sum(box_basis[leaf] * spread, axis=0, keepdims=True)
 
 
-def first_image_kernel(patches, span, box, box_far, *refs):
+def first_image_kernel(patches, span, box, *refs):
     boxes = refs[:patches]
     part, initial, basis, box_basis, box_coupling = refs[patches : patches + 5]
-    message, basis_one, numbers, gather, image = refs[patches + 5 :]
+    message, basis_one, numbers, starts, image = refs[patches + 5 :]
     slots, rank, width = basis.shape
     height = boxes[0].shape[0]
-    for place, ref in enumerate(boxes):
-        gather[place * height : (place + 1) * height, :] = ref[...]
+    row_starts = [(ref, at) for ref in boxes for at in range(0, height, span)]
+    count = len(row_starts)
+    for place, (ref, at) in enumerate(row_starts):
+        starts[place : place + 1, :] = ref[at : at + 1, :]
+    number = (iota((count, LANES), 0) ^ box[0]).astype(jnp.float32)
     coupled = jnp.zeros((rank, rank), jnp.float32)
     for place in range(box_coupling.shape[0]):
-        row = (box_far[place] ^ box[0]) * span
-        coupled = coupled + box_coupling[place] * gather[pl.ds(row, 1), 0:rank]
+        wanted = boxes[0][1:2, 2 + place : 3 + place]
+        row = jnp.sum(jnp.where(number == wanted, starts[...], 0.0), axis=0, keepdims=True)
+        coupled = coupled + box_coupling[place] * row[:, 0:rank]
     image[...] = part[...]
     box_images(box_basis, jnp.sum(coupled, axis=1, keepdims=True), image)
     sums = tree_sum(
@@ -331,10 +325,10 @@
         part[pl.ds(leaf, 1), :] = jnp.sum(total.T, axis=0, keepdims=True)
         return carry
 
+    local = leaf_part([ref[slots : 2 * slots, 0:rank] for ref in messages], picks, coupling)
     copy.wait()
     lax.fori_loop(0, slots, target, 0, unroll=True)
-    moments = [ref[slots : 2 * slots, 0:rank] for ref in messages]
-    add_leaf_far(counts, moments, picks, coupling, basis, part)
+    add_leaf_far(counts, local, basis, part)
     first, one, second = messages[0][0:slots, :], basis_one[...], part[...]
     products = [one * first, first * first, one * second, first * second, second * second]
     sums = lane_row([jnp.sum(product, keepdims=True) for product in products])
@@ -459,10 +453,9 @@
     far_count = leaf_far.shape[1]
     subs, patches = lax.axis_size("sub"), lax.axis_size("patch")
     sources = subs * slots
-    rows = f32(slots, width)
+    rows = kept(slots, width)
     this_box = lax.axis_index("patch") * subs + lax.axis_index("sub")
     box = this_box.astype(jnp.int32).reshape(1)
-    box_far = box_far.reshape(-1)
     far_list = leaf_far.T
     rank = leaf_basis.shape[1]
     span = TILE_ROWS + rank // 2
@@ -470,32 +463,32 @@
     list_scratch = [pltpu.SMEM(near_list.shape, jnp.int32), pltpu.SemaphoreType.DMA]
     block = pltpu.VMEM((sources, width), jnp.float32)
 
+    matrices = [leaf_basis, leaf_coupling, box_coupling]
     geometry, initial, message, box_basis, *matrices = device_call(
         start_kernel,
         [
-            f32(slots, 8, width),
+            kept(slots, 8, width),
             rows,
-            f32(slots + span, LANES),
-            kept(leaf_basis),
-            kept(leaf_basis),
-            kept(leaf_coupling),
-            kept(box_coupling),
-        ],
-        [counts, box_far],
+            kept(slots + span, LANES),
+            kept(*leaf_basis.shape),
+            *[kept(*matrix.shape) for matrix in matrices],
+        ],
+        [counts],
         [],
         [
             pltpu.VMEM((7, slots, width), jnp.float32),
+            pltpu.SMEM(box_far.shape, jnp.int32),
             pltpu.VMEM(leaf_to_box_transfer.shape, jnp.float32),
-            pltpu.SemaphoreType.DMA((7,)),
+            pltpu.VMEM((3 * rank, slots * width), jnp.bfloat16),
+            pltpu.SemaphoreType.DMA((8,)),
         ],
         [
             points.transpose(1, 0, 2),
             normals.transpose(1, 0, 2),
             density,
+            box_far,
             leaf_to_box_transfer,
-            leaf_basis,
-            leaf_coupling,
-            box_coupling,
+            *matrices,
         ],
     )
     leaf_basis, leaf_coupling, box_coupling = matrices
@@ -509,8 +502,8 @@
         functools.partial(first_near_kernel, subs),
         [
             rows,
-            pltpu.VMEM((slots * neighbours, width, width), jnp.float32),
-            pltpu.VMEM((far_count * slots, sources), jnp.bfloat16),
+            kept(slots * neighbours, width, width),
+            kept(far_count * slots, sources, dtype=jnp.bfloat16),
         ],
         [box, counts],
         [*geometry, *messages, leaf_coupling, leaf_basis],
@@ -527,15 +520,18 @@
     )
     message, basis_one, numbers = device_call(
         functools.partial(first_image_kernel, patches, span),
-        [f32(2 * slots, LANES), rows, f32(TILE_ROWS, LANES)],
-        [box, box_far],
+        [kept(2 * slots, LANES), rows, kept(TILE_ROWS, LANES)],
+        [box],
         [*boxes, part, initial, leaf_basis, box_basis, box_coupling],
-        [gather, pltpu.VMEM((slots, width), jnp.float32)],
+        [
+            pltpu.VMEM((patches * subs, LANES), jnp.float32),
+            pltpu.VMEM((slots, width), jnp.float32),
+        ],
     )
     messages = from_peers(message, "sub")
     part, shares = device_call(
         functools.partial(second_near_kernel, subs),
-        [rows, f32(2 * patches * subs, LANES)],
+        [rows, kept(2 * patches * subs, LANES)],
         [box, counts],
         [*messages, picks, leaf_coupling, leaf_basis, box_basis, basis_one, values],
         [block, *list_scratch],
@@ -544,7 +540,7 @@
     shares = lax.all_to_all(shares, ("patch", "sub"), 0, 0, tiled=True)
     basis_three, hessenberg = device_call(
         functools.partial(last_kernel, patches, span),
-        [rows, f32(2, 3)],
+        [f32(slots, width), f32(2, 3)],
         [box],
         [*boxes, shares, message, basis_one, part, numbers, box_basis, box_coupling],
         [

time: 54.7 us -> 50.1 us (0.916)
  Pallas kernels: 20.7 us -> 17.4 us
  local copies, waits for them, and re-layouts: 4.77 us -> 3.46 us
    pallas_call x5, Pallas kernels: 20.7 us -> 17.4 us  [device_call(): pl.pallas_call(kernel, out_shape=tuple(outputs), in_specs=[smem] * len(sc...]
    unnamed x16 -> x12, local copies, waits for them, and re-layouts: 4.76 us -> 3.45 us
  transfers between devices with their start and end apart: 12 -> 12, of which waited for: 4 -> 4; matrix products, arithmetic and copies ran while one was open for 0% -> 0% of each run, Pallas kernels for 15% -> 14%
where the time goes in v7:
time: 50.1 us; the launch traced here: 49.7 us
  Pallas kernels  17.4 us (35%)
  blocking collectives  11.7 us (23%)
  starting transfers between devices  11.6 us (23%)
  waiting for transfers between devices  4.05 us (8%)
  local copies, waits for them, and re-layouts  3.46 us (7%)
  between operations  1.4 us (3%)
    pallas_call x5, Pallas kernels, device_call(): pl.pallas_call(kernel, out_shape=tuple(outputs), in_specs=[smem] * len(sc...  17.4 us
    all_to_all x1, blocking collectives, shards(): shares = lax.all_to_all(shares, ('patch', 'sub'), 0, 0, tiled=True)  11.7 us
    ppermute x12, starting transfers between devices, from_peers(): lax.ppermute(value, axis, [(i, i ^ turn) for i in range(size)])  11.6 us
    ppermute x12, waiting for transfers between devices, from_peers(): lax.ppermute(value, axis, [(i, i ^ turn) for i in range(size)])  4.05 us
    unnamed x12, local copies, waits for them, and re-layouts  3.45 us
  transfers between devices with their start and end apart: 12, of which 4 were waited for; matrix products, arithmetic and copies ran while one was open for 0% of the time, Pallas kernels for 14%

profile of v7, /device:TPU:0, one launch (start us, length us, event | category | flops | bytes accessed | tf_op | source)
XLA Modules:
  0.0 49.7 jit_solution(15519365262108148535)
XLA Ops:
  1.3 3.6 %shard_map.122 = (f32[32,8,128]{2,1,0:T(8,128)S(1)}, f32[32,128]{1,0:T(8,128)S(1)}, f32[72,128]{1,0:T(8,128)S(1)}, f32[32,64,128]{2,1,0:T(8,128)S(1)}, f32[32,64...) custom-call(s32[1]{0:T(128)S(6)} %copy.13.counts, f32[3,32,128]{2,1,0:T(8,128)} %bitcast.10, ...), custom_call_target="tpu_custom_call" | custom-call | tf_op jit(solution)/shard_map/pallas_call | solution.py:38
  4.8 0.0 copy-start.4
  4.9 0.6 %copy-done.4 = f32[32,128]{1,0:T(8,128)} copy-done((f32[32,128]{1,0:T(8,128)}, f32[32,128]{1,0:T(8,128)S(1)}, u32[]{:S(2)}) %copy-start.4) | copy-done | bytes 16408
  5.5 0.5 collective-permute-start
  5.9 2.5 %collective-permute-start.1 = (f32[72,128]{1,0:T(8,128)S(1)}, f32[72,128]{1,0:T(8,128)S(1)}, u32[]{:S(2)}, u32[]{:S(2)}) collective-permute-start(f32[72,128]{1,0:T(8,128)S(1)} %get-tuple-element.19.refs_4_), channel_id=1, source_target_pairs={{0,2},{1,3},{2,0},{3,1},{4,6},{5,7},{6,4},{7,5},{8,10},{9,11},{10,... | collective-permute-start | bytes 110600 | tf_op jit(solution)/shard_map/ppermute | solution.py:23
  8.4 0.1 collective-permute-start.2
  8.5 0.1 collective-permute-start.6
  8.6 1.9 %collective-permute-start.7 = (f32[32,8,128]{2,1,0:T(8,128)S(1)}, f32[32,8,128]{2,1,0:T(8,128)S(1)}, u32[]{:S(2)}, u32[]{:S(2)}) collective-permute-start(f32[32,8,128]{2,1,0:T(8,128)S(1)} %get-tuple-element.20.refs_0_), channel_id=1, source_target_pairs={{0,2},{1,3},{2,0},{3,1},{4,6},{5,7},{6,4},{7,5},{8,10},{9,11},{10,... | collective-permute-start | bytes 393224 | tf_op jit(solution)/shard_map/ppermute | solution.py:23
  10.5 0.0 collective-permute-done.refs_5_
  10.5 0.0 collective-permute-start.8
  10.5 0.0 collective-permute-done.1.refs_6_
  10.6 1.2 %collective-permute-done.2.refs_7_ = f32[72,128]{1,0:T(8,128)S(1)} collective-permute-done((f32[72,128]{1,0:T(8,128)S(1)}, f32[72,128]{1,0:T(8,128)S(1)}, u32[]{:S(2)}, u32[]{:S(2)}) %collective-permute-start.2) | collective-permute-done | bytes 36896 | tf_op jit(solution)/shard_map/ppermute | solution.py:23
  11.8 0.6 %copy-done.2 = f32[72,128]{1,0:T(8,128)} copy-done((f32[72,128]{1,0:T(8,128)}, f32[72,128]{1,0:T(8,128)S(1)}, u32[]{:S(2)}) %copy-start.2) | copy-done | bytes 36888
  12.4 1.6 %collective-permute-start.3 = (f32[160,128]{1,0:T(8,128)S(1)}, f32[160,128]{1,0:T(8,128)S(1)}, u32[]{:S(2)}, u32[]{:S(2)}) collective-permute-start(f32[160,128]{1,0:T(8,128)S(1)} %pad_maximum_fusion.refs_0_), channel_id=1, source_target_pairs={{0,4},{4,0},{8,12},{12,8},{1,5},{5,1},{9,13},{13,9},{2,6},{6,2},{1... | collective-permute-start | bytes 245768 | tf_op jit(solution)/shard_map/ppermute | solution.py:23
  14.0 2.6 %collective-permute-start.4 = (f32[160,128]{1,0:T(8,128)S(1)}, f32[160,128]{1,0:T(8,128)S(1)}, u32[]{:S(2)}, u32[]{:S(2)}) collective-permute-start(f32[160,128]{1,0:T(8,128)S(1)} %pad_maximum_fusion.refs_0_), channel_id=1, source_target_pairs={{0,8},{4,12},{8,0},{12,4},{1,9},{5,13},{9,1},{13,5},{2,10},{6,14},... | collective-permute-start | bytes 245768 | tf_op jit(solution)/shard_map/ppermute | solution.py:23
  16.5 0.0 collective-permute-done.6.refs_1_
  16.5 0.2 collective-permute-start.5
  16.8 0.7 %collective-permute-done.8.refs_3_ = f32[32,8,128]{2,1,0:T(8,128)S(1)} collective-permute-done((f32[32,8,128]{2,1,0:T(8,128)S(1)}, f32[32,8,128]{2,1,0:T(8,128)S(1)}, u32[]{:S(2)}, u32[]{:S(2)}) %collective-permute-start.8) | collective-permute-done | bytes 131104 | tf_op jit(solution)/shard_map/ppermute | solution.py:23
  17.5 0.8 %copy-done.1 = f32[72,128]{1,0:T(8,128)S(1)} copy-done((f32[72,128]{1,0:T(8,128)S(1)}, f32[72,128]{1,0:T(8,128)}, u32[]{:S(2)}) %copy-start.1) | copy-done | bytes 36888
  18.2 0.8 %copy-done.3 = f32[72,128]{1,0:T(8,128)S(1)} copy-done((f32[72,128]{1,0:T(8,128)S(1)}, f32[72,128]{1,0:T(8,128)}, u32[]{:S(2)}) %copy-start.3) | copy-done | bytes 36888
  19.0 7.1 %shard_map.123 = (f32[32,128]{1,0:T(8,128)S(1)}, f32[288,128,128]{2,1,0:T(8,128)S(1)}, bf16[256,128]{1,0:T(8,128)(2,1)S(1)}) custom-call(s32[1]{0:T(128)} %bitcast.box, s32[1]{0:T(128)S(6)} %copy.13.counts, f32[32,8,128]{2,1,0:T(8,128)S(1)} %get-tuple-element.20.refs_0_, f32[32,8,128]{2,1,0:T(8,128)S(1)} %collective-permute-done.6.refs_1_, ...), custom_call_target="tpu_custom_call" | custom-call | tf_op jit(solution)/shard_map/pallas_call | solution.py:38
  26.1 0.0 copy-start.5
  26.1 0.7 %copy-done.5 = f32[32,128]{1,0:T(8,128)S(1)} copy-done((f32[32,128]{1,0:T(8,128)S(1)}, f32[32,128]{1,0:T(8,128)}, u32[]{:S(2)}) %copy-start.5) | copy-done | bytes 16408
  26.9 0.7 %shard_map.124 = (f32[64,128]{1,0:T(8,128)S(1)}, f32[32,128]{1,0:T(8,128)S(1)}, f32[8,128]{1,0:T(8,128)S(1)}) custom-call(s32[1]{0:T(128)} %bitcast.box, f32[160,128]{1,0:T(8,128)S(1)} %pad_maximum_fusion.refs_0_, f32[160,128]{1,0:T(8,128)S(1)} %collective-permute-done.3.refs_1_, f32[160,128]{1,0:T(8,128)S(1)} %collective-permute-done.4.refs_2_, ...), custom_call_target="tpu_custom_call" | custom-call | tf_op jit(solution)/shard_map/pallas_call | solution.py:38
  27.5 0.8 %collective-permute-start.10 = (f32[64,128]{1,0:T(8,128)S(1)}, f32[64,128]{1,0:T(8,128)S(1)}, u32[]{:S(2)}, u32[]{:S(2)}) collective-permute-start(f32[64,128]{1,0:T(8,128)S(1)} %get-tuple-element.27.refs_0_.refs_5_), channel_id=1, source_target_pairs={{0,2},{1,3},{2,0},{3,1},{4,6},{5,7},{6,4},{7,5},{8,10},{9,11},{10,... | collective-permute-start | bytes 98312 | tf_op jit(solution)/shard_map/ppermute | solution.py:23
  28.3 0.7 %collective-permute-start.11 = (f32[64,128]{1,0:T(8,128)S(1)}, f32[64,128]{1,0:T(8,128)S(1)}, u32[]{:S(2)}, u32[]{:S(2)}) collective-permute-start(f32[64,128]{1,0:T(8,128)S(1)} %get-tuple-element.27.refs_0_.refs_5_), channel_id=1, source_target_pairs={{0,3},{1,2},{2,1},{3,0},{4,7},{5,6},{6,5},{7,4},{8,11},{9,10},{10,... | collective-permute-start | bytes 98312 | tf_op jit(solution)/shard_map/ppermute | solution.py:23
  29.0 0.6 %collective-permute-start.9 = (f32[64,128]{1,0:T(8,128)S(1)}, f32[64,128]{1,0:T(8,128)S(1)}, u32[]{:S(2)}, u32[]{:S(2)}) collective-permute-start(f32[64,128]{1,0:T(8,128)S(1)} %get-tuple-element.27.refs_0_.refs_5_), channel_id=1, source_target_pairs={{0,1},{1,0},{2,3},{3,2},{4,5},{5,4},{6,7},{7,6},{8,9},{9,8},{10,11... | collective-permute-start | bytes 98312 | tf_op jit(solution)/shard_map/ppermute | solution.py:23
  29.7 1.9 %collective-permute-done.10.refs_2_ = f32[64,128]{1,0:T(8,128)S(1)} collective-permute-done((f32[64,128]{1,0:T(8,128)S(1)}, f32[64,128]{1,0:T(8,128)S(1)}, u32[]{:S(2)}, u32[]{:S(2)}) %collective-permute-start.10) | collective-permute-done | bytes 32800 | tf_op jit(solution)/shard_map/ppermute | solution.py:23
  31.5 0.3 collective-permute-done.11.refs_3_
  31.8 3.3 %shard_map.125 = (f32[32,128]{1,0:T(8,128)S(1)}, f32[32,128]{1,0:T(8,128)S(1)}) custom-call(s32[1]{0:T(128)} %bitcast.box, s32[1]{0:T(128)S(6)} %copy.13.counts, f32[64,128]{1,0:T(8,128)S(1)} %get-tuple-element.27.refs_0_.refs_5_, f32[64,128]{1,0:T(8,128)S(1)} %collective-permute-done.9.refs_1_, f32[64,128]{1,0:T(8,128)S(1)} %collective-permute-done.10.refs_2_, ...), custom_call_target="tpu_custom_call" | custom-call | tf_op jit(solution)/shard_map/pallas_call | solution.py:38
  35.1 11.7 %all_to_all.11 = f32[16,2,128]{2,1,0:T(2,128)S(1)} all-to-all(f32[16,2,128]{2,1,0:T(2,128)S(1)} %bitcast.9), channel_id=1, replica_groups=mesh['groups'=2,'patch'=4,'sub'=4] {'patch','sub'}, dimensions={0} | all-to-all | bytes 32768 | tf_op jit(solution)/shard_map/all_to_all | solution.py:540
  46.8 2.9 %shard_map.126 = (f32[32,128]{1,0:T(8,128)}, f32[2,3]{1,0:T(2,128)}) custom-call(s32[1]{0:T(128)} %bitcast.box, f32[160,128]{1,0:T(8,128)S(1)} %pad_maximum_fusion.refs_0_, f32[160,128]{1,0:T(8,128)S(1)} %collective-permute-done.3.refs_1_, f32[160,128]{1,0:T(8,128)S(1)} %collective-permute-done.4.refs_2_, f32[160,128]{1,0:T(8,128)S(1)} %collective-permute-done.5.refs_3_, ...), custom_call_target="tpu_custom_call" | custom-call | tf_op jit(solution)/shard_map/pallas_call | solution.py:38
  (15 shorter events, 0.0 us)
Async XLA Ops:
  4.8 0.6 %copy-start.4 = (f32[32,128]{1,0:T(8,128)}, f32[32,128]{1,0:T(8,128)S(1)}, u32[]{:S(2)}) copy-start(f32[32,128]{1,0:T(8,128)S(1)} %get-tuple-element.24.refs_5_) | copy-start | bytes 49156
  5.5 5.1 %collective-permute-start = (f32[72,128]{1,0:T(8,128)S(1)}, f32[72,128]{1,0:T(8,128)S(1)}, u32[]{:S(2)}, u32[]{:S(2)}) collective-permute-start(f32[72,128]{1,0:T(8,128)S(1)} %get-tuple-element.19.refs_4_), channel_id=1, source_target_pairs={{0,1},{1,0},{2,3},{3,2},{4,5},{5,4},{6,7},{7,6},{8,9},{9,8},{10,11... | collective-permute-start | bytes 110600 | tf_op jit(solution)/shard_map/ppermute | solution.py:23
  5.9 4.6 %collective-permute-start.1 = (f32[72,128]{1,0:T(8,128)S(1)}, f32[72,128]{1,0:T(8,128)S(1)}, u32[]{:S(2)}, u32[]{:S(2)}) collective-permute-start(f32[72,128]{1,0:T(8,128)S(1)} %get-tuple-element.19.refs_4_), channel_id=1, source_target_pairs={{0,2},{1,3},{2,0},{3,1},{4,6},{5,7},{6,4},{7,5},{8,10},{9,11},{10,... | collective-permute-start | bytes 110600 | tf_op jit(solution)/shard_map/ppermute | solution.py:23
  8.4 3.4 %collective-permute-start.2 = (f32[72,128]{1,0:T(8,128)S(1)}, f32[72,128]{1,0:T(8,128)S(1)}, u32[]{:S(2)}, u32[]{:S(2)}) collective-permute-start(f32[72,128]{1,0:T(8,128)S(1)} %get-tuple-element.19.refs_4_), channel_id=1, source_target_pairs={{0,3},{1,2},{2,1},{3,0},{4,7},{5,6},{6,5},{7,4},{8,11},{9,10},{10,... | collective-permute-start | bytes 110600 | tf_op jit(solution)/shard_map/ppermute | solution.py:23
  8.5 8.0 %collective-permute-start.6 = (f32[32,8,128]{2,1,0:T(8,128)S(1)}, f32[32,8,128]{2,1,0:T(8,128)S(1)}, u32[]{:S(2)}, u32[]{:S(2)}) collective-permute-start(f32[32,8,128]{2,1,0:T(8,128)S(1)} %get-tuple-element.20.refs_0_), channel_id=1, source_target_pairs={{0,1},{1,0},{2,3},{3,2},{4,5},{5,4},{6,7},{7,6},{8,9},{9,8},{10,11... | collective-permute-start | bytes 393224 | tf_op jit(solution)/shard_map/ppermute | solution.py:23
  8.6 8.2 %collective-permute-start.7 = (f32[32,8,128]{2,1,0:T(8,128)S(1)}, f32[32,8,128]{2,1,0:T(8,128)S(1)}, u32[]{:S(2)}, u32[]{:S(2)}) collective-permute-start(f32[32,8,128]{2,1,0:T(8,128)S(1)} %get-tuple-element.20.refs_0_), channel_id=1, source_target_pairs={{0,2},{1,3},{2,0},{3,1},{4,6},{5,7},{6,4},{7,5},{8,10},{9,11},{10,... | collective-permute-start | bytes 393224 | tf_op jit(solution)/shard_map/ppermute | solution.py:23
  10.5 6.9 %collective-permute-start.8 = (f32[32,8,128]{2,1,0:T(8,128)S(1)}, f32[32,8,128]{2,1,0:T(8,128)S(1)}, u32[]{:S(2)}, u32[]{:S(2)}) collective-permute-start(f32[32,8,128]{2,1,0:T(8,128)S(1)} %get-tuple-element.20.refs_0_), channel_id=1, source_target_pairs={{0,3},{1,2},{2,1},{3,0},{4,7},{5,6},{6,5},{7,4},{8,11},{9,10},{10,... | collective-permute-start | bytes 393224 | tf_op jit(solution)/shard_map/ppermute | solution.py:23
  10.6 1.2 %copy-start = (f32[72,128]{1,0:T(8,128)}, f32[72,128]{1,0:T(8,128)S(1)}, u32[]{:S(2)}) copy-start(f32[72,128]{1,0:T(8,128)S(1)} %collective-permute-done.1.refs_6_) | copy-start | bytes 110596
  11.8 0.6 %copy-start.2 = (f32[72,128]{1,0:T(8,128)}, f32[72,128]{1,0:T(8,128)S(1)}, u32[]{:S(2)}) copy-start(f32[72,128]{1,0:T(8,128)S(1)} %collective-permute-done.2.refs_7_) | copy-start | bytes 110596
  12.4 13.7 %collective-permute-start.3 = (f32[160,128]{1,0:T(8,128)S(1)}, f32[160,128]{1,0:T(8,128)S(1)}, u32[]{:S(2)}, u32[]{:S(2)}) collective-permute-start(f32[160,128]{1,0:T(8,128)S(1)} %pad_maximum_fusion.refs_0_), channel_id=1, source_target_pairs={{0,4},{4,0},{8,12},{12,8},{1,5},{5,1},{9,13},{13,9},{2,6},{6,2},{1... | collective-permute-start | bytes 245768 | tf_op jit(solution)/shard_map/ppermute | solution.py:23
  14.0 12.1 %collective-permute-start.4 = (f32[160,128]{1,0:T(8,128)S(1)}, f32[160,128]{1,0:T(8,128)S(1)}, u32[]{:S(2)}, u32[]{:S(2)}) collective-permute-start(f32[160,128]{1,0:T(8,128)S(1)} %pad_maximum_fusion.refs_0_), channel_id=1, source_target_pairs={{0,8},{4,12},{8,0},{12,4},{1,9},{5,13},{9,1},{13,5},{2,10},{6,14},... | collective-permute-start | bytes 245768 | tf_op jit(solution)/shard_map/ppermute | solution.py:23
  16.5 9.6 %collective-permute-start.5 = (f32[160,128]{1,0:T(8,128)S(1)}, f32[160,128]{1,0:T(8,128)S(1)}, u32[]{:S(2)}, u32[]{:S(2)}) collective-permute-start(f32[160,128]{1,0:T(8,128)S(1)} %pad_maximum_fusion.refs_0_), channel_id=1, source_target_pairs={{0,12},{4,8},{8,4},{12,0},{1,13},{5,9},{9,5},{13,1},{2,14},{6,10},... | collective-permute-start | bytes 245768 | tf_op jit(solution)/shard_map/ppermute | solution.py:23
  17.4 0.8 %copy-start.1 = (f32[72,128]{1,0:T(8,128)S(1)}, f32[72,128]{1,0:T(8,128)}, u32[]{:S(2)}) copy-start(f32[72,128]{1,0:T(8,128)} %copy-done) | copy-start | bytes 110596
  18.2 0.8 %copy-start.3 = (f32[72,128]{1,0:T(8,128)S(1)}, f32[72,128]{1,0:T(8,128)}, u32[]{:S(2)}) copy-start(f32[72,128]{1,0:T(8,128)} %copy-done.2) | copy-start | bytes 110596
  26.1 0.7 %copy-start.5 = (f32[32,128]{1,0:T(8,128)S(1)}, f32[32,128]{1,0:T(8,128)}, u32[]{:S(2)}) copy-start(f32[32,128]{1,0:T(8,128)} %copy-done.4) | copy-start | bytes 49156
  27.5 4.0 %collective-permute-start.10 = (f32[64,128]{1,0:T(8,128)S(1)}, f32[64,128]{1,0:T(8,128)S(1)}, u32[]{:S(2)}, u32[]{:S(2)}) collective-permute-start(f32[64,128]{1,0:T(8,128)S(1)} %get-tuple-element.27.refs_0_.refs_5_), channel_id=1, source_target_pairs={{0,2},{1,3},{2,0},{3,1},{4,6},{5,7},{6,4},{7,5},{8,10},{9,11},{10,... | collective-permute-start | bytes 98312 | tf_op jit(solution)/shard_map/ppermute | solution.py:23
  28.3 3.5 %collective-permute-start.11 = (f32[64,128]{1,0:T(8,128)S(1)}, f32[64,128]{1,0:T(8,128)S(1)}, u32[]{:S(2)}, u32[]{:S(2)}) collective-permute-start(f32[64,128]{1,0:T(8,128)S(1)} %get-tuple-element.27.refs_0_.refs_5_), channel_id=1, source_target_pairs={{0,3},{1,2},{2,1},{3,0},{4,7},{5,6},{6,5},{7,4},{8,11},{9,10},{10,... | collective-permute-start | bytes 98312 | tf_op jit(solution)/shard_map/ppermute | solution.py:23
  29.0 2.8 %collective-permute-start.9 = (f32[64,128]{1,0:T(8,128)S(1)}, f32[64,128]{1,0:T(8,128)S(1)}, u32[]{:S(2)}, u32[]{:S(2)}) collective-permute-start(f32[64,128]{1,0:T(8,128)S(1)} %get-tuple-element.27.refs_0_.refs_5_), channel_id=1, source_target_pairs={{0,1},{1,0},{2,3},{3,2},{4,5},{5,4},{6,7},{7,6},{8,9},{9,8},{10,11... | collective-permute-start | bytes 98312 | tf_op jit(solution)/shard_map/ppermute | solution.py:23

commit v8 on v7

--- a/solution.py
+++ b/solution.py
@@ -109,9 +109,9 @@
 
 
 def start_kernel(counts, *refs):
-    sources, (geometry, initial, message, box_basis) = refs[:8], refs[8:12]
-    basis, leaf_coupling, box_coupling = refs[12:15]
-    at, box_far, transfer, parts, arrived = refs[15:]
+    sources, (geometry, message, box_basis) = refs[:8], refs[8:11]
+    basis, leaf_coupling, box_coupling = refs[11:14]
+    at, initial, box_far, transfer, parts, arrived = refs[14:]
     dims, slots, width = sources[0].shape
     rank = basis.shape[1]
     targets = [at.at[0:dims], at.at[dims : 2 * dims], at.at[2 * dims], box_far]
@@ -160,11 +160,19 @@
         copy.wait()
 
 
+def join_kernel(subs, *refs):
+    messages, (moments, blocks) = refs[:subs], refs[subs:]
+    slots, span = moments.shape[0] // subs, blocks.shape[0] // subs
+    for sub, message in enumerate(messages):
+        moments[sub * slots : (sub + 1) * slots, :] = message[0:slots, :]
+        blocks[sub * span : (sub + 1) * span, :] = message[slots : slots + span, :]
+
+
 def leaf_part(moments, picks, coupling):
     count, rank, _ = coupling.shape
     slots = picks.shape[0] // count
     chosen = jnp.zeros((picks.shape[0], rank), jnp.float32)
-    for part in split_three(jnp.concatenate(moments, axis=0)):
+    for part in split_three(moments):
         chosen = chosen + jnp.dot(
             picks[...], part.astype(jnp.bfloat16), preferred_element_type=jnp.float32
         )
@@ -196,9 +204,9 @@
 
 
 def first_near_kernel(subs, box, counts, *refs):
-    geometry, messages = refs[:subs], refs[subs : 2 * subs]
-    coupling, basis, near_source, far_source, near, values, picks = refs[2 * subs : 2 * subs + 7]
-    features, squares, fields, inner, near_list, far_list, arrived = refs[2 * subs + 7 :]
+    geometry, (moments, coupling, basis) = refs[:subs], refs[subs : subs + 3]
+    near_source, far_source, near, initial, values, picks = refs[subs + 3 : subs + 9]
+    features, squares, fields, inner, near_list, far_list, arrived = refs[subs + 9 :]
     copies = copy_all([(near_source, near_list), (far_source, far_list)], arrived)
     slots, height, width = geometry[0].shape
     neighbours = near_list.shape[0]
@@ -260,7 +268,8 @@
     for place in range(far_count):
         chosen = jnp.where(far_rows[0:slots, place : place + 1] == leaves, 1.0, 0.0)
         picks[place * slots : (place + 1) * slots, :] = chosen.astype(jnp.bfloat16)
-    local = leaf_part([ref[0:slots, 0:rank] for ref in messages], picks, coupling)
+    local = leaf_part(moments[:, 0:rank], picks, coupling)
+    initial[...] = fields[0:slots, :]
     lax.fori_loop(0, slots, target, 0, unroll=True)
     add_leaf_far(counts, local, basis, near)
 
@@ -325,7 +334,8 @@
         part[pl.ds(leaf, 1), :] = jnp.sum(total.T, axis=0, keepdims=True)
         return carry
 
-    local = leaf_part([ref[slots : 2 * slots, 0:rank] for ref in messages], picks, coupling)
+    moments = jnp.concatenate([ref[slots : 2 * slots, 0:rank] for ref in messages], axis=0)
+    local = leaf_part(moments, picks, coupling)
     copy.wait()
     lax.fori_loop(0, slots, target, 0, unroll=True)
     add_leaf_far(counts, local, basis, part)
@@ -464,11 +474,10 @@
     block = pltpu.VMEM((sources, width), jnp.float32)
 
     matrices = [leaf_basis, leaf_coupling, box_coupling]
-    geometry, initial, message, box_basis, *matrices = device_call(
+    geometry, message, box_basis, *matrices = device_call(
         start_kernel,
         [
             kept(slots, 8, width),
-            rows,
             kept(slots + span, LANES),
             kept(*leaf_basis.shape),
             *[kept(*matrix.shape) for matrix in matrices],
@@ -477,6 +486,7 @@
         [],
         [
             pltpu.VMEM((7, slots, width), jnp.float32),
+            pltpu.VMEM((slots, width), jnp.float32),
             pltpu.SMEM(box_far.shape, jnp.int32),
             pltpu.VMEM(leaf_to_box_transfer.shape, jnp.float32),
             pltpu.VMEM((3 * rank, slots * width), jnp.bfloat16),
@@ -494,19 +504,24 @@
     leaf_basis, leaf_coupling, box_coupling = matrices
     geometry = from_peers(geometry, "sub")
     messages = from_peers(message, "sub")
-    boxes = from_peers(
-        jnp.concatenate([part[slots : slots + span] for part in messages], axis=0), "patch"
-    )
+    moments, blocks = device_call(
+        functools.partial(join_kernel, subs),
+        [kept(sources, LANES), kept(subs * span, LANES)],
+        [],
+        messages,
+    )
+    boxes = from_peers(blocks, "patch")
     gather = pltpu.VMEM((patches * subs * span, LANES), jnp.float32)
-    part, values, picks = device_call(
+    part, initial, values, picks = device_call(
         functools.partial(first_near_kernel, subs),
         [
+            rows,
             rows,
             kept(slots * neighbours, width, width),
             kept(far_count * slots, sources, dtype=jnp.bfloat16),
         ],
         [box, counts],
-        [*geometry, *messages, leaf_coupling, leaf_basis],
+        [*geometry, moments, leaf_coupling, leaf_basis],
         [
             pltpu.VMEM((sources, 32, 2 * width), jnp.bfloat16),
             block,

time: 50.1 us -> 51.3 us (1.024)
  waiting for transfers between devices: 4.05 us -> 8.87 us
  local copies, waits for them, and re-layouts: 3.46 us -> 0 us
    ppermute x12, waiting for transfers between devices: 4.05 us -> 8.87 us  [from_peers(): lax.ppermute(value, axis, [(i, i ^ turn) for i in range(size)])]
    unnamed x12 -> x0, local copies, waits for them, and re-layouts: 3.45 us -> none
    pallas_call x5 -> x6, Pallas kernels: 17.4 us -> 17.3 us  [device_call(): pl.pallas_call(kernel, out_shape=tuple(outputs), in_specs=[smem] * len(sc...]
  transfers between devices with their start and end apart: 12 -> 12, of which waited for: 4 -> 3; matrix products, arithmetic and copies ran while one was open for 0% -> 0% of each run, Pallas kernels for 14% -> 14%
where the time goes in v8:
time: 51.3 us; the launch traced here: 51.1 us
  Pallas kernels  17.3 us (34%)
  starting transfers between devices  11.9 us (23%)
  blocking collectives  11.6 us (23%)
  waiting for transfers between devices  8.87 us (17%)
  between operations  1.35 us (3%)
    pallas_call x6, Pallas kernels, device_call(): pl.pallas_call(kernel, out_shape=tuple(outputs), in_specs=[smem] * len(sc...  17.3 us
    ppermute x12, starting transfers between devices, from_peers(): lax.ppermute(value, axis, [(i, i ^ turn) for i in range(size)])  11.9 us
    all_to_all x1, blocking collectives, shards(): shares = lax.all_to_all(shares, ('patch', 'sub'), 0, 0, tiled=True)  11.6 us
    ppermute x12, waiting for transfers between devices, from_peers(): lax.ppermute(value, axis, [(i, i ^ turn) for i in range(size)])  8.87 us
  transfers between devices with their start and end apart: 12, of which 3 were waited for; matrix products, arithmetic and copies ran while one was open for 0% of the time, Pallas kernels for 14%

profile of v8, /device:TPU:0, one launch (start us, length us, event | category | flops | bytes accessed | tf_op | source)
XLA Modules:
  0.0 51.1 jit_solution(18337304853729052035)
XLA Ops:
  1.3 3.6 %shard_map.122 = (f32[32,8,128]{2,1,0:T(8,128)S(1)}, f32[72,128]{1,0:T(8,128)S(1)}, f32[32,64,128]{2,1,0:T(8,128)S(1)}, f32[32,64,128]{2,1,0:T(8,128)S(1)}, f32[...) custom-call(s32[1]{0:T(128)S(6)} %copy.13.counts, f32[3,32,128]{2,1,0:T(8,128)} %bitcast.10, f32[3,32,128]{2,1,0:T(8,128)} %bitcast.11, ...), custom_call_target="tpu_custom_call" | custom-call | tf_op jit(solution)/shard_map/pallas_call | solution.py:38
  4.8 0.5 %collective-permute-start.6 = (f32[32,8,128]{2,1,0:T(8,128)S(1)}, f32[32,8,128]{2,1,0:T(8,128)S(1)}, u32[]{:S(2)}, u32[]{:S(2)}) collective-permute-start(f32[32,8,128]{2,1,0:T(8,128)S(1)} %get-tuple-element.23.refs_0_), channel_id=1, source_target_pairs={{0,1},{1,0},{2,3},{3,2},{4,5},{5,4},{6,7},{7,6},{8,9},{9,8},{10,11... | collective-permute-start | bytes 393224 | tf_op jit(solution)/shard_map/ppermute | solution.py:23
  5.4 0.1 collective-permute-start
  5.4 2.9 %collective-permute-start.7 = (f32[32,8,128]{2,1,0:T(8,128)S(1)}, f32[32,8,128]{2,1,0:T(8,128)S(1)}, u32[]{:S(2)}, u32[]{:S(2)}) collective-permute-start(f32[32,8,128]{2,1,0:T(8,128)S(1)} %get-tuple-element.23.refs_0_), channel_id=1, source_target_pairs={{0,2},{1,3},{2,0},{3,1},{4,6},{5,7},{6,4},{7,5},{8,10},{9,11},{10,... | collective-permute-start | bytes 393224 | tf_op jit(solution)/shard_map/ppermute | solution.py:23
  8.4 0.0 collective-permute-start.8
  8.4 1.4 %collective-permute-start.1 = (f32[72,128]{1,0:T(8,128)S(1)}, f32[72,128]{1,0:T(8,128)S(1)}, u32[]{:S(2)}, u32[]{:S(2)}) collective-permute-start(f32[72,128]{1,0:T(8,128)S(1)} %get-tuple-element.21.refs_0_), channel_id=1, source_target_pairs={{0,2},{1,3},{2,0},{3,1},{4,6},{5,7},{6,4},{7,5},{8,10},{9,11},{10,... | collective-permute-start | bytes 110600 | tf_op jit(solution)/shard_map/ppermute | solution.py:23
  9.8 0.0 collective-permute-done.refs_1_
  9.8 0.3 collective-permute-start.2
  10.1 6.0 %collective-permute-done.1.refs_2_ = f32[72,128]{1,0:T(8,128)S(1)} collective-permute-done((f32[72,128]{1,0:T(8,128)S(1)}, f32[72,128]{1,0:T(8,128)S(1)}, u32[]{:S(2)}, u32[]{:S(2)}) %collective-permute-start.1) | collective-permute-done | bytes 36896 | tf_op jit(solution)/shard_map/ppermute | solution.py:23
  16.1 0.0 collective-permute-done.2.refs_3_
  16.1 1.9 %collective-permute-start.3 = (f32[160,128]{1,0:T(8,128)S(1)}, f32[160,128]{1,0:T(8,128)S(1)}, u32[]{:S(2)}, u32[]{:S(2)}) collective-permute-start(f32[160,128]{1,0:T(8,128)S(1)} %get-tuple-element.22.refs_0_), channel_id=1, source_target_pairs={{0,4},{4,0},{8,12},{12,8},{1,5},{5,1},{9,13},{13,9},{2,6},{6,2},{1... | collective-permute-start | bytes 245768 | tf_op jit(solution)/shard_map/ppermute | solution.py:23
  18.0 2.6 %collective-permute-start.4 = (f32[160,128]{1,0:T(8,128)S(1)}, f32[160,128]{1,0:T(8,128)S(1)}, u32[]{:S(2)}, u32[]{:S(2)}) collective-permute-start(f32[160,128]{1,0:T(8,128)S(1)} %get-tuple-element.22.refs_0_), channel_id=1, source_target_pairs={{0,8},{4,12},{8,0},{12,4},{1,9},{5,13},{9,1},{13,5},{2,10},{6,14},... | collective-permute-start | bytes 245768 | tf_op jit(solution)/shard_map/ppermute | solution.py:23
  20.6 0.0 collective-permute-done.6.refs_1_
  20.6 0.0 collective-permute-start.5
  20.6 0.0 collective-permute-done.7.refs_2_
  20.6 0.0 collective-permute-done.8.refs_3_
  20.6 6.9 %shard_map.124 = (f32[32,128]{1,0:T(8,128)S(1)}, f32[32,128]{1,0:T(8,128)S(1)}, f32[288,128,128]{2,1,0:T(8,128)S(1)}, bf16[256,128]{1,0:T(8,128)(2,1)S(1)}) custom-call(s32[1]{0:T(128)} %bitcast.box, s32[1]{0:T(128)S(6)} %copy.13.counts, f32[32,8,128]{2,1,0:T(8,128)S(1)} %get-tuple-element.23.refs_0_, f32[32,8,128]{2,1,0:T(8,128)S(1)} %collective-permute-done.6.refs_1_, ...), custom_call_target="tpu_custom_call" | custom-call | tf_op jit(solution)/shard_map/pallas_call | solution.py:38
  27.6 0.0 collective-permute-done.3.refs_1_
  27.6 0.0 collective-permute-done.4.refs_2_
  27.6 0.0 collective-permute-done.5.refs_3_
  27.6 0.7 %shard_map.125 = (f32[64,128]{1,0:T(8,128)S(1)}, f32[32,128]{1,0:T(8,128)S(1)}, f32[8,128]{1,0:T(8,128)S(1)}) custom-call(s32[1]{0:T(128)} %bitcast.box, f32[160,128]{1,0:T(8,128)S(1)} %get-tuple-element.22.refs_0_, f32[160,128]{1,0:T(8,128)S(1)} %collective-permute-done.3.refs_1_, f32[160,128]{1,0:T(8,128)S(1)} %collective-permute-done.4.refs_2_, ...), custom_call_target="tpu_custom_call" | custom-call | tf_op jit(solution)/shard_map/pallas_call | solution.py:38
  28.3 1.7 %collective-permute-start.10 = (f32[64,128]{1,0:T(8,128)S(1)}, f32[64,128]{1,0:T(8,128)S(1)}, u32[]{:S(2)}, u32[]{:S(2)}) collective-permute-start(f32[64,128]{1,0:T(8,128)S(1)} %get-tuple-element.31.refs_0_.refs_5_), channel_id=1, source_target_pairs={{0,2},{1,3},{2,0},{3,1},{4,6},{5,7},{6,4},{7,5},{8,10},{9,11},{10,... | collective-permute-start | bytes 98312 | tf_op jit(solution)/shard_map/ppermute | solution.py:23
  30.0 0.0 collective-permute-start.11
  30.0 0.4 collective-permute-start.9
  30.4 1.8 %collective-permute-done.10.refs_2_ = f32[64,128]{1,0:T(8,128)S(1)} collective-permute-done((f32[64,128]{1,0:T(8,128)S(1)}, f32[64,128]{1,0:T(8,128)S(1)}, u32[]{:S(2)}, u32[]{:S(2)}) %collective-permute-start.10) | collective-permute-done | bytes 32800 | tf_op jit(solution)/shard_map/ppermute | solution.py:23
  32.2 1.1 %collective-permute-done.11.refs_3_ = f32[64,128]{1,0:T(8,128)S(1)} collective-permute-done((f32[64,128]{1,0:T(8,128)S(1)}, f32[64,128]{1,0:T(8,128)S(1)}, u32[]{:S(2)}, u32[]{:S(2)}) %collective-permute-start.11) | collective-permute-done | bytes 32800 | tf_op jit(solution)/shard_map/ppermute | solution.py:23
  33.3 0.0 collective-permute-done.9.refs_1_
  33.3 3.3 %shard_map.126 = (f32[32,128]{1,0:T(8,128)S(1)}, f32[32,128]{1,0:T(8,128)S(1)}) custom-call(s32[1]{0:T(128)} %bitcast.box, s32[1]{0:T(128)S(6)} %copy.13.counts, f32[64,128]{1,0:T(8,128)S(1)} %get-tuple-element.31.refs_0_.refs_5_, f32[64,128]{1,0:T(8,128)S(1)} %collective-permute-done.9.refs_1_, f32[64,128]{1,0:T(8,128)S(1)} %collective-permute-done.10.refs_2_, ...), custom_call_target="tpu_custom_call" | custom-call | tf_op jit(solution)/shard_map/pallas_call | solution.py:38
  36.6 11.6 %all_to_all.11 = f32[16,2,128]{2,1,0:T(2,128)S(1)} all-to-all(f32[16,2,128]{2,1,0:T(2,128)S(1)} %bitcast.9), channel_id=1, replica_groups=mesh['groups'=2,'patch'=4,'sub'=4] {'patch','sub'}, dimensions={0} | all-to-all | bytes 32768 | tf_op jit(solution)/shard_map/all_to_all | solution.py:555
  48.2 2.9 %shard_map.127 = (f32[32,128]{1,0:T(8,128)}, f32[2,3]{1,0:T(2,128)}) custom-call(s32[1]{0:T(128)} %bitcast.box, f32[160,128]{1,0:T(8,128)S(1)} %get-tuple-element.22.refs_0_, f32[160,128]{1,0:T(8,128)S(1)} %collective-permute-done.3.refs_1_, f32[160,128]{1,0:T(8,128)S(1)} %collective-permute-done.4.refs_2_, f32[160,128]{1,0:T(8,128)S(1)} %collective-permute-done.5.refs_3_, ...), custom_call_target="tpu_custom_call" | custom-call | tf_op jit(solution)/shard_map/pallas_call | solution.py:38
  (1 shorter events, 0.0 us)
Async XLA Ops:
  4.8 15.7 %collective-permute-start.6 = (f32[32,8,128]{2,1,0:T(8,128)S(1)}, f32[32,8,128]{2,1,0:T(8,128)S(1)}, u32[]{:S(2)}, u32[]{:S(2)}) collective-permute-start(f32[32,8,128]{2,1,0:T(8,128)S(1)} %get-tuple-element.23.refs_0_), channel_id=1, source_target_pairs={{0,1},{1,0},{2,3},{3,2},{4,5},{5,4},{6,7},{7,6},{8,9},{9,8},{10,11... | collective-permute-start | bytes 393224 | tf_op jit(solution)/shard_map/ppermute | solution.py:23
  5.4 4.4 %collective-permute-start = (f32[72,128]{1,0:T(8,128)S(1)}, f32[72,128]{1,0:T(8,128)S(1)}, u32[]{:S(2)}, u32[]{:S(2)}) collective-permute-start(f32[72,128]{1,0:T(8,128)S(1)} %get-tuple-element.21.refs_0_), channel_id=1, source_target_pairs={{0,1},{1,0},{2,3},{3,2},{4,5},{5,4},{6,7},{7,6},{8,9},{9,8},{10,11... | collective-permute-start | bytes 110600 | tf_op jit(solution)/shard_map/ppermute | solution.py:23
  5.4 15.2 %collective-permute-start.7 = (f32[32,8,128]{2,1,0:T(8,128)S(1)}, f32[32,8,128]{2,1,0:T(8,128)S(1)}, u32[]{:S(2)}, u32[]{:S(2)}) collective-permute-start(f32[32,8,128]{2,1,0:T(8,128)S(1)} %get-tuple-element.23.refs_0_), channel_id=1, source_target_pairs={{0,2},{1,3},{2,0},{3,1},{4,6},{5,7},{6,4},{7,5},{8,10},{9,11},{10,... | collective-permute-start | bytes 393224 | tf_op jit(solution)/shard_map/ppermute | solution.py:23
  8.4 12.2 %collective-permute-start.8 = (f32[32,8,128]{2,1,0:T(8,128)S(1)}, f32[32,8,128]{2,1,0:T(8,128)S(1)}, u32[]{:S(2)}, u32[]{:S(2)}) collective-permute-start(f32[32,8,128]{2,1,0:T(8,128)S(1)} %get-tuple-element.23.refs_0_), channel_id=1, source_target_pairs={{0,3},{1,2},{2,1},{3,0},{4,7},{5,6},{6,5},{7,4},{8,11},{9,10},{10,... | collective-permute-start | bytes 393224 | tf_op jit(solution)/shard_map/ppermute | solution.py:23
  8.4 7.7 %collective-permute-start.1 = (f32[72,128]{1,0:T(8,128)S(1)}, f32[72,128]{1,0:T(8,128)S(1)}, u32[]{:S(2)}, u32[]{:S(2)}) collective-permute-start(f32[72,128]{1,0:T(8,128)S(1)} %get-tuple-element.21.refs_0_), channel_id=1, source_target_pairs={{0,2},{1,3},{2,0},{3,1},{4,6},{5,7},{6,4},{7,5},{8,10},{9,11},{10,... | collective-permute-start | bytes 110600 | tf_op jit(solution)/shard_map/ppermute | solution.py:23
  9.8 6.3 %collective-permute-start.2 = (f32[72,128]{1,0:T(8,128)S(1)}, f32[72,128]{1,0:T(8,128)S(1)}, u32[]{:S(2)}, u32[]{:S(2)}) collective-permute-start(f32[72,128]{1,0:T(8,128)S(1)} %get-tuple-element.21.refs_0_), channel_id=1, source_target_pairs={{0,3},{1,2},{2,1},{3,0},{4,7},{5,6},{6,5},{7,4},{8,11},{9,10},{10,... | collective-permute-start | bytes 110600 | tf_op jit(solution)/shard_map/ppermute | solution.py:23
  16.1 11.5 %collective-permute-start.3 = (f32[160,128]{1,0:T(8,128)S(1)}, f32[160,128]{1,0:T(8,128)S(1)}, u32[]{:S(2)}, u32[]{:S(2)}) collective-permute-start(f32[160,128]{1,0:T(8,128)S(1)} %get-tuple-element.22.refs_0_), channel_id=1, source_target_pairs={{0,4},{4,0},{8,12},{12,8},{1,5},{5,1},{9,13},{13,9},{2,6},{6,2},{1... | collective-permute-start | bytes 245768 | tf_op jit(solution)/shard_map/ppermute | solution.py:23
  18.0 9.6 %collective-permute-start.4 = (f32[160,128]{1,0:T(8,128)S(1)}, f32[160,128]{1,0:T(8,128)S(1)}, u32[]{:S(2)}, u32[]{:S(2)}) collective-permute-start(f32[160,128]{1,0:T(8,128)S(1)} %get-tuple-element.22.refs_0_), channel_id=1, source_target_pairs={{0,8},{4,12},{8,0},{12,4},{1,9},{5,13},{9,1},{13,5},{2,10},{6,14},... | collective-permute-start | bytes 245768 | tf_op jit(solution)/shard_map/ppermute | solution.py:23
  20.6 7.0 %collective-permute-start.5 = (f32[160,128]{1,0:T(8,128)S(1)}, f32[160,128]{1,0:T(8,128)S(1)}, u32[]{:S(2)}, u32[]{:S(2)}) collective-permute-start(f32[160,128]{1,0:T(8,128)S(1)} %get-tuple-element.22.refs_0_), channel_id=1, source_target_pairs={{0,12},{4,8},{8,4},{12,0},{1,13},{5,9},{9,5},{13,1},{2,14},{6,10},... | collective-permute-start | bytes 245768 | tf_op jit(solution)/shard_map/ppermute | solution.py:23
  28.3 3.9 %collective-permute-start.10 = (f32[64,128]{1,0:T(8,128)S(1)}, f32[64,128]{1,0:T(8,128)S(1)}, u32[]{:S(2)}, u32[]{:S(2)}) collective-permute-start(f32[64,128]{1,0:T(8,128)S(1)} %get-tuple-element.31.refs_0_.refs_5_), channel_id=1, source_target_pairs={{0,2},{1,3},{2,0},{3,1},{4,6},{5,7},{6,4},{7,5},{8,10},{9,11},{10,... | collective-permute-start | bytes 98312 | tf_op jit(solution)/shard_map/ppermute | solution.py:23
  30.0 3.3 %collective-permute-start.11 = (f32[64,128]{1,0:T(8,128)S(1)}, f32[64,128]{1,0:T(8,128)S(1)}, u32[]{:S(2)}, u32[]{:S(2)}) collective-permute-start(f32[64,128]{1,0:T(8,128)S(1)} %get-tuple-element.31.refs_0_.refs_5_), channel_id=1, source_target_pairs={{0,3},{1,2},{2,1},{3,0},{4,7},{5,6},{6,5},{7,4},{8,11},{9,10},{10,... | collective-permute-start | bytes 98312 | tf_op jit(solution)/shard_map/ppermute | solution.py:23
  30.0 3.3 %collective-permute-start.9 = (f32[64,128]{1,0:T(8,128)S(1)}, f32[64,128]{1,0:T(8,128)S(1)}, u32[]{:S(2)}, u32[]{:S(2)}) collective-permute-start(f32[64,128]{1,0:T(8,128)S(1)} %get-tuple-element.31.refs_0_.refs_5_), channel_id=1, source_target_pairs={{0,1},{1,0},{2,3},{3,2},{4,5},{5,4},{6,7},{7,6},{8,9},{9,8},{10,11... | collective-permute-start | bytes 98312 | tf_op jit(solution)/shard_map/ppermute | solution.py:23

commit v9 on v8

--- a/solution.py
+++ b/solution.py
@@ -502,8 +502,9 @@
         ],
     )
     leaf_basis, leaf_coupling, box_coupling = matrices
+    messages = from_peers(message, "sub")
+    geometry, messages = lax.optimization_barrier((geometry, messages))
     geometry = from_peers(geometry, "sub")
-    messages = from_peers(message, "sub")
     moments, blocks = device_call(
         functools.partial(join_kernel, subs),
         [kept(sources, LANES), kept(subs * span, LANES)],

time: 51.3 us -> 49.7 us (0.969)
  waiting for transfers between devices: 8.87 us -> 7.38 us
    ppermute x12, waiting for transfers between devices: 8.87 us -> 7.38 us  [from_peers(): lax.ppermute(value, axis, [(i, i ^ turn) for i in range(size)])]
  transfers between devices with their start and end apart: 12 -> 12, of which waited for: 3 -> 6; matrix products, arithmetic and copies ran while one was open for 0% -> 0% of each run, Pallas kernels for 14% -> 14%
where the time goes in v9:
time: 49.7 us; the launch traced here: 49.4 us
  Pallas kernels  17.3 us (35%)
  blocking collectives  11.8 us (24%)
  starting transfers between devices  11.6 us (23%)
  waiting for transfers between devices  7.38 us (15%)
  between operations  1.34 us (3%)
    pallas_call x6, Pallas kernels, device_call(): pl.pallas_call(kernel, out_shape=tuple(outputs), in_specs=[smem] * len(sc...  17.3 us
    all_to_all x1, blocking collectives, shards(): shares = lax.all_to_all(shares, ('patch', 'sub'), 0, 0, tiled=True)  11.8 us
    ppermute x12, starting transfers between devices, from_peers(): lax.ppermute(value, axis, [(i, i ^ turn) for i in range(size)])  11.6 us
    ppermute x12, waiting for transfers between devices, from_peers(): lax.ppermute(value, axis, [(i, i ^ turn) for i in range(size)])  7.38 us
  transfers between devices with their start and end apart: 12, of which 6 were waited for; matrix products, arithmetic and copies ran while one was open for 0% of the time, Pallas kernels for 14%

profile of v9, /device:TPU:0, one launch (start us, length us, event | category | flops | bytes accessed | tf_op | source)
XLA Modules:
  0.0 49.4 jit_solution(17208185295050124603)
XLA Ops:
  1.3 3.6 %shard_map.122 = (f32[32,8,128]{2,1,0:T(8,128)S(1)}, f32[72,128]{1,0:T(8,128)S(1)}, f32[32,64,128]{2,1,0:T(8,128)S(1)}, f32[32,64,128]{2,1,0:T(8,128)S(1)}, f32[...) custom-call(s32[1]{0:T(128)S(6)} %copy.13.counts, f32[3,32,128]{2,1,0:T(8,128)} %bitcast.10, f32[3,32,128]{2,1,0:T(8,128)} %bitcast.11, ...), custom_call_target="tpu_custom_call" | custom-call | tf_op jit(solution)/shard_map/pallas_call | solution.py:38
  4.8 0.5 %collective-permute-start = (f32[72,128]{1,0:T(8,128)S(1)}, f32[72,128]{1,0:T(8,128)S(1)}, u32[]{:S(2)}, u32[]{:S(2)}) collective-permute-start(f32[72,128]{1,0:T(8,128)S(1)} %get-tuple-element.28.refs_0_), channel_id=1, source_target_pairs={{0,1},{1,0},{2,3},{3,2},{4,5},{5,4},{6,7},{7,6},{8,9},{9,8},{10,11... | collective-permute-start | bytes 110600 | tf_op jit(solution)/shard_map/ppermute | solution.py:23
  5.4 2.6 %collective-permute-start.1 = (f32[72,128]{1,0:T(8,128)S(1)}, f32[72,128]{1,0:T(8,128)S(1)}, u32[]{:S(2)}, u32[]{:S(2)}) collective-permute-start(f32[72,128]{1,0:T(8,128)S(1)} %get-tuple-element.28.refs_0_), channel_id=1, source_target_pairs={{0,2},{1,3},{2,0},{3,1},{4,6},{5,7},{6,4},{7,5},{8,10},{9,11},{10,... | collective-permute-start | bytes 110600 | tf_op jit(solution)/shard_map/ppermute | solution.py:23
  7.9 0.1 collective-permute-start.2
  8.0 0.0 collective-permute-done.refs_1_
  8.0 2.0 %collective-permute-done.1.refs_2_ = f32[72,128]{1,0:T(8,128)S(1)} collective-permute-done((f32[72,128]{1,0:T(8,128)S(1)}, f32[72,128]{1,0:T(8,128)S(1)}, u32[]{:S(2)}, u32[]{:S(2)}) %collective-permute-start.1) | collective-permute-done | bytes 36896 | tf_op jit(solution)/shard_map/ppermute | solution.py:23
  10.0 1.4 %collective-permute-done.2.refs_3_ = f32[72,128]{1,0:T(8,128)S(1)} collective-permute-done((f32[72,128]{1,0:T(8,128)S(1)}, f32[72,128]{1,0:T(8,128)S(1)}, u32[]{:S(2)}, u32[]{:S(2)}) %collective-permute-start.2) | collective-permute-done | bytes 36896 | tf_op jit(solution)/shard_map/ppermute | solution.py:23
  11.4 0.2 collective-permute-start.6
  11.5 0.8 %collective-permute-start.7 = (f32[32,8,128]{2,1,0:T(8,128)S(1)}, f32[32,8,128]{2,1,0:T(8,128)S(1)}, u32[]{:S(2)}, u32[]{:S(2)}) collective-permute-start(f32[32,8,128]{2,1,0:T(8,128)S(1)} %get-tuple-element.33.refs_0_), channel_id=1, source_target_pairs={{0,2},{1,3},{2,0},{3,1},{4,6},{5,7},{6,4},{7,5},{8,10},{9,11},{10,... | collective-permute-start | bytes 393224 | tf_op jit(solution)/shard_map/ppermute | solution.py:23
  12.4 0.9 %collective-permute-start.8 = (f32[32,8,128]{2,1,0:T(8,128)S(1)}, f32[32,8,128]{2,1,0:T(8,128)S(1)}, u32[]{:S(2)}, u32[]{:S(2)}) collective-permute-start(f32[32,8,128]{2,1,0:T(8,128)S(1)} %get-tuple-element.33.refs_0_), channel_id=1, source_target_pairs={{0,3},{1,2},{2,1},{3,0},{4,7},{5,6},{6,5},{7,4},{8,11},{9,10},{10,... | collective-permute-start | bytes 393224 | tf_op jit(solution)/shard_map/ppermute | solution.py:23
  13.2 1.6 %collective-permute-start.3 = (f32[160,128]{1,0:T(8,128)S(1)}, f32[160,128]{1,0:T(8,128)S(1)}, u32[]{:S(2)}, u32[]{:S(2)}) collective-permute-start(f32[160,128]{1,0:T(8,128)S(1)} %get-tuple-element.32.refs_0_), channel_id=1, source_target_pairs={{0,4},{4,0},{8,12},{12,8},{1,5},{5,1},{9,13},{13,9},{2,6},{6,2},{1... | collective-permute-start | bytes 245768 | tf_op jit(solution)/shard_map/ppermute | solution.py:23
  14.9 2.6 %collective-permute-start.4 = (f32[160,128]{1,0:T(8,128)S(1)}, f32[160,128]{1,0:T(8,128)S(1)}, u32[]{:S(2)}, u32[]{:S(2)}) collective-permute-start(f32[160,128]{1,0:T(8,128)S(1)} %get-tuple-element.32.refs_0_), channel_id=1, source_target_pairs={{0,8},{4,12},{8,0},{12,4},{1,9},{5,13},{9,1},{13,5},{2,10},{6,14},... | collective-permute-start | bytes 245768 | tf_op jit(solution)/shard_map/ppermute | solution.py:23
  17.5 0.0 collective-permute-done.6.refs_1_
  17.5 0.2 collective-permute-start.5
  17.7 0.1 collective-permute-done.7.refs_2_
  17.9 1.7 %collective-permute-done.8.refs_3_ = f32[32,8,128]{2,1,0:T(8,128)S(1)} collective-permute-done((f32[32,8,128]{2,1,0:T(8,128)S(1)}, f32[32,8,128]{2,1,0:T(8,128)S(1)}, u32[]{:S(2)}, u32[]{:S(2)}) %collective-permute-start.8) | collective-permute-done | bytes 131104 | tf_op jit(solution)/shard_map/ppermute | solution.py:23
  19.5 6.9 %shard_map.124 = (f32[32,128]{1,0:T(8,128)S(1)}, f32[32,128]{1,0:T(8,128)S(1)}, f32[288,128,128]{2,1,0:T(8,128)S(1)}, bf16[256,128]{1,0:T(8,128)(2,1)S(1)}) custom-call(s32[1]{0:T(128)} %bitcast.box, s32[1]{0:T(128)S(6)} %copy.13.counts, f32[32,8,128]{2,1,0:T(8,128)S(1)} %get-tuple-element.33.refs_0_, f32[32,8,128]{2,1,0:T(8,128)S(1)} %collective-permute-done.6.refs_1_, ...), custom_call_target="tpu_custom_call" | custom-call | tf_op jit(solution)/shard_map/pallas_call | solution.py:38
  26.4 0.0 collective-permute-done.3.refs_1_
  26.5 0.0 collective-permute-done.4.refs_2_
  26.5 0.0 collective-permute-done.5.refs_3_
  26.5 0.7 %shard_map.125 = (f32[64,128]{1,0:T(8,128)S(1)}, f32[32,128]{1,0:T(8,128)S(1)}, f32[8,128]{1,0:T(8,128)S(1)}) custom-call(s32[1]{0:T(128)} %bitcast.box, f32[160,128]{1,0:T(8,128)S(1)} %get-tuple-element.32.refs_0_, f32[160,128]{1,0:T(8,128)S(1)} %collective-permute-done.3.refs_1_, f32[160,128]{1,0:T(8,128)S(1)} %collective-permute-done.4.refs_2_, ...), custom_call_target="tpu_custom_call" | custom-call | tf_op jit(solution)/shard_map/pallas_call | solution.py:38
  27.1 0.8 %collective-permute-start.10 = (f32[64,128]{1,0:T(8,128)S(1)}, f32[64,128]{1,0:T(8,128)S(1)}, u32[]{:S(2)}, u32[]{:S(2)}) collective-permute-start(f32[64,128]{1,0:T(8,128)S(1)} %get-tuple-element.41.refs_0_.refs_5_), channel_id=1, source_target_pairs={{0,2},{1,3},{2,0},{3,1},{4,6},{5,7},{6,4},{7,5},{8,10},{9,11},{10,... | collective-permute-start | bytes 98312 | tf_op jit(solution)/shard_map/ppermute | solution.py:23
  27.9 1.3 %collective-permute-start.11 = (f32[64,128]{1,0:T(8,128)S(1)}, f32[64,128]{1,0:T(8,128)S(1)}, u32[]{:S(2)}, u32[]{:S(2)}) collective-permute-start(f32[64,128]{1,0:T(8,128)S(1)} %get-tuple-element.41.refs_0_.refs_5_), channel_id=1, source_target_pairs={{0,3},{1,2},{2,1},{3,0},{4,7},{5,6},{6,5},{7,4},{8,11},{9,10},{10,... | collective-permute-start | bytes 98312 | tf_op jit(solution)/shard_map/ppermute | solution.py:23
  29.2 0.1 collective-permute-start.9
  29.3 2.1 %collective-permute-done.10.refs_2_ = f32[64,128]{1,0:T(8,128)S(1)} collective-permute-done((f32[64,128]{1,0:T(8,128)S(1)}, f32[64,128]{1,0:T(8,128)S(1)}, u32[]{:S(2)}, u32[]{:S(2)}) %collective-permute-start.10) | collective-permute-done | bytes 32800 | tf_op jit(solution)/shard_map/ppermute | solution.py:23
  31.4 0.1 collective-permute-done.11.refs_3_
  31.5 0.0 collective-permute-done.9.refs_1_
  31.5 3.2 %shard_map.126 = (f32[32,128]{1,0:T(8,128)S(1)}, f32[32,128]{1,0:T(8,128)S(1)}) custom-call(s32[1]{0:T(128)} %bitcast.box, s32[1]{0:T(128)S(6)} %copy.13.counts, f32[64,128]{1,0:T(8,128)S(1)} %get-tuple-element.41.refs_0_.refs_5_, f32[64,128]{1,0:T(8,128)S(1)} %collective-permute-done.9.refs_1_, f32[64,128]{1,0:T(8,128)S(1)} %collective-permute-done.10.refs_2_, ...), custom_call_target="tpu_custom_call" | custom-call | tf_op jit(solution)/shard_map/pallas_call | solution.py:38
  34.8 11.8 %all_to_all.11 = f32[16,2,128]{2,1,0:T(2,128)S(1)} all-to-all(f32[16,2,128]{2,1,0:T(2,128)S(1)} %bitcast.9), channel_id=1, replica_groups=mesh['groups'=2,'patch'=4,'sub'=4] {'patch','sub'}, dimensions={0} | all-to-all | bytes 32768 | tf_op jit(solution)/shard_map/all_to_all | solution.py:556
  46.6 2.9 %shard_map.127 = (f32[32,128]{1,0:T(8,128)}, f32[2,3]{1,0:T(2,128)}) custom-call(s32[1]{0:T(128)} %bitcast.box, f32[160,128]{1,0:T(8,128)S(1)} %get-tuple-element.32.refs_0_, f32[160,128]{1,0:T(8,128)S(1)} %collective-permute-done.3.refs_1_, f32[160,128]{1,0:T(8,128)S(1)} %collective-permute-done.4.refs_2_, f32[160,128]{1,0:T(8,128)S(1)} %collective-permute-done.5.refs_3_, ...), custom_call_target="tpu_custom_call" | custom-call | tf_op jit(solution)/shard_map/pallas_call | solution.py:38
  (1 shorter events, 0.0 us)
Async XLA Ops:
  4.8 3.2 %collective-permute-start = (f32[72,128]{1,0:T(8,128)S(1)}, f32[72,128]{1,0:T(8,128)S(1)}, u32[]{:S(2)}, u32[]{:S(2)}) collective-permute-start(f32[72,128]{1,0:T(8,128)S(1)} %get-tuple-element.28.refs_0_), channel_id=1, source_target_pairs={{0,1},{1,0},{2,3},{3,2},{4,5},{5,4},{6,7},{7,6},{8,9},{9,8},{10,11... | collective-permute-start | bytes 110600 | tf_op jit(solution)/shard_map/ppermute | solution.py:23
  5.4 4.6 %collective-permute-start.1 = (f32[72,128]{1,0:T(8,128)S(1)}, f32[72,128]{1,0:T(8,128)S(1)}, u32[]{:S(2)}, u32[]{:S(2)}) collective-permute-start(f32[72,128]{1,0:T(8,128)S(1)} %get-tuple-element.28.refs_0_), channel_id=1, source_target_pairs={{0,2},{1,3},{2,0},{3,1},{4,6},{5,7},{6,4},{7,5},{8,10},{9,11},{10,... | collective-permute-start | bytes 110600 | tf_op jit(solution)/shard_map/ppermute | solution.py:23
  7.9 3.4 %collective-permute-start.2 = (f32[72,128]{1,0:T(8,128)S(1)}, f32[72,128]{1,0:T(8,128)S(1)}, u32[]{:S(2)}, u32[]{:S(2)}) collective-permute-start(f32[72,128]{1,0:T(8,128)S(1)} %get-tuple-element.28.refs_0_), channel_id=1, source_target_pairs={{0,3},{1,2},{2,1},{3,0},{4,7},{5,6},{6,5},{7,4},{8,11},{9,10},{10,... | collective-permute-start | bytes 110600 | tf_op jit(solution)/shard_map/ppermute | solution.py:23
  11.4 6.1 %collective-permute-start.6 = (f32[32,8,128]{2,1,0:T(8,128)S(1)}, f32[32,8,128]{2,1,0:T(8,128)S(1)}, u32[]{:S(2)}, u32[]{:S(2)}) collective-permute-start(f32[32,8,128]{2,1,0:T(8,128)S(1)} %get-tuple-element.33.refs_0_), channel_id=1, source_target_pairs={{0,1},{1,0},{2,3},{3,2},{4,5},{5,4},{6,7},{7,6},{8,9},{9,8},{10,11... | collective-permute-start | bytes 393224 | tf_op jit(solution)/shard_map/ppermute | solution.py:23
  11.5 6.3 %collective-permute-start.7 = (f32[32,8,128]{2,1,0:T(8,128)S(1)}, f32[32,8,128]{2,1,0:T(8,128)S(1)}, u32[]{:S(2)}, u32[]{:S(2)}) collective-permute-start(f32[32,8,128]{2,1,0:T(8,128)S(1)} %get-tuple-element.33.refs_0_), channel_id=1, source_target_pairs={{0,2},{1,3},{2,0},{3,1},{4,6},{5,7},{6,4},{7,5},{8,10},{9,11},{10,... | collective-permute-start | bytes 393224 | tf_op jit(solution)/shard_map/ppermute | solution.py:23
  12.4 7.1 %collective-permute-start.8 = (f32[32,8,128]{2,1,0:T(8,128)S(1)}, f32[32,8,128]{2,1,0:T(8,128)S(1)}, u32[]{:S(2)}, u32[]{:S(2)}) collective-permute-start(f32[32,8,128]{2,1,0:T(8,128)S(1)} %get-tuple-element.33.refs_0_), channel_id=1, source_target_pairs={{0,3},{1,2},{2,1},{3,0},{4,7},{5,6},{6,5},{7,4},{8,11},{9,10},{10,... | collective-permute-start | bytes 393224 | tf_op jit(solution)/shard_map/ppermute | solution.py:23
  13.2 13.2 %collective-permute-start.3 = (f32[160,128]{1,0:T(8,128)S(1)}, f32[160,128]{1,0:T(8,128)S(1)}, u32[]{:S(2)}, u32[]{:S(2)}) collective-permute-start(f32[160,128]{1,0:T(8,128)S(1)} %get-tuple-element.32.refs_0_), channel_id=1, source_target_pairs={{0,4},{4,0},{8,12},{12,8},{1,5},{5,1},{9,13},{13,9},{2,6},{6,2},{1... | collective-permute-start | bytes 245768 | tf_op jit(solution)/shard_map/ppermute | solution.py:23
  14.9 11.6 %collective-permute-start.4 = (f32[160,128]{1,0:T(8,128)S(1)}, f32[160,128]{1,0:T(8,128)S(1)}, u32[]{:S(2)}, u32[]{:S(2)}) collective-permute-start(f32[160,128]{1,0:T(8,128)S(1)} %get-tuple-element.32.refs_0_), channel_id=1, source_target_pairs={{0,8},{4,12},{8,0},{12,4},{1,9},{5,13},{9,1},{13,5},{2,10},{6,14},... | collective-permute-start | bytes 245768 | tf_op jit(solution)/shard_map/ppermute | solution.py:23
  17.5 9.0 %collective-permute-start.5 = (f32[160,128]{1,0:T(8,128)S(1)}, f32[160,128]{1,0:T(8,128)S(1)}, u32[]{:S(2)}, u32[]{:S(2)}) collective-permute-start(f32[160,128]{1,0:T(8,128)S(1)} %get-tuple-element.32.refs_0_), channel_id=1, source_target_pairs={{0,12},{4,8},{8,4},{12,0},{1,13},{5,9},{9,5},{13,1},{2,14},{6,10},... | collective-permute-start | bytes 245768 | tf_op jit(solution)/shard_map/ppermute | solution.py:23
  27.1 4.2 %collective-permute-start.10 = (f32[64,128]{1,0:T(8,128)S(1)}, f32[64,128]{1,0:T(8,128)S(1)}, u32[]{:S(2)}, u32[]{:S(2)}) collective-permute-start(f32[64,128]{1,0:T(8,128)S(1)} %get-tuple-element.41.refs_0_.refs_5_), channel_id=1, source_target_pairs={{0,2},{1,3},{2,0},{3,1},{4,6},{5,7},{6,4},{7,5},{8,10},{9,11},{10,... | collective-permute-start | bytes 98312 | tf_op jit(solution)/shard_map/ppermute | solution.py:23
  27.9 3.6 %collective-permute-start.11 = (f32[64,128]{1,0:T(8,128)S(1)}, f32[64,128]{1,0:T(8,128)S(1)}, u32[]{:S(2)}, u32[]{:S(2)}) collective-permute-start(f32[64,128]{1,0:T(8,128)S(1)} %get-tuple-element.41.refs_0_.refs_5_), channel_id=1, source_target_pairs={{0,3},{1,2},{2,1},{3,0},{4,7},{5,6},{6,5},{7,4},{8,11},{9,10},{10,... | collective-permute-start | bytes 98312 | tf_op jit(solution)/shard_map/ppermute | solution.py:23
  29.2 2.3 %collective-permute-start.9 = (f32[64,128]{1,0:T(8,128)S(1)}, f32[64,128]{1,0:T(8,128)S(1)}, u32[]{:S(2)}, u32[]{:S(2)}) collective-permute-start(f32[64,128]{1,0:T(8,128)S(1)} %get-tuple-element.41.refs_0_.refs_5_), channel_id=1, source_target_pairs={{0,1},{1,0},{2,3},{3,2},{4,5},{5,4},{6,7},{7,6},{8,9},{9,8},{10,11... | collective-permute-start | bytes 98312 | tf_op jit(solution)/shard_map/ppermute | solution.py:23

commit v10 on v9

--- a/solution.py
+++ b/solution.py
@@ -15,6 +15,7 @@
 LANES = 128
 TILE_ROWS = 8
 VMEM_LIMIT = 16 << 20
+FIRST = pl.CostEstimate(flops=10**11, bytes_accessed=10**10, transcendentals=0)
 
 
 def from_peers(value, axis):
@@ -31,7 +32,7 @@
     return parts[0]
 
 
-def device_call(kernel, outputs, scalars, arrays, scratch=(), remote=()):
+def device_call(kernel, outputs, scalars, arrays, scratch=(), remote=(), cost=None):
     smem = pl.BlockSpec(memory_space=pltpu.SMEM)
     vmem = pl.BlockSpec(memory_space=pltpu.VMEM)
     hbm = pl.BlockSpec(memory_space=pltpu.HBM)
@@ -42,6 +43,7 @@
         out_specs=tuple([vmem] * len(outputs)),
         scratch_shapes=tuple(scratch),
         compiler_params=pltpu.CompilerParams(vmem_limit_bytes=VMEM_LIMIT),
+        cost_estimate=cost,
     )(
         *scalars,
         *[pltpu.with_memory_space_constraint(array, pltpu.VMEM) for array in arrays],
@@ -503,13 +505,13 @@
     )
     leaf_basis, leaf_coupling, box_coupling = matrices
     messages = from_peers(message, "sub")
-    geometry, messages = lax.optimization_barrier((geometry, messages))
     geometry = from_peers(geometry, "sub")
     moments, blocks = device_call(
         functools.partial(join_kernel, subs),
         [kept(sources, LANES), kept(subs * span, LANES)],
         [],
         messages,
+        cost=FIRST,
     )
     boxes = from_peers(blocks, "patch")
     gather = pltpu.VMEM((patches * subs * span, LANES), jnp.float32)

time: 49.7 us -> 47 us (0.946)
  waiting for transfers between devices: 7.38 us -> 4.56 us
    ppermute x12, waiting for transfers between devices: 7.38 us -> 4.56 us  [from_peers(): lax.ppermute(value, axis, [(i, i ^ turn) for i in range(size)])]
  transfers between devices with their start and end apart: 12 -> 12, of which waited for: 6 -> 4; matrix products, arithmetic and copies ran while one was open for 0% -> 0% of each run, Pallas kernels for 14% -> 15%
where the time goes in v10:
time: 47 us; the launch traced here: 46.7 us
  Pallas kernels  17.3 us (37%)
  starting transfers between devices  11.8 us (25%)
  blocking collectives  11.7 us (25%)
  waiting for transfers between devices  4.56 us (10%)
  between operations  1.34 us (3%)
    pallas_call x6, Pallas kernels, device_call(): pl.pallas_call(kernel, out_shape=tuple(outputs), in_specs=[smem] * len(sc...  17.3 us
    ppermute x12, starting transfers between devices, from_peers(): lax.ppermute(value, axis, [(i, i ^ turn) for i in range(size)])  11.8 us
    all_to_all x1, blocking collectives, shards(): shares = lax.all_to_all(shares, ('patch', 'sub'), 0, 0, tiled=True)  11.7 us
    ppermute x12, waiting for transfers between devices, from_peers(): lax.ppermute(value, axis, [(i, i ^ turn) for i in range(size)])  4.56 us
  transfers between devices with their start and end apart: 12, of which 4 were waited for; matrix products, arithmetic and copies ran while one was open for 0% of the time, Pallas kernels for 15%

profile of v10, /device:TPU:0, one launch (start us, length us, event | category | flops | bytes accessed | tf_op | source)
XLA Modules:
  0.0 46.7 jit_solution(5598502675158466314)
XLA Ops:
  1.3 3.6 %shard_map.122 = (f32[32,8,128]{2,1,0:T(8,128)S(1)}, f32[72,128]{1,0:T(8,128)S(1)}, f32[32,64,128]{2,1,0:T(8,128)S(1)}, f32[32,64,128]{2,1,0:T(8,128)S(1)}, f32[...) custom-call(s32[1]{0:T(128)S(6)} %copy.13.counts, f32[3,32,128]{2,1,0:T(8,128)} %bitcast.10, f32[3,32,128]{2,1,0:T(8,128)} %bitcast.11, ...), custom_call_target="tpu_custom_call" | custom-call | tf_op jit(solution)/shard_map/pallas_call | solution.py:39
  4.8 0.5 %collective-permute-start = (f32[72,128]{1,0:T(8,128)S(1)}, f32[72,128]{1,0:T(8,128)S(1)}, u32[]{:S(2)}, u32[]{:S(2)}) collective-permute-start(f32[72,128]{1,0:T(8,128)S(1)} %get-tuple-element.21.refs_0_), channel_id=1, source_target_pairs={{0,1},{1,0},{2,3},{3,2},{4,5},{5,4},{6,7},{7,6},{8,9},{9,8},{10,11... | collective-permute-start | bytes 110600 | tf_op jit(solution)/shard_map/ppermute | solution.py:24
  5.4 2.6 %collective-permute-start.1 = (f32[72,128]{1,0:T(8,128)S(1)}, f32[72,128]{1,0:T(8,128)S(1)}, u32[]{:S(2)}, u32[]{:S(2)}) collective-permute-start(f32[72,128]{1,0:T(8,128)S(1)} %get-tuple-element.21.refs_0_), channel_id=1, source_target_pairs={{0,2},{1,3},{2,0},{3,1},{4,6},{5,7},{6,4},{7,5},{8,10},{9,11},{10,... | collective-permute-start | bytes 110600 | tf_op jit(solution)/shard_map/ppermute | solution.py:24
  7.9 0.1 collective-permute-start.2
  8.0 0.1 collective-permute-start.6
  8.1 1.9 %collective-permute-start.7 = (f32[32,8,128]{2,1,0:T(8,128)S(1)}, f32[32,8,128]{2,1,0:T(8,128)S(1)}, u32[]{:S(2)}, u32[]{:S(2)}) collective-permute-start(f32[32,8,128]{2,1,0:T(8,128)S(1)} %get-tuple-element.23.refs_0_), channel_id=1, source_target_pairs={{0,2},{1,3},{2,0},{3,1},{4,6},{5,7},{6,4},{7,5},{8,10},{9,11},{10,... | collective-permute-start | bytes 393224 | tf_op jit(solution)/shard_map/ppermute | solution.py:24
  10.1 0.0 collective-permute-done.refs_1_
  10.1 0.0 collective-permute-start.8
  10.1 0.0 collective-permute-done.1.refs_2_
  10.1 1.3 %collective-permute-done.2.refs_3_ = f32[72,128]{1,0:T(8,128)S(1)} collective-permute-done((f32[72,128]{1,0:T(8,128)S(1)}, f32[72,128]{1,0:T(8,128)S(1)}, u32[]{:S(2)}, u32[]{:S(2)}) %collective-permute-start.2) | collective-permute-done | bytes 36896 | tf_op jit(solution)/shard_map/ppermute | solution.py:24
  11.4 1.6 %collective-permute-start.3 = (f32[160,128]{1,0:T(8,128)S(1)}, f32[160,128]{1,0:T(8,128)S(1)}, u32[]{:S(2)}, u32[]{:S(2)}) collective-permute-start(f32[160,128]{1,0:T(8,128)S(1)} %get-tuple-element.22.refs_0_), channel_id=1, source_target_pairs={{0,4},{4,0},{8,12},{12,8},{1,5},{5,1},{9,13},{13,9},{2,6},{6,2},{1... | collective-permute-start | bytes 245768 | tf_op jit(solution)/shard_map/ppermute | solution.py:24
  13.0 2.6 %collective-permute-start.4 = (f32[160,128]{1,0:T(8,128)S(1)}, f32[160,128]{1,0:T(8,128)S(1)}, u32[]{:S(2)}, u32[]{:S(2)}) collective-permute-start(f32[160,128]{1,0:T(8,128)S(1)} %get-tuple-element.22.refs_0_), channel_id=1, source_target_pairs={{0,8},{4,12},{8,0},{12,4},{1,9},{5,13},{9,1},{13,5},{2,10},{6,14},... | collective-permute-start | bytes 245768 | tf_op jit(solution)/shard_map/ppermute | solution.py:24
  15.6 0.0 collective-permute-done.6.refs_1_
  15.6 0.2 collective-permute-start.5
  15.8 0.0 collective-permute-done.7.refs_2_
  15.8 1.1 %collective-permute-done.8.refs_3_ = f32[32,8,128]{2,1,0:T(8,128)S(1)} collective-permute-done((f32[32,8,128]{2,1,0:T(8,128)S(1)}, f32[32,8,128]{2,1,0:T(8,128)S(1)}, u32[]{:S(2)}, u32[]{:S(2)}) %collective-permute-start.8) | collective-permute-done | bytes 131104 | tf_op jit(solution)/shard_map/ppermute | solution.py:24
  17.0 6.9 %shard_map.124 = (f32[32,128]{1,0:T(8,128)S(1)}, f32[32,128]{1,0:T(8,128)S(1)}, f32[288,128,128]{2,1,0:T(8,128)S(1)}, bf16[256,128]{1,0:T(8,128)(2,1)S(1)}) custom-call(s32[1]{0:T(128)} %bitcast.box, s32[1]{0:T(128)S(6)} %copy.13.counts, f32[32,8,128]{2,1,0:T(8,128)S(1)} %get-tuple-element.23.refs_0_, f32[32,8,128]{2,1,0:T(8,128)S(1)} %collective-permute-done.6.refs_1_, ...), custom_call_target="tpu_custom_call" | custom-call | tf_op jit(solution)/shard_map/pallas_call | solution.py:39
  23.9 0.0 collective-permute-done.3.refs_1_
  23.9 0.0 collective-permute-done.4.refs_2_
  23.9 0.0 collective-permute-done.5.refs_3_
  23.9 0.7 %shard_map.125 = (f32[64,128]{1,0:T(8,128)S(1)}, f32[32,128]{1,0:T(8,128)S(1)}, f32[8,128]{1,0:T(8,128)S(1)}) custom-call(s32[1]{0:T(128)} %bitcast.box, f32[160,128]{1,0:T(8,128)S(1)} %get-tuple-element.22.refs_0_, f32[160,128]{1,0:T(8,128)S(1)} %collective-permute-done.3.refs_1_, f32[160,128]{1,0:T(8,128)S(1)} %collective-permute-done.4.refs_2_, ...), custom_call_target="tpu_custom_call" | custom-call | tf_op jit(solution)/shard_map/pallas_call | solution.py:39
  24.6 0.7 %collective-permute-start.10 = (f32[64,128]{1,0:T(8,128)S(1)}, f32[64,128]{1,0:T(8,128)S(1)}, u32[]{:S(2)}, u32[]{:S(2)}) collective-permute-start(f32[64,128]{1,0:T(8,128)S(1)} %get-tuple-element.31.refs_0_.refs_5_), channel_id=1, source_target_pairs={{0,2},{1,3},{2,0},{3,1},{4,6},{5,7},{6,4},{7,5},{8,10},{9,11},{10,... | collective-permute-start | bytes 98312 | tf_op jit(solution)/shard_map/ppermute | solution.py:24
  25.3 0.8 %collective-permute-start.11 = (f32[64,128]{1,0:T(8,128)S(1)}, f32[64,128]{1,0:T(8,128)S(1)}, u32[]{:S(2)}, u32[]{:S(2)}) collective-permute-start(f32[64,128]{1,0:T(8,128)S(1)} %get-tuple-element.31.refs_0_.refs_5_), channel_id=1, source_target_pairs={{0,3},{1,2},{2,1},{3,0},{4,7},{5,6},{6,5},{7,4},{8,11},{9,10},{10,... | collective-permute-start | bytes 98312 | tf_op jit(solution)/shard_map/ppermute | solution.py:24
  26.1 0.6 %collective-permute-start.9 = (f32[64,128]{1,0:T(8,128)S(1)}, f32[64,128]{1,0:T(8,128)S(1)}, u32[]{:S(2)}, u32[]{:S(2)}) collective-permute-start(f32[64,128]{1,0:T(8,128)S(1)} %get-tuple-element.31.refs_0_.refs_5_), channel_id=1, source_target_pairs={{0,1},{1,0},{2,3},{3,2},{4,5},{5,4},{6,7},{7,6},{8,9},{9,8},{10,11... | collective-permute-start | bytes 98312 | tf_op jit(solution)/shard_map/ppermute | solution.py:24
  26.8 2.0 %collective-permute-done.10.refs_2_ = f32[64,128]{1,0:T(8,128)S(1)} collective-permute-done((f32[64,128]{1,0:T(8,128)S(1)}, f32[64,128]{1,0:T(8,128)S(1)}, u32[]{:S(2)}, u32[]{:S(2)}) %collective-permute-start.10) | collective-permute-done | bytes 32800 | tf_op jit(solution)/shard_map/ppermute | solution.py:24
  28.8 0.1 collective-permute-done.11.refs_3_
  28.9 0.0 collective-permute-done.9.refs_1_
  28.9 3.3 %shard_map.126 = (f32[32,128]{1,0:T(8,128)S(1)}, f32[32,128]{1,0:T(8,128)S(1)}) custom-call(s32[1]{0:T(128)} %bitcast.box, s32[1]{0:T(128)S(6)} %copy.13.counts, f32[64,128]{1,0:T(8,128)S(1)} %get-tuple-element.31.refs_0_.refs_5_, f32[64,128]{1,0:T(8,128)S(1)} %collective-permute-done.9.refs_1_, f32[64,128]{1,0:T(8,128)S(1)} %collective-permute-done.10.refs_2_, ...), custom_call_target="tpu_custom_call" | custom-call | tf_op jit(solution)/shard_map/pallas_call | solution.py:39
  32.2 11.7 %all_to_all.11 = f32[16,2,128]{2,1,0:T(2,128)S(1)} all-to-all(f32[16,2,128]{2,1,0:T(2,128)S(1)} %bitcast.9), channel_id=1, replica_groups=mesh['groups'=2,'patch'=4,'sub'=4] {'patch','sub'}, dimensions={0} | all-to-all | bytes 32768 | tf_op jit(solution)/shard_map/all_to_all | solution.py:558
  43.9 2.9 %shard_map.127 = (f32[32,128]{1,0:T(8,128)}, f32[2,3]{1,0:T(2,128)}) custom-call(s32[1]{0:T(128)} %bitcast.box, f32[160,128]{1,0:T(8,128)S(1)} %get-tuple-element.22.refs_0_, f32[160,128]{1,0:T(8,128)S(1)} %collective-permute-done.3.refs_1_, f32[160,128]{1,0:T(8,128)S(1)} %collective-permute-done.4.refs_2_, f32[160,128]{1,0:T(8,128)S(1)} %collective-permute-done.5.refs_3_, ...), custom_call_target="tpu_custom_call" | custom-call | tf_op jit(solution)/shard_map/pallas_call | solution.py:39
  (1 shorter events, 0.0 us)
Async XLA Ops:
  4.8 5.2 %collective-permute-start = (f32[72,128]{1,0:T(8,128)S(1)}, f32[72,128]{1,0:T(8,128)S(1)}, u32[]{:S(2)}, u32[]{:S(2)}) collective-permute-start(f32[72,128]{1,0:T(8,128)S(1)} %get-tuple-element.21.refs_0_), channel_id=1, source_target_pairs={{0,1},{1,0},{2,3},{3,2},{4,5},{5,4},{6,7},{7,6},{8,9},{9,8},{10,11... | collective-permute-start | bytes 110600 | tf_op jit(solution)/shard_map/ppermute | solution.py:24
  5.4 4.7 %collective-permute-start.1 = (f32[72,128]{1,0:T(8,128)S(1)}, f32[72,128]{1,0:T(8,128)S(1)}, u32[]{:S(2)}, u32[]{:S(2)}) collective-permute-start(f32[72,128]{1,0:T(8,128)S(1)} %get-tuple-element.21.refs_0_), channel_id=1, source_target_pairs={{0,2},{1,3},{2,0},{3,1},{4,6},{5,7},{6,4},{7,5},{8,10},{9,11},{10,... | collective-permute-start | bytes 110600 | tf_op jit(solution)/shard_map/ppermute | solution.py:24
  7.9 3.4 %collective-permute-start.2 = (f32[72,128]{1,0:T(8,128)S(1)}, f32[72,128]{1,0:T(8,128)S(1)}, u32[]{:S(2)}, u32[]{:S(2)}) collective-permute-start(f32[72,128]{1,0:T(8,128)S(1)} %get-tuple-element.21.refs_0_), channel_id=1, source_target_pairs={{0,3},{1,2},{2,1},{3,0},{4,7},{5,6},{6,5},{7,4},{8,11},{9,10},{10,... | collective-permute-start | bytes 110600 | tf_op jit(solution)/shard_map/ppermute | solution.py:24
  8.0 7.6 %collective-permute-start.6 = (f32[32,8,128]{2,1,0:T(8,128)S(1)}, f32[32,8,128]{2,1,0:T(8,128)S(1)}, u32[]{:S(2)}, u32[]{:S(2)}) collective-permute-start(f32[32,8,128]{2,1,0:T(8,128)S(1)} %get-tuple-element.23.refs_0_), channel_id=1, source_target_pairs={{0,1},{1,0},{2,3},{3,2},{4,5},{5,4},{6,7},{7,6},{8,9},{9,8},{10,11... | collective-permute-start | bytes 393224 | tf_op jit(solution)/shard_map/ppermute | solution.py:24
  8.1 7.7 %collective-permute-start.7 = (f32[32,8,128]{2,1,0:T(8,128)S(1)}, f32[32,8,128]{2,1,0:T(8,128)S(1)}, u32[]{:S(2)}, u32[]{:S(2)}) collective-permute-start(f32[32,8,128]{2,1,0:T(8,128)S(1)} %get-tuple-element.23.refs_0_), channel_id=1, source_target_pairs={{0,2},{1,3},{2,0},{3,1},{4,6},{5,7},{6,4},{7,5},{8,10},{9,11},{10,... | collective-permute-start | bytes 393224 | tf_op jit(solution)/shard_map/ppermute | solution.py:24
  10.1 6.9 %collective-permute-start.8 = (f32[32,8,128]{2,1,0:T(8,128)S(1)}, f32[32,8,128]{2,1,0:T(8,128)S(1)}, u32[]{:S(2)}, u32[]{:S(2)}) collective-permute-start(f32[32,8,128]{2,1,0:T(8,128)S(1)} %get-tuple-element.23.refs_0_), channel_id=1, source_target_pairs={{0,3},{1,2},{2,1},{3,0},{4,7},{5,6},{6,5},{7,4},{8,11},{9,10},{10,... | collective-permute-start | bytes 393224 | tf_op jit(solution)/shard_map/ppermute | solution.py:24
  11.4 12.5 %collective-permute-start.3 = (f32[160,128]{1,0:T(8,128)S(1)}, f32[160,128]{1,0:T(8,128)S(1)}, u32[]{:S(2)}, u32[]{:S(2)}) collective-permute-start(f32[160,128]{1,0:T(8,128)S(1)} %get-tuple-element.22.refs_0_), channel_id=1, source_target_pairs={{0,4},{4,0},{8,12},{12,8},{1,5},{5,1},{9,13},{13,9},{2,6},{6,2},{1... | collective-permute-start | bytes 245768 | tf_op jit(solution)/shard_map/ppermute | solution.py:24
  13.0 10.9 %collective-permute-start.4 = (f32[160,128]{1,0:T(8,128)S(1)}, f32[160,128]{1,0:T(8,128)S(1)}, u32[]{:S(2)}, u32[]{:S(2)}) collective-permute-start(f32[160,128]{1,0:T(8,128)S(1)} %get-tuple-element.22.refs_0_), channel_id=1, source_target_pairs={{0,8},{4,12},{8,0},{12,4},{1,9},{5,13},{9,1},{13,5},{2,10},{6,14},... | collective-permute-start | bytes 245768 | tf_op jit(solution)/shard_map/ppermute | solution.py:24
  15.6 8.3 %collective-permute-start.5 = (f32[160,128]{1,0:T(8,128)S(1)}, f32[160,128]{1,0:T(8,128)S(1)}, u32[]{:S(2)}, u32[]{:S(2)}) collective-permute-start(f32[160,128]{1,0:T(8,128)S(1)} %get-tuple-element.22.refs_0_), channel_id=1, source_target_pairs={{0,12},{4,8},{8,4},{12,0},{1,13},{5,9},{9,5},{13,1},{2,14},{6,10},... | collective-permute-start | bytes 245768 | tf_op jit(solution)/shard_map/ppermute | solution.py:24
  24.6 4.2 %collective-permute-start.10 = (f32[64,128]{1,0:T(8,128)S(1)}, f32[64,128]{1,0:T(8,128)S(1)}, u32[]{:S(2)}, u32[]{:S(2)}) collective-permute-start(f32[64,128]{1,0:T(8,128)S(1)} %get-tuple-element.31.refs_0_.refs_5_), channel_id=1, source_target_pairs={{0,2},{1,3},{2,0},{3,1},{4,6},{5,7},{6,4},{7,5},{8,10},{9,11},{10,... | collective-permute-start | bytes 98312 | tf_op jit(solution)/shard_map/ppermute | solution.py:24
  25.3 3.6 %collective-permute-start.11 = (f32[64,128]{1,0:T(8,128)S(1)}, f32[64,128]{1,0:T(8,128)S(1)}, u32[]{:S(2)}, u32[]{:S(2)}) collective-permute-start(f32[64,128]{1,0:T(8,128)S(1)} %get-tuple-element.31.refs_0_.refs_5_), channel_id=1, source_target_pairs={{0,3},{1,2},{2,1},{3,0},{4,7},{5,6},{6,5},{7,4},{8,11},{9,10},{10,... | collective-permute-start | bytes 98312 | tf_op jit(solution)/shard_map/ppermute | solution.py:24
  26.1 2.8 %collective-permute-start.9 = (f32[64,128]{1,0:T(8,128)S(1)}, f32[64,128]{1,0:T(8,128)S(1)}, u32[]{:S(2)}, u32[]{:S(2)}) collective-permute-start(f32[64,128]{1,0:T(8,128)S(1)} %get-tuple-element.31.refs_0_.refs_5_), channel_id=1, source_target_pairs={{0,1},{1,0},{2,3},{3,2},{4,5},{5,4},{6,7},{7,6},{8,9},{9,8},{10,11... | collective-permute-start | bytes 98312 | tf_op jit(solution)/shard_map/ppermute | solution.py:24

commit v11 on v10

--- a/solution.py
+++ b/solution.py
@@ -15,6 +15,7 @@
 LANES = 128
 TILE_ROWS = 8
 VMEM_LIMIT = 16 << 20
+CHUNKS = 4
 FIRST = pl.CostEstimate(flops=10**11, bytes_accessed=10**10, transcendentals=0)
 
 
@@ -117,8 +118,13 @@
     dims, slots, width = sources[0].shape
     rank = basis.shape[1]
     targets = [at.at[0:dims], at.at[dims : 2 * dims], at.at[2 * dims], box_far]
-    targets += [transfer, basis, leaf_coupling, box_coupling]
-    copies = copy_all(zip(sources, targets), arrived)
+    pairs = list(zip(sources[:4], targets))
+    step = slots // CHUNKS
+    for first in range(0, slots, step):
+        for source, target in zip(sources[4:6], (transfer, basis)):
+            pairs.append((source.at[first : first + step], target.at[first : first + step]))
+    pairs += zip(sources[6:], (leaf_coupling, box_coupling))
+    copies = copy_all(pairs, arrived)
     for copy in copies[:4]:
         copy.wait()
     for row in range(2 * dims):
@@ -133,9 +139,10 @@
     ]
     message[slots : slots + TILE_ROWS, :] = jnp.zeros((TILE_ROWS, LANES), jnp.float32)
     message[slots + 1 : slots + 2, :] = lane_row(entries)
-    for copy in copies[4:6]:
-        copy.wait()
     for leaf in range(slots):
+        if leaf % step == 0:
+            for copy in copies[4 + 2 * (leaf // step) : 6 + 2 * (leaf // step)]:
+                copy.wait()
         product = jnp.dot(
             transfer[leaf],
             basis[leaf],
@@ -144,8 +151,7 @@
         )
         product = jnp.where(leaf < counts[0], product, 0.0)
         box_basis[leaf] = product
-        split = jnp.concatenate(split_three(product)).astype(jnp.bfloat16)
-        parts[:, leaf * width : (leaf + 1) * width] = split
+        parts[:, leaf * width : (leaf + 1) * width] = split_rows(product)
     write_moments(initial, basis, message, 0)
     message[slots : slots + 1, :] = box_moments(initial, box_basis)
     products = lax.dot_general(
@@ -158,7 +164,7 @@
     start, half = slots + TILE_ROWS, rank // 2
     message[start : start + half, 0:rank] = gram[0:half]
     message[start : start + half, rank : 2 * rank] = gram[half:rank]
-    for copy in copies[6:]:
+    for copy in copies[4 + 2 * CHUNKS :]:
         copy.wait()
 
 
@@ -170,24 +176,44 @@
         blocks[sub * span : (sub + 1) * span, :] = message[slots : slots + span, :]
 
 
-def leaf_part(moments, picks, coupling):
-    count, rank, _ = coupling.shape
-    slots = picks.shape[0] // count
-    chosen = jnp.zeros((picks.shape[0], rank), jnp.float32)
-    for part in split_three(moments):
-        chosen = chosen + jnp.dot(
+def split_rows(rows):
+    return jnp.concatenate(split_three(rows)).astype(jnp.bfloat16)
+
+
+def write_weights(coupling, weights):
+    for place in range(coupling.shape[0]):
+        parts = jnp.concatenate(split_three(coupling[place].T), axis=1)
+        weights[place] = parts.astype(jnp.bfloat16)
+
+
+def coupled_rows(chosen, weights):
+    total = None
+    for place in range(weights.shape[0]):
+        product = jnp.dot(chosen(place), weights[place], preferred_element_type=jnp.float32)
+        total = product if total is None else total + product
+    count, rank = total.shape[0] // 3, total.shape[1] // 3
+    part = [
+        [total[row * count : (row + 1) * count, at * rank : (at + 1) * rank] for at in range(3)]
+        for row in range(3)
+    ]
+    return part[0][0] + (
+        (part[0][1] + part[1][0]) + (part[0][2] + part[2][0] + part[1][1])
+    )
+
+
+def leaf_part(moments, picks, weights):
+    slots = picks.shape[0] // weights.shape[0]
+    parts = [
+        jnp.dot(
             picks[...], part.astype(jnp.bfloat16), preferred_element_type=jnp.float32
-        )
-    local = jnp.zeros((slots, rank), jnp.float32)
-    for place in range(count):
-        local = local + lax.dot_general(
-            chosen[place * slots : (place + 1) * slots],
-            coupling[place],
-            (((1,), (1,)), ((), ())),
-            precision=HIGH_PRECISION,
-            preferred_element_type=jnp.float32,
-        )
-    return local
+        ).astype(jnp.bfloat16)
+        for part in split_three(moments)
+    ]
+
+    def chosen(place):
+        return jnp.concatenate([part[place * slots : (place + 1) * slots] for part in parts])
+
+    return coupled_rows(chosen, weights)
 
 
 def wide_transpose(rows):
@@ -206,9 +232,10 @@
 
 
 def first_near_kernel(subs, box, counts, *refs):
-    geometry, (moments, coupling, basis) = refs[:subs], refs[subs : subs + 3]
-    near_source, far_source, near, initial, values, picks = refs[subs + 3 : subs + 9]
-    features, squares, fields, inner, near_list, far_list, arrived = refs[subs + 9 :]
+    geometry, (moments, coupling, box_coupling, basis) = refs[:subs], refs[subs : subs + 4]
+    near_source, far_source, near, initial, values, picks = refs[subs + 4 : subs + 10]
+    weights, box_weights = refs[subs + 10 : subs + 12]
+    features, squares, fields, inner, near_list, far_list, arrived = refs[subs + 12 :]
     copies = copy_all([(near_source, near_list), (far_source, far_list)], arrived)
     slots, height, width = geometry[0].shape
     neighbours = near_list.shape[0]
@@ -270,7 +297,9 @@
     for place in range(far_count):
         chosen = jnp.where(far_rows[0:slots, place : place + 1] == leaves, 1.0, 0.0)
         picks[place * slots : (place + 1) * slots, :] = chosen.astype(jnp.bfloat16)
-    local = leaf_part(moments[:, 0:rank], picks, coupling)
+    write_weights(coupling, weights)
+    write_weights(box_coupling, box_weights)
+    local = leaf_part(moments[:, 0:rank], picks, weights)
     initial[...] = fields[0:slots, :]
     lax.fori_loop(0, slots, target, 0, unroll=True)
     add_leaf_far(counts, local, basis, near)
@@ -316,15 +345,24 @@
     write_moments(message, basis, message, slots)
 
 
+def share_kernel(message, basis_one, box_basis, share):
+    slots = basis_one.shape[0]
+    first, one = message[0:slots, :], basis_one[...]
+    products = [one * first, first * first]
+    share[...] = jnp.zeros_like(share)
+    share[0:1, :] = box_moments(message, box_basis)
+    share[1:2, :] = lane_row([jnp.sum(product, keepdims=True) for product in products])
+
+
 def second_near_kernel(subs, box, counts, *refs):
     messages = refs[:subs]
-    picks, coupling, basis, box_basis, basis_one, values, near_source = refs[subs : subs + 7]
-    part, shares, fields, near_list, arrived = refs[subs + 7 :]
+    picks, weights, basis, box_basis, basis_one, share, values = refs[subs : subs + 7]
+    near_source, part, shares, fields, near_list, arrived = refs[subs + 7 :]
     copy = pltpu.make_async_copy(near_source, near_list, arrived)
     copy.start()
     slots, width = part.shape
     neighbours = near_list.shape[0]
-    rank = coupling.shape[1]
+    rank = basis.shape[1]
     for sub in range(subs):
         fields[sub * slots : (sub + 1) * slots, :] = messages[sub][0:slots, :]
 
@@ -337,25 +375,21 @@
         return carry
 
     moments = jnp.concatenate([ref[slots : 2 * slots, 0:rank] for ref in messages], axis=0)
-    local = leaf_part(moments, picks, coupling)
+    local = leaf_part(moments, picks, weights)
     copy.wait()
     lax.fori_loop(0, slots, target, 0, unroll=True)
     add_leaf_far(counts, local, basis, part)
     first, one, second = messages[0][0:slots, :], basis_one[...], part[...]
-    products = [one * first, first * first, one * second, first * second, second * second]
+    products = [one * second, first * second, second * second]
     sums = lane_row([jnp.sum(product, keepdims=True) for product in products])
-    lane = iota((1, LANES), 1)
-    both = jnp.where(
-        lane < rank,
-        box_moments(messages[0], box_basis),
-        pltpu.roll(box_moments(part, box_basis), rank, 1),
-    )
+    sums = share[1:2, :] + pltpu.roll(sums, 2, 1)
+    both = share[0:1, :] + pltpu.roll(box_moments(part, box_basis), rank, 1)
     shares[...] = jnp.where(iota(shares.shape, 0) % 2 == 0, both, sums)
 
 
 def last_kernel(patches, span, box, *refs):
     boxes, (shares, message, basis_one, part, numbers) = refs[:patches], refs[patches : patches + 5]
-    box_basis, box_coupling = refs[patches + 5 : patches + 7]
+    box_basis, box_weights = refs[patches + 5 : patches + 7]
     basis_three, hessenberg, gather, starts, lists, pairs, image = refs[patches + 7 :]
     slots, rank, width = box_basis.shape
     height = boxes[0].shape[0]
@@ -369,21 +403,23 @@
         pairs[other : other + 1, :] = shares[2 * other : 2 * other + 1, :]
         pairs[count + other : count + other + 1, :] = shares[2 * other + 1 : 2 * other + 2, :]
     first_box, second_box = pairs[0:count, 0:rank], pairs[0:count, rank : 2 * rank]
-    parts = [part.astype(jnp.bfloat16) for part in split_three(first_box)]
-    lane = iota((count, count), 1).astype(jnp.float32)
-    box_local = jnp.zeros((count, rank), jnp.float32)
-    for place in range(box_coupling.shape[0]):
-        pick = jnp.where(lists[:, 2 + place : 3 + place] == lane, 1.0, 0.0).astype(jnp.bfloat16)
-        chosen = jnp.zeros((count, rank), jnp.float32)
-        for split in parts:
-            chosen = chosen + jnp.dot(pick, split, preferred_element_type=jnp.float32)
-        box_local = box_local + lax.dot_general(
-            chosen,
-            box_coupling[place],
-            (((1,), (1,)), ((), ())),
-            precision=HIGH_PRECISION,
-            preferred_element_type=jnp.float32,
-        )
+    column = iota((count, 3 * count), 1)
+    rows = []
+    for place in range(box_weights.shape[0]):
+        wanted = lists[:, 2 + place : 3 + place]
+        for split in range(3):
+            number = (column - split * count).astype(jnp.float32)
+            rows.append(jnp.where(wanted == number, 1.0, 0.0))
+    chosen_rows = jnp.dot(
+        jnp.concatenate(rows).astype(jnp.bfloat16),
+        split_rows(first_box),
+        preferred_element_type=jnp.float32,
+    ).astype(jnp.bfloat16)
+
+    def chosen(place):
+        return chosen_rows[place * 3 * count : (place + 1) * 3 * count]
+
+    box_local = coupled_rows(chosen, box_weights)
     twice = jnp.concatenate([box_local, box_local], axis=1)
     columns = twice.T
     half = rank // 2
@@ -492,7 +528,7 @@
             pltpu.SMEM(box_far.shape, jnp.int32),
             pltpu.VMEM(leaf_to_box_transfer.shape, jnp.float32),
             pltpu.VMEM((3 * rank, slots * width), jnp.bfloat16),
-            pltpu.SemaphoreType.DMA((8,)),
+            pltpu.SemaphoreType.DMA((6 + 2 * CHUNKS,)),
         ],
         [
             points.transpose(1, 0, 2),
@@ -515,16 +551,18 @@
     )
     boxes = from_peers(blocks, "patch")
     gather = pltpu.VMEM((patches * subs * span, LANES), jnp.float32)
-    part, initial, values, picks = device_call(
+    part, initial, values, picks, weights, box_weights = device_call(
         functools.partial(first_near_kernel, subs),
         [
             rows,
             rows,
             kept(slots * neighbours, width, width),
             kept(far_count * slots, sources, dtype=jnp.bfloat16),
+            kept(far_count, rank, 3 * rank, dtype=jnp.bfloat16),
+            kept(box_coupling.shape[0], rank, 3 * rank, dtype=jnp.bfloat16),
         ],
         [box, counts],
-        [*geometry, moments, leaf_coupling, leaf_basis],
+        [*geometry, moments, leaf_coupling, box_coupling, leaf_basis],
         [
             pltpu.VMEM((sources, 32, 2 * width), jnp.bfloat16),
             block,
@@ -547,11 +585,14 @@
         ],
     )
     messages = from_peers(message, "sub")
+    (share,) = device_call(
+        share_kernel, [kept(TILE_ROWS, LANES)], [], [message, basis_one, box_basis]
+    )
     part, shares = device_call(
         functools.partial(second_near_kernel, subs),
         [rows, kept(2 * patches * subs, LANES)],
         [box, counts],
-        [*messages, picks, leaf_coupling, leaf_basis, box_basis, basis_one, values],
+        [*messages, picks, weights, leaf_basis, box_basis, basis_one, share, values],
         [block, *list_scratch],
         [near_list],
     )
@@ -560,7 +601,7 @@
         functools.partial(last_kernel, patches, span),
         [f32(slots, width), f32(2, 3)],
         [box],
-        [*boxes, shares, message, basis_one, part, numbers, box_basis, box_coupling],
+        [*boxes, shares, message, basis_one, part, numbers, box_basis, box_weights],
         [
             gather,
             pltpu.VMEM((patches * subs, LANES), jnp.float32),

time: 47 us -> 45.7 us (0.972)
  Pallas kernels: 17.3 us -> 16.2 us
    pallas_call x6 -> x7, Pallas kernels: 17.3 us -> 16.2 us  [device_call(): pl.pallas_call(kernel, out_shape=tuple(outputs), in_specs=[smem] * len(sc...]
  transfers between devices with their start and end apart: 12 -> 12, of which waited for: 4 -> 4; matrix products, arithmetic and copies ran while one was open for 0% -> 0% of each run, Pallas kernels for 15% -> 16%
where the time goes in v11:
time: 45.7 us; the launch traced here: 45.5 us
  Pallas kernels  16.2 us (35%)
  starting transfers between devices  11.8 us (26%)
  blocking collectives  11.7 us (26%)
  waiting for transfers between devices  4.37 us (10%)
  between operations  1.34 us (3%)
    pallas_call x7, Pallas kernels, device_call(): pl.pallas_call(kernel, out_shape=tuple(outputs), in_specs=[smem] * len(sc...  16.2 us
    ppermute x12, starting transfers between devices, from_peers(): lax.ppermute(value, axis, [(i, i ^ turn) for i in range(size)])  11.8 us
    all_to_all x1, blocking collectives, shards(): shares = lax.all_to_all(shares, ('patch', 'sub'), 0, 0, tiled=True)  11.7 us
    ppermute x12, waiting for transfers between devices, from_peers(): lax.ppermute(value, axis, [(i, i ^ turn) for i in range(size)])  4.37 us
  transfers between devices with their start and end apart: 12, of which 4 were waited for; matrix products, arithmetic and copies ran while one was open for 0% of the time, Pallas kernels for 16%

profile of v11, /device:TPU:0, one launch (start us, length us, event | category | flops | bytes accessed | tf_op | source)
XLA Modules:
  0.0 45.5 jit_solution(14705388851518244672)
XLA Ops:
  1.3 3.5 %shard_map.122 = (f32[32,8,128]{2,1,0:T(8,128)S(1)}, f32[72,128]{1,0:T(8,128)S(1)}, f32[32,64,128]{2,1,0:T(8,128)S(1)}, f32[32,64,128]{2,1,0:T(8,128)S(1)}, f32[...) custom-call(s32[1]{0:T(128)S(6)} %copy.13.counts, f32[3,32,128]{2,1,0:T(8,128)} %bitcast.10, f32[3,32,128]{2,1,0:T(8,128)} %bitcast.11, ...), custom_call_target="tpu_custom_call" | custom-call | tf_op jit(solution)/shard_map/pallas_call | solution.py:40
  4.8 0.5 %collective-permute-start = (f32[72,128]{1,0:T(8,128)S(1)}, f32[72,128]{1,0:T(8,128)S(1)}, u32[]{:S(2)}, u32[]{:S(2)}) collective-permute-start(f32[72,128]{1,0:T(8,128)S(1)} %get-tuple-element.23.refs_0_), channel_id=1, source_target_pairs={{0,1},{1,0},{2,3},{3,2},{4,5},{5,4},{6,7},{7,6},{8,9},{9,8},{10,11... | collective-permute-start | bytes 110600 | tf_op jit(solution)/shard_map/ppermute | solution.py:25
  5.3 2.6 %collective-permute-start.1 = (f32[72,128]{1,0:T(8,128)S(1)}, f32[72,128]{1,0:T(8,128)S(1)}, u32[]{:S(2)}, u32[]{:S(2)}) collective-permute-start(f32[72,128]{1,0:T(8,128)S(1)} %get-tuple-element.23.refs_0_), channel_id=1, source_target_pairs={{0,2},{1,3},{2,0},{3,1},{4,6},{5,7},{6,4},{7,5},{8,10},{9,11},{10,... | collective-permute-start | bytes 110600 | tf_op jit(solution)/shard_map/ppermute | solution.py:25
  7.9 0.1 collective-permute-start.2
  7.9 0.1 collective-permute-start.6
  8.1 1.9 %collective-permute-start.7 = (f32[32,8,128]{2,1,0:T(8,128)S(1)}, f32[32,8,128]{2,1,0:T(8,128)S(1)}, u32[]{:S(2)}, u32[]{:S(2)}) collective-permute-start(f32[32,8,128]{2,1,0:T(8,128)S(1)} %get-tuple-element.25.refs_0_), channel_id=1, source_target_pairs={{0,2},{1,3},{2,0},{3,1},{4,6},{5,7},{6,4},{7,5},{8,10},{9,11},{10,... | collective-permute-start | bytes 393224 | tf_op jit(solution)/shard_map/ppermute | solution.py:25
  10.0 0.0 collective-permute-done.refs_1_
  10.0 0.0 collective-permute-start.8
  10.0 0.0 collective-permute-done.1.refs_2_
  10.0 1.3 %collective-permute-done.2.refs_3_ = f32[72,128]{1,0:T(8,128)S(1)} collective-permute-done((f32[72,128]{1,0:T(8,128)S(1)}, f32[72,128]{1,0:T(8,128)S(1)}, u32[]{:S(2)}, u32[]{:S(2)}) %collective-permute-start.2) | collective-permute-done | bytes 36896 | tf_op jit(solution)/shard_map/ppermute | solution.py:25
  11.3 1.6 %collective-permute-start.3 = (f32[160,128]{1,0:T(8,128)S(1)}, f32[160,128]{1,0:T(8,128)S(1)}, u32[]{:S(2)}, u32[]{:S(2)}) collective-permute-start(f32[160,128]{1,0:T(8,128)S(1)} %get-tuple-element.24.refs_0_), channel_id=1, source_target_pairs={{0,4},{4,0},{8,12},{12,8},{1,5},{5,1},{9,13},{13,9},{2,6},{6,2},{1... | collective-permute-start | bytes 245768 | tf_op jit(solution)/shard_map/ppermute | solution.py:25
  12.9 2.6 %collective-permute-start.4 = (f32[160,128]{1,0:T(8,128)S(1)}, f32[160,128]{1,0:T(8,128)S(1)}, u32[]{:S(2)}, u32[]{:S(2)}) collective-permute-start(f32[160,128]{1,0:T(8,128)S(1)} %get-tuple-element.24.refs_0_), channel_id=1, source_target_pairs={{0,8},{4,12},{8,0},{12,4},{1,9},{5,13},{9,1},{13,5},{2,10},{6,14},... | collective-permute-start | bytes 245768 | tf_op jit(solution)/shard_map/ppermute | solution.py:25
  15.5 0.0 collective-permute-done.6.refs_1_
  15.5 0.2 collective-permute-start.5
  15.8 0.0 collective-permute-done.7.refs_2_
  15.8 1.1 %collective-permute-done.8.refs_3_ = f32[32,8,128]{2,1,0:T(8,128)S(1)} collective-permute-done((f32[32,8,128]{2,1,0:T(8,128)S(1)}, f32[32,8,128]{2,1,0:T(8,128)S(1)}, u32[]{:S(2)}, u32[]{:S(2)}) %collective-permute-start.8) | collective-permute-done | bytes 131104 | tf_op jit(solution)/shard_map/ppermute | solution.py:25
  16.9 6.9 %shard_map.124 = (f32[32,128]{1,0:T(8,128)S(1)}, f32[32,128]{1,0:T(8,128)S(1)}, f32[288,128,128]{2,1,0:T(8,128)S(1)}, bf16[256,128]{1,0:T(8,128)(2,1)S(1)}, bf16...) custom-call(s32[1]{0:T(128)} %bitcast.box, s32[1]{0:T(128)S(6)} %copy.13.counts, ...), custom_call_target="tpu_custom_call" | custom-call | tf_op jit(solution)/shard_map/pallas_call | solution.py:40
  23.8 0.0 collective-permute-done.3.refs_1_
  23.9 0.0 collective-permute-done.4.refs_2_
  23.9 0.0 collective-permute-done.5.refs_3_
  23.9 0.7 %shard_map.125 = (f32[64,128]{1,0:T(8,128)S(1)}, f32[32,128]{1,0:T(8,128)S(1)}, f32[8,128]{1,0:T(8,128)S(1)}) custom-call(s32[1]{0:T(128)} %bitcast.box, f32[160,128]{1,0:T(8,128)S(1)} %get-tuple-element.24.refs_0_, f32[160,128]{1,0:T(8,128)S(1)} %collective-permute-done.3.refs_1_, f32[160,128]{1,0:T(8,128)S(1)} %collective-permute-done.4.refs_2_, ...), custom_call_target="tpu_custom_call" | custom-call | tf_op jit(solution)/shard_map/pallas_call | solution.py:40
  24.5 0.7 %collective-permute-start.10 = (f32[64,128]{1,0:T(8,128)S(1)}, f32[64,128]{1,0:T(8,128)S(1)}, u32[]{:S(2)}, u32[]{:S(2)}) collective-permute-start(f32[64,128]{1,0:T(8,128)S(1)} %get-tuple-element.33.message.refs_0_.refs_5_), channel_id=1, source_target_pairs={{0,2},{1,3},{2,0},{3,1},{4,6},{5,7},{6,4},{7,5},{8,10},{9,11},{10,... | collective-permute-start | bytes 98312 | tf_op jit(solution)/shard_map/ppermute | solution.py:25
  25.2 0.8 %collective-permute-start.11 = (f32[64,128]{1,0:T(8,128)S(1)}, f32[64,128]{1,0:T(8,128)S(1)}, u32[]{:S(2)}, u32[]{:S(2)}) collective-permute-start(f32[64,128]{1,0:T(8,128)S(1)} %get-tuple-element.33.message.refs_0_.refs_5_), channel_id=1, source_target_pairs={{0,3},{1,2},{2,1},{3,0},{4,7},{5,6},{6,5},{7,4},{8,11},{9,10},{10,... | collective-permute-start | bytes 98312 | tf_op jit(solution)/shard_map/ppermute | solution.py:25
  26.1 0.6 %collective-permute-start.9 = (f32[64,128]{1,0:T(8,128)S(1)}, f32[64,128]{1,0:T(8,128)S(1)}, u32[]{:S(2)}, u32[]{:S(2)}) collective-permute-start(f32[64,128]{1,0:T(8,128)S(1)} %get-tuple-element.33.message.refs_0_.refs_5_), channel_id=1, source_target_pairs={{0,1},{1,0},{2,3},{3,2},{4,5},{5,4},{6,7},{7,6},{8,9},{9,8},{10,11... | collective-permute-start | bytes 98312 | tf_op jit(solution)/shard_map/ppermute | solution.py:25
  26.7 0.2 shard_map.126.refs_9_
  26.9 1.8 %collective-permute-done.10.refs_2_ = f32[64,128]{1,0:T(8,128)S(1)} collective-permute-done((f32[64,128]{1,0:T(8,128)S(1)}, f32[64,128]{1,0:T(8,128)S(1)}, u32[]{:S(2)}, u32[]{:S(2)}) %collective-permute-start.10) | collective-permute-done | bytes 32800 | tf_op jit(solution)/shard_map/ppermute | solution.py:25
  28.7 0.1 collective-permute-done.11.refs_3_
  28.8 0.0 collective-permute-done.9.refs_1_
  28.8 2.7 %shard_map.127 = (f32[32,128]{1,0:T(8,128)S(1)}, f32[32,128]{1,0:T(8,128)S(1)}) custom-call(s32[1]{0:T(128)} %bitcast.box, s32[1]{0:T(128)S(6)} %copy.13.counts, f32[64,128]{1,0:T(8,128)S(1)} %get-tuple-element.33.message.refs_0_.refs_5_, f32[64,128]{1,0:T(8,128)S(1)} %collective-permute-done.9.refs_1_, f32[64,128]{1,0:T(8,128)S(1)} %collective-permute-done.10.refs_2_, ...), custom_call_target="tpu_custom_call" | custom-call | tf_op jit(solution)/shard_map/pallas_call | solution.py:40
  31.6 11.7 %all_to_all.11 = f32[16,2,128]{2,1,0:T(2,128)S(1)} all-to-all(f32[16,2,128]{2,1,0:T(2,128)S(1)} %bitcast.9), channel_id=1, replica_groups=mesh['groups'=2,'patch'=4,'sub'=4] {'patch','sub'}, dimensions={0} | all-to-all | bytes 32768 | tf_op jit(solution)/shard_map/all_to_all | solution.py:599
  43.3 2.2 %shard_map.128 = (f32[32,128]{1,0:T(8,128)}, f32[2,3]{1,0:T(2,128)}) custom-call(s32[1]{0:T(128)} %bitcast.box, f32[160,128]{1,0:T(8,128)S(1)} %get-tuple-element.24.refs_0_, f32[160,128]{1,0:T(8,128)S(1)} %collective-permute-done.3.refs_1_, f32[160,128]{1,0:T(8,128)S(1)} %collective-permute-done.4.refs_2_, f32[160,128]{1,0:T(8,128)S(1)} %collective-permute-done.5.refs_3_, ...), custom_call_target="tpu_custom_call" | custom-call | tf_op jit(solution)/shard_map/pallas_call | solution.py:40
  (1 shorter events, 0.0 us)
Async XLA Ops:
  4.8 5.2 %collective-permute-start = (f32[72,128]{1,0:T(8,128)S(1)}, f32[72,128]{1,0:T(8,128)S(1)}, u32[]{:S(2)}, u32[]{:S(2)}) collective-permute-start(f32[72,128]{1,0:T(8,128)S(1)} %get-tuple-element.23.refs_0_), channel_id=1, source_target_pairs={{0,1},{1,0},{2,3},{3,2},{4,5},{5,4},{6,7},{7,6},{8,9},{9,8},{10,11... | collective-permute-start | bytes 110600 | tf_op jit(solution)/shard_map/ppermute | solution.py:25
  5.3 4.7 %collective-permute-start.1 = (f32[72,128]{1,0:T(8,128)S(1)}, f32[72,128]{1,0:T(8,128)S(1)}, u32[]{:S(2)}, u32[]{:S(2)}) collective-permute-start(f32[72,128]{1,0:T(8,128)S(1)} %get-tuple-element.23.refs_0_), channel_id=1, source_target_pairs={{0,2},{1,3},{2,0},{3,1},{4,6},{5,7},{6,4},{7,5},{8,10},{9,11},{10,... | collective-permute-start | bytes 110600 | tf_op jit(solution)/shard_map/ppermute | solution.py:25
  7.9 3.4 %collective-permute-start.2 = (f32[72,128]{1,0:T(8,128)S(1)}, f32[72,128]{1,0:T(8,128)S(1)}, u32[]{:S(2)}, u32[]{:S(2)}) collective-permute-start(f32[72,128]{1,0:T(8,128)S(1)} %get-tuple-element.23.refs_0_), channel_id=1, source_target_pairs={{0,3},{1,2},{2,1},{3,0},{4,7},{5,6},{6,5},{7,4},{8,11},{9,10},{10,... | collective-permute-start | bytes 110600 | tf_op jit(solution)/shard_map/ppermute | solution.py:25
  7.9 7.6 %collective-permute-start.6 = (f32[32,8,128]{2,1,0:T(8,128)S(1)}, f32[32,8,128]{2,1,0:T(8,128)S(1)}, u32[]{:S(2)}, u32[]{:S(2)}) collective-permute-start(f32[32,8,128]{2,1,0:T(8,128)S(1)} %get-tuple-element.25.refs_0_), channel_id=1, source_target_pairs={{0,1},{1,0},{2,3},{3,2},{4,5},{5,4},{6,7},{7,6},{8,9},{9,8},{10,11... | collective-permute-start | bytes 393224 | tf_op jit(solution)/shard_map/ppermute | solution.py:25
  8.1 7.7 %collective-permute-start.7 = (f32[32,8,128]{2,1,0:T(8,128)S(1)}, f32[32,8,128]{2,1,0:T(8,128)S(1)}, u32[]{:S(2)}, u32[]{:S(2)}) collective-permute-start(f32[32,8,128]{2,1,0:T(8,128)S(1)} %get-tuple-element.25.refs_0_), channel_id=1, source_target_pairs={{0,2},{1,3},{2,0},{3,1},{4,6},{5,7},{6,4},{7,5},{8,10},{9,11},{10,... | collective-permute-start | bytes 393224 | tf_op jit(solution)/shard_map/ppermute | solution.py:25
  10.0 6.9 %collective-permute-start.8 = (f32[32,8,128]{2,1,0:T(8,128)S(1)}, f32[32,8,128]{2,1,0:T(8,128)S(1)}, u32[]{:S(2)}, u32[]{:S(2)}) collective-permute-start(f32[32,8,128]{2,1,0:T(8,128)S(1)} %get-tuple-element.25.refs_0_), channel_id=1, source_target_pairs={{0,3},{1,2},{2,1},{3,0},{4,7},{5,6},{6,5},{7,4},{8,11},{9,10},{10,... | collective-permute-start | bytes 393224 | tf_op jit(solution)/shard_map/ppermute | solution.py:25
  11.3 12.5 %collective-permute-start.3 = (f32[160,128]{1,0:T(8,128)S(1)}, f32[160,128]{1,0:T(8,128)S(1)}, u32[]{:S(2)}, u32[]{:S(2)}) collective-permute-start(f32[160,128]{1,0:T(8,128)S(1)} %get-tuple-element.24.refs_0_), channel_id=1, source_target_pairs={{0,4},{4,0},{8,12},{12,8},{1,5},{5,1},{9,13},{13,9},{2,6},{6,2},{1... | collective-permute-start | bytes 245768 | tf_op jit(solution)/shard_map/ppermute | solution.py:25
  12.9 10.9 %collective-permute-start.4 = (f32[160,128]{1,0:T(8,128)S(1)}, f32[160,128]{1,0:T(8,128)S(1)}, u32[]{:S(2)}, u32[]{:S(2)}) collective-permute-start(f32[160,128]{1,0:T(8,128)S(1)} %get-tuple-element.24.refs_0_), channel_id=1, source_target_pairs={{0,8},{4,12},{8,0},{12,4},{1,9},{5,13},{9,1},{13,5},{2,10},{6,14},... | collective-permute-start | bytes 245768 | tf_op jit(solution)/shard_map/ppermute | solution.py:25
  15.5 8.3 %collective-permute-start.5 = (f32[160,128]{1,0:T(8,128)S(1)}, f32[160,128]{1,0:T(8,128)S(1)}, u32[]{:S(2)}, u32[]{:S(2)}) collective-permute-start(f32[160,128]{1,0:T(8,128)S(1)} %get-tuple-element.24.refs_0_), channel_id=1, source_target_pairs={{0,12},{4,8},{8,4},{12,0},{1,13},{5,9},{9,5},{13,1},{2,14},{6,10},... | collective-permute-start | bytes 245768 | tf_op jit(solution)/shard_map/ppermute | solution.py:25
  24.5 4.2 %collective-permute-start.10 = (f32[64,128]{1,0:T(8,128)S(1)}, f32[64,128]{1,0:T(8,128)S(1)}, u32[]{:S(2)}, u32[]{:S(2)}) collective-permute-start(f32[64,128]{1,0:T(8,128)S(1)} %get-tuple-element.33.message.refs_0_.refs_5_), channel_id=1, source_target_pairs={{0,2},{1,3},{2,0},{3,1},{4,6},{5,7},{6,4},{7,5},{8,10},{9,11},{10,... | collective-permute-start | bytes 98312 | tf_op jit(solution)/shard_map/ppermute | solution.py:25
  25.2 3.6 %collective-permute-start.11 = (f32[64,128]{1,0:T(8,128)S(1)}, f32[64,128]{1,0:T(8,128)S(1)}, u32[]{:S(2)}, u32[]{:S(2)}) collective-permute-start(f32[64,128]{1,0:T(8,128)S(1)} %get-tuple-element.33.message.refs_0_.refs_5_), channel_id=1, source_target_pairs={{0,3},{1,2},{2,1},{3,0},{4,7},{5,6},{6,5},{7,4},{8,11},{9,10},{10,... | collective-permute-start | bytes 98312 | tf_op jit(solution)/shard_map/ppermute | solution.py:25
  26.1 2.8 %collective-permute-start.9 = (f32[64,128]{1,0:T(8,128)S(1)}, f32[64,128]{1,0:T(8,128)S(1)}, u32[]{:S(2)}, u32[]{:S(2)}) collective-permute-start(f32[64,128]{1,0:T(8,128)S(1)} %get-tuple-element.33.message.refs_0_.refs_5_), channel_id=1, source_target_pairs={{0,1},{1,0},{2,3},{3,2},{4,5},{5,4},{6,7},{7,6},{8,9},{9,8},{10,11... | collective-permute-start | bytes 98312 | tf_op jit(solution)/shard_map/ppermute | solution.py:25

commit v12 on v11

--- a/solution.py
+++ b/solution.py
@@ -112,9 +112,9 @@
 
 
 def start_kernel(counts, *refs):
-    sources, (geometry, message, box_basis) = refs[:8], refs[8:11]
-    basis, leaf_coupling, box_coupling = refs[11:14]
-    at, initial, box_far, transfer, parts, arrived = refs[14:]
+    sources, (geometry, message, box_basis) = refs[:10], refs[10:13]
+    basis, leaf_coupling, box_coupling, near_list, far_list = refs[13:18]
+    at, initial, box_far, transfer, parts, arrived = refs[18:]
     dims, slots, width = sources[0].shape
     rank = basis.shape[1]
     targets = [at.at[0:dims], at.at[dims : 2 * dims], at.at[2 * dims], box_far]
@@ -123,7 +123,7 @@
     for first in range(0, slots, step):
         for source, target in zip(sources[4:6], (transfer, basis)):
             pairs.append((source.at[first : first + step], target.at[first : first + step]))
-    pairs += zip(sources[6:], (leaf_coupling, box_coupling))
+    pairs += zip(sources[6:], (leaf_coupling, box_coupling, near_list, far_list))
     copies = copy_all(pairs, arrived)
     for copy in copies[:4]:
         copy.wait()
@@ -231,15 +231,28 @@
         )
 
 
+def leaf_kernel(box, counts, moments, coupling, box_coupling, basis, far_list, *refs):
+    far, picks, weights, box_weights = refs
+    slots, rank, width = basis.shape
+    far_count, sources = far_list.shape[0], moments.shape[0]
+    far_rows = wide_transpose(far_list[...].astype(jnp.float32))
+    leaves = (iota((slots, sources), 1) ^ (box[0] * slots)).astype(jnp.float32)
+    for place in range(far_count):
+        chosen = jnp.where(far_rows[0:slots, place : place + 1] == leaves, 1.0, 0.0)
+        picks[place * slots : (place + 1) * slots, :] = chosen.astype(jnp.bfloat16)
+    write_weights(coupling, weights)
+    write_weights(box_coupling, box_weights)
+    far[...] = jnp.zeros((slots, width), jnp.float32)
+    add_leaf_far(counts, leaf_part(moments[:, 0:rank], picks, weights), basis, far)
+
+
 def first_near_kernel(subs, box, counts, *refs):
-    geometry, (moments, coupling, box_coupling, basis) = refs[:subs], refs[subs : subs + 4]
-    near_source, far_source, near, initial, values, picks = refs[subs + 4 : subs + 10]
-    weights, box_weights = refs[subs + 10 : subs + 12]
-    features, squares, fields, inner, near_list, far_list, arrived = refs[subs + 12 :]
-    copies = copy_all([(near_source, near_list), (far_source, far_list)], arrived)
+    geometry, (far, near_source) = refs[:subs], refs[subs : subs + 2]
+    near, initial, values, features, squares, fields, inner, near_list, arrived = refs[subs + 2 :]
+    copy = pltpu.make_async_copy(near_source, near_list, arrived)
+    copy.start()
     slots, height, width = geometry[0].shape
     neighbours = near_list.shape[0]
-    rank = coupling.shape[1]
     row = iota((height, width), 0)
     scale_square = jnp.where(row < 3, -2.0, 0.0)
     ones = jnp.where(row == 7, 1.0, 0.0)
@@ -265,7 +278,7 @@
                 features[place, 16:32, lanes] = jnp.concatenate([one, three]).astype(jnp.bfloat16)
             return carry
 
-        lax.fori_loop(0, slots, source, 0, unroll=4)
+        lax.fori_loop(0, slots, source, 0, unroll=True)
 
     own = geometry[0]
 
@@ -289,20 +302,11 @@
         near[pl.ds(leaf, 1), :] = jnp.sum(total.T, axis=0, keepdims=True)
         return carry
 
-    for copy in copies:
-        copy.wait()
-    far_count, sources = far_list.shape[0], subs * slots
-    far_rows = wide_transpose(far_list[...].astype(jnp.float32))
-    leaves = (iota((slots, sources), 1) ^ (box[0] * slots)).astype(jnp.float32)
-    for place in range(far_count):
-        chosen = jnp.where(far_rows[0:slots, place : place + 1] == leaves, 1.0, 0.0)
-        picks[place * slots : (place + 1) * slots, :] = chosen.astype(jnp.bfloat16)
-    write_weights(coupling, weights)
-    write_weights(box_coupling, box_weights)
-    local = leaf_part(moments[:, 0:rank], picks, weights)
+    copy.wait()
     initial[...] = fields[0:slots, :]
     lax.fori_loop(0, slots, target, 0, unroll=True)
-    add_leaf_far(counts, local, basis, near)
+    in_use = iota((slots, width), 0) < counts[0]
+    near[...] = jnp.where(in_use, near[...] + far[...], 0.0)
 
 
 def box_images(box_basis, coefficients, image):
@@ -511,14 +515,15 @@
     list_scratch = [pltpu.SMEM(near_list.shape, jnp.int32), pltpu.SemaphoreType.DMA]
     block = pltpu.VMEM((sources, width), jnp.float32)
 
-    matrices = [leaf_basis, leaf_coupling, box_coupling]
-    geometry, message, box_basis, *matrices = device_call(
+    matrices, lists = [leaf_basis, leaf_coupling, box_coupling], [near_list, far_list]
+    geometry, message, box_basis, *held = device_call(
         start_kernel,
         [
             kept(slots, 8, width),
             kept(slots + span, LANES),
             kept(*leaf_basis.shape),
             *[kept(*matrix.shape) for matrix in matrices],
+            *[kept(*entries.shape, dtype=jnp.int32) for entries in lists],
         ],
         [counts],
         [],
@@ -528,7 +533,7 @@
             pltpu.SMEM(box_far.shape, jnp.int32),
             pltpu.VMEM(leaf_to_box_transfer.shape, jnp.float32),
             pltpu.VMEM((3 * rank, slots * width), jnp.bfloat16),
-            pltpu.SemaphoreType.DMA((6 + 2 * CHUNKS,)),
+            pltpu.SemaphoreType.DMA((8 + 2 * CHUNKS,)),
         ],
         [
             points.transpose(1, 0, 2),
@@ -537,9 +542,10 @@
             box_far,
             leaf_to_box_transfer,
             *matrices,
+            *lists,
         ],
     )
-    leaf_basis, leaf_coupling, box_coupling = matrices
+    leaf_basis, leaf_coupling, box_coupling, near_list, far_list = held
     messages = from_peers(message, "sub")
     geometry = from_peers(geometry, "sub")
     moments, blocks = device_call(
@@ -551,28 +557,29 @@
     )
     boxes = from_peers(blocks, "patch")
     gather = pltpu.VMEM((patches * subs * span, LANES), jnp.float32)
-    part, initial, values, picks, weights, box_weights = device_call(
-        functools.partial(first_near_kernel, subs),
+    far, picks, weights, box_weights = device_call(
+        leaf_kernel,
         [
             rows,
-            rows,
-            kept(slots * neighbours, width, width),
             kept(far_count * slots, sources, dtype=jnp.bfloat16),
             kept(far_count, rank, 3 * rank, dtype=jnp.bfloat16),
             kept(box_coupling.shape[0], rank, 3 * rank, dtype=jnp.bfloat16),
         ],
         [box, counts],
-        [*geometry, moments, leaf_coupling, box_coupling, leaf_basis],
+        [moments, leaf_coupling, box_coupling, leaf_basis, far_list],
+    )
+    part, initial, values = device_call(
+        functools.partial(first_near_kernel, subs),
+        [rows, rows, kept(slots * neighbours, width, width)],
+        [box, counts],
+        [*geometry, far, near_list],
         [
             pltpu.VMEM((sources, 32, 2 * width), jnp.bfloat16),
             block,
             block,
             pltpu.VMEM((slots, width), jnp.float32),
-            pltpu.SMEM(near_list.shape, jnp.int32),
-            pltpu.VMEM(far_list.shape, jnp.int32),
-            pltpu.SemaphoreType.DMA((2,)),
+            *list_scratch,
         ],
-        [near_list, far_list],
     )
     message, basis_one, numbers = device_call(
         functools.partial(first_image_kernel, patches, span),
@@ -592,9 +599,8 @@
         functools.partial(second_near_kernel, subs),
         [rows, kept(2 * patches * subs, LANES)],
         [box, counts],
-        [*messages, picks, weights, leaf_basis, box_basis, basis_one, share, values],
+        [*messages, picks, weights, leaf_basis, box_basis, basis_one, share, values, near_list],
         [block, *list_scratch],
-        [near_list],
     )
     shares = lax.all_to_all(shares, ("patch", "sub"), 0, 0, tiled=True)
     basis_three, hessenberg = device_call(

time: 45.7 us -> 45.6 us (level)
  waiting for transfers between devices: 4.37 us -> 3.39 us
  Pallas kernels: 16.2 us -> 16.8 us
    ppermute x12, waiting for transfers between devices: 4.37 us -> 3.39 us  [from_peers(): lax.ppermute(value, axis, [(i, i ^ turn) for i in range(size)])]
    pallas_call x7 -> x8, Pallas kernels: 16.2 us -> 16.8 us  [device_call(): pl.pallas_call(kernel, out_shape=tuple(outputs), in_specs=[smem] * len(sc...]
  transfers between devices with their start and end apart: 12 -> 12, of which waited for: 4 -> 3; matrix products, arithmetic and copies ran while one was open for 0% -> 0% of each run, Pallas kernels for 16% -> 17%
where the time goes in v12:
time: 45.6 us; the launch traced here: 45.4 us
  Pallas kernels  16.8 us (37%)
  blocking collectives  12 us (26%)
  starting transfers between devices  11.8 us (26%)
  waiting for transfers between devices  3.39 us (7%)
  between operations  1.37 us (3%)
    pallas_call x8, Pallas kernels, device_call(): pl.pallas_call(kernel, out_shape=tuple(outputs), in_specs=[smem] * len(sc...  16.8 us
    all_to_all x1, blocking collectives, shards(): shares = lax.all_to_all(shares, ('patch', 'sub'), 0, 0, tiled=True)  12 us
    ppermute x12, starting transfers between devices, from_peers(): lax.ppermute(value, axis, [(i, i ^ turn) for i in range(size)])  11.8 us
    ppermute x12, waiting for transfers between devices, from_peers(): lax.ppermute(value, axis, [(i, i ^ turn) for i in range(size)])  3.39 us
  transfers between devices with their start and end apart: 12, of which 3 were waited for; matrix products, arithmetic and copies ran while one was open for 0% of the time, Pallas kernels for 17%

profile of v12, /device:TPU:0, one launch (start us, length us, event | category | flops | bytes accessed | tf_op | source)
XLA Modules:
  0.0 45.4 jit_solution(13948190787483469614)
XLA Ops:
  1.3 3.5 %shard_map.122 = (f32[32,8,128]{2,1,0:T(8,128)S(1)}, f32[72,128]{1,0:T(8,128)S(1)}, f32[32,64,128]{2,1,0:T(8,128)S(1)}, f32[32,64,128]{2,1,0:T(8,128)S(1)}, f32[...) custom-call(s32[1]{0:T(128)S(6)} %copy.13.counts, ...), custom_call_target="tpu_custom_call" | custom-call | tf_op jit(solution)/shard_map/pallas_call | solution.py:40
  4.8 0.5 %collective-permute-start = (f32[72,128]{1,0:T(8,128)S(1)}, f32[72,128]{1,0:T(8,128)S(1)}, u32[]{:S(2)}, u32[]{:S(2)}) collective-permute-start(f32[72,128]{1,0:T(8,128)S(1)} %get-tuple-element.26.refs_0_), channel_id=1, source_target_pairs={{0,1},{1,0},{2,3},{3,2},{4,5},{5,4},{6,7},{7,6},{8,9},{9,8},{10,11... | collective-permute-start | bytes 110600 | tf_op jit(solution)/shard_map/ppermute | solution.py:25
  5.3 2.6 %collective-permute-start.1 = (f32[72,128]{1,0:T(8,128)S(1)}, f32[72,128]{1,0:T(8,128)S(1)}, u32[]{:S(2)}, u32[]{:S(2)}) collective-permute-start(f32[72,128]{1,0:T(8,128)S(1)} %get-tuple-element.26.refs_0_), channel_id=1, source_target_pairs={{0,2},{1,3},{2,0},{3,1},{4,6},{5,7},{6,4},{7,5},{8,10},{9,11},{10,... | collective-permute-start | bytes 110600 | tf_op jit(solution)/shard_map/ppermute | solution.py:25
  7.9 0.1 collective-permute-start.2
  7.9 0.1 collective-permute-start.6
  8.1 1.9 %collective-permute-start.7 = (f32[32,8,128]{2,1,0:T(8,128)S(1)}, f32[32,8,128]{2,1,0:T(8,128)S(1)}, u32[]{:S(2)}, u32[]{:S(2)}) collective-permute-start(f32[32,8,128]{2,1,0:T(8,128)S(1)} %get-tuple-element.28.refs_0_), channel_id=1, source_target_pairs={{0,2},{1,3},{2,0},{3,1},{4,6},{5,7},{6,4},{7,5},{8,10},{9,11},{10,... | collective-permute-start | bytes 393224 | tf_op jit(solution)/shard_map/ppermute | solution.py:25
  10.0 0.0 collective-permute-done.refs_1_
  10.0 0.0 collective-permute-start.8
  10.0 0.0 collective-permute-done.1.refs_2_
  10.0 1.3 %collective-permute-done.2.refs_3_ = f32[72,128]{1,0:T(8,128)S(1)} collective-permute-done((f32[72,128]{1,0:T(8,128)S(1)}, f32[72,128]{1,0:T(8,128)S(1)}, u32[]{:S(2)}, u32[]{:S(2)}) %collective-permute-start.2) | collective-permute-done | bytes 36896 | tf_op jit(solution)/shard_map/ppermute | solution.py:25
  11.3 1.6 %collective-permute-start.3 = (f32[160,128]{1,0:T(8,128)S(1)}, f32[160,128]{1,0:T(8,128)S(1)}, u32[]{:S(2)}, u32[]{:S(2)}) collective-permute-start(f32[160,128]{1,0:T(8,128)S(1)} %get-tuple-element.27.refs_0_), channel_id=1, source_target_pairs={{0,4},{4,0},{8,12},{12,8},{1,5},{5,1},{9,13},{13,9},{2,6},{6,2},{1... | collective-permute-start | bytes 245768 | tf_op jit(solution)/shard_map/ppermute | solution.py:25
  13.0 2.6 %collective-permute-start.4 = (f32[160,128]{1,0:T(8,128)S(1)}, f32[160,128]{1,0:T(8,128)S(1)}, u32[]{:S(2)}, u32[]{:S(2)}) collective-permute-start(f32[160,128]{1,0:T(8,128)S(1)} %get-tuple-element.27.refs_0_), channel_id=1, source_target_pairs={{0,8},{4,12},{8,0},{12,4},{1,9},{5,13},{9,1},{13,5},{2,10},{6,14},... | collective-permute-start | bytes 245768 | tf_op jit(solution)/shard_map/ppermute | solution.py:25
  15.6 0.0 collective-permute-done.6.refs_1_
  15.6 0.2 collective-permute-start.5
  15.8 1.5 %shard_map.124 = (f32[32,128]{1,0:T(8,128)S(1)}, bf16[256,128]{1,0:T(8,128)(2,1)S(1)}, bf16[8,64,192]{2,1,0:T(8,128)(2,1)S(1)}, bf16[8,64,192]{2,1,0:T(8,128)(2,1)S(1)}) custom-call(s32[1]{0:T(128)} %bitcast.box, s32[1]{0:T(128)S(6)} %copy.13.counts, f32[128,128]{1,0:T(8,128)S(1)} %get-tuple-element.29.moments, f32[8,64,64]{2,1,0:T(8,128)S(1)} %get-tuple-element.30.coupling, ...), custom_call_target="tpu_custom_call" | custom-call | tf_op jit(solution)/shard_map/pallas_call | solution.py:40
  17.3 0.0 collective-permute-done.7.refs_2_
  17.3 0.0 collective-permute-done.8.refs_3_
  17.3 6.1 %shard_map.125 = (f32[32,128]{1,0:T(8,128)S(1)}, f32[32,128]{1,0:T(8,128)S(1)}, f32[288,128,128]{2,1,0:T(8,128)S(1)}) custom-call(s32[1]{0:T(128)} %bitcast.box, s32[1]{0:T(128)S(6)} %copy.13.counts, f32[32,8,128]{2,1,0:T(8,128)S(1)} %get-tuple-element.28.refs_0_, f32[32,8,128]{2,1,0:T(8,128)S(1)} %collective-permute-done.6.refs_1_, ...), custom_call_target="tpu_custom_call" | custom-call | tf_op jit(solution)/shard_map/pallas_call | solution.py:40
  23.4 0.0 collective-permute-done.3.refs_1_
  23.4 0.0 collective-permute-done.4.refs_2_
  23.4 0.0 collective-permute-done.5.refs_3_
  23.4 0.7 %shard_map.126 = (f32[64,128]{1,0:T(8,128)S(1)}, f32[32,128]{1,0:T(8,128)S(1)}, f32[8,128]{1,0:T(8,128)S(1)}) custom-call(s32[1]{0:T(128)} %bitcast.box, f32[160,128]{1,0:T(8,128)S(1)} %get-tuple-element.27.refs_0_, f32[160,128]{1,0:T(8,128)S(1)} %collective-permute-done.3.refs_1_, f32[160,128]{1,0:T(8,128)S(1)} %collective-permute-done.4.refs_2_, ...), custom_call_target="tpu_custom_call" | custom-call | tf_op jit(solution)/shard_map/pallas_call | solution.py:40
  24.1 0.8 %collective-permute-start.10 = (f32[64,128]{1,0:T(8,128)S(1)}, f32[64,128]{1,0:T(8,128)S(1)}, u32[]{:S(2)}, u32[]{:S(2)}) collective-permute-start(f32[64,128]{1,0:T(8,128)S(1)} %get-tuple-element.39.message.refs_0_.refs_5_), channel_id=1, source_target_pairs={{0,2},{1,3},{2,0},{3,1},{4,6},{5,7},{6,4},{7,5},{8,10},{9,11},{10,... | collective-permute-start | bytes 98312 | tf_op jit(solution)/shard_map/ppermute | solution.py:25
  24.9 0.3 collective-permute-start.11
  25.2 1.0 %collective-permute-start.9 = (f32[64,128]{1,0:T(8,128)S(1)}, f32[64,128]{1,0:T(8,128)S(1)}, u32[]{:S(2)}, u32[]{:S(2)}) collective-permute-start(f32[64,128]{1,0:T(8,128)S(1)} %get-tuple-element.39.message.refs_0_.refs_5_), channel_id=1, source_target_pairs={{0,1},{1,0},{2,3},{3,2},{4,5},{5,4},{6,7},{7,6},{8,9},{9,8},{10,11... | collective-permute-start | bytes 98312 | tf_op jit(solution)/shard_map/ppermute | solution.py:25
  26.2 0.2 shard_map.127.refs_9_
  26.4 1.7 %collective-permute-done.10.refs_2_ = f32[64,128]{1,0:T(8,128)S(1)} collective-permute-done((f32[64,128]{1,0:T(8,128)S(1)}, f32[64,128]{1,0:T(8,128)S(1)}, u32[]{:S(2)}, u32[]{:S(2)}) %collective-permute-start.10) | collective-permute-done | bytes 32800 | tf_op jit(solution)/shard_map/ppermute | solution.py:25
  28.1 0.4 collective-permute-done.11.refs_3_
  28.5 0.0 collective-permute-done.9.refs_1_
  28.5 2.7 %shard_map.128 = (f32[32,128]{1,0:T(8,128)S(1)}, f32[32,128]{1,0:T(8,128)S(1)}) custom-call(s32[1]{0:T(128)} %bitcast.box, s32[1]{0:T(128)S(6)} %copy.13.counts, f32[64,128]{1,0:T(8,128)S(1)} %get-tuple-element.39.message.refs_0_.refs_5_, f32[64,128]{1,0:T(8,128)S(1)} %collective-permute-done.9.refs_1_, f32[64,128]{1,0:T(8,128)S(1)} %collective-permute-done.10.refs_2_, ...), custom_call_target="tpu_custom_call" | custom-call | tf_op jit(solution)/shard_map/pallas_call | solution.py:40
  31.2 12.0 %all_to_all.11 = f32[16,2,128]{2,1,0:T(2,128)S(1)} all-to-all(f32[16,2,128]{2,1,0:T(2,128)S(1)} %bitcast.9), channel_id=1, replica_groups=mesh['groups'=2,'patch'=4,'sub'=4] {'patch','sub'}, dimensions={0} | all-to-all | bytes 32768 | tf_op jit(solution)/shard_map/all_to_all | solution.py:605
  43.2 2.2 %shard_map.129 = (f32[32,128]{1,0:T(8,128)}, f32[2,3]{1,0:T(2,128)}) custom-call(s32[1]{0:T(128)} %bitcast.box, f32[160,128]{1,0:T(8,128)S(1)} %get-tuple-element.27.refs_0_, f32[160,128]{1,0:T(8,128)S(1)} %collective-permute-done.3.refs_1_, f32[160,128]{1,0:T(8,128)S(1)} %collective-permute-done.4.refs_2_, f32[160,128]{1,0:T(8,128)S(1)} %collective-permute-done.5.refs_3_, ...), custom_call_target="tpu_custom_call" | custom-call | tf_op jit(solution)/shard_map/pallas_call | solution.py:40
  (1 shorter events, 0.0 us)
Async XLA Ops:
  4.8 5.2 %collective-permute-start = (f32[72,128]{1,0:T(8,128)S(1)}, f32[72,128]{1,0:T(8,128)S(1)}, u32[]{:S(2)}, u32[]{:S(2)}) collective-permute-start(f32[72,128]{1,0:T(8,128)S(1)} %get-tuple-element.26.refs_0_), channel_id=1, source_target_pairs={{0,1},{1,0},{2,3},{3,2},{4,5},{5,4},{6,7},{7,6},{8,9},{9,8},{10,11... | collective-permute-start | bytes 110600 | tf_op jit(solution)/shard_map/ppermute | solution.py:25
  5.3 4.7 %collective-permute-start.1 = (f32[72,128]{1,0:T(8,128)S(1)}, f32[72,128]{1,0:T(8,128)S(1)}, u32[]{:S(2)}, u32[]{:S(2)}) collective-permute-start(f32[72,128]{1,0:T(8,128)S(1)} %get-tuple-element.26.refs_0_), channel_id=1, source_target_pairs={{0,2},{1,3},{2,0},{3,1},{4,6},{5,7},{6,4},{7,5},{8,10},{9,11},{10,... | collective-permute-start | bytes 110600 | tf_op jit(solution)/shard_map/ppermute | solution.py:25
  7.9 3.4 %collective-permute-start.2 = (f32[72,128]{1,0:T(8,128)S(1)}, f32[72,128]{1,0:T(8,128)S(1)}, u32[]{:S(2)}, u32[]{:S(2)}) collective-permute-start(f32[72,128]{1,0:T(8,128)S(1)} %get-tuple-element.26.refs_0_), channel_id=1, source_target_pairs={{0,3},{1,2},{2,1},{3,0},{4,7},{5,6},{6,5},{7,4},{8,11},{9,10},{10,... | collective-permute-start | bytes 110600 | tf_op jit(solution)/shard_map/ppermute | solution.py:25
  7.9 7.6 %collective-permute-start.6 = (f32[32,8,128]{2,1,0:T(8,128)S(1)}, f32[32,8,128]{2,1,0:T(8,128)S(1)}, u32[]{:S(2)}, u32[]{:S(2)}) collective-permute-start(f32[32,8,128]{2,1,0:T(8,128)S(1)} %get-tuple-element.28.refs_0_), channel_id=1, source_target_pairs={{0,1},{1,0},{2,3},{3,2},{4,5},{5,4},{6,7},{7,6},{8,9},{9,8},{10,11... | collective-permute-start | bytes 393224 | tf_op jit(solution)/shard_map/ppermute | solution.py:25
  8.1 9.2 %collective-permute-start.7 = (f32[32,8,128]{2,1,0:T(8,128)S(1)}, f32[32,8,128]{2,1,0:T(8,128)S(1)}, u32[]{:S(2)}, u32[]{:S(2)}) collective-permute-start(f32[32,8,128]{2,1,0:T(8,128)S(1)} %get-tuple-element.28.refs_0_), channel_id=1, source_target_pairs={{0,2},{1,3},{2,0},{3,1},{4,6},{5,7},{6,4},{7,5},{8,10},{9,11},{10,... | collective-permute-start | bytes 393224 | tf_op jit(solution)/shard_map/ppermute | solution.py:25
  10.0 7.3 %collective-permute-start.8 = (f32[32,8,128]{2,1,0:T(8,128)S(1)}, f32[32,8,128]{2,1,0:T(8,128)S(1)}, u32[]{:S(2)}, u32[]{:S(2)}) collective-permute-start(f32[32,8,128]{2,1,0:T(8,128)S(1)} %get-tuple-element.28.refs_0_), channel_id=1, source_target_pairs={{0,3},{1,2},{2,1},{3,0},{4,7},{5,6},{6,5},{7,4},{8,11},{9,10},{10,... | collective-permute-start | bytes 393224 | tf_op jit(solution)/shard_map/ppermute | solution.py:25
  11.3 12.0 %collective-permute-start.3 = (f32[160,128]{1,0:T(8,128)S(1)}, f32[160,128]{1,0:T(8,128)S(1)}, u32[]{:S(2)}, u32[]{:S(2)}) collective-permute-start(f32[160,128]{1,0:T(8,128)S(1)} %get-tuple-element.27.refs_0_), channel_id=1, source_target_pairs={{0,4},{4,0},{8,12},{12,8},{1,5},{5,1},{9,13},{13,9},{2,6},{6,2},{1... | collective-permute-start | bytes 245768 | tf_op jit(solution)/shard_map/ppermute | solution.py:25
  13.0 10.4 %collective-permute-start.4 = (f32[160,128]{1,0:T(8,128)S(1)}, f32[160,128]{1,0:T(8,128)S(1)}, u32[]{:S(2)}, u32[]{:S(2)}) collective-permute-start(f32[160,128]{1,0:T(8,128)S(1)} %get-tuple-element.27.refs_0_), channel_id=1, source_target_pairs={{0,8},{4,12},{8,0},{12,4},{1,9},{5,13},{9,1},{13,5},{2,10},{6,14},... | collective-permute-start | bytes 245768 | tf_op jit(solution)/shard_map/ppermute | solution.py:25
  15.6 7.8 %collective-permute-start.5 = (f32[160,128]{1,0:T(8,128)S(1)}, f32[160,128]{1,0:T(8,128)S(1)}, u32[]{:S(2)}, u32[]{:S(2)}) collective-permute-start(f32[160,128]{1,0:T(8,128)S(1)} %get-tuple-element.27.refs_0_), channel_id=1, source_target_pairs={{0,12},{4,8},{8,4},{12,0},{1,13},{5,9},{9,5},{13,1},{2,14},{6,10},... | collective-permute-start | bytes 245768 | tf_op jit(solution)/shard_map/ppermute | solution.py:25
  24.1 4.1 %collective-permute-start.10 = (f32[64,128]{1,0:T(8,128)S(1)}, f32[64,128]{1,0:T(8,128)S(1)}, u32[]{:S(2)}, u32[]{:S(2)}) collective-permute-start(f32[64,128]{1,0:T(8,128)S(1)} %get-tuple-element.39.message.refs_0_.refs_5_), channel_id=1, source_target_pairs={{0,2},{1,3},{2,0},{3,1},{4,6},{5,7},{6,4},{7,5},{8,10},{9,11},{10,... | collective-permute-start | bytes 98312 | tf_op jit(solution)/shard_map/ppermute | solution.py:25
  24.9 3.6 %collective-permute-start.11 = (f32[64,128]{1,0:T(8,128)S(1)}, f32[64,128]{1,0:T(8,128)S(1)}, u32[]{:S(2)}, u32[]{:S(2)}) collective-permute-start(f32[64,128]{1,0:T(8,128)S(1)} %get-tuple-element.39.message.refs_0_.refs_5_), channel_id=1, source_target_pairs={{0,3},{1,2},{2,1},{3,0},{4,7},{5,6},{6,5},{7,4},{8,11},{9,10},{10,... | collective-permute-start | bytes 98312 | tf_op jit(solution)/shard_map/ppermute | solution.py:25
  25.2 3.3 %collective-permute-start.9 = (f32[64,128]{1,0:T(8,128)S(1)}, f32[64,128]{1,0:T(8,128)S(1)}, u32[]{:S(2)}, u32[]{:S(2)}) collective-permute-start(f32[64,128]{1,0:T(8,128)S(1)} %get-tuple-element.39.message.refs_0_.refs_5_), channel_id=1, source_target_pairs={{0,1},{1,0},{2,3},{3,2},{4,5},{5,4},{6,7},{7,6},{8,9},{9,8},{10,11... | collective-permute-start | bytes 98312 | tf_op jit(solution)/shard_map/ppermute | solution.py:25

commit v13 on v12

--- a/solution.py
+++ b/solution.py
@@ -90,15 +90,21 @@
     return copies
 
 
-def write_moments(vector, basis, message, start):
-    slots, rank, _ = basis.shape
-    lane = iota((rank, LANES), 1)
-    columns = jnp.zeros((rank, LANES), jnp.float32)
-    for leaf in range(slots):
-        column = jnp.sum(basis[leaf] * vector[leaf : leaf + 1, :], axis=1, keepdims=True)
-        columns = jnp.where(lane == leaf, column, columns)
+def add_moment(columns, vector, basis, leaf):
+    column = jnp.sum(basis[leaf] * vector[leaf : leaf + 1, :], axis=1, keepdims=True)
+    return jnp.where(iota(columns.shape, 1) == leaf, column, columns)
+
+
+def write_moments(columns, message, start, slots):
+    rank = columns.shape[0]
     message[start : start + slots, :] = jnp.zeros((slots, LANES), jnp.float32)
     message[start : start + slots, 0:rank] = columns.T[0:slots]
+
+
+def sum_lanes(rows):
+    column = jnp.sum(rows, axis=1, keepdims=True)
+    diagonal = iota((rows.shape[0], LANES), 0) == iota((rows.shape[0], LANES), 1)
+    return jnp.sum(jnp.where(diagonal, column, 0.0), axis=0, keepdims=True)
 
 
 def box_moments(vector, box_basis):
@@ -106,9 +112,7 @@
     total = jnp.zeros((rank, width), jnp.float32)
     for leaf in range(slots):
         total = total + box_basis[leaf] * vector[leaf : leaf + 1, :]
-    column = jnp.sum(total, axis=1, keepdims=True)
-    diagonal = iota((rank, LANES), 0) == iota((rank, LANES), 1)
-    return jnp.sum(jnp.where(diagonal, column, 0.0), axis=0, keepdims=True)
+    return sum_lanes(total)
 
 
 def start_kernel(counts, *refs):
@@ -139,10 +143,13 @@
     ]
     message[slots : slots + TILE_ROWS, :] = jnp.zeros((TILE_ROWS, LANES), jnp.float32)
     message[slots + 1 : slots + 2, :] = lane_row(entries)
+    columns = jnp.zeros((rank, LANES), jnp.float32)
+    products = jnp.zeros((3 * rank, 3 * rank), jnp.float32)
     for leaf in range(slots):
         if leaf % step == 0:
             for copy in copies[4 + 2 * (leaf // step) : 6 + 2 * (leaf // step)]:
                 copy.wait()
+        columns = add_moment(columns, vector, basis, leaf)
         product = jnp.dot(
             transfer[leaf],
             basis[leaf],
@@ -152,11 +159,13 @@
         product = jnp.where(leaf < counts[0], product, 0.0)
         box_basis[leaf] = product
         parts[:, leaf * width : (leaf + 1) * width] = split_rows(product)
-    write_moments(initial, basis, message, 0)
+        if leaf % step == step - 1:
+            chunk = parts[:, (leaf + 1 - step) * width : (leaf + 1) * width]
+            products = products + lax.dot_general(
+                chunk, chunk, (((1,), (1,)), ((), ())), preferred_element_type=jnp.float32
+            )
+    write_moments(columns, message, 0, slots)
     message[slots : slots + 1, :] = box_moments(initial, box_basis)
-    products = lax.dot_general(
-        parts[...], parts[...], (((1,), (1,)), ((), ())), preferred_element_type=jnp.float32
-    )
     mixed = products[rank : 2 * rank, 0:rank] + products[2 * rank : 3 * rank, 0:rank]
     gram = products[0:rank, 0:rank] + (
         mixed + mixed.T + products[rank : 2 * rank, rank : 2 * rank]
@@ -169,7 +178,7 @@
 
 
 def join_kernel(subs, *refs):
-    messages, (moments, blocks) = refs[:subs], refs[subs:]
+    messages, (moments, blocks) = refs[:subs], refs[subs + 1 :]
     slots, span = moments.shape[0] // subs, blocks.shape[0] // subs
     for sub, message in enumerate(messages):
         moments[sub * slots : (sub + 1) * slots, :] = message[0:slots, :]
@@ -221,29 +230,29 @@
     return jnp.concatenate([rows, jnp.zeros((count, LANES - lanes), rows.dtype)], axis=1).T
 
 
-def add_leaf_far(counts, local, basis, near):
-    slots, rank, width = basis.shape
-    columns = wide_transpose(local)
-    for leaf in range(slots):
-        far = jnp.sum(basis[leaf] * columns[0:rank, leaf : leaf + 1], axis=0, keepdims=True)
-        near[leaf : leaf + 1, :] = jnp.where(
-            leaf < counts[0], near[leaf : leaf + 1, :] + far, 0.0
-        )
-
-
-def leaf_kernel(box, counts, moments, coupling, box_coupling, basis, far_list, *refs):
-    far, picks, weights, box_weights = refs
-    slots, rank, width = basis.shape
-    far_count, sources = far_list.shape[0], moments.shape[0]
+def leaf_far_row(counts, columns, basis, leaf, near):
+    rank = basis.shape[1]
+    far = jnp.sum(basis[leaf] * columns[0:rank, leaf : leaf + 1], axis=0, keepdims=True)
+    return jnp.where(leaf < counts[0], near + far, 0.0)
+
+
+def weights_kernel(box, coupling, box_coupling, far_list, *refs):
+    picks, weights, box_weights = refs
+    far_count, slots = far_list.shape
     far_rows = wide_transpose(far_list[...].astype(jnp.float32))
-    leaves = (iota((slots, sources), 1) ^ (box[0] * slots)).astype(jnp.float32)
+    leaves = (iota((slots, picks.shape[1]), 1) ^ (box[0] * slots)).astype(jnp.float32)
     for place in range(far_count):
         chosen = jnp.where(far_rows[0:slots, place : place + 1] == leaves, 1.0, 0.0)
         picks[place * slots : (place + 1) * slots, :] = chosen.astype(jnp.bfloat16)
     write_weights(coupling, weights)
     write_weights(box_coupling, box_weights)
-    far[...] = jnp.zeros((slots, width), jnp.float32)
-    add_leaf_far(counts, leaf_part(moments[:, 0:rank], picks, weights), basis, far)
+
+
+def leaf_kernel(counts, moments, basis, picks, weights, far):
+    slots, rank, width = basis.shape
+    columns = wide_transpose(leaf_part(moments[:, 0:rank], picks, weights))
+    for leaf in range(slots):
+        far[leaf : leaf + 1, :] = leaf_far_row(counts, columns, basis, leaf, 0.0)
 
 
 def first_near_kernel(subs, box, counts, *refs):
@@ -344,9 +353,13 @@
     start_scale = jnp.sqrt(square_sum / unknowns + EPSILON)
     one_one = square_sum / (start_scale * start_scale)
     basis_one[...] = initial[...] / start_scale
-    message[0:slots, :] = image[...] / start_scale
+    vector = image[...] / start_scale
+    message[0:slots, :] = vector
     numbers[...] = jnp.broadcast_to(lane_row([one_one, unknowns, start_scale]), numbers.shape)
-    write_moments(message, basis, message, slots)
+    columns = jnp.zeros((rank, LANES), jnp.float32)
+    for leaf in range(slots):
+        columns = add_moment(columns, vector, basis, leaf)
+    write_moments(columns, message, slots, slots)
 
 
 def share_kernel(message, basis_one, box_basis, share):
@@ -370,24 +383,24 @@
     for sub in range(subs):
         fields[sub * slots : (sub + 1) * slots, :] = messages[sub][0:slots, :]
 
-    def target(leaf, carry):
+    moments = jnp.concatenate([ref[slots : 2 * slots, 0:rank] for ref in messages], axis=0)
+    columns = wide_transpose(leaf_part(moments, picks, weights))
+    copy.wait()
+    box_sum = jnp.zeros(box_basis.shape[1:], jnp.float32)
+    for leaf in range(slots):
         total = jnp.zeros((width, width), jnp.float32)
         for column in range(neighbours):
             place = near_list[column, leaf] ^ (box[0] * slots)
             total = total + values[leaf * neighbours + column] * fields[pl.ds(place, 1), :]
-        part[pl.ds(leaf, 1), :] = jnp.sum(total.T, axis=0, keepdims=True)
-        return carry
-
-    moments = jnp.concatenate([ref[slots : 2 * slots, 0:rank] for ref in messages], axis=0)
-    local = leaf_part(moments, picks, weights)
-    copy.wait()
-    lax.fori_loop(0, slots, target, 0, unroll=True)
-    add_leaf_far(counts, local, basis, part)
+        near = jnp.sum(total.T, axis=0, keepdims=True)
+        near = leaf_far_row(counts, columns, basis, leaf, near)
+        part[leaf : leaf + 1, :] = near
+        box_sum = box_sum + box_basis[leaf] * near
     first, one, second = messages[0][0:slots, :], basis_one[...], part[...]
     products = [one * second, first * second, second * second]
     sums = lane_row([jnp.sum(product, keepdims=True) for product in products])
     sums = share[1:2, :] + pltpu.roll(sums, 2, 1)
-    both = share[0:1, :] + pltpu.roll(box_moments(part, box_basis), rank, 1)
+    both = share[0:1, :] + pltpu.roll(sum_lanes(box_sum), rank, 1)
     shares[...] = jnp.where(iota(shares.shape, 0) % 2 == 0, both, sums)
 
 
@@ -548,26 +561,26 @@
     leaf_basis, leaf_coupling, box_coupling, near_list, far_list = held
     messages = from_peers(message, "sub")
     geometry = from_peers(geometry, "sub")
+    picks, weights, box_weights = device_call(
+        weights_kernel,
+        [
+            kept(far_count * slots, sources, dtype=jnp.bfloat16),
+            kept(far_count, rank, 3 * rank, dtype=jnp.bfloat16),
+            kept(box_coupling.shape[0], rank, 3 * rank, dtype=jnp.bfloat16),
+        ],
+        [box],
+        [leaf_coupling, box_coupling, far_list],
+    )
     moments, blocks = device_call(
         functools.partial(join_kernel, subs),
         [kept(sources, LANES), kept(subs * span, LANES)],
         [],
-        messages,
+        [*messages, box_weights],
         cost=FIRST,
     )
     boxes = from_peers(blocks, "patch")
     gather = pltpu.VMEM((patches * subs * span, LANES), jnp.float32)
-    far, picks, weights, box_weights = device_call(
-        leaf_kernel,
-        [
-            rows,
-            kept(far_count * slots, sources, dtype=jnp.bfloat16),
-            kept(far_count, rank, 3 * rank, dtype=jnp.bfloat16),
-            kept(box_coupling.shape[0], rank, 3 * rank, dtype=jnp.bfloat16),
-        ],
-        [box, counts],
-        [moments, leaf_coupling, box_coupling, leaf_basis, far_list],
-    )
+    (far,) = device_call(leaf_kernel, [rows], [counts], [moments, leaf_basis, picks, weights])
     part, initial, values = device_call(
         functools.partial(first_near_kernel, subs),
         [rows, rows, kept(slots * neighbours, width, width)],

time: 45.6 us -> 45.8 us (level)
  Pallas kernels: 16.8 us -> 17.6 us
  waiting for transfers between devices: 3.39 us -> 2.78 us
    pallas_call x8 -> x9, Pallas kernels: 16.8 us -> 17.6 us  [device_call(): pl.pallas_call(kernel, out_shape=tuple(outputs), in_specs=[smem] * len(sc...]
    ppermute x12, waiting for transfers between devices: 3.39 us -> 2.78 us  [from_peers(): lax.ppermute(value, axis, [(i, i ^ turn) for i in range(size)])]
where the time goes in v13:
time: 45.8 us; the launch traced here: 45.6 us
  Pallas kernels  17.6 us (38%)
  starting transfers between devices  11.9 us (26%)
  blocking collectives  11.9 us (26%)
  waiting for transfers between devices  2.78 us (6%)
  between operations  1.39 us (3%)
    pallas_call x9, Pallas kernels, device_call(): pl.pallas_call(kernel, out_shape=tuple(outputs), in_specs=[smem] * len(sc...  17.6 us
    all_to_all x1, blocking collectives, shards(): shares = lax.all_to_all(shares, ('patch', 'sub'), 0, 0, tiled=True)  11.9 us
    ppermute x12, starting transfers between devices, from_peers(): lax.ppermute(value, axis, [(i, i ^ turn) for i in range(size)])  11.9 us
    ppermute x12, waiting for transfers between devices, from_peers(): lax.ppermute(value, axis, [(i, i ^ turn) for i in range(size)])  2.78 us
  transfers between devices with their start and end apart: 12, of which 3 were waited for; matrix products, arithmetic and copies ran while one was open for 0% of the time, Pallas kernels for 17%

profile of v13, /device:TPU:0, one launch (start us, length us, event | category | flops | bytes accessed | tf_op | source)
XLA Modules:
  0.0 45.6 jit_solution(18431123326976556425)
XLA Ops:
  1.3 4.2 %shard_map.122 = (f32[32,8,128]{2,1,0:T(8,128)S(1)}, f32[72,128]{1,0:T(8,128)S(1)}, f32[32,64,128]{2,1,0:T(8,128)S(1)}, f32[32,64,128]{2,1,0:T(8,128)S(1)}, f32[...) custom-call(s32[1]{0:T(128)S(6)} %copy.13.counts, ...), custom_call_target="tpu_custom_call" | custom-call | tf_op jit(solution)/shard_map/pallas_call | solution.py:40
  5.4 0.5 %collective-permute-start = (f32[72,128]{1,0:T(8,128)S(1)}, f32[72,128]{1,0:T(8,128)S(1)}, u32[]{:S(2)}, u32[]{:S(2)}) collective-permute-start(f32[72,128]{1,0:T(8,128)S(1)} %get-tuple-element.25.refs_0_), channel_id=1, source_target_pairs={{0,1},{1,0},{2,3},{3,2},{4,5},{5,4},{6,7},{7,6},{8,9},{9,8},{10,11... | collective-permute-start | bytes 110600 | tf_op jit(solution)/shard_map/ppermute | solution.py:25
  6.0 2.6 %collective-permute-start.1 = (f32[72,128]{1,0:T(8,128)S(1)}, f32[72,128]{1,0:T(8,128)S(1)}, u32[]{:S(2)}, u32[]{:S(2)}) collective-permute-start(f32[72,128]{1,0:T(8,128)S(1)} %get-tuple-element.25.refs_0_), channel_id=1, source_target_pairs={{0,2},{1,3},{2,0},{3,1},{4,6},{5,7},{6,4},{7,5},{8,10},{9,11},{10,... | collective-permute-start | bytes 110600 | tf_op jit(solution)/shard_map/ppermute | solution.py:25
  8.5 0.1 collective-permute-start.2
  8.6 0.1 collective-permute-start.6
  8.7 1.9 %collective-permute-start.7 = (f32[32,8,128]{2,1,0:T(8,128)S(1)}, f32[32,8,128]{2,1,0:T(8,128)S(1)}, u32[]{:S(2)}, u32[]{:S(2)}) collective-permute-start(f32[32,8,128]{2,1,0:T(8,128)S(1)} %get-tuple-element.31.refs_0_), channel_id=1, source_target_pairs={{0,2},{1,3},{2,0},{3,1},{4,6},{5,7},{6,4},{7,5},{8,10},{9,11},{10,... | collective-permute-start | bytes 393224 | tf_op jit(solution)/shard_map/ppermute | solution.py:25
  10.7 0.4 shard_map.123
  11.0 0.0 collective-permute-done.refs_1_
  11.0 0.1 collective-permute-start.8
  11.1 0.0 collective-permute-done.1.refs_2_
  11.1 0.8 %collective-permute-done.2.refs_3_ = f32[72,128]{1,0:T(8,128)S(1)} collective-permute-done((f32[72,128]{1,0:T(8,128)S(1)}, f32[72,128]{1,0:T(8,128)S(1)}, u32[]{:S(2)}, u32[]{:S(2)}) %collective-permute-start.2) | collective-permute-done | bytes 36896 | tf_op jit(solution)/shard_map/ppermute | solution.py:25
  12.0 1.6 %collective-permute-start.3 = (f32[160,128]{1,0:T(8,128)S(1)}, f32[160,128]{1,0:T(8,128)S(1)}, u32[]{:S(2)}, u32[]{:S(2)}) collective-permute-start(f32[160,128]{1,0:T(8,128)S(1)} %get-tuple-element.30.refs_0_), channel_id=1, source_target_pairs={{0,4},{4,0},{8,12},{12,8},{1,5},{5,1},{9,13},{13,9},{2,6},{6,2},{1... | collective-permute-start | bytes 245768 | tf_op jit(solution)/shard_map/ppermute | solution.py:25
  13.6 2.6 %collective-permute-start.4 = (f32[160,128]{1,0:T(8,128)S(1)}, f32[160,128]{1,0:T(8,128)S(1)}, u32[]{:S(2)}, u32[]{:S(2)}) collective-permute-start(f32[160,128]{1,0:T(8,128)S(1)} %get-tuple-element.30.refs_0_), channel_id=1, source_target_pairs={{0,8},{4,12},{8,0},{12,4},{1,9},{5,13},{9,1},{13,5},{2,10},{6,14},... | collective-permute-start | bytes 245768 | tf_op jit(solution)/shard_map/ppermute | solution.py:25
  16.2 0.0 collective-permute-done.6.refs_1_
  16.2 0.2 collective-permute-start.5
  16.4 1.2 %shard_map.125.refs_4_ = f32[32,128]{1,0:T(8,128)S(1)} custom-call(s32[1]{0:T(128)S(6)} %copy.13.counts, f32[128,128]{1,0:T(8,128)S(1)} %get-tuple-element.32.moments, f32[32,64,128]{2,1,0:T(8,128)S(1)} %get-tuple-element.33.basis.refs_6_, bf16[256,128]{1,0:T(8,128)(2,1)S(1)} %get-tuple-element.34.picks.refs_4_, ...), custom_call_target="tpu_custom_call" | custom-call | tf_op jit(solution)/shard_map/pallas_call | solution.py:40
  17.6 0.0 collective-permute-done.7.refs_2_
  17.7 0.0 collective-permute-done.8.refs_3_
  17.7 6.1 %shard_map.126 = (f32[32,128]{1,0:T(8,128)S(1)}, f32[32,128]{1,0:T(8,128)S(1)}, f32[288,128,128]{2,1,0:T(8,128)S(1)}) custom-call(s32[1]{0:T(128)} %bitcast.box, s32[1]{0:T(128)S(6)} %copy.13.counts, f32[32,8,128]{2,1,0:T(8,128)S(1)} %get-tuple-element.31.refs_0_, f32[32,8,128]{2,1,0:T(8,128)S(1)} %collective-permute-done.6.refs_1_, ...), custom_call_target="tpu_custom_call" | custom-call | tf_op jit(solution)/shard_map/pallas_call | solution.py:40
  23.7 0.0 collective-permute-done.3.refs_1_
  23.8 0.0 collective-permute-done.4.refs_2_
  23.8 0.0 collective-permute-done.5.refs_3_
  23.8 0.7 %shard_map.127 = (f32[64,128]{1,0:T(8,128)S(1)}, f32[32,128]{1,0:T(8,128)S(1)}, f32[8,128]{1,0:T(8,128)S(1)}) custom-call(s32[1]{0:T(128)} %bitcast.box, f32[160,128]{1,0:T(8,128)S(1)} %get-tuple-element.30.refs_0_, f32[160,128]{1,0:T(8,128)S(1)} %collective-permute-done.3.refs_1_, f32[160,128]{1,0:T(8,128)S(1)} %collective-permute-done.4.refs_2_, ...), custom_call_target="tpu_custom_call" | custom-call | tf_op jit(solution)/shard_map/pallas_call | solution.py:40
  24.4 0.8 %collective-permute-start.10 = (f32[64,128]{1,0:T(8,128)S(1)}, f32[64,128]{1,0:T(8,128)S(1)}, u32[]{:S(2)}, u32[]{:S(2)}) collective-permute-start(f32[64,128]{1,0:T(8,128)S(1)} %get-tuple-element.40.message.refs_0_.refs_5_), channel_id=1, source_target_pairs={{0,2},{1,3},{2,0},{3,1},{4,6},{5,7},{6,4},{7,5},{8,10},{9,11},{10,... | collective-permute-start | bytes 98312 | tf_op jit(solution)/shard_map/ppermute | solution.py:25
  25.2 0.6 %collective-permute-start.11 = (f32[64,128]{1,0:T(8,128)S(1)}, f32[64,128]{1,0:T(8,128)S(1)}, u32[]{:S(2)}, u32[]{:S(2)}) collective-permute-start(f32[64,128]{1,0:T(8,128)S(1)} %get-tuple-element.40.message.refs_0_.refs_5_), channel_id=1, source_target_pairs={{0,3},{1,2},{2,1},{3,0},{4,7},{5,6},{6,5},{7,4},{8,11},{9,10},{10,... | collective-permute-start | bytes 98312 | tf_op jit(solution)/shard_map/ppermute | solution.py:25
  25.9 0.7 %collective-permute-start.9 = (f32[64,128]{1,0:T(8,128)S(1)}, f32[64,128]{1,0:T(8,128)S(1)}, u32[]{:S(2)}, u32[]{:S(2)}) collective-permute-start(f32[64,128]{1,0:T(8,128)S(1)} %get-tuple-element.40.message.refs_0_.refs_5_), channel_id=1, source_target_pairs={{0,1},{1,0},{2,3},{3,2},{4,5},{5,4},{6,7},{7,6},{8,9},{9,8},{10,11... | collective-permute-start | bytes 98312 | tf_op jit(solution)/shard_map/ppermute | solution.py:25
  26.6 0.2 shard_map.128.refs_9_
  26.8 1.7 %collective-permute-done.10.refs_2_ = f32[64,128]{1,0:T(8,128)S(1)} collective-permute-done((f32[64,128]{1,0:T(8,128)S(1)}, f32[64,128]{1,0:T(8,128)S(1)}, u32[]{:S(2)}, u32[]{:S(2)}) %collective-permute-start.10) | collective-permute-done | bytes 32800 | tf_op jit(solution)/shard_map/ppermute | solution.py:25
  28.5 0.2 collective-permute-done.11.refs_3_
  28.7 2.8 %shard_map.129 = (f32[32,128]{1,0:T(8,128)S(1)}, f32[32,128]{1,0:T(8,128)S(1)}) custom-call(s32[1]{0:T(128)} %bitcast.box, s32[1]{0:T(128)S(6)} %copy.13.counts, f32[64,128]{1,0:T(8,128)S(1)} %get-tuple-element.40.message.refs_0_.refs_5_, f32[64,128]{1,0:T(8,128)S(1)} %collective-permute-done.9.refs_1_, f32[64,128]{1,0:T(8,128)S(1)} %collective-permute-done.10.refs_2_, ...), custom_call_target="tpu_custom_call" | custom-call | tf_op jit(solution)/shard_map/pallas_call | solution.py:40
  31.5 11.9 %all_to_all.11 = f32[16,2,128]{2,1,0:T(2,128)S(1)} all-to-all(f32[16,2,128]{2,1,0:T(2,128)S(1)} %bitcast.9), channel_id=1, replica_groups=mesh['groups'=2,'patch'=4,'sub'=4] {'patch','sub'}, dimensions={0} | all-to-all | bytes 32768 | tf_op jit(solution)/shard_map/all_to_all | solution.py:618
  43.4 2.2 %shard_map.130 = (f32[32,128]{1,0:T(8,128)}, f32[2,3]{1,0:T(2,128)}) custom-call(s32[1]{0:T(128)} %bitcast.box, f32[160,128]{1,0:T(8,128)S(1)} %get-tuple-element.30.refs_0_, f32[160,128]{1,0:T(8,128)S(1)} %collective-permute-done.3.refs_1_, f32[160,128]{1,0:T(8,128)S(1)} %collective-permute-done.4.refs_2_, f32[160,128]{1,0:T(8,128)S(1)} %collective-permute-done.5.refs_3_, ...), custom_call_target="tpu_custom_call" | custom-call | tf_op jit(solution)/shard_map/pallas_call | solution.py:40
  (2 shorter events, 0.0 us)
Async XLA Ops:
  5.4 5.6 %collective-permute-start = (f32[72,128]{1,0:T(8,128)S(1)}, f32[72,128]{1,0:T(8,128)S(1)}, u32[]{:S(2)}, u32[]{:S(2)}) collective-permute-start(f32[72,128]{1,0:T(8,128)S(1)} %get-tuple-element.25.refs_0_), channel_id=1, source_target_pairs={{0,1},{1,0},{2,3},{3,2},{4,5},{5,4},{6,7},{7,6},{8,9},{9,8},{10,11... | collective-permute-start | bytes 110600 | tf_op jit(solution)/shard_map/ppermute | solution.py:25
  6.0 5.2 %collective-permute-start.1 = (f32[72,128]{1,0:T(8,128)S(1)}, f32[72,128]{1,0:T(8,128)S(1)}, u32[]{:S(2)}, u32[]{:S(2)}) collective-permute-start(f32[72,128]{1,0:T(8,128)S(1)} %get-tuple-element.25.refs_0_), channel_id=1, source_target_pairs={{0,2},{1,3},{2,0},{3,1},{4,6},{5,7},{6,4},{7,5},{8,10},{9,11},{10,... | collective-permute-start | bytes 110600 | tf_op jit(solution)/shard_map/ppermute | solution.py:25
  8.5 3.4 %collective-permute-start.2 = (f32[72,128]{1,0:T(8,128)S(1)}, f32[72,128]{1,0:T(8,128)S(1)}, u32[]{:S(2)}, u32[]{:S(2)}) collective-permute-start(f32[72,128]{1,0:T(8,128)S(1)} %get-tuple-element.25.refs_0_), channel_id=1, source_target_pairs={{0,3},{1,2},{2,1},{3,0},{4,7},{5,6},{6,5},{7,4},{8,11},{9,10},{10,... | collective-permute-start | bytes 110600 | tf_op jit(solution)/shard_map/ppermute | solution.py:25
  8.6 7.6 %collective-permute-start.6 = (f32[32,8,128]{2,1,0:T(8,128)S(1)}, f32[32,8,128]{2,1,0:T(8,128)S(1)}, u32[]{:S(2)}, u32[]{:S(2)}) collective-permute-start(f32[32,8,128]{2,1,0:T(8,128)S(1)} %get-tuple-element.31.refs_0_), channel_id=1, source_target_pairs={{0,1},{1,0},{2,3},{3,2},{4,5},{5,4},{6,7},{7,6},{8,9},{9,8},{10,11... | collective-permute-start | bytes 393224 | tf_op jit(solution)/shard_map/ppermute | solution.py:25
  8.7 8.9 %collective-permute-start.7 = (f32[32,8,128]{2,1,0:T(8,128)S(1)}, f32[32,8,128]{2,1,0:T(8,128)S(1)}, u32[]{:S(2)}, u32[]{:S(2)}) collective-permute-start(f32[32,8,128]{2,1,0:T(8,128)S(1)} %get-tuple-element.31.refs_0_), channel_id=1, source_target_pairs={{0,2},{1,3},{2,0},{3,1},{4,6},{5,7},{6,4},{7,5},{8,10},{9,11},{10,... | collective-permute-start | bytes 393224 | tf_op jit(solution)/shard_map/ppermute | solution.py:25
  11.0 6.6 %collective-permute-start.8 = (f32[32,8,128]{2,1,0:T(8,128)S(1)}, f32[32,8,128]{2,1,0:T(8,128)S(1)}, u32[]{:S(2)}, u32[]{:S(2)}) collective-permute-start(f32[32,8,128]{2,1,0:T(8,128)S(1)} %get-tuple-element.31.refs_0_), channel_id=1, source_target_pairs={{0,3},{1,2},{2,1},{3,0},{4,7},{5,6},{6,5},{7,4},{8,11},{9,10},{10,... | collective-permute-start | bytes 393224 | tf_op jit(solution)/shard_map/ppermute | solution.py:25
  12.0 11.8 %collective-permute-start.3 = (f32[160,128]{1,0:T(8,128)S(1)}, f32[160,128]{1,0:T(8,128)S(1)}, u32[]{:S(2)}, u32[]{:S(2)}) collective-permute-start(f32[160,128]{1,0:T(8,128)S(1)} %get-tuple-element.30.refs_0_), channel_id=1, source_target_pairs={{0,4},{4,0},{8,12},{12,8},{1,5},{5,1},{9,13},{13,9},{2,6},{6,2},{1... | collective-permute-start | bytes 245768 | tf_op jit(solution)/shard_map/ppermute | solution.py:25
  13.6 10.1 %collective-permute-start.4 = (f32[160,128]{1,0:T(8,128)S(1)}, f32[160,128]{1,0:T(8,128)S(1)}, u32[]{:S(2)}, u32[]{:S(2)}) collective-permute-start(f32[160,128]{1,0:T(8,128)S(1)} %get-tuple-element.30.refs_0_), channel_id=1, source_target_pairs={{0,8},{4,12},{8,0},{12,4},{1,9},{5,13},{9,1},{13,5},{2,10},{6,14},... | collective-permute-start | bytes 245768 | tf_op jit(solution)/shard_map/ppermute | solution.py:25
  16.2 7.6 %collective-permute-start.5 = (f32[160,128]{1,0:T(8,128)S(1)}, f32[160,128]{1,0:T(8,128)S(1)}, u32[]{:S(2)}, u32[]{:S(2)}) collective-permute-start(f32[160,128]{1,0:T(8,128)S(1)} %get-tuple-element.30.refs_0_), channel_id=1, source_target_pairs={{0,12},{4,8},{8,4},{12,0},{1,13},{5,9},{9,5},{13,1},{2,14},{6,10},... | collective-permute-start | bytes 245768 | tf_op jit(solution)/shard_map/ppermute | solution.py:25
  24.4 4.1 %collective-permute-start.10 = (f32[64,128]{1,0:T(8,128)S(1)}, f32[64,128]{1,0:T(8,128)S(1)}, u32[]{:S(2)}, u32[]{:S(2)}) collective-permute-start(f32[64,128]{1,0:T(8,128)S(1)} %get-tuple-element.40.message.refs_0_.refs_5_), channel_id=1, source_target_pairs={{0,2},{1,3},{2,0},{3,1},{4,6},{5,7},{6,4},{7,5},{8,10},{9,11},{10,... | collective-permute-start | bytes 98312 | tf_op jit(solution)/shard_map/ppermute | solution.py:25
  25.2 3.5 %collective-permute-start.11 = (f32[64,128]{1,0:T(8,128)S(1)}, f32[64,128]{1,0:T(8,128)S(1)}, u32[]{:S(2)}, u32[]{:S(2)}) collective-permute-start(f32[64,128]{1,0:T(8,128)S(1)} %get-tuple-element.40.message.refs_0_.refs_5_), channel_id=1, source_target_pairs={{0,3},{1,2},{2,1},{3,0},{4,7},{5,6},{6,5},{7,4},{8,11},{9,10},{10,... | collective-permute-start | bytes 98312 | tf_op jit(solution)/shard_map/ppermute | solution.py:25
  25.9 2.8 %collective-permute-start.9 = (f32[64,128]{1,0:T(8,128)S(1)}, f32[64,128]{1,0:T(8,128)S(1)}, u32[]{:S(2)}, u32[]{:S(2)}) collective-permute-start(f32[64,128]{1,0:T(8,128)S(1)} %get-tuple-element.40.message.refs_0_.refs_5_), channel_id=1, source_target_pairs={{0,1},{1,0},{2,3},{3,2},{4,5},{5,4},{6,7},{7,6},{8,9},{9,8},{10,11... | collective-permute-start | bytes 98312 | tf_op jit(solution)/shard_map/ppermute | solution.py:25

commit v14 on v13

--- a/solution.py
+++ b/solution.py
@@ -15,7 +15,7 @@
 LANES = 128
 TILE_ROWS = 8
 VMEM_LIMIT = 16 << 20
-CHUNKS = 4
+CHUNKS = 2
 FIRST = pl.CostEstimate(flops=10**11, bytes_accessed=10**10, transcendentals=0)
 
 
@@ -144,7 +144,6 @@
     message[slots : slots + TILE_ROWS, :] = jnp.zeros((TILE_ROWS, LANES), jnp.float32)
     message[slots + 1 : slots + 2, :] = lane_row(entries)
     columns = jnp.zeros((rank, LANES), jnp.float32)
-    products = jnp.zeros((3 * rank, 3 * rank), jnp.float32)
     for leaf in range(slots):
         if leaf % step == 0:
             for copy in copies[4 + 2 * (leaf // step) : 6 + 2 * (leaf // step)]:
@@ -159,13 +158,11 @@
         product = jnp.where(leaf < counts[0], product, 0.0)
         box_basis[leaf] = product
         parts[:, leaf * width : (leaf + 1) * width] = split_rows(product)
-        if leaf % step == step - 1:
-            chunk = parts[:, (leaf + 1 - step) * width : (leaf + 1) * width]
-            products = products + lax.dot_general(
-                chunk, chunk, (((1,), (1,)), ((), ())), preferred_element_type=jnp.float32
-            )
     write_moments(columns, message, 0, slots)
     message[slots : slots + 1, :] = box_moments(initial, box_basis)
+    products = lax.dot_general(
+        parts[...], parts[...], (((1,), (1,)), ((), ())), preferred_element_type=jnp.float32
+    )
     mixed = products[rank : 2 * rank, 0:rank] + products[2 * rank : 3 * rank, 0:rank]
     gram = products[0:rank, 0:rank] + (
         mixed + mixed.T + products[rank : 2 * rank, rank : 2 * rank]
@@ -362,13 +359,31 @@
     write_moments(columns, message, slots, slots)
 
 
-def share_kernel(message, basis_one, box_basis, share):
-    slots = basis_one.shape[0]
+def share_kernel(patches, span, box, *refs):
+    boxes, (message, basis_one, box_basis) = refs[:patches], refs[patches : patches + 3]
+    share, starts, rows, grams, gather, lists = refs[patches + 3 :]
+    slots, rank, _ = box_basis.shape
     first, one = message[0:slots, :], basis_one[...]
     products = [one * first, first * first]
     share[...] = jnp.zeros_like(share)
     share[0:1, :] = box_moments(message, box_basis)
     share[1:2, :] = lane_row([jnp.sum(product, keepdims=True) for product in products])
+    height, count, half = boxes[0].shape[0], starts.shape[0], rank // 2
+    for place, ref in enumerate(boxes):
+        gather[place * height : (place + 1) * height, :] = ref[...]
+    for other in range(count):
+        row = (box[0] ^ other) * span
+        starts[other : other + 1, :] = gather[pl.ds(row, 1), :]
+        lists[other : other + 1, :] = gather[pl.ds(row + 1, 1), :]
+        grams[other * half : (other + 1) * half, :] = gather[pl.ds(row + TILE_ROWS, half), :]
+    column = iota((count, 3 * count), 1)
+    chosen = []
+    for place in range(rows.shape[0] // (3 * count)):
+        wanted = lists[:, 2 + place : 3 + place]
+        for split in range(3):
+            number = (column - split * count).astype(jnp.float32)
+            chosen.append(jnp.where(wanted == number, 1.0, 0.0))
+    rows[...] = jnp.concatenate(chosen).astype(jnp.bfloat16)
 
 
 def second_near_kernel(subs, box, counts, *refs):
@@ -404,33 +419,17 @@
     shares[...] = jnp.where(iota(shares.shape, 0) % 2 == 0, both, sums)
 
 
-def last_kernel(patches, span, box, *refs):
-    boxes, (shares, message, basis_one, part, numbers) = refs[:patches], refs[patches : patches + 5]
-    box_basis, box_weights = refs[patches + 5 : patches + 7]
-    basis_three, hessenberg, gather, starts, lists, pairs, image = refs[patches + 7 :]
+def last_kernel(box, *refs):
+    shares, message, basis_one, part, numbers, starts, rows, grams = refs[:8]
+    box_basis, box_weights, basis_three, hessenberg, pairs, image = refs[8:]
     slots, rank, width = box_basis.shape
-    height = boxes[0].shape[0]
-    count = patches * (height // span)
-    for place, ref in enumerate(boxes):
-        gather[place * height : (place + 1) * height, :] = ref[...]
+    count = starts.shape[0]
     for other in range(count):
-        row = (box[0] ^ other) * span
-        starts[other : other + 1, :] = gather[pl.ds(row, 1), :]
-        lists[other : other + 1, :] = gather[pl.ds(row + 1, 1), :]
         pairs[other : other + 1, :] = shares[2 * other : 2 * other + 1, :]
         pairs[count + other : count + other + 1, :] = shares[2 * other + 1 : 2 * other + 2, :]
     first_box, second_box = pairs[0:count, 0:rank], pairs[0:count, rank : 2 * rank]
-    column = iota((count, 3 * count), 1)
-    rows = []
-    for place in range(box_weights.shape[0]):
-        wanted = lists[:, 2 + place : 3 + place]
-        for split in range(3):
-            number = (column - split * count).astype(jnp.float32)
-            rows.append(jnp.where(wanted == number, 1.0, 0.0))
     chosen_rows = jnp.dot(
-        jnp.concatenate(rows).astype(jnp.bfloat16),
-        split_rows(first_box),
-        preferred_element_type=jnp.float32,
+        rows[...], split_rows(first_box), preferred_element_type=jnp.float32
     ).astype(jnp.bfloat16)
 
     def chosen(place):
@@ -443,11 +442,11 @@
     low = iota((half, 2 * rank), 1) < rank
     quadratic = jnp.zeros((half, 2 * rank), jnp.float32)
     for other in range(count):
-        row = (box[0] ^ other) * span + TILE_ROWS
         column = jnp.where(
             low, columns[0:half, other : other + 1], columns[half:rank, other : other + 1]
         )
-        quadratic = quadratic + gather[pl.ds(row, half), :] * twice[other : other + 1, :] * column
+        gram = grams[other * half : (other + 1) * half, :]
+        quadratic = quadratic + gram * twice[other : other + 1, :] * column
     one_one, unknowns, start_scale = [numbers[0:1, place : place + 1] for place in range(3)]
     sums = jnp.sum(pairs[count : 2 * count, :], axis=0, keepdims=True)
     along, image_sq, one_part, first_part, part_sq = [
@@ -579,7 +578,6 @@
         cost=FIRST,
     )
     boxes = from_peers(blocks, "patch")
-    gather = pltpu.VMEM((patches * subs * span, LANES), jnp.float32)
     (far,) = device_call(leaf_kernel, [rows], [counts], [moments, leaf_basis, picks, weights])
     part, initial, values = device_call(
         functools.partial(first_near_kernel, subs),
@@ -605,8 +603,21 @@
         ],
     )
     messages = from_peers(message, "sub")
-    (share,) = device_call(
-        share_kernel, [kept(TILE_ROWS, LANES)], [], [message, basis_one, box_basis]
+    count, places = patches * subs, box_far.shape[1]
+    share, starts, chosen, grams = device_call(
+        functools.partial(share_kernel, patches, span),
+        [
+            kept(TILE_ROWS, LANES),
+            kept(count, LANES),
+            kept(places * 3 * count, 3 * count, dtype=jnp.bfloat16),
+            kept(count * (rank // 2), LANES),
+        ],
+        [box],
+        [*boxes, message, basis_one, box_basis],
+        [
+            pltpu.VMEM((count * span, LANES), jnp.float32),
+            pltpu.VMEM((count, LANES), jnp.float32),
+        ],
     )
     part, shares = device_call(
         functools.partial(second_near_kernel, subs),
@@ -617,15 +628,23 @@
     )
     shares = lax.all_to_all(shares, ("patch", "sub"), 0, 0, tiled=True)
     basis_three, hessenberg = device_call(
-        functools.partial(last_kernel, patches, span),
+        last_kernel,
         [f32(slots, width), f32(2, 3)],
         [box],
-        [*boxes, shares, message, basis_one, part, numbers, box_basis, box_weights],
-        [
-            gather,
-            pltpu.VMEM((patches * subs, LANES), jnp.float32),
-            pltpu.VMEM((patches * subs, LANES), jnp.float32),
-            pltpu.VMEM((2 * patches * subs, LANES), jnp.float32),
+        [
+            shares,
+            message,
+            basis_one,
+            part,
+            numbers,
+            starts,
+            chosen,
+            grams,
+            box_basis,
+            box_weights,
+        ],
+        [
+            pltpu.VMEM((2 * count, LANES), jnp.float32),
             pltpu.VMEM((slots, width), jnp.float32),
         ],
     )

time: 45.8 us -> 44.9 us (0.980)
  Pallas kernels: 17.6 us -> 16.8 us
    pallas_call x9, Pallas kernels: 17.6 us -> 16.8 us  [device_call(): pl.pallas_call(kernel, out_shape=tuple(outputs), in_specs=[smem] * len(sc...]
  transfers between devices with their start and end apart: 12 -> 12, of which waited for: 3 -> 3; matrix products, arithmetic and copies ran while one was open for 0% -> 0% of each run, Pallas kernels for 17% -> 18%
where the time goes in v14:
time: 44.9 us; the launch traced here: 44.7 us
  Pallas kernels  16.8 us (37%)
  starting transfers between devices  11.9 us (27%)
  blocking collectives  11.9 us (27%)
  waiting for transfers between devices  2.68 us (6%)
  between operations  1.4 us (3%)
    pallas_call x9, Pallas kernels, device_call(): pl.pallas_call(kernel, out_shape=tuple(outputs), in_specs=[smem] * len(sc...  16.8 us
    all_to_all x1, blocking collectives, shards(): shares = lax.all_to_all(shares, ('patch', 'sub'), 0, 0, tiled=True)  11.9 us
    ppermute x12, starting transfers between devices, from_peers(): lax.ppermute(value, axis, [(i, i ^ turn) for i in range(size)])  11.9 us
    ppermute x12, waiting for transfers between devices, from_peers(): lax.ppermute(value, axis, [(i, i ^ turn) for i in range(size)])  2.68 us
  transfers between devices with their start and end apart: 12, of which 3 were waited for; matrix products, arithmetic and copies ran while one was open for 0% of the time, Pallas kernels for 18%

profile of v14, /device:TPU:0, one launch (start us, length us, event | category | flops | bytes accessed | tf_op | source)
XLA Modules:
  0.0 44.7 jit_solution(11900671822031241264)
XLA Ops:
  1.3 3.4 %shard_map.122 = (f32[32,8,128]{2,1,0:T(8,128)S(1)}, f32[72,128]{1,0:T(8,128)S(1)}, f32[32,64,128]{2,1,0:T(8,128)S(1)}, f32[32,64,128]{2,1,0:T(8,128)S(1)}, f32[...) custom-call(s32[1]{0:T(128)S(6)} %copy.13.counts, ...), custom_call_target="tpu_custom_call" | custom-call | tf_op jit(solution)/shard_map/pallas_call | solution.py:40
  4.7 0.5 %collective-permute-start = (f32[72,128]{1,0:T(8,128)S(1)}, f32[72,128]{1,0:T(8,128)S(1)}, u32[]{:S(2)}, u32[]{:S(2)}) collective-permute-start(f32[72,128]{1,0:T(8,128)S(1)} %get-tuple-element.29.refs_0_), channel_id=1, source_target_pairs={{0,1},{1,0},{2,3},{3,2},{4,5},{5,4},{6,7},{7,6},{8,9},{9,8},{10,11... | collective-permute-start | bytes 110600 | tf_op jit(solution)/shard_map/ppermute | solution.py:25
  5.2 2.6 %collective-permute-start.1 = (f32[72,128]{1,0:T(8,128)S(1)}, f32[72,128]{1,0:T(8,128)S(1)}, u32[]{:S(2)}, u32[]{:S(2)}) collective-permute-start(f32[72,128]{1,0:T(8,128)S(1)} %get-tuple-element.29.refs_0_), channel_id=1, source_target_pairs={{0,2},{1,3},{2,0},{3,1},{4,6},{5,7},{6,4},{7,5},{8,10},{9,11},{10,... | collective-permute-start | bytes 110600 | tf_op jit(solution)/shard_map/ppermute | solution.py:25
  7.7 0.1 collective-permute-start.2
  7.8 0.1 collective-permute-start.6
  7.9 1.9 %collective-permute-start.7 = (f32[32,8,128]{2,1,0:T(8,128)S(1)}, f32[32,8,128]{2,1,0:T(8,128)S(1)}, u32[]{:S(2)}, u32[]{:S(2)}) collective-permute-start(f32[32,8,128]{2,1,0:T(8,128)S(1)} %get-tuple-element.35.refs_0_), channel_id=1, source_target_pairs={{0,2},{1,3},{2,0},{3,1},{4,6},{5,7},{6,4},{7,5},{8,10},{9,11},{10,... | collective-permute-start | bytes 393224 | tf_op jit(solution)/shard_map/ppermute | solution.py:25
  9.9 0.4 shard_map.123
  10.2 0.0 collective-permute-done.refs_1_
  10.2 0.1 collective-permute-start.8
  10.3 0.0 collective-permute-done.1.refs_2_
  10.3 0.8 %collective-permute-done.2.refs_3_ = f32[72,128]{1,0:T(8,128)S(1)} collective-permute-done((f32[72,128]{1,0:T(8,128)S(1)}, f32[72,128]{1,0:T(8,128)S(1)}, u32[]{:S(2)}, u32[]{:S(2)}) %collective-permute-start.2) | collective-permute-done | bytes 36896 | tf_op jit(solution)/shard_map/ppermute | solution.py:25
  11.2 1.6 %collective-permute-start.3 = (f32[160,128]{1,0:T(8,128)S(1)}, f32[160,128]{1,0:T(8,128)S(1)}, u32[]{:S(2)}, u32[]{:S(2)}) collective-permute-start(f32[160,128]{1,0:T(8,128)S(1)} %get-tuple-element.34.refs_0_), channel_id=1, source_target_pairs={{0,4},{4,0},{8,12},{12,8},{1,5},{5,1},{9,13},{13,9},{2,6},{6,2},{1... | collective-permute-start | bytes 245768 | tf_op jit(solution)/shard_map/ppermute | solution.py:25
  12.8 2.6 %collective-permute-start.4 = (f32[160,128]{1,0:T(8,128)S(1)}, f32[160,128]{1,0:T(8,128)S(1)}, u32[]{:S(2)}, u32[]{:S(2)}) collective-permute-start(f32[160,128]{1,0:T(8,128)S(1)} %get-tuple-element.34.refs_0_), channel_id=1, source_target_pairs={{0,8},{4,12},{8,0},{12,4},{1,9},{5,13},{9,1},{13,5},{2,10},{6,14},... | collective-permute-start | bytes 245768 | tf_op jit(solution)/shard_map/ppermute | solution.py:25
  15.4 0.0 collective-permute-done.6.refs_1_
  15.4 0.2 collective-permute-start.5
  15.6 1.2 %shard_map.125.refs_4_ = f32[32,128]{1,0:T(8,128)S(1)} custom-call(s32[1]{0:T(128)S(6)} %copy.13.counts, f32[128,128]{1,0:T(8,128)S(1)} %get-tuple-element.36.moments, f32[32,64,128]{2,1,0:T(8,128)S(1)} %get-tuple-element.37.basis.refs_6_, bf16[256,128]{1,0:T(8,128)(2,1)S(1)} %get-tuple-element.38.picks.refs_4_, ...), custom_call_target="tpu_custom_call" | custom-call | tf_op jit(solution)/shard_map/pallas_call | solution.py:40
  16.9 0.0 collective-permute-done.7.refs_2_
  16.9 0.0 collective-permute-done.8.refs_3_
  16.9 6.1 %shard_map.126 = (f32[32,128]{1,0:T(8,128)S(1)}, f32[32,128]{1,0:T(8,128)S(1)}, f32[288,128,128]{2,1,0:T(8,128)S(1)}) custom-call(s32[1]{0:T(128)} %bitcast.box, s32[1]{0:T(128)S(6)} %copy.13.counts, f32[32,8,128]{2,1,0:T(8,128)S(1)} %get-tuple-element.35.refs_0_, f32[32,8,128]{2,1,0:T(8,128)S(1)} %collective-permute-done.6.refs_1_, ...), custom_call_target="tpu_custom_call" | custom-call | tf_op jit(solution)/shard_map/pallas_call | solution.py:40
  23.0 0.0 collective-permute-done.3.refs_1_
  23.0 0.0 collective-permute-done.4.refs_2_
  23.0 0.0 collective-permute-done.5.refs_3_
  23.0 0.7 %shard_map.127 = (f32[64,128]{1,0:T(8,128)S(1)}, f32[32,128]{1,0:T(8,128)S(1)}, f32[8,128]{1,0:T(8,128)S(1)}) custom-call(s32[1]{0:T(128)} %bitcast.box, f32[160,128]{1,0:T(8,128)S(1)} %get-tuple-element.34.refs_0_, f32[160,128]{1,0:T(8,128)S(1)} %collective-permute-done.3.refs_1_, f32[160,128]{1,0:T(8,128)S(1)} %collective-permute-done.4.refs_2_, ...), custom_call_target="tpu_custom_call" | custom-call | tf_op jit(solution)/shard_map/pallas_call | solution.py:40
  23.6 0.8 %collective-permute-start.10 = (f32[64,128]{1,0:T(8,128)S(1)}, f32[64,128]{1,0:T(8,128)S(1)}, u32[]{:S(2)}, u32[]{:S(2)}) collective-permute-start(f32[64,128]{1,0:T(8,128)S(1)} %get-tuple-element.44.refs_4_.refs_0_.refs_1_), channel_id=1, source_target_pairs={{0,2},{1,3},{2,0},{3,1},{4,6},{5,7},{6,4},{7,5},{8,10},{9,11},{10,... | collective-permute-start | bytes 98312 | tf_op jit(solution)/shard_map/ppermute | solution.py:25
  24.4 0.6 %collective-permute-start.11 = (f32[64,128]{1,0:T(8,128)S(1)}, f32[64,128]{1,0:T(8,128)S(1)}, u32[]{:S(2)}, u32[]{:S(2)}) collective-permute-start(f32[64,128]{1,0:T(8,128)S(1)} %get-tuple-element.44.refs_4_.refs_0_.refs_1_), channel_id=1, source_target_pairs={{0,3},{1,2},{2,1},{3,0},{4,7},{5,6},{6,5},{7,4},{8,11},{9,10},{10,... | collective-permute-start | bytes 98312 | tf_op jit(solution)/shard_map/ppermute | solution.py:25
  25.1 0.7 %collective-permute-start.9 = (f32[64,128]{1,0:T(8,128)S(1)}, f32[64,128]{1,0:T(8,128)S(1)}, u32[]{:S(2)}, u32[]{:S(2)}) collective-permute-start(f32[64,128]{1,0:T(8,128)S(1)} %get-tuple-element.44.refs_4_.refs_0_.refs_1_), channel_id=1, source_target_pairs={{0,1},{1,0},{2,3},{3,2},{4,5},{5,4},{6,7},{7,6},{8,9},{9,8},{10,11... | collective-permute-start | bytes 98312 | tf_op jit(solution)/shard_map/ppermute | solution.py:25
  25.8 0.3 shard_map.128
  26.1 1.6 %collective-permute-done.10.refs_2_ = f32[64,128]{1,0:T(8,128)S(1)} collective-permute-done((f32[64,128]{1,0:T(8,128)S(1)}, f32[64,128]{1,0:T(8,128)S(1)}, u32[]{:S(2)}, u32[]{:S(2)}) %collective-permute-start.10) | collective-permute-done | bytes 32800 | tf_op jit(solution)/shard_map/ppermute | solution.py:25
  27.7 0.2 collective-permute-done.11.refs_3_
  27.9 2.8 %shard_map.129 = (f32[32,128]{1,0:T(8,128)S(1)}, f32[32,128]{1,0:T(8,128)S(1)}) custom-call(s32[1]{0:T(128)} %bitcast.box, s32[1]{0:T(128)S(6)} %copy.13.counts, f32[64,128]{1,0:T(8,128)S(1)} %get-tuple-element.44.refs_4_.refs_0_.refs_1_, f32[64,128]{1,0:T(8,128)S(1)} %collective-permute-done.9.refs_1_, f32[64,128]{1,0:T(8,128)S(1)} %collective-permute-done.10.refs_2_, ...), custom_call_target="tpu_custom_call" | custom-call | tf_op jit(solution)/shard_map/pallas_call | solution.py:40
  30.7 11.9 %all_to_all.11 = f32[16,2,128]{2,1,0:T(2,128)S(1)} all-to-all(f32[16,2,128]{2,1,0:T(2,128)S(1)} %bitcast.9), channel_id=1, replica_groups=mesh['groups'=2,'patch'=4,'sub'=4] {'patch','sub'}, dimensions={0} | all-to-all | bytes 32768 | tf_op jit(solution)/shard_map/all_to_all | solution.py:629
  42.6 2.1 %shard_map.130 = (f32[32,128]{1,0:T(8,128)}, f32[2,3]{1,0:T(2,128)}) custom-call(s32[1]{0:T(128)} %bitcast.box, f32[32,128]{1,0:T(8,128)S(1)} %bitcast.8, f32[64,128]{1,0:T(8,128)S(1)} %get-tuple-element.44.refs_4_.refs_0_.refs_1_, f32[32,128]{1,0:T(8,128)S(1)} %get-tuple-element.45.refs_5_.refs_8_.refs_2_, f32[32,128]{1,0:T(8,128)S(1)} %get-tuple-element.49.refs_3_, ...), custom_call_target="tpu_custom_call" | custom-call | tf_op jit(solution)/shard_map/pallas_call | solution.py:40
  (2 shorter events, 0.0 us)
Async XLA Ops:
  4.7 5.6 %collective-permute-start = (f32[72,128]{1,0:T(8,128)S(1)}, f32[72,128]{1,0:T(8,128)S(1)}, u32[]{:S(2)}, u32[]{:S(2)}) collective-permute-start(f32[72,128]{1,0:T(8,128)S(1)} %get-tuple-element.29.refs_0_), channel_id=1, source_target_pairs={{0,1},{1,0},{2,3},{3,2},{4,5},{5,4},{6,7},{7,6},{8,9},{9,8},{10,11... | collective-permute-start | bytes 110600 | tf_op jit(solution)/shard_map/ppermute | solution.py:25
  5.2 5.2 %collective-permute-start.1 = (f32[72,128]{1,0:T(8,128)S(1)}, f32[72,128]{1,0:T(8,128)S(1)}, u32[]{:S(2)}, u32[]{:S(2)}) collective-permute-start(f32[72,128]{1,0:T(8,128)S(1)} %get-tuple-element.29.refs_0_), channel_id=1, source_target_pairs={{0,2},{1,3},{2,0},{3,1},{4,6},{5,7},{6,4},{7,5},{8,10},{9,11},{10,... | collective-permute-start | bytes 110600 | tf_op jit(solution)/shard_map/ppermute | solution.py:25
  7.7 3.4 %collective-permute-start.2 = (f32[72,128]{1,0:T(8,128)S(1)}, f32[72,128]{1,0:T(8,128)S(1)}, u32[]{:S(2)}, u32[]{:S(2)}) collective-permute-start(f32[72,128]{1,0:T(8,128)S(1)} %get-tuple-element.29.refs_0_), channel_id=1, source_target_pairs={{0,3},{1,2},{2,1},{3,0},{4,7},{5,6},{6,5},{7,4},{8,11},{9,10},{10,... | collective-permute-start | bytes 110600 | tf_op jit(solution)/shard_map/ppermute | solution.py:25
  7.8 7.6 %collective-permute-start.6 = (f32[32,8,128]{2,1,0:T(8,128)S(1)}, f32[32,8,128]{2,1,0:T(8,128)S(1)}, u32[]{:S(2)}, u32[]{:S(2)}) collective-permute-start(f32[32,8,128]{2,1,0:T(8,128)S(1)} %get-tuple-element.35.refs_0_), channel_id=1, source_target_pairs={{0,1},{1,0},{2,3},{3,2},{4,5},{5,4},{6,7},{7,6},{8,9},{9,8},{10,11... | collective-permute-start | bytes 393224 | tf_op jit(solution)/shard_map/ppermute | solution.py:25
  7.9 8.9 %collective-permute-start.7 = (f32[32,8,128]{2,1,0:T(8,128)S(1)}, f32[32,8,128]{2,1,0:T(8,128)S(1)}, u32[]{:S(2)}, u32[]{:S(2)}) collective-permute-start(f32[32,8,128]{2,1,0:T(8,128)S(1)} %get-tuple-element.35.refs_0_), channel_id=1, source_target_pairs={{0,2},{1,3},{2,0},{3,1},{4,6},{5,7},{6,4},{7,5},{8,10},{9,11},{10,... | collective-permute-start | bytes 393224 | tf_op jit(solution)/shard_map/ppermute | solution.py:25
  10.2 6.6 %collective-permute-start.8 = (f32[32,8,128]{2,1,0:T(8,128)S(1)}, f32[32,8,128]{2,1,0:T(8,128)S(1)}, u32[]{:S(2)}, u32[]{:S(2)}) collective-permute-start(f32[32,8,128]{2,1,0:T(8,128)S(1)} %get-tuple-element.35.refs_0_), channel_id=1, source_target_pairs={{0,3},{1,2},{2,1},{3,0},{4,7},{5,6},{6,5},{7,4},{8,11},{9,10},{10,... | collective-permute-start | bytes 393224 | tf_op jit(solution)/shard_map/ppermute | solution.py:25
  11.2 11.8 %collective-permute-start.3 = (f32[160,128]{1,0:T(8,128)S(1)}, f32[160,128]{1,0:T(8,128)S(1)}, u32[]{:S(2)}, u32[]{:S(2)}) collective-permute-start(f32[160,128]{1,0:T(8,128)S(1)} %get-tuple-element.34.refs_0_), channel_id=1, source_target_pairs={{0,4},{4,0},{8,12},{12,8},{1,5},{5,1},{9,13},{13,9},{2,6},{6,2},{1... | collective-permute-start | bytes 245768 | tf_op jit(solution)/shard_map/ppermute | solution.py:25
  12.8 10.1 %collective-permute-start.4 = (f32[160,128]{1,0:T(8,128)S(1)}, f32[160,128]{1,0:T(8,128)S(1)}, u32[]{:S(2)}, u32[]{:S(2)}) collective-permute-start(f32[160,128]{1,0:T(8,128)S(1)} %get-tuple-element.34.refs_0_), channel_id=1, source_target_pairs={{0,8},{4,12},{8,0},{12,4},{1,9},{5,13},{9,1},{13,5},{2,10},{6,14},... | collective-permute-start | bytes 245768 | tf_op jit(solution)/shard_map/ppermute | solution.py:25
  15.4 7.6 %collective-permute-start.5 = (f32[160,128]{1,0:T(8,128)S(1)}, f32[160,128]{1,0:T(8,128)S(1)}, u32[]{:S(2)}, u32[]{:S(2)}) collective-permute-start(f32[160,128]{1,0:T(8,128)S(1)} %get-tuple-element.34.refs_0_), channel_id=1, source_target_pairs={{0,12},{4,8},{8,4},{12,0},{1,13},{5,9},{9,5},{13,1},{2,14},{6,10},... | collective-permute-start | bytes 245768 | tf_op jit(solution)/shard_map/ppermute | solution.py:25
  23.6 4.1 %collective-permute-start.10 = (f32[64,128]{1,0:T(8,128)S(1)}, f32[64,128]{1,0:T(8,128)S(1)}, u32[]{:S(2)}, u32[]{:S(2)}) collective-permute-start(f32[64,128]{1,0:T(8,128)S(1)} %get-tuple-element.44.refs_4_.refs_0_.refs_1_), channel_id=1, source_target_pairs={{0,2},{1,3},{2,0},{3,1},{4,6},{5,7},{6,4},{7,5},{8,10},{9,11},{10,... | collective-permute-start | bytes 98312 | tf_op jit(solution)/shard_map/ppermute | solution.py:25
  24.4 3.5 %collective-permute-start.11 = (f32[64,128]{1,0:T(8,128)S(1)}, f32[64,128]{1,0:T(8,128)S(1)}, u32[]{:S(2)}, u32[]{:S(2)}) collective-permute-start(f32[64,128]{1,0:T(8,128)S(1)} %get-tuple-element.44.refs_4_.refs_0_.refs_1_), channel_id=1, source_target_pairs={{0,3},{1,2},{2,1},{3,0},{4,7},{5,6},{6,5},{7,4},{8,11},{9,10},{10,... | collective-permute-start | bytes 98312 | tf_op jit(solution)/shard_map/ppermute | solution.py:25
  25.1 2.9 %collective-permute-start.9 = (f32[64,128]{1,0:T(8,128)S(1)}, f32[64,128]{1,0:T(8,128)S(1)}, u32[]{:S(2)}, u32[]{:S(2)}) collective-permute-start(f32[64,128]{1,0:T(8,128)S(1)} %get-tuple-element.44.refs_4_.refs_0_.refs_1_), channel_id=1, source_target_pairs={{0,1},{1,0},{2,3},{3,2},{4,5},{5,4},{6,7},{7,6},{8,9},{9,8},{10,11... | collective-permute-start | bytes 98312 | tf_op jit(solution)/shard_map/ppermute | solution.py:25

commit v15 on v14

--- a/solution.py
+++ b/solution.py
@@ -245,16 +245,14 @@
     write_weights(box_coupling, box_weights)
 
 
-def leaf_kernel(counts, moments, basis, picks, weights, far):
-    slots, rank, width = basis.shape
-    columns = wide_transpose(leaf_part(moments[:, 0:rank], picks, weights))
-    for leaf in range(slots):
-        far[leaf : leaf + 1, :] = leaf_far_row(counts, columns, basis, leaf, 0.0)
+def leaf_kernel(moments, picks, weights, columns):
+    rank = weights.shape[1]
+    columns[...] = wide_transpose(leaf_part(moments[:, 0:rank], picks, weights))
 
 
 def first_near_kernel(subs, box, counts, *refs):
-    geometry, (far, near_source) = refs[:subs], refs[subs : subs + 2]
-    near, initial, values, features, squares, fields, inner, near_list, arrived = refs[subs + 2 :]
+    geometry, (columns, basis, near_source) = refs[:subs], refs[subs : subs + 3]
+    near, initial, values, features, squares, fields, inner, near_list, arrived = refs[subs + 3 :]
     copy = pltpu.make_async_copy(near_source, near_list, arrived)
     copy.start()
     slots, height, width = geometry[0].shape
@@ -288,7 +286,10 @@
 
     own = geometry[0]
 
-    def target(leaf, carry):
+    copy.wait()
+    initial[...] = fields[0:slots, :]
+    locals_of = columns[...]
+    for leaf in range(slots):
         plain = own[leaf]
         shifted = pltpu.roll(plain, 3, 0)
         square = squares[pl.ds(leaf, 1), :]
@@ -305,14 +306,8 @@
             tile = both[:, width : 2 * width] * (inverse * inverse * inverse)
             values[leaf * neighbours + column] = tile
             total = total + tile * fields[pl.ds(place, 1), :]
-        near[pl.ds(leaf, 1), :] = jnp.sum(total.T, axis=0, keepdims=True)
-        return carry
-
-    copy.wait()
-    initial[...] = fields[0:slots, :]
-    lax.fori_loop(0, slots, target, 0, unroll=True)
-    in_use = iota((slots, width), 0) < counts[0]
-    near[...] = jnp.where(in_use, near[...] + far[...], 0.0)
+        near_row = jnp.sum(total.T, axis=0, keepdims=True)
+        near[leaf : leaf + 1, :] = leaf_far_row(counts, locals_of, basis, leaf, near_row)
 
 
 def box_images(box_basis, coefficients, image):
@@ -578,12 +573,12 @@
         cost=FIRST,
     )
     boxes = from_peers(blocks, "patch")
-    (far,) = device_call(leaf_kernel, [rows], [counts], [moments, leaf_basis, picks, weights])
+    (columns,) = device_call(leaf_kernel, [kept(LANES, slots)], [], [moments, picks, weights])
     part, initial, values = device_call(
         functools.partial(first_near_kernel, subs),
         [rows, rows, kept(slots * neighbours, width, width)],
         [box, counts],
-        [*geometry, far, near_list],
+        [*geometry, columns, leaf_basis, near_list],
         [
             pltpu.VMEM((sources, 32, 2 * width), jnp.bfloat16),
             block,

time: 44.9 us -> 44.6 us (level)
  transfers between devices with their start and end apart: 12 -> 12, of which waited for: 3 -> 4; matrix products, arithmetic and copies ran while one was open for 0% -> 0% of each run, Pallas kernels for 18% -> 17%
where the time goes in v15:
time: 44.6 us; the launch traced here: 44.4 us
  Pallas kernels  16.4 us (37%)
  starting transfers between devices  11.9 us (27%)
  blocking collectives  11.7 us (26%)
  waiting for transfers between devices  3.06 us (7%)
  between operations  1.39 us (3%)
    pallas_call x9, Pallas kernels, device_call(): pl.pallas_call(kernel, out_shape=tuple(outputs), in_specs=[smem] * len(sc...  16.4 us
    ppermute x12, starting transfers between devices, from_peers(): lax.ppermute(value, axis, [(i, i ^ turn) for i in range(size)])  11.9 us
    all_to_all x1, blocking collectives, shards(): shares = lax.all_to_all(shares, ('patch', 'sub'), 0, 0, tiled=True)  11.7 us
    ppermute x12, waiting for transfers between devices, from_peers(): lax.ppermute(value, axis, [(i, i ^ turn) for i in range(size)])  3.06 us
  transfers between devices with their start and end apart: 12, of which 4 were waited for; matrix products, arithmetic and copies ran while one was open for 0% of the time, Pallas kernels for 17%

profile of v15, /device:TPU:0, one launch (start us, length us, event | category | flops | bytes accessed | tf_op | source)
XLA Modules:
  0.0 44.4 jit_solution(10306419296991787028)
XLA Ops:
  1.3 3.4 %shard_map.122 = (f32[32,8,128]{2,1,0:T(8,128)S(1)}, f32[72,128]{1,0:T(8,128)S(1)}, f32[32,64,128]{2,1,0:T(8,128)S(1)}, f32[32,64,128]{2,1,0:T(8,128)S(1)}, f32[...) custom-call(s32[1]{0:T(128)S(6)} %copy.13.counts, ...), custom_call_target="tpu_custom_call" | custom-call | tf_op jit(solution)/shard_map/pallas_call | solution.py:40
  4.7 0.5 %collective-permute-start = (f32[72,128]{1,0:T(8,128)S(1)}, f32[72,128]{1,0:T(8,128)S(1)}, u32[]{:S(2)}, u32[]{:S(2)}) collective-permute-start(f32[72,128]{1,0:T(8,128)S(1)} %get-tuple-element.29.refs_0_), channel_id=1, source_target_pairs={{0,1},{1,0},{2,3},{3,2},{4,5},{5,4},{6,7},{7,6},{8,9},{9,8},{10,11... | collective-permute-start | bytes 110600 | tf_op jit(solution)/shard_map/ppermute | solution.py:25
  5.2 2.6 %collective-permute-start.1 = (f32[72,128]{1,0:T(8,128)S(1)}, f32[72,128]{1,0:T(8,128)S(1)}, u32[]{:S(2)}, u32[]{:S(2)}) collective-permute-start(f32[72,128]{1,0:T(8,128)S(1)} %get-tuple-element.29.refs_0_), channel_id=1, source_target_pairs={{0,2},{1,3},{2,0},{3,1},{4,6},{5,7},{6,4},{7,5},{8,10},{9,11},{10,... | collective-permute-start | bytes 110600 | tf_op jit(solution)/shard_map/ppermute | solution.py:25
  7.7 0.1 collective-permute-start.2
  7.8 0.1 collective-permute-start.6
  7.9 1.9 %collective-permute-start.7 = (f32[32,8,128]{2,1,0:T(8,128)S(1)}, f32[32,8,128]{2,1,0:T(8,128)S(1)}, u32[]{:S(2)}, u32[]{:S(2)}) collective-permute-start(f32[32,8,128]{2,1,0:T(8,128)S(1)} %get-tuple-element.35.refs_0_), channel_id=1, source_target_pairs={{0,2},{1,3},{2,0},{3,1},{4,6},{5,7},{6,4},{7,5},{8,10},{9,11},{10,... | collective-permute-start | bytes 393224 | tf_op jit(solution)/shard_map/ppermute | solution.py:25
  9.9 0.4 shard_map.123
  10.2 0.0 collective-permute-done.refs_1_
  10.2 0.1 collective-permute-start.8
  10.3 0.0 collective-permute-done.1.refs_2_
  10.3 0.8 %collective-permute-done.2.refs_3_ = f32[72,128]{1,0:T(8,128)S(1)} collective-permute-done((f32[72,128]{1,0:T(8,128)S(1)}, f32[72,128]{1,0:T(8,128)S(1)}, u32[]{:S(2)}, u32[]{:S(2)}) %collective-permute-start.2) | collective-permute-done | bytes 36896 | tf_op jit(solution)/shard_map/ppermute | solution.py:25
  11.2 1.6 %collective-permute-start.3 = (f32[160,128]{1,0:T(8,128)S(1)}, f32[160,128]{1,0:T(8,128)S(1)}, u32[]{:S(2)}, u32[]{:S(2)}) collective-permute-start(f32[160,128]{1,0:T(8,128)S(1)} %get-tuple-element.34.refs_0_), channel_id=1, source_target_pairs={{0,4},{4,0},{8,12},{12,8},{1,5},{5,1},{9,13},{13,9},{2,6},{6,2},{1... | collective-permute-start | bytes 245768 | tf_op jit(solution)/shard_map/ppermute | solution.py:25
  12.8 2.6 %collective-permute-start.4 = (f32[160,128]{1,0:T(8,128)S(1)}, f32[160,128]{1,0:T(8,128)S(1)}, u32[]{:S(2)}, u32[]{:S(2)}) collective-permute-start(f32[160,128]{1,0:T(8,128)S(1)} %get-tuple-element.34.refs_0_), channel_id=1, source_target_pairs={{0,8},{4,12},{8,0},{12,4},{1,9},{5,13},{9,1},{13,5},{2,10},{6,14},... | collective-permute-start | bytes 245768 | tf_op jit(solution)/shard_map/ppermute | solution.py:25
  15.4 0.0 collective-permute-done.6.refs_1_
  15.4 0.2 collective-permute-start.5
  15.6 0.8 %shard_map.125.refs_4_ = f32[128,32]{1,0:T(8,128)S(1)} custom-call(f32[128,128]{1,0:T(8,128)S(1)} %get-tuple-element.36.moments, bf16[256,128]{1,0:T(8,128)(2,1)S(1)} %get-tuple-element.37.picks.refs_4_, bf16[8,64,192]{2,1,0:T(8,128)(2,1)S(1)} %get-tuple-element.38.weights.refs_5_), custom_call_target="tpu_custom_call" | custom-call | tf_op jit(solution)/shard_map/pallas_call | solution.py:40
  16.4 0.0 collective-permute-done.7.refs_2_
  16.4 0.4 collective-permute-done.8.refs_3_
  16.8 6.1 %shard_map.126 = (f32[32,128]{1,0:T(8,128)S(1)}, f32[32,128]{1,0:T(8,128)S(1)}, f32[288,128,128]{2,1,0:T(8,128)S(1)}) custom-call(s32[1]{0:T(128)} %bitcast.box, s32[1]{0:T(128)S(6)} %copy.13.counts, f32[32,8,128]{2,1,0:T(8,128)S(1)} %get-tuple-element.35.refs_0_, f32[32,8,128]{2,1,0:T(8,128)S(1)} %collective-permute-done.6.refs_1_, ...), custom_call_target="tpu_custom_call" | custom-call | tf_op jit(solution)/shard_map/pallas_call | solution.py:40
  22.9 0.0 collective-permute-done.3.refs_1_
  22.9 0.0 collective-permute-done.4.refs_2_
  22.9 0.0 collective-permute-done.5.refs_3_
  22.9 0.6 %shard_map.127 = (f32[64,128]{1,0:T(8,128)S(1)}, f32[32,128]{1,0:T(8,128)S(1)}, f32[8,128]{1,0:T(8,128)S(1)}) custom-call(s32[1]{0:T(128)} %bitcast.box, f32[160,128]{1,0:T(8,128)S(1)} %get-tuple-element.34.refs_0_, f32[160,128]{1,0:T(8,128)S(1)} %collective-permute-done.3.refs_1_, f32[160,128]{1,0:T(8,128)S(1)} %collective-permute-done.4.refs_2_, ...), custom_call_target="tpu_custom_call" | custom-call | tf_op jit(solution)/shard_map/pallas_call | solution.py:40
  23.6 0.7 %collective-permute-start.10 = (f32[64,128]{1,0:T(8,128)S(1)}, f32[64,128]{1,0:T(8,128)S(1)}, u32[]{:S(2)}, u32[]{:S(2)}) collective-permute-start(f32[64,128]{1,0:T(8,128)S(1)} %get-tuple-element.44.refs_4_.refs_0_.refs_1_), channel_id=1, source_target_pairs={{0,2},{1,3},{2,0},{3,1},{4,6},{5,7},{6,4},{7,5},{8,10},{9,11},{10,... | collective-permute-start | bytes 98312 | tf_op jit(solution)/shard_map/ppermute | solution.py:25
  24.3 0.8 %collective-permute-start.11 = (f32[64,128]{1,0:T(8,128)S(1)}, f32[64,128]{1,0:T(8,128)S(1)}, u32[]{:S(2)}, u32[]{:S(2)}) collective-permute-start(f32[64,128]{1,0:T(8,128)S(1)} %get-tuple-element.44.refs_4_.refs_0_.refs_1_), channel_id=1, source_target_pairs={{0,3},{1,2},{2,1},{3,0},{4,7},{5,6},{6,5},{7,4},{8,11},{9,10},{10,... | collective-permute-start | bytes 98312 | tf_op jit(solution)/shard_map/ppermute | solution.py:25
  25.1 0.6 %collective-permute-start.9 = (f32[64,128]{1,0:T(8,128)S(1)}, f32[64,128]{1,0:T(8,128)S(1)}, u32[]{:S(2)}, u32[]{:S(2)}) collective-permute-start(f32[64,128]{1,0:T(8,128)S(1)} %get-tuple-element.44.refs_4_.refs_0_.refs_1_), channel_id=1, source_target_pairs={{0,1},{1,0},{2,3},{3,2},{4,5},{5,4},{6,7},{7,6},{8,9},{9,8},{10,11... | collective-permute-start | bytes 98312 | tf_op jit(solution)/shard_map/ppermute | solution.py:25
  25.7 0.3 shard_map.128
  26.0 1.7 %collective-permute-done.10.refs_2_ = f32[64,128]{1,0:T(8,128)S(1)} collective-permute-done((f32[64,128]{1,0:T(8,128)S(1)}, f32[64,128]{1,0:T(8,128)S(1)}, u32[]{:S(2)}, u32[]{:S(2)}) %collective-permute-start.10) | collective-permute-done | bytes 32800 | tf_op jit(solution)/shard_map/ppermute | solution.py:25
  27.7 0.1 collective-permute-done.11.refs_3_
  27.9 2.8 %shard_map.129 = (f32[32,128]{1,0:T(8,128)S(1)}, f32[32,128]{1,0:T(8,128)S(1)}) custom-call(s32[1]{0:T(128)} %bitcast.box, s32[1]{0:T(128)S(6)} %copy.13.counts, f32[64,128]{1,0:T(8,128)S(1)} %get-tuple-element.44.refs_4_.refs_0_.refs_1_, f32[64,128]{1,0:T(8,128)S(1)} %collective-permute-done.9.refs_1_, f32[64,128]{1,0:T(8,128)S(1)} %collective-permute-done.10.refs_2_, ...), custom_call_target="tpu_custom_call" | custom-call | tf_op jit(solution)/shard_map/pallas_call | solution.py:40
  30.6 11.7 %all_to_all.11 = f32[16,2,128]{2,1,0:T(2,128)S(1)} all-to-all(f32[16,2,128]{2,1,0:T(2,128)S(1)} %bitcast.9), channel_id=1, replica_groups=mesh['groups'=2,'patch'=4,'sub'=4] {'patch','sub'}, dimensions={0} | all-to-all | bytes 32768 | tf_op jit(solution)/shard_map/all_to_all | solution.py:624
  42.3 2.1 %shard_map.130 = (f32[32,128]{1,0:T(8,128)}, f32[2,3]{1,0:T(2,128)}) custom-call(s32[1]{0:T(128)} %bitcast.box, f32[32,128]{1,0:T(8,128)S(1)} %bitcast.8, f32[64,128]{1,0:T(8,128)S(1)} %get-tuple-element.44.refs_4_.refs_0_.refs_1_, f32[32,128]{1,0:T(8,128)S(1)} %get-tuple-element.45.refs_5_.refs_8_.refs_2_, f32[32,128]{1,0:T(8,128)S(1)} %get-tuple-element.49.refs_3_, ...), custom_call_target="tpu_custom_call" | custom-call | tf_op jit(solution)/shard_map/pallas_call | solution.py:40
  (2 shorter events, 0.0 us)
Async XLA Ops:
  4.7 5.6 %collective-permute-start = (f32[72,128]{1,0:T(8,128)S(1)}, f32[72,128]{1,0:T(8,128)S(1)}, u32[]{:S(2)}, u32[]{:S(2)}) collective-permute-start(f32[72,128]{1,0:T(8,128)S(1)} %get-tuple-element.29.refs_0_), channel_id=1, source_target_pairs={{0,1},{1,0},{2,3},{3,2},{4,5},{5,4},{6,7},{7,6},{8,9},{9,8},{10,11... | collective-permute-start | bytes 110600 | tf_op jit(solution)/shard_map/ppermute | solution.py:25
  5.2 5.2 %collective-permute-start.1 = (f32[72,128]{1,0:T(8,128)S(1)}, f32[72,128]{1,0:T(8,128)S(1)}, u32[]{:S(2)}, u32[]{:S(2)}) collective-permute-start(f32[72,128]{1,0:T(8,128)S(1)} %get-tuple-element.29.refs_0_), channel_id=1, source_target_pairs={{0,2},{1,3},{2,0},{3,1},{4,6},{5,7},{6,4},{7,5},{8,10},{9,11},{10,... | collective-permute-start | bytes 110600 | tf_op jit(solution)/shard_map/ppermute | solution.py:25
  7.7 3.4 %collective-permute-start.2 = (f32[72,128]{1,0:T(8,128)S(1)}, f32[72,128]{1,0:T(8,128)S(1)}, u32[]{:S(2)}, u32[]{:S(2)}) collective-permute-start(f32[72,128]{1,0:T(8,128)S(1)} %get-tuple-element.29.refs_0_), channel_id=1, source_target_pairs={{0,3},{1,2},{2,1},{3,0},{4,7},{5,6},{6,5},{7,4},{8,11},{9,10},{10,... | collective-permute-start | bytes 110600 | tf_op jit(solution)/shard_map/ppermute | solution.py:25
  7.8 7.6 %collective-permute-start.6 = (f32[32,8,128]{2,1,0:T(8,128)S(1)}, f32[32,8,128]{2,1,0:T(8,128)S(1)}, u32[]{:S(2)}, u32[]{:S(2)}) collective-permute-start(f32[32,8,128]{2,1,0:T(8,128)S(1)} %get-tuple-element.35.refs_0_), channel_id=1, source_target_pairs={{0,1},{1,0},{2,3},{3,2},{4,5},{5,4},{6,7},{7,6},{8,9},{9,8},{10,11... | collective-permute-start | bytes 393224 | tf_op jit(solution)/shard_map/ppermute | solution.py:25
  7.9 8.5 %collective-permute-start.7 = (f32[32,8,128]{2,1,0:T(8,128)S(1)}, f32[32,8,128]{2,1,0:T(8,128)S(1)}, u32[]{:S(2)}, u32[]{:S(2)}) collective-permute-start(f32[32,8,128]{2,1,0:T(8,128)S(1)} %get-tuple-element.35.refs_0_), channel_id=1, source_target_pairs={{0,2},{1,3},{2,0},{3,1},{4,6},{5,7},{6,4},{7,5},{8,10},{9,11},{10,... | collective-permute-start | bytes 393224 | tf_op jit(solution)/shard_map/ppermute | solution.py:25
  10.2 6.5 %collective-permute-start.8 = (f32[32,8,128]{2,1,0:T(8,128)S(1)}, f32[32,8,128]{2,1,0:T(8,128)S(1)}, u32[]{:S(2)}, u32[]{:S(2)}) collective-permute-start(f32[32,8,128]{2,1,0:T(8,128)S(1)} %get-tuple-element.35.refs_0_), channel_id=1, source_target_pairs={{0,3},{1,2},{2,1},{3,0},{4,7},{5,6},{6,5},{7,4},{8,11},{9,10},{10,... | collective-permute-start | bytes 393224 | tf_op jit(solution)/shard_map/ppermute | solution.py:25
  11.2 11.7 %collective-permute-start.3 = (f32[160,128]{1,0:T(8,128)S(1)}, f32[160,128]{1,0:T(8,128)S(1)}, u32[]{:S(2)}, u32[]{:S(2)}) collective-permute-start(f32[160,128]{1,0:T(8,128)S(1)} %get-tuple-element.34.refs_0_), channel_id=1, source_target_pairs={{0,4},{4,0},{8,12},{12,8},{1,5},{5,1},{9,13},{13,9},{2,6},{6,2},{1... | collective-permute-start | bytes 245768 | tf_op jit(solution)/shard_map/ppermute | solution.py:25
  12.8 10.1 %collective-permute-start.4 = (f32[160,128]{1,0:T(8,128)S(1)}, f32[160,128]{1,0:T(8,128)S(1)}, u32[]{:S(2)}, u32[]{:S(2)}) collective-permute-start(f32[160,128]{1,0:T(8,128)S(1)} %get-tuple-element.34.refs_0_), channel_id=1, source_target_pairs={{0,8},{4,12},{8,0},{12,4},{1,9},{5,13},{9,1},{13,5},{2,10},{6,14},... | collective-permute-start | bytes 245768 | tf_op jit(solution)/shard_map/ppermute | solution.py:25
  15.4 7.5 %collective-permute-start.5 = (f32[160,128]{1,0:T(8,128)S(1)}, f32[160,128]{1,0:T(8,128)S(1)}, u32[]{:S(2)}, u32[]{:S(2)}) collective-permute-start(f32[160,128]{1,0:T(8,128)S(1)} %get-tuple-element.34.refs_0_), channel_id=1, source_target_pairs={{0,12},{4,8},{8,4},{12,0},{1,13},{5,9},{9,5},{13,1},{2,14},{6,10},... | collective-permute-start | bytes 245768 | tf_op jit(solution)/shard_map/ppermute | solution.py:25
  23.6 4.2 %collective-permute-start.10 = (f32[64,128]{1,0:T(8,128)S(1)}, f32[64,128]{1,0:T(8,128)S(1)}, u32[]{:S(2)}, u32[]{:S(2)}) collective-permute-start(f32[64,128]{1,0:T(8,128)S(1)} %get-tuple-element.44.refs_4_.refs_0_.refs_1_), channel_id=1, source_target_pairs={{0,2},{1,3},{2,0},{3,1},{4,6},{5,7},{6,4},{7,5},{8,10},{9,11},{10,... | collective-permute-start | bytes 98312 | tf_op jit(solution)/shard_map/ppermute | solution.py:25
  24.3 3.6 %collective-permute-start.11 = (f32[64,128]{1,0:T(8,128)S(1)}, f32[64,128]{1,0:T(8,128)S(1)}, u32[]{:S(2)}, u32[]{:S(2)}) collective-permute-start(f32[64,128]{1,0:T(8,128)S(1)} %get-tuple-element.44.refs_4_.refs_0_.refs_1_), channel_id=1, source_target_pairs={{0,3},{1,2},{2,1},{3,0},{4,7},{5,6},{6,5},{7,4},{8,11},{9,10},{10,... | collective-permute-start | bytes 98312 | tf_op jit(solution)/shard_map/ppermute | solution.py:25
  25.1 2.7 %collective-permute-start.9 = (f32[64,128]{1,0:T(8,128)S(1)}, f32[64,128]{1,0:T(8,128)S(1)}, u32[]{:S(2)}, u32[]{:S(2)}) collective-permute-start(f32[64,128]{1,0:T(8,128)S(1)} %get-tuple-element.44.refs_4_.refs_0_.refs_1_), channel_id=1, source_target_pairs={{0,1},{1,0},{2,3},{3,2},{4,5},{5,4},{6,7},{7,6},{8,9},{9,8},{10,11... | collective-permute-start | bytes 98312 | tf_op jit(solution)/shard_map/ppermute | solution.py:25
